TPU v7x, 128 devices: a whole 4x4x4 slice. The times are simulated.
128 devices in a mesh: fsdp: 4 (over x_lo, core), ctx: 32 (over y, z, x_hi).
Axes of the slice: x: 4 (x_hi: 2, x_lo: 2; x = x_hi * 2 + x_lo), y: 4, z: 4, core: 2. Of those that a mesh axis runs over, the one named last changes fastest.
Arguments:
- tokens: bfloat16 [4, 4096, 768], P('fsdp', 'ctx'), may hold values from -6 to 6
- cotangent: bfloat16 [4, 4096, 768], P('fsdp', 'ctx'), may hold values from -6 to 6
- ln1_gain: bfloat16 [2, 768], P(None, 'fsdp'), may hold values from 0.5 to 1.5
- ln1_bias: bfloat16 [2, 768], P(None, 'fsdp'), may hold values from -1.5 to 1.5
- ln2_gain: bfloat16 [2, 768], P(None, 'fsdp'), may hold values from 0.5 to 1.5
- ln2_bias: bfloat16 [2, 768], P(None, 'fsdp'), may hold values from -1.5 to 1.5
- qkv_weight: bfloat16 [2, 768, 2304], P(None, 'fsdp'), may hold values from -0.3125 to 0.3125
- qkv_bias: bfloat16 [2, 2304], P(None, 'fsdp'), may hold values from -2.5 to 2.5
- out_weight: bfloat16 [2, 768, 768], P(None, 'fsdp'), may hold values from -0.625 to 0.625
- out_bias: bfloat16 [2, 768], P(None, 'fsdp'), may hold values from -1.5 to 1.5
- up_weight: bfloat16 [2, 768, 3072], P(None, 'fsdp'), may hold values from -0.21875 to 0.21875
- up_bias: bfloat16 [2, 3072], P(None, 'fsdp'), may hold values from -2.5 to 2.5
- down_weight: bfloat16 [2, 3072, 768], P(None, 'fsdp'), may hold values from -0.109375 to 0.109375
- down_bias: bfloat16 [2, 768], P(None, 'fsdp'), may hold values from -1.5 to 1.5
Outputs:
- output: bfloat16 [4, 4096, 768], P('fsdp', 'ctx')
- input_grad: float32 [4, 4096, 768], P('fsdp', 'ctx')
- ln1_gain_grad: float32 [2, 768], P(None, 'fsdp')
- ln1_bias_grad: float32 [2, 768], P(None, 'fsdp')
- ln2_gain_grad: float32 [2, 768], P(None, 'fsdp')
- ln2_bias_grad: float32 [2, 768], P(None, 'fsdp')
- qkv_weight_grad: float32 [2, 768, 2304], P(None, 'fsdp')
- qkv_bias_grad: float32 [2, 2304], P(None, 'fsdp')
- out_weight_grad: float32 [2, 768, 768], P(None, 'fsdp')
- out_bias_grad: float32 [2, 768], P(None, 'fsdp')
- up_weight_grad: float32 [2, 768, 3072], P(None, 'fsdp')
- up_bias_grad: float32 [2, 3072], P(None, 'fsdp')
- down_weight_grad: float32 [2, 3072, 768], P(None, 'fsdp')
- down_bias_grad: float32 [2, 768], P(None, 'fsdp')
All inputs are finite; a program needn't handle non-finite values.
Results may differ from a plain program's by a relative error of at most 0.04.
Values may be sent and summed in bfloat16 or wider, within the bound.
A program may use at most 256 MiB of HBM per device.

v0:
```python
import jax
import jax.numpy as jnp
from jax import lax
from jax.sharding import PartitionSpec as P

D = 768
HEADS = 12
HEAD_DIM = 64
ROTARY = 16
LAYERS = 2


epsilon = 1e-05
masked_score = -1e30


def layer_norm(values, norm_gain, norm_bias):
    centre = jnp.mean(values, -1, keepdims=True)
    shifted = values - centre
    spread = jnp.mean(shifted * shifted, -1, keepdims=True)
    return shifted * lax.rsqrt(spread + epsilon) * norm_gain + norm_bias


def rotate(values, positions):
    half_rot = ROTARY // 2
    exponent = jnp.arange(half_rot, dtype=jnp.float32) * (2.0 / ROTARY)
    frequency = jnp.power(10000.0, -exponent)
    angle = positions.astype(jnp.float32)[:, None] * frequency[None, :]
    cosine = jnp.cos(angle)[:, None, :]
    sine_part = jnp.sin(angle)[:, None, :]
    first_half = values[..., :half_rot]
    second_half = values[..., half_rot:ROTARY]
    return jnp.concatenate(
        [
            first_half * cosine - second_half * sine_part,
            second_half * cosine + first_half * sine_part,
            values[..., ROTARY:],
        ],
        -1,
    )


def rotate_back(gradient, positions):
    _, pull_back = jax.vjp(lambda head_part: rotate(head_part, positions), jnp.zeros_like(gradient))
    return pull_back(gradient)[0]


def gelu_exact(values):
    return jax.nn.gelu(values, approximate=False)


def keep_state(same_state):
    return same_state


def attend_forward(queries, key_rows, value_rows, first_row):
    row_count = queries.shape[0]
    query_pos = first_row + jnp.arange(row_count, dtype=jnp.int32)
    last_row = first_row + row_count - 1

    def absorb(running, key_piece, first_key):
        key_block, value_block = key_piece
        piece_rows = key_block.shape[0]

        def update(state):
            row_top, row_total, weighted = state
            scores = (
                jnp.einsum("qhd,khd->hqk", queries, key_block, preferred_element_type=jnp.float32)
                * 0.125
            )
            key_pos = jnp.arange(piece_rows, dtype=jnp.int32)
            allowed = (key_pos[None, :] <= query_pos[:, None])[None]
            scores = jnp.where(allowed, scores, masked_score)
            new_top = jnp.maximum(row_top, jnp.max(scores, -1))
            weights = jnp.where(allowed, jnp.exp(scores - new_top[:, :, None]), 0.0)
            row_total = jnp.sum(weights, -1)
            weighted = jnp.einsum(
                "hqk,khd->qhd",
                weights.astype(jnp.bfloat16),
                value_block,
                preferred_element_type=jnp.float32,
            )
            return (new_top, row_total, weighted)

        return lax.cond(first_key <= last_row, update, keep_state, running)

    start_state = (
        jnp.full((HEADS, row_count), masked_score, jnp.float32),
        jnp.zeros((HEADS, row_count), jnp.float32),
        jnp.zeros((row_count, HEADS, HEAD_DIM), jnp.float32),
    )
    row_top, row_total, weighted = absorb(
        start_state,
        (
            lax.all_gather(key_rows, "ctx", axis=0, tiled=True),
            lax.all_gather(value_rows, "ctx", axis=0, tiled=True),
        ),
        jnp.int32(0),
    )
    mixed = weighted / jnp.transpose(row_total)[:, :, None]
    return (mixed, row_top + jnp.log(row_total))


def score_terms(
    query_block, grad_block, log_block, delta_block, key_block, value_block, query_pos, key_pos
):
    scores = (
        jnp.einsum("qhd,khd->hqk", query_block, key_block, preferred_element_type=jnp.float32)
        * 0.125
    )
    allowed = (key_pos[None, :] <= query_pos[:, None])[None]
    chances = jnp.where(allowed, jnp.exp(scores - log_block[:, :, None]), 0.0)
    grad_chance = jnp.einsum(
        "qhd,khd->hqk", grad_block, value_block, preferred_element_type=jnp.float32
    )
    grad_score = (chances * (grad_chance - delta_block[:, :, None])).astype(jnp.bfloat16)
    return (chances.astype(jnp.bfloat16), grad_score)


def attend_backward(queries, key_rows, value_rows, grad_mixed, mixed, log_total, first_row):
    row_count = queries.shape[0]
    head_shape = (row_count, HEADS, HEAD_DIM)
    query_pos = first_row + jnp.arange(row_count, dtype=jnp.int32)
    last_row = first_row + row_count - 1
    row_delta = jnp.transpose(jnp.sum(grad_mixed.astype(jnp.float32) * mixed, -1))
    seq_length = row_count * lax.axis_size("ctx")

    def absorb(running, key_piece, first_key):
        key_block, value_block = key_piece
        piece_rows = key_block.shape[0]

        def update(state):
            key_pos = jnp.arange(piece_rows, dtype=jnp.int32)
            chances_low, grad_score = score_terms(
                queries,
                grad_mixed,
                log_total,
                row_delta,
                key_block,
                value_block,
                query_pos,
                key_pos,
            )
            grad_query = (
                jnp.einsum(
                    "hqk,khd->qhd", grad_score, key_block, preferred_element_type=jnp.float32
                )
                * 0.125
            )
            grad_key = (
                jnp.einsum("hqk,qhd->khd", grad_score, queries, preferred_element_type=jnp.float32)
                * 0.125
            )
            grad_value = jnp.einsum(
                "hqk,qhd->khd", chances_low, grad_mixed, preferred_element_type=jnp.float32
            )
            fresh = jnp.stack(
                [grad_key.reshape(piece_rows, D), grad_value.reshape(piece_rows, D)], 1
            )
            return (grad_query, fresh)

        return lax.cond(first_key <= last_row, update, keep_state, running)

    start_state = (jnp.zeros(head_shape, jnp.float32), jnp.zeros((seq_length, 2, D), jnp.float32))
    grad_query, grad_pair = absorb(
        start_state,
        (
            lax.all_gather(key_rows, "ctx", axis=0, tiled=True),
            lax.all_gather(value_rows, "ctx", axis=0, tiled=True),
        ),
        jnp.int32(0),
    )
    own_rows = lax.psum_scatter(
        grad_pair.astype(jnp.bfloat16), "ctx", scatter_dimension=0, tiled=True
    ).astype(jnp.float32)
    return (grad_query, own_rows[:, 0].reshape(head_shape), own_rows[:, 1].reshape(head_shape))


def reduce_grads(collected):
    (
        part_gain_one,
        part_bias_one,
        part_gain_two,
        part_bias_two,
        part_qkv_w,
        part_qkv_b,
        part_out_w,
        part_out_b,
        part_up_w,
        part_up_b,
        part_down_w,
        part_down_b,
    ) = collected
    owned_parts = (
        lax.psum_scatter(
            part_gain_one.astype(jnp.bfloat16), "fsdp", scatter_dimension=0, tiled=True
        ).astype(jnp.float32),
        lax.psum_scatter(
            part_bias_one.astype(jnp.bfloat16), "fsdp", scatter_dimension=0, tiled=True
        ).astype(jnp.float32),
        lax.psum_scatter(
            part_gain_two.astype(jnp.bfloat16), "fsdp", scatter_dimension=0, tiled=True
        ).astype(jnp.float32),
        lax.psum_scatter(
            part_bias_two.astype(jnp.bfloat16), "fsdp", scatter_dimension=0, tiled=True
        ).astype(jnp.float32),
        lax.psum_scatter(
            part_qkv_w.astype(jnp.bfloat16), "fsdp", scatter_dimension=0, tiled=True
        ).astype(jnp.float32),
        lax.psum_scatter(
            part_qkv_b.astype(jnp.bfloat16), "fsdp", scatter_dimension=0, tiled=True
        ).astype(jnp.float32),
        lax.psum_scatter(
            part_out_w.astype(jnp.bfloat16), "fsdp", scatter_dimension=0, tiled=True
        ).astype(jnp.float32),
        lax.psum_scatter(
            part_out_b.astype(jnp.bfloat16), "fsdp", scatter_dimension=0, tiled=True
        ).astype(jnp.float32),
        lax.psum_scatter(
            part_up_w.astype(jnp.bfloat16), "fsdp", scatter_dimension=0, tiled=True
        ).astype(jnp.float32),
        lax.psum_scatter(
            part_up_b.astype(jnp.bfloat16), "fsdp", scatter_dimension=0, tiled=True
        ).astype(jnp.float32),
        lax.psum_scatter(
            part_down_w.astype(jnp.bfloat16), "fsdp", scatter_dimension=0, tiled=True
        ).astype(jnp.float32),
        lax.psum_scatter(
            part_down_b.astype(jnp.bfloat16), "fsdp", scatter_dimension=0, tiled=True
        ).astype(jnp.float32),
    )
    (
        own_gain_one,
        own_bias_one,
        own_gain_two,
        own_bias_two,
        own_qkv_w,
        own_qkv_b,
        own_out_w,
        own_out_b,
        own_up_w,
        own_up_b,
        own_down_w,
        own_down_b,
    ) = owned_parts
    return (
        lax.psum(own_gain_one.astype(jnp.bfloat16), "ctx").astype(jnp.float32),
        lax.psum(own_bias_one.astype(jnp.bfloat16), "ctx").astype(jnp.float32),
        lax.psum(own_gain_two.astype(jnp.bfloat16), "ctx").astype(jnp.float32),
        lax.psum(own_bias_two.astype(jnp.bfloat16), "ctx").astype(jnp.float32),
        lax.psum(own_qkv_w.astype(jnp.bfloat16), "ctx").astype(jnp.float32),
        lax.psum(own_qkv_b.astype(jnp.bfloat16), "ctx").astype(jnp.float32),
        lax.psum(own_out_w.astype(jnp.bfloat16), "ctx").astype(jnp.float32),
        lax.psum(own_out_b.astype(jnp.bfloat16), "ctx").astype(jnp.float32),
        lax.psum(own_up_w.astype(jnp.bfloat16), "ctx").astype(jnp.float32),
        lax.psum(own_up_b.astype(jnp.bfloat16), "ctx").astype(jnp.float32),
        lax.psum(own_down_w.astype(jnp.bfloat16), "ctx").astype(jnp.float32),
        lax.psum(own_down_b.astype(jnp.bfloat16), "ctx").astype(jnp.float32),
    )


def shards(
    tokens,
    cotangent,
    ln1_gain,
    ln1_bias,
    ln2_gain,
    ln2_bias,
    qkv_weight,
    qkv_bias,
    out_weight,
    out_bias,
    up_weight,
    up_bias,
    down_weight,
    down_bias,
):
    row_count = tokens.shape[1]
    first_row = lax.axis_index("ctx") * row_count
    positions = first_row + jnp.arange(row_count, dtype=jnp.int32)
    head_shape = (row_count, HEADS, HEAD_DIM)
    stream = tokens[0].astype(jnp.float32)
    saved = []
    for layer_index in range(LAYERS):
        fetched = (
            lax.all_gather(ln1_gain[layer_index], "fsdp", axis=0, tiled=True),
            lax.all_gather(ln1_bias[layer_index], "fsdp", axis=0, tiled=True),
            lax.all_gather(ln2_gain[layer_index], "fsdp", axis=0, tiled=True),
            lax.all_gather(ln2_bias[layer_index], "fsdp", axis=0, tiled=True),
            lax.all_gather(qkv_weight[layer_index], "fsdp", axis=0, tiled=True),
            lax.all_gather(qkv_bias[layer_index], "fsdp", axis=0, tiled=True),
            lax.all_gather(out_weight[layer_index], "fsdp", axis=0, tiled=True),
            lax.all_gather(out_bias[layer_index], "fsdp", axis=0, tiled=True),
            lax.all_gather(up_weight[layer_index], "fsdp", axis=0, tiled=True),
            lax.all_gather(up_bias[layer_index], "fsdp", axis=0, tiled=True),
            lax.all_gather(down_weight[layer_index], "fsdp", axis=0, tiled=True),
            lax.all_gather(down_bias[layer_index], "fsdp", axis=0, tiled=True),
        )
        (
            gain_one,
            bias_one,
            gain_two,
            bias_two,
            w_qkv,
            b_qkv,
            w_out,
            b_out,
            w_up,
            b_up,
            w_down,
            b_down,
        ) = fetched
        norm_one = layer_norm(
            stream, gain_one.astype(jnp.float32), bias_one.astype(jnp.float32)
        ).astype(jnp.bfloat16)
        norm_two = layer_norm(
            stream, gain_two.astype(jnp.float32), bias_two.astype(jnp.float32)
        ).astype(jnp.bfloat16)
        joined = jnp.dot(norm_one, w_qkv, preferred_element_type=jnp.float32) + b_qkv.astype(
            jnp.float32
        )
        queries = rotate(joined[:, :D].reshape(head_shape), positions).astype(jnp.bfloat16)
        key_rows = rotate(joined[:, D : 2 * D].reshape(head_shape), positions).astype(jnp.bfloat16)
        value_rows = joined[:, 2 * D :].reshape(head_shape).astype(jnp.bfloat16)
        mixed, log_total = attend_forward(queries, key_rows, value_rows, first_row)
        mixed_low = mixed.reshape(row_count, D).astype(jnp.bfloat16)
        attn_branch = jnp.dot(mixed_low, w_out, preferred_element_type=jnp.float32)
        hidden_pre = jnp.dot(norm_two, w_up, preferred_element_type=jnp.float32) + b_up.astype(
            jnp.float32
        )
        hidden_low = gelu_exact(hidden_pre).astype(jnp.bfloat16)
        mlp_branch = jnp.dot(hidden_low, w_down, preferred_element_type=jnp.float32)
        kept_weights = None
        saved.append(
            (
                stream,
                norm_one,
                norm_two,
                queries,
                key_rows,
                value_rows,
                mixed,
                log_total,
                mixed_low,
                hidden_pre,
                hidden_low,
                kept_weights,
            )
        )
        stream = (
            stream
            + attn_branch
            + b_out.astype(jnp.float32)
            + mlp_branch
            + b_down.astype(jnp.float32)
        )
    gradient = cotangent[0].astype(jnp.float32)
    owned = [None] * LAYERS
    for layer_index in range(LAYERS - 1, -1, -1):
        (
            stream_in,
            norm_one,
            norm_two,
            queries,
            key_rows,
            value_rows,
            mixed,
            log_total,
            mixed_low,
            hidden_pre,
            hidden_low,
            kept_weights,
        ) = saved[layer_index]
        fetched = (
            lax.all_gather(ln1_gain[layer_index], "fsdp", axis=0, tiled=True),
            lax.all_gather(ln1_bias[layer_index], "fsdp", axis=0, tiled=True),
            lax.all_gather(ln2_gain[layer_index], "fsdp", axis=0, tiled=True),
            lax.all_gather(ln2_bias[layer_index], "fsdp", axis=0, tiled=True),
            lax.all_gather(qkv_weight[layer_index], "fsdp", axis=0, tiled=True),
            lax.all_gather(qkv_bias[layer_index], "fsdp", axis=0, tiled=True),
            lax.all_gather(out_weight[layer_index], "fsdp", axis=0, tiled=True),
            lax.all_gather(out_bias[layer_index], "fsdp", axis=0, tiled=True),
            lax.all_gather(up_weight[layer_index], "fsdp", axis=0, tiled=True),
            lax.all_gather(up_bias[layer_index], "fsdp", axis=0, tiled=True),
            lax.all_gather(down_weight[layer_index], "fsdp", axis=0, tiled=True),
            lax.all_gather(down_bias[layer_index], "fsdp", axis=0, tiled=True),
        )
        (
            gain_one,
            bias_one,
            gain_two,
            bias_two,
            w_qkv,
            b_qkv,
            w_out,
            b_out,
            w_up,
            b_up,
            w_down,
            b_down,
        ) = fetched
        grad_low = gradient.astype(jnp.bfloat16)
        grad_mixed = (
            jnp.einsum("te,de->td", grad_low, w_out, preferred_element_type=jnp.float32)
            .reshape(head_shape)
            .astype(jnp.bfloat16)
        )
        grad_query, grad_key, grad_value = attend_backward(
            queries, key_rows, value_rows, grad_mixed, mixed, log_total, first_row
        )
        grad_joined = jnp.concatenate(
            [
                rotate_back(grad_query, positions).reshape(row_count, D),
                rotate_back(grad_key, positions).reshape(row_count, D),
                grad_value.reshape(row_count, D),
            ],
            -1,
        ).astype(jnp.bfloat16)
        grad_qkv_weight = jnp.einsum(
            "td,te->de", norm_one, grad_joined, preferred_element_type=jnp.float32
        )
        grad_qkv_bias = jnp.sum(grad_joined.astype(jnp.float32), 0)
        grad_norm_one = jnp.einsum(
            "te,de->td", grad_joined, w_qkv, preferred_element_type=jnp.float32
        )
        grad_out_weight = jnp.einsum(
            "td,te->de", mixed_low, grad_low, preferred_element_type=jnp.float32
        )
        grad_bias_sum = jnp.sum(gradient, 0)
        grad_hidden = jnp.einsum("te,fe->tf", grad_low, w_down, preferred_element_type=jnp.float32)
        _, gelu_pull = jax.vjp(gelu_exact, hidden_pre)
        grad_pre = gelu_pull(grad_hidden)[0].astype(jnp.bfloat16)
        grad_down_weight = jnp.einsum(
            "tf,te->fe", hidden_low, grad_low, preferred_element_type=jnp.float32
        )
        grad_up_weight = jnp.einsum(
            "td,tf->df", norm_two, grad_pre, preferred_element_type=jnp.float32
        )
        grad_up_bias = jnp.sum(grad_pre.astype(jnp.float32), 0)
        grad_norm_two = jnp.einsum("tf,df->td", grad_pre, w_up, preferred_element_type=jnp.float32)
        _, norm_pull_one = jax.vjp(
            layer_norm, stream_in, gain_one.astype(jnp.float32), bias_one.astype(jnp.float32)
        )
        input_one, grad_gain_one, grad_bias_one = norm_pull_one(grad_norm_one)
        _, norm_pull_two = jax.vjp(
            layer_norm, stream_in, gain_two.astype(jnp.float32), bias_two.astype(jnp.float32)
        )
        input_two, grad_gain_two, grad_bias_two = norm_pull_two(grad_norm_two)
        owned[layer_index] = reduce_grads(
            (
                grad_gain_one,
                grad_bias_one,
                grad_gain_two,
                grad_bias_two,
                grad_qkv_weight,
                grad_qkv_bias,
                grad_out_weight,
                grad_bias_sum,
                grad_up_weight,
                grad_up_bias,
                grad_down_weight,
                grad_bias_sum,
            )
        )
        gradient = gradient + input_one + input_two
    stacked = [
        jnp.stack([owned[layer_index][member_index] for layer_index in range(LAYERS)], 0)
        for member_index in range(12)
    ]
    return (
        stream.astype(jnp.bfloat16)[None],
        gradient[None],
        stacked[0],
        stacked[1],
        stacked[2],
        stacked[3],
        stacked[4],
        stacked[5],
        stacked[6],
        stacked[7],
        stacked[8],
        stacked[9],
        stacked[10],
        stacked[11],
    )


def solution(mesh):
    placed = (
        P("fsdp", "ctx", None),
        P("fsdp", "ctx", None),
        P(None, "fsdp"),
        P(None, "fsdp"),
        P(None, "fsdp"),
        P(None, "fsdp"),
        P(None, "fsdp", None),
        P(None, "fsdp"),
        P(None, "fsdp", None),
        P(None, "fsdp"),
        P(None, "fsdp", None),
        P(None, "fsdp"),
        P(None, "fsdp", None),
        P(None, "fsdp"),
    )
    return jax.shard_map(
        shards,
        mesh=mesh,
        in_specs=placed,
        out_specs=(
            P("fsdp", "ctx", None),
            P("fsdp", "ctx", None),
            P(None, "fsdp"),
            P(None, "fsdp"),
            P(None, "fsdp"),
            P(None, "fsdp"),
            P(None, "fsdp", None),
            P(None, "fsdp"),
            P(None, "fsdp", None),
            P(None, "fsdp"),
            P(None, "fsdp", None),
            P(None, "fsdp"),
            P(None, "fsdp", None),
            P(None, "fsdp"),
        ),
        check_vma=False,
    )
```

profile of v0, /device:TPU:0, one launch (start us, length us, event | category | flops | bytes accessed | tf_op | source)
XLA Modules:
  0.0 2191.7 jit_solution(15612756405096089153)
XLA Ops:
  7.2 2.9 fusion.153
  12.0 3.2 fusion.151
  21.1 13.0 all-reduce.43
  34.5 19.6 all-gather.45.cloned.1.call-done
  54.1 2.7 convolution_add_fusion.1
  61.5 5.6 all-gather.9
  67.2 40.6 %all-gather.49.cloned.1.call-done = bf16[1,768,3072]{2,1,0:T(8,128)(2,1)} async-done(((bf16[1,192,3072]{2,1,0:T(8,128)(2,1)}), bf16[1,768,3072]{2,1,0:T(8,128)(2,1)}) %all-gather.49.cloned.1.call-update) | async-done | bytes 4718608 | tf_op jit(solution)/shard_map/all_gather | solution.py:294
  107.8 8.4 multiply_convert_fusion.3
  116.2 45.7 %all-gather.51.cloned.1.call-done = bf16[1,3072,768]{2,1,0:T(8,128)(2,1)} async-done(((bf16[1,768,768]{2,1,0:T(8,128)(2,1)}), bf16[1,3072,768]{2,1,0:T(8,128)(2,1)}) %all-gather.51.cloned.1.call-update) | async-done | bytes 4718608 | tf_op jit(solution)/shard_map/all_gather | solution.py:296
  161.9 3.1 fusion.54
  165.0 112.2 %all-gather.39.cloned.1.call-done = bf16[4096,12,64]{0,2,1:T(8,128)(2,1)} async-done(((bf16[128,12,64]{0,2,1:T(8,128)(2,1)}), bf16[4096,12,64]{0,2,1:T(8,128)(2,1)}) %all-gather.39.cloned.1.call-update) | async-done | bytes 6291472 | tf_op jit(solution)/shard_map/all_gather | solution.py:96
  277.2 112.2 %all-gather.37.cloned.1.call-done = bf16[4096,12,64]{0,2,1:T(8,128)(2,1)} async-done(((bf16[128,12,64]{0,2,1:T(8,128)(2,1)}), bf16[4096,12,64]{0,2,1:T(8,128)(2,1)}) %all-gather.37.cloned.1.call-update) | async-done | bytes 6291472 | tf_op jit(solution)/shard_map/all_gather | solution.py:95
  389.5 41.2 %conditional.4 = (f32[12,128]{1,0:T(8,128)}, f32[12,128]{1,0:T(8,128)}, f32[128,12,64]{0,2,1:T(8,128)S(1)}, f32[12,128]{1,0:T(8,128)S(1)}) conditional(s32[]{:T(128)} %convert_element_type.153, () %tuple.44, (s32[128]{0:T(128)S(1)}, bf16[128,12,64]{0,2,1:T(8,128)(2,1)S(1)}, bf16[4096,12,64]{0,2,1:T(8,128)(2,1)}, bf16[4096,12,64]{0,2,1:T(8,128)(2,1)}) %tuple.45), branch_computations={%region_2.0_spmd, %region_3.6_spmd} | conditional | flops 1692924416 | bytes 90817056 | solution.py:85
  389.8 12.8 fusion
  403.2 13.4 fusion.6
  416.6 13.4 fusion.2
  434.1 19.5 all-gather.53.cloned.1.call-done
  460.6 109.3 %all-gather.43.cloned.1.call-done = bf16[4096,12,64]{0,2,1:T(8,128)(2,1)} async-done(((bf16[128,12,64]{0,2,1:T(8,128)(2,1)}), bf16[4096,12,64]{0,2,1:T(8,128)(2,1)}) %all-gather.43.cloned.1.call-update) | async-done | bytes 6291472 | tf_op jit(solution)/shard_map/all_gather | solution.py:96
  569.9 112.4 %all-gather.41.cloned.1.call-done = bf16[4096,12,64]{0,2,1:T(8,128)(2,1)} async-done(((bf16[128,12,64]{0,2,1:T(8,128)(2,1)}), bf16[4096,12,64]{0,2,1:T(8,128)(2,1)}) %all-gather.41.cloned.1.call-update) | async-done | bytes 6291472 | tf_op jit(solution)/shard_map/all_gather | solution.py:95
  682.3 41.3 %conditional.5 = (f32[12,128]{1,0:T(8,128)}, f32[12,128]{1,0:T(8,128)}, f32[128,12,64]{0,2,1:T(8,128)S(1)}, f32[12,128]{1,0:T(8,128)S(1)}) conditional(s32[]{:T(128)} %convert_element_type.153, () %tuple.46, (s32[128]{0:T(128)S(1)}, bf16[128,12,64]{0,2,1:T(8,128)(2,1)S(1)}, bf16[4096,12,64]{0,2,1:T(8,128)(2,1)}, ...), branch_computations={%region_8.9_spmd, %region_9.12_spmd} | conditional | flops 1692924416 | bytes 90817056 | solution.py:85
  682.7 12.8 fusion.12
  696.0 13.4 fusion.18
  709.4 13.5 fusion.14
  726.0 70.0 %conditional.6 = (f32[128,12,64]{0,2,1:T(8,128)S(1)}, bf16[4096,2,768]{0,2,1:T(8,128)(2,1)}) conditional(s32[]{:T(128)} %convert_element_type.153, () %tuple.48, (s32[128]{0:T(128)S(1)}, bf16[128,12,64]{0,2,1:T(8,128)(2,1)S(1)}, bf16[4096,12,64]{0,2,1:T(8,128)(2,1)}, f32[12,128]{1,0:T(8,128)}, f32[12,128]{1,0:T(8,128)S(1)}, ...), branch_computations={%region_13.14_spmd, %region_14.0_spmd} | conditional | flops 4102653440 | bytes 197825072 | solution.py:162
  727.0 14.8 fusion.164
  741.9 18.0 multiply_convert_fusion
  759.9 12.9 fusion.25
  772.8 10.9 fusion.31
  783.8 6.7 convolution_multiply_fusion
  790.5 5.4 pad_maximum_fusion
  795.9 16.8 copy.62
  813.5 5.2 all-gather.21
  818.7 8.4 multiply_convert_fusion.2
  827.1 5.7 fusion.162
  833.5 233.4 %reduce-scatter.31.cloned.1.call-done = bf16[128,1536]{1,0:T(8,128)(2,1)} async-done(((bf16[4096,1536]{1,0:T(8,128)(2,1)}), bf16[128,1536]{1,0:T(8,128)(2,1)}) %reduce-scatter.31.cloned.1.call-update) | async-done | bytes 393232
  1082.6 70.8 %conditional.7 = (f32[128,12,64]{0,2,1:T(8,128)S(1)}, bf16[4096,2,768]{0,2,1:T(8,128)(2,1)}) conditional(s32[]{:T(128)} %convert_element_type.153, () %tuple.50, (s32[128]{0:T(128)}, bf16[128,12,64]{0,2,1:T(8,128)(2,1)S(1)}, bf16[4096,12,64]{0,2,1:T(8,128)(2,1)}, f32[12,128]{1,0:T(8,128)}, f32[12,128]{1,0:T(8,128)}, ...), branch_computations={%region_21.22_spmd, %region_22.23_spmd} | conditional | flops 4102653440 | bytes 198636144 | solution.py:162
  1085.1 14.6 fusion.165
  1099.7 17.9 multiply_convert_fusion.1
  1117.6 13.0 fusion.35
  1130.6 10.8 fusion.41
  1141.5 6.6 convolution_multiply_fusion.2
  1148.1 5.4 pad_maximum_fusion.1
  1153.5 16.8 copy.64
  1171.0 3.7 convolution_convert_fusion.2
  1174.7 3.5 convolution_convert_fusion
  1182.3 3.0 convolution_convert_fusion.4
  1186.5 3.6 convolution_convert_fusion.1
  1190.2 5.8 fusion.163
  1196.0 3.7 convolution_convert_fusion.3
  1201.5 215.5 %reduce-scatter.33.cloned.1.call-done = bf16[128,1536]{1,0:T(8,128)(2,1)} async-done(((bf16[4096,1536]{1,0:T(8,128)(2,1)}), bf16[128,1536]{1,0:T(8,128)(2,1)}) %reduce-scatter.33.cloned.1.call-update) | async-done | bytes 393232
  1419.4 3.0 convolution_convert_fusion.5
  1422.8 43.5 %reduce-scatter.25.cloned.1.call-done = bf16[192,3072]{1,0:T(8,128)(2,1)} async-done(((bf16[768,3072]{1,0:T(8,128)(2,1)}), bf16[192,3072]{1,0:T(8,128)(2,1)}) %reduce-scatter.25.cloned.1.call-update) | async-done | bytes 1179664 | tf_op jit(solution)/shard_map/reduce_scatter | solution.py:219
  1466.3 52.9 %reduce-scatter.29.cloned.1.call-done = bf16[768,768]{1,0:T(8,128)(2,1)} async-done(((bf16[3072,768]{1,0:T(8,128)(2,1)}), bf16[768,768]{1,0:T(8,128)(2,1)}) %reduce-scatter.29.cloned.1.call-update) | async-done | bytes 1179664 | tf_op jit(solution)/shard_map/reduce_scatter | solution.py:225
  1519.2 24.5 %reduce-scatter.21.cloned.1.call-done = bf16[192,768]{1,0:T(8,128)(2,1)} async-done(((bf16[768,768]{1,0:T(8,128)(2,1)}), bf16[192,768]{1,0:T(8,128)(2,1)}) %reduce-scatter.21.cloned.1.call-update) | async-done | bytes 294928 | tf_op jit(solution)/shard_map/reduce_scatter | solution.py:213
  1543.7 24.0 %reduce-scatter.19.cloned.1.call-done = bf16[192,768]{1,0:T(8,128)(2,1)} async-done(((bf16[768,768]{1,0:T(8,128)(2,1)}), bf16[192,768]{1,0:T(8,128)(2,1)}) %reduce-scatter.19.cloned.1.call-update) | async-done | bytes 294928 | tf_op jit(solution)/shard_map/reduce_scatter | solution.py:213
  1567.6 44.0 %reduce-scatter.17.cloned.1.call-done = bf16[192,2304]{1,0:T(8,128)(2,1)} async-done(((bf16[768,2304]{1,0:T(8,128)(2,1)}), bf16[192,2304]{1,0:T(8,128)(2,1)}) %reduce-scatter.17.cloned.1.call-update) | async-done | bytes 884752 | tf_op jit(solution)/shard_map/reduce_scatter | solution.py:207
  1611.6 52.9 %reduce-scatter.27.cloned.1.call-done = bf16[768,768]{1,0:T(8,128)(2,1)} async-done(((bf16[3072,768]{1,0:T(8,128)(2,1)}), bf16[768,768]{1,0:T(8,128)(2,1)}) %reduce-scatter.27.cloned.1.call-update) | async-done | bytes 1179664 | tf_op jit(solution)/shard_map/reduce_scatter | solution.py:225
  1664.5 53.6 %reduce-scatter.23.cloned.1.call-done = bf16[192,3072]{1,0:T(8,128)(2,1)} async-done(((bf16[768,3072]{1,0:T(8,128)(2,1)}), bf16[192,3072]{1,0:T(8,128)(2,1)}) %reduce-scatter.23.cloned.1.call-update) | async-done | bytes 1179664 | tf_op jit(solution)/shard_map/reduce_scatter | solution.py:219
  1718.1 43.4 %reduce-scatter.15.cloned.1.call-done = bf16[192,2304]{1,0:T(8,128)(2,1)} async-done(((bf16[768,2304]{1,0:T(8,128)(2,1)}), bf16[192,2304]{1,0:T(8,128)(2,1)}) %reduce-scatter.15.cloned.1.call-update) | async-done | bytes 884752 | tf_op jit(solution)/shard_map/reduce_scatter | solution.py:207
  1764.3 3.9 fusion.46
  1769.1 4.2 fusion.56
  1775.7 11.7 all-reduce.42
  1788.7 186.2 %all-reduce.40 = (bf16[1,192]{1,0:T(2,128)(2,1)S(1)}, bf16[1,192]{1,0:T(2,128)(2,1)S(1)}, bf16[1,192]{1,0:T(2,128)(2,1)S(1)}, bf16[1,192]{1,0:T(2,128)(2,1)S(1)}...) all-reduce(bf16[1,192]{1,0:T(2,128)(2,1)S(1)} %stack.164, ...), channel_id=1, replica_groups=mesh['fsdp'=4,'ctx'=32] {'ctx'}, use_global_device_ids=true, to_apply=%region_33.34 | all-reduce | flops 4608 | bytes 18432 | tf_op jit(solution)/shard_map/psum | solution.py:247
  1981.8 192.2 %all-reduce.46.cloned.1.call-done = (bf16[1,192,2304]{2,1,0:T(8,128)(2,1)}, bf16[1,192,2304]{2,1,0:T(8,128)(2,1)}, bf16[1,192,768]{2,1,0:T(8,128)(2,1)}, bf16[1,...) async-done(((bf16[1,192,2304]{2,1,0:T(8,128)(2,1)}, ...) | async-done | bytes 7077904 | tf_op jit(solution)/shard_map/psum | solution.py:251
  (434 shorter events, 80.9 us)
Async XLA Ops:
  7.2 46.9 %all-gather.45.cloned.1.call-start = ((), (), s32[]{:S(2)}) async-start(), calls=%async_computation.22 | async-start | bytes 4423680 | tf_op jit(solution)/shard_map/all_gather | solution.py:290
  10.2 97.7 %all-gather.49.cloned.1.call-start = ((), (), s32[]{:S(2)}) async-start(), calls=%async_computation.24 | async-start | bytes 5898240 | tf_op jit(solution)/shard_map/all_gather | solution.py:294
  11.8 5.4 copy-start.87
  11.8 5.6 copy-start.88
  11.8 5.9 copy-start.89
  11.8 6.2 copy-start.90
  11.9 6.4 copy-start.91
  11.9 7.1 copy-start.92
  11.9 8.7 copy-start.72
  11.9 22.2 %copy-start = (bf16[1,128,768]{2,1,0:T(8,128)(2,1)S(1)}, bf16[1,128,768]{2,1,0:T(8,128)(2,1)}, u32[]{:S(2)}) copy-start(bf16[1,128,768]{2,1,0:T(8,128)(2,1)} %param.22) | copy-start | bytes 589828
  11.9 149.9 %all-gather.51.cloned.1.call-start = ((), (), s32[]{:S(2)}) async-start(), calls=%async_computation.25 | async-start | bytes 5898240 | tf_op jit(solution)/shard_map/all_gather | solution.py:296
  15.2 262.0 %all-gather.39.cloned.1.call-start = ((), (), s32[]{:S(2)}) async-start(), calls=%async_computation.11 | async-start | bytes 6488064 | tf_op jit(solution)/shard_map/all_gather | solution.py:96
  34.1 20.0 copy-start.42
  34.1 20.0 copy-start.46
  34.2 73.6 %copy-start.55 = (f32[128]{0:T(128)}, f32[128]{0:T(128)S(1)}, u32[]{:S(2)}) copy-start(f32[128]{0:T(128)S(1)} %broadcast_multiply_fusion.1) | copy-start | bytes 1540
  34.4 19.7 copy-start.93
  34.5 73.4 %copy-start.62 = (f32[128]{0:T(128)}, f32[128]{0:T(128)S(1)}, u32[]{:S(2)}) copy-start(f32[128]{0:T(128)S(1)} %fusion.133) | copy-start | bytes 1540
  57.7 331.8 %all-gather.37.cloned.1.call-start = ((), (), s32[]{:S(2)}) async-start(), calls=%async_computation.10 | async-start | bytes 6488064 | tf_op jit(solution)/shard_map/all_gather | solution.py:95
  59.1 373.0 %all-gather.47.cloned.1.call-start = ((), (), s32[]{:S(2)}) async-start(), calls=%async_computation.23 | async-start | bytes 1474560 | tf_op jit(solution)/shard_map/all_gather | solution.py:292
  60.0 393.7 %all-gather.53.cloned.1.call-start = ((), (), s32[]{:S(2)}) async-start(), calls=%async_computation.26 | async-start | bytes 4423680 | tf_op jit(solution)/shard_map/all_gather | solution.py:290
  60.7 509.2 %all-gather.43.cloned.1.call-start = ((), (), s32[]{:S(2)}) async-start(), calls=%async_computation.13 | async-start | bytes 6488064 | tf_op jit(solution)/shard_map/all_gather | solution.py:96
  60.8 55.4 %copy-start.50 = (f32[768]{0:T(1024)}, f32[768]{0:T(1024)S(1)}, u32[]{:S(2)}) copy-start(f32[768]{0:T(1024)S(1)} %convert_element_type.396) | copy-start | bytes 9220
  60.8 55.4 %copy-start.44 = (f32[768]{0:T(1024)}, f32[768]{0:T(1024)S(1)}, u32[]{:S(2)}) copy-start(f32[768]{0:T(1024)S(1)} %convert_element_type.395) | copy-start | bytes 9220
  60.9 392.8 %copy-start.48 = (f32[768]{0:T(1024)}, f32[768]{0:T(1024)S(1)}, u32[]{:S(2)}) copy-start(f32[768]{0:T(1024)S(1)} %convert_element_type.399) | copy-start | bytes 9220
  67.1 658.8 %copy-start.74 = (s32[128]{0:T(128)}, s32[128]{0:T(128)S(1)}, u32[]{:S(2)}) copy-start(s32[128]{0:T(128)S(1)} %iota_add_fusion) | copy-start | bytes 1540
  116.2 48.8 %copy-start.4 = (bf16[128,3072]{1,0:T(8,128)(2,1)}, bf16[128,3072]{1,0:T(8,128)(2,1)S(1)}, u32[]{:S(2)}) copy-start(bf16[128,3072]{1,0:T(8,128)(2,1)S(1)} %get-tuple-element.216) | copy-start | bytes 2359300
  433.9 384.8 %copy-start.59 = (f32[128]{0:T(128)}, f32[128]{0:T(128)S(1)}, u32[]{:S(2)}) copy-start(f32[128]{0:T(128)S(1)} %broadcast_multiply_fusion) | copy-start | bytes 1540
  434.1 22.2 %copy-start.95 = (f32[128]{0:T(128)}, f32[128]{0:T(128)S(1)}, u32[]{:S(2)}) copy-start(f32[128]{0:T(128)S(1)} %multiply_reduce_fusion.6) | copy-start | bytes 1540
  434.1 384.5 %copy-start.66 = (f32[128]{0:T(128)}, f32[128]{0:T(128)S(1)}, u32[]{:S(2)}) copy-start(f32[128]{0:T(128)S(1)} %fusion.134) | copy-start | bytes 1540
  457.2 225.1 %all-gather.41.cloned.1.call-start = ((), (), s32[]{:S(2)}) async-start(), calls=%async_computation.12 | async-start | bytes 6488064 | tf_op jit(solution)/shard_map/all_gather | solution.py:95
  458.6 265.0 %all-gather.55.cloned.1.call-start = ((), (), s32[]{:S(2)}) async-start(), calls=%async_computation.27 | async-start | bytes 1474560 | tf_op jit(solution)/shard_map/all_gather | solution.py:292
  459.2 359.4 %all-gather.57.cloned.1.call-start = ((), (), s32[]{:S(2)}) async-start(), calls=%async_computation.28 | async-start | bytes 5898240 | tf_op jit(solution)/shard_map/all_gather | solution.py:294
  460.0 367.1 %all-gather.59.cloned.1.call-start = ((), (), s32[]{:S(2)}) async-start(), calls=%async_computation.29 | async-start | bytes 5898240 | tf_op jit(solution)/shard_map/all_gather | solution.py:296
  460.5 606.3 %reduce-scatter.31.cloned.1.call-start = ((), (), s32[]{:S(2)}) async-start(), calls=%async_computation.30 | async-start | bytes 12976128
  682.3 41.3 %copy-start.10 = (bf16[1,128,768]{2,1,0:T(8,128)(2,1)S(1)}, bf16[1,128,768]{2,1,0:T(8,128)(2,1)}, u32[]{:S(2)}) copy-start(bf16[1,128,768]{2,1,0:T(8,128)(2,1)} %param.23) | copy-start | bytes 589828
  783.8 6.7 copy-start.2
  795.9 36.8 %copy-start.28 = (f32[128,12,64]{0,2,1:T(8,128)}, f32[128,12,64]{0,2,1:T(8,128)S(1)}, u32[]{:S(2)}) copy-start(f32[128,12,64]{0,2,1:T(8,128)S(1)} %get-tuple-element.108) | copy-start | bytes 1179652
  812.8 604.2 %reduce-scatter.33.cloned.1.call-start = ((), (), s32[]{:S(2)}) async-start(), calls=%async_computation.31 | async-start | bytes 12976128
  813.5 13.6 copy-start.52
  1072.0 110.3 %copy-start.19 = (bf16[128,12,64]{0,2,1:T(8,128)(2,1)}, bf16[128,12,64]{0,2,1:T(8,128)(2,1)S(1)}, u32[]{:S(2)}) copy-start(bf16[128,12,64]{0,2,1:T(8,128)(2,1)S(1)} %get-tuple-element.285) | copy-start | bytes 589828
  1078.1 102.6 %copy-start.12 = (bf16[128,768]{1,0:T(8,128)(2,1)}, bf16[128,768]{1,0:T(8,128)(2,1)S(1)}, u32[]{:S(2)}) copy-start(bf16[128,768]{1,0:T(8,128)(2,1)S(1)} %convert_element_type.352) | copy-start | bytes 589828
  1085.1 14.6 copy-start.40
  1085.1 14.6 copy-start.73
  1141.5 6.6 copy-start.3
  1153.5 16.8 copy-start.29
  1170.3 296.0 %reduce-scatter.25.cloned.1.call-start = ((), (), s32[]{:S(2)}) async-start(), calls=%async_computation.19 | async-start | bytes 5898240 | tf_op jit(solution)/shard_map/reduce_scatter | solution.py:219
  1174.7 344.5 %reduce-scatter.29.cloned.1.call-start = ((), (), s32[]{:S(2)}) async-start(), calls=%async_computation.21 | async-start | bytes 5898240 | tf_op jit(solution)/shard_map/reduce_scatter | solution.py:225
  1178.3 365.4 %reduce-scatter.21.cloned.1.call-start = ((), (), s32[]{:S(2)}) async-start(), calls=%async_computation.17 | async-start | bytes 1474560 | tf_op jit(solution)/shard_map/reduce_scatter | solution.py:213
  1180.7 387.0 %reduce-scatter.19.cloned.1.call-start = ((), (), s32[]{:S(2)}) async-start(), calls=%async_computation.16 | async-start | bytes 1474560 | tf_op jit(solution)/shard_map/reduce_scatter | solution.py:213
  1182.3 429.4 %reduce-scatter.17.cloned.1.call-start = ((), (), s32[]{:S(2)}) async-start(), calls=%async_computation.15 | async-start | bytes 4423680 | tf_op jit(solution)/shard_map/reduce_scatter | solution.py:207
  1185.4 479.1 %reduce-scatter.27.cloned.1.call-start = ((), (), s32[]{:S(2)}) async-start(), calls=%async_computation.20 | async-start | bytes 5898240 | tf_op jit(solution)/shard_map/reduce_scatter | solution.py:225
  1190.1 528.0 %reduce-scatter.23.cloned.1.call-start = ((), (), s32[]{:S(2)}) async-start(), calls=%async_computation.18 | async-start | bytes 5898240 | tf_op jit(solution)/shard_map/reduce_scatter | solution.py:219
  1190.2 5.8 copy-start.1
  1190.2 5.8 copy-start.45
  1190.2 5.8 copy-start.51
  1190.2 5.8 copy-start.56
  1190.2 5.8 copy-start.63
  1199.8 561.7 %reduce-scatter.15.cloned.1.call-start = ((), (), s32[]{:S(2)}) async-start(), calls=%async_computation.14 | async-start | bytes 4423680 | tf_op jit(solution)/shard_map/reduce_scatter | solution.py:207
  1422.5 751.5 %all-reduce.46.cloned.1.call-start = ((), (), s32[]{:S(2)}) async-start(), calls=%async_computation.32 | async-start | bytes 14155776 | tf_op jit(solution)/shard_map/psum | solution.py:251
  1769.1 4.4 copy-start.9
  1769.1 4.4 copy-start.58
  1773.7 204.7 %copy-start.27 = (f32[128,768]{1,0:T(8,128)S(1)}, f32[128,768]{1,0:T(8,128)}, u32[]{:S(2)}) copy-start(f32[128,768]{1,0:T(8,128)} %fusion.46) | copy-start | bytes 1179652
  1773.7 204.7 %copy-start.39 = (bf16[128,12,64]{0,2,1:T(8,128)(2,1)S(1)}, bf16[128,12,64]{0,2,1:T(8,128)(2,1)}, u32[]{:S(2)}) copy-start(bf16[128,12,64]{0,2,1:T(8,128)(2,1)} %get-tuple-element.243) | copy-start | bytes 589828
  1974.9 209.2 %copy-start.84 = (f32[2,192]{1,0:T(2,128)}, f32[2,192]{1,0:T(2,128)S(1)}, u32[]{:S(2)}) copy-start(f32[2,192]{1,0:T(2,128)S(1)} %maximum_convert_fusion.10) | copy-start | bytes 4612
  (61 other events, 121.0 us)
Sparse Core Ops, SparseCore 0:
  10.3 43.7 all-gather.44
  56.3 51.4 all-gather.48
  110.1 51.7 all-gather.50
  164.5 112.7 all-gather.38
  280.4 109.0 all-gather.36
  391.0 19.3 all-gather.46
  412.0 41.6 all-gather.52
  457.3 112.5 all-gather.42
  573.2 109.0 all-gather.40
  684.4 19.3 all-gather.54
  706.0 51.2 all-gather.56
  758.8 51.7 all-gather.58
  815.9 250.9 reduce-scatter.30
  1170.4 246.5 reduce-scatter.32
  1419.9 46.3 reduce-scatter.24
  1468.5 50.5 reduce-scatter.28
  1522.0 21.6 reduce-scatter.20
  1546.0 21.6 reduce-scatter.18
  1570.6 40.9 reduce-scatter.16
  1613.9 50.5 reduce-scatter.26
  1667.5 50.5 reduce-scatter.22
  1720.5 40.9 reduce-scatter.14
  1764.6 409.3 all-reduce.45
where the time goes:
time: 2200 us; the launch traced here: 2190 us
  waiting for transfers between devices  1550 us (70%)
  matrix products  260 us (12%)
  blocking collectives  222 us (10%)
  local copies, waits for them, and re-layouts  68 us (3%)
  other arithmetic  67.2 us (3%)
    unnamed x25, waiting for transfers between devices  452 us
    all_gather x2, waiting for transfers between devices, attend_forward(): lax.all_gather(key_rows, 'ctx', axis=0, tiled=True)  225 us
    all_gather x2, waiting for transfers between devices, attend_forward(): lax.all_gather(value_rows, 'ctx', axis=0, tiled=True)  221 us
    psum x1, waiting for transfers between devices, reduce_grads(): lax.psum(own_qkv_w.astype(jnp.bfloat16), 'ctx').astype(jnp.float32)  192 us
    psum x1, blocking collectives, reduce_grads(): lax.psum(own_gain_one.astype(jnp.bfloat16), 'ctx').astype(jnp.float32)  186 us
    reduce_scatter x2, waiting for transfers between devices, reduce_grads(): lax.psum_scatter(part_down_w.astype(jnp.bfloat16), 'fsdp', scatter_dimens...  106 us
    reduce_scatter x2, waiting for transfers between devices, reduce_grads(): lax.psum_scatter(part_up_w.astype(jnp.bfloat16), 'fsdp', scatter_dimensio...  97.1 us
    reduce_scatter x2, waiting for transfers between devices, reduce_grads(): lax.psum_scatter(part_qkv_w.astype(jnp.bfloat16), 'fsdp', scatter_dimensi...  87.4 us
  transfers between devices with their start and end apart: 23, of which 19 were waited for; matrix products, arithmetic and copies ran while one was open for 12% of the time, Pallas kernels for 0%

commit v1 on v0

v1 whole, which is shorter than its diff:
```python
import functools

import jax
import jax.numpy as jnp
from jax import lax
from jax.experimental import pallas as pl
from jax.experimental.pallas import tpu as pltpu
from jax.sharding import PartitionSpec as P

D = 768
HEADS = 12
HEAD_DIM = 64
FF = 3072
ROTARY = 16
LAYERS = 2
HALF = 384
BLOCK = 128
BLOCKS = 32
TILE = 512
PAIRS = 3

epsilon = 1e-05
masked_score = -1e30
MESH = pl.DeviceIdType.MESH
BF = jnp.bfloat16
F32 = jnp.float32


def mirrored(values):
    pairs = [(f * 32 + c, f * 32 + 31 - c) for f in range(4) for c in range(32)]
    return lax.ppermute(values, ("fsdp", "ctx"), pairs)


class Place:
    def __init__(self):
        self.fsdp = lax.axis_index("fsdp")
        self.ctx = lax.axis_index("ctx")
        self.y, self.z, self.h = self.ctx // 8, (self.ctx // 2) % 4, self.ctx % 2
        self.x_lo, self.core = self.fsdp // 2, self.fsdp % 2
        self.beside = (self.fsdp + 1 - 2 * self.core, self.ctx)
        self.mirror = (self.fsdp, BLOCKS - 1 - self.ctx)
        self.half = (self.fsdp, self.ctx + 1 - 2 * self.h)

    def along_x(self, step):
        x = (2 * self.h + self.x_lo + step) % 4
        return (2 * (x % 2) + self.core, self.y * 8 + self.z * 2 + x // 2)

    def ctx_at(self, dy, dz):
        return ((self.y + dy) % 4) * 8 + ((self.z + dz) % 4) * 2 + self.h

    def ring(self, t, da, db):
        return self.ctx_at(da, db) if t == 0 else self.ctx_at(db, da)

    def near(self, t, axis, sign):
        steps = (sign, 0) if axis == 0 else (0, sign)
        return (self.fsdp, self.ring(t, *steps))

    def around(self):
        return [self.near(0, axis, sign) for axis in (0, 1) for sign in (1, -1)]

    def greet(self, partners):
        barrier = pltpu.get_barrier_semaphore()
        for partner in partners:
            pl.semaphore_signal(barrier, inc=1, device_id=partner, device_id_type=MESH)
        pl.semaphore_wait(barrier, len(partners))


class Wire:
    def __init__(self, send_sem, recv_sem, local_sem=None):
        self.send_sem, self.recv_sem, self.local_sem = send_sem, recv_sem, local_sem
        self.sent, self.local = [], []

    def push(self, source, target, partner):
        number = len(self.sent)
        copy = pltpu.make_async_remote_copy(
            src_ref=source,
            dst_ref=target,
            send_sem=self.send_sem.at[number],
            recv_sem=self.recv_sem.at[number],
            device_id=partner,
            device_id_type=MESH,
        )
        copy.start()
        self.sent.append(copy)
        return copy

    def keep(self, source, target):
        copy = pltpu.make_async_copy(source, target, self.local_sem.at[len(self.local)])
        copy.start()
        self.local.append(copy)

    def drain(self):
        for copy in self.sent:
            copy.wait_send()
        for copy in self.local:
            copy.wait()


def share_param(place, wire, source, target):
    rows = source.shape[0]
    cut = rows // 2
    mine, far = place.fsdp * rows, ((place.fsdp + 2) % 4) * rows
    parts = (
        [(0, cut, 1), (cut, cut, 3)] if rows % 32 == 0 else [(0, rows, 1)]
    )
    across = [
        wire.push(
            source.at[pl.ds(start, count)],
            target.at[pl.ds(mine + start, count)],
            place.along_x(step),
        )
        for start, count, step in parts
    ]
    beside = wire.push(source, target.at[pl.ds(mine, rows)], place.beside)
    wire.keep(source, target.at[pl.ds(mine, rows)])
    last = [beside]

    def onward(copy, start, count):
        copy.wait_recv()
        spot = target.at[pl.ds(far + start, count)]
        last.append(wire.push(spot, spot, place.beside))

    steps = [
        functools.partial(onward, copy, start, count)
        for copy, (start, count, _) in zip(across, parts)
    ]
    return steps, last


def share_rows(place, wire, source, target):
    rows = source.shape[0]
    cut = rows // 2
    parts = [(0, cut, 1), (cut, cut, 3)] if rows % 32 == 0 else [(0, rows, 1)]
    across = [
        wire.push(
            source.at[pl.ds(start, count)],
            target.at[pl.ds(2 * rows + start, count)],
            place.along_x(step),
        )
        for start, count, step in parts
    ]
    last = [wire.push(source, target.at[pl.ds(rows, rows)], place.beside)]
    wire.keep(source, target.at[pl.ds(0, rows)])

    def onward(copy, start, count):
        copy.wait_recv()
        last.append(
            wire.push(
                target.at[pl.ds(2 * rows + start, count)],
                target.at[pl.ds(3 * rows + start, count)],
                place.beside,
            )
        )

    steps = [
        functools.partial(onward, copy, start, count)
        for copy, (start, count, _) in zip(across, parts)
    ]
    return steps, last


def share_slices(place, wire, source, target, stage):
    rows = source.shape[1]
    cut = rows // 2
    fsdp, core = place.fsdp, place.core
    parts = [(0, cut, 1), (cut, cut, 3)]
    passing, last = [], []
    for start, count, step in parts:
        partner = place.along_x(step)
        passing.append(
            wire.push(
                source.at[3 - fsdp, pl.ds(start, count)], stage.at[pl.ds(start, count)], partner
            )
        )
    for start, count, step in parts:
        last.append(
            wire.push(
                source.at[(fsdp + 2) % 4, pl.ds(start, count)],
                target.at[pl.ds(2 * rows + start, count)],
                place.along_x(step),
            )
        )
    last.append(
        wire.push(source.at[fsdp + 1 - 2 * core], target.at[pl.ds(rows, rows)], place.beside)
    )
    wire.keep(source.at[fsdp], target.at[pl.ds(0, rows)])

    def onward(copy, start, count):
        copy.wait_recv()
        last.append(
            wire.push(
                stage.at[pl.ds(start, count)],
                target.at[pl.ds(3 * rows + start, count)],
                place.beside,
            )
        )

    steps = [
        functools.partial(onward, copy, start, count)
        for copy, (start, count, _) in zip(passing, parts)
    ]
    return steps, last


def spread(place, wire, own, spot, ready, between=()):
    between = list(between)
    arrivals = {}

    def push(t, da, db, b, axis, sign):
        target = spot(t, place.ring(t, da, db), b)
        source = own(t, b) if da == 0 and db == 0 else target
        sa, sb = (sign, 0) if axis == 0 else (0, sign)
        arrivals[t, (da - sa) % 4, (db - sb) % 4, b] = wire.push(
            source, target, place.near(t, axis, sign)
        )

    def landed(t, da, db):
        for b in (0, 1):
            arrivals[t, da, db, b].wait_recv()

    def pause():
        if between:
            between.pop(0)()

    for b in (0, 1):
        for t in (0, 1):
            ready(t, b)
            for axis in (0, 1):
                for sign in (1, -1):
                    push(t, 0, 0, b, axis, sign)
    for da, keep, onward in ((1, 0, -1), (3, 1, 1)):
        for t in (0, 1):
            landed(t, da, 0)
            push(t, da, 0, keep, 0, onward)
            for sign in (1, -1):
                for b in (0, 1):
                    push(t, da, 0, b, 1, sign)
    for db, keep, onward in ((1, 0, -1), (3, 1, 1)):
        for t in (0, 1):
            landed(t, 0, db)
            push(t, 0, db, keep, 1, onward)
    for t in (0, 1):
        landed(t, 2, 0)
        for sign in (1, -1):
            for b in (0, 1):
                push(t, 2, 0, b, 1, sign)
    pause()
    for da in (1, 3, 2):
        for db, keep, onward in ((1, 0, -1), (3, 1, 1)):
            for t in (0, 1):
                landed(t, da, db)
                push(t, da, db, keep, 1, onward)
            pause()
    while between:
        pause()
    for da in (0, 1, 3, 2):
        for t in (0, 1):
            landed(t, da, 2)


ANY = pl.BlockSpec(memory_space=pl.ANY)
VM = pl.BlockSpec(memory_space=pltpu.VMEM)
SM = pl.BlockSpec(memory_space=pltpu.SMEM)


def room(*shape):
    return pltpu.VMEM(shape, BF)


def sems(count, local):
    return [
        pltpu.SemaphoreType.DMA((count,)),
        pltpu.SemaphoreType.DMA((count,)),
        pltpu.SemaphoreType.DMA((local,)),
    ]


def full_shape(shard):
    return jax.ShapeDtypeStruct((4 * shard.shape[-2], shard.shape[-1]), BF)


def first_kernel(weight_ref, vector_ref, weight_out, vector_out, *sem):
    place, wire = Place(), Wire(*sem)
    place.greet([place.beside, place.along_x(1), place.along_x(3)])
    steps, last = share_param(place, wire, vector_ref, vector_out)
    more, ends = share_param(place, wire, weight_ref.at[0], weight_out)
    for step in more + steps:
        step()
    for copy in last + ends:
        copy.wait_recv()
    wire.drain()


def gather_first(weight, vectors):
    return pl.pallas_call(
        first_kernel,
        out_shape=(full_shape(weight), full_shape(vectors)),
        in_specs=[ANY] * 2,
        out_specs=(ANY,) * 2,
        scratch_shapes=sems(16, 4),
        compiler_params=pltpu.CompilerParams(collective_id=0, has_side_effects=True),
        name="gather_first",
    )(weight, vectors)


def gather_kernel(jobs, q_ref, k_ref, v_ref, k_own, v_own, *refs):
    count = len(jobs)
    weights, refs = refs[:count], refs[count:]
    q_out, k_out, v_out = refs[:3]
    weights_out, refs = refs[3 : 3 + count], refs[3 + count :]
    place, wire = Place(), Wire(*refs)
    place.greet(
        place.around() + [place.mirror, place.beside, place.along_x(1), place.along_x(3)]
    )
    ins, outs = (k_own, v_own), (k_out, v_out)
    ctx = place.ctx
    swapped = [
        wire.push(source, out.at[ctx], place.mirror) for source, out in zip((k_ref, v_ref), outs)
    ]
    swapped.append(wire.push(q_ref, q_out, place.mirror))
    for t in (0, 1):
        wire.keep(ins[t], outs[t].at[ctx])
    work = []

    def ready(t, b):
        if b == 1:
            if t == 0:
                for layer, weight, target in zip(jobs, weights, weights_out):
                    work.append(share_param(place, wire, weight.at[layer], target))
            swapped[t].wait_recv()

    def spot(t, origin, b):
        return outs[t].at[origin if b == 0 else BLOCKS - 1 - origin]

    def own(t, b):
        return ins[t] if b == 0 else spot(t, ctx, 1)

    def onward(number):
        for steps, _ in work:
            for step in steps[number : number + 1]:
                step()

    spread(
        place,
        wire,
        own,
        spot,
        ready,
        [lambda: None] * 4 + [functools.partial(onward, 0), functools.partial(onward, 1)],
    )
    swapped[2].wait_recv()
    for _, last in work:
        for copy in last:
            copy.wait_recv()
    wire.drain()


def gather_pair(name, number, away, own, jobs):
    layers = [layer for layer, _ in jobs]
    weights = [weight for _, weight in jobs]
    whole = jax.ShapeDtypeStruct((BLOCKS, BLOCK, HALF), BF)
    return pl.pallas_call(
        functools.partial(gather_kernel, layers),
        out_shape=(jax.ShapeDtypeStruct((BLOCK, HALF), BF), whole, whole)
        + tuple(full_shape(weight) for weight in weights),
        in_specs=[ANY] * (5 + len(jobs)),
        out_specs=(ANY,) * (3 + len(jobs)),
        scratch_shapes=sems(96, 8),
        compiler_params=pltpu.CompilerParams(collective_id=number, has_side_effects=True),
        name=name,
    )(*away, *own, *weights)


def scatter_kernel(count, gk_ref, gv_ref, gq_ref, stack_ref, *refs):
    sources, refs = refs[:count], refs[count:]
    own_out, back_out, back_q, stack_out = refs[:4]
    targets, refs = refs[4 : 4 + count], refs[4 + count :]
    far, near, mix, total, last_far, last_near, last_mix, leave, stage = refs[:9]
    place, wire = Place(), Wire(*refs[9:])
    place.greet(
        place.around() + [place.mirror, place.beside, place.along_x(1), place.along_x(3)]
    )
    ins = (gk_ref, gv_ref)

    def block_at(t, da, db, b):
        origin = place.ring(t, da, db)
        return origin if b == 0 else BLOCKS - 1 - origin

    order = (2, 1, 3, 0)
    first, second = {}, {}
    for da in order:
        for t in (0, 1):
            first[t, da] = [
                wire.push(
                    ins[t].at[block_at(t, da, 2, b)], far.at[t, da, b], place.near(t, 1, sign)
                )
                for b, sign in ((0, 1), (1, -1))
            ]
    swapped = [wire.push(gq_ref, back_q, place.mirror)]
    work = [share_slices(place, wire, stack_ref, stack_out, stage)]
    for source, target in zip(sources, targets):
        work.append(share_rows(place, wire, source, target))
    for da in order:
        for t in (0, 1):
            copies = []
            for b, sign, db in ((0, 1, 1), (1, -1, 3)):
                copies.append(
                    wire.push(
                        ins[t].at[block_at(t, da, db, 1 - b)],
                        near.at[t, da, b, 1 - b],
                        place.near(t, 1, sign),
                    )
                )
                first[t, da][b].wait_recv()
                mix[t, da, b] = (
                    ins[t][block_at(t, da, db, b)].astype(F32) + far[t, da, b].astype(F32)
                ).astype(BF)
                copies.append(
                    wire.push(mix.at[t, da, b], near.at[t, da, b, b], place.near(t, 1, sign))
                )
            second[t, da] = copies

    def settle(t, da):
        for copy in second[t, da]:
            copy.wait_recv()
        for b in (0, 1):
            total[t, da, b] = (
                ins[t][block_at(t, da, 0, b)].astype(F32)
                + near[t, da, 0, b].astype(F32)
                + near[t, da, 1, b].astype(F32)
            ).astype(BF)

    third, fourth = {}, {}
    for t in (0, 1):
        settle(t, 2)
        third[t] = [
            wire.push(total.at[t, 2, b], last_far.at[t, b], place.near(t, 0, sign))
            for b, sign in ((0, 1), (1, -1))
        ]
    for t in (0, 1):
        fourth[t] = []
        for b, sign, da in ((0, 1, 1), (1, -1, 3)):
            settle(t, da)
            fourth[t].append(
                wire.push(
                    total.at[t, da, 1 - b], last_near.at[t, b, 1 - b], place.near(t, 0, sign)
                )
            )
    for t in (0, 1):
        for b, sign, da in ((0, 1, 1), (1, -1, 3)):
            third[t][b].wait_recv()
            last_mix[t, b] = (total[t, da, b].astype(F32) + last_far[t, b].astype(F32)).astype(BF)
            fourth[t].append(
                wire.push(last_mix.at[t, b], last_near.at[t, b, b], place.near(t, 0, sign))
            )
    for t in (0, 1):
        settle(t, 0)
    for steps, _ in work:
        for step in steps:
            step()
    for t in (0, 1):
        for copy in fourth[t]:
            copy.wait_recv()
        for b in (1, 0):
            done = (
                total[t, 0, b].astype(F32)
                + last_near[t, 0, b].astype(F32)
                + last_near[t, 1, b].astype(F32)
            )
            if b == 1:
                leave[t] = done.astype(BF)
                swapped.append(wire.push(leave.at[t], back_out.at[t], place.mirror))
            else:
                own_out[t] = done
    for _, last in work:
        for copy in last:
            copy.wait_recv()
    for copy in swapped:
        copy.wait_recv()
    wire.drain()


def rows_shape(source):
    return jax.ShapeDtypeStruct((4 * source.shape[0], source.shape[1]), BF)


def scatter_pair(name, number, grad_keys, grad_values, away, stacked, sources):
    return pl.pallas_call(
        functools.partial(scatter_kernel, len(sources)),
        out_shape=(
            jax.ShapeDtypeStruct((2, BLOCK, HALF), F32),
            jax.ShapeDtypeStruct((2, BLOCK, HALF), BF),
            jax.ShapeDtypeStruct((BLOCK, HALF), BF),
            rows_shape(stacked[0]),
        )
        + tuple(rows_shape(source) for source in sources),
        in_specs=[VM, VM] + [ANY] * (2 + len(sources)),
        out_specs=(VM,) + (ANY,) * (3 + len(sources)),
        scratch_shapes=[
            room(2, 4, 2, BLOCK, HALF),
            room(2, 4, 2, 2, BLOCK, HALF),
            room(2, 4, 2, BLOCK, HALF),
            room(2, 4, 2, BLOCK, HALF),
            room(2, 2, BLOCK, HALF),
            room(2, 2, 2, BLOCK, HALF),
            room(2, 2, BLOCK, HALF),
            room(2, BLOCK, HALF),
            room(*stacked.shape[1:]),
        ]
        + sems(112, 8),
        compiler_params=pltpu.CompilerParams(
            collective_id=number, has_side_effects=True, vmem_limit_bytes=40 * 2**20
        ),
        name=name,
    )(grad_keys, grad_values, away, stacked, *sources)


def late_kernel(one_ref, two_ref, one_out, two_out, *sem):
    place, wire = Place(), Wire(*sem)
    place.greet([place.beside, place.along_x(1), place.along_x(3)])
    work = [
        share_rows(place, wire, one_ref, one_out),
        share_rows(place, wire, two_ref, two_out),
    ]
    for steps, _ in work:
        for step in steps:
            step()
    for _, last in work:
        for copy in last:
            copy.wait_recv()
    wire.drain()


def gather_late(one, two):
    return pl.pallas_call(
        late_kernel,
        out_shape=(rows_shape(one), rows_shape(two)),
        in_specs=[ANY] * 2,
        out_specs=(ANY,) * 2,
        scratch_shapes=sems(16, 4),
        compiler_params=pltpu.CompilerParams(collective_id=5, has_side_effects=True),
        name="gather_late",
    )(one, two)


PIECE = 144
CUT = 80


def sum_kernel(
    one_ref, two_ref, small_ref, out_ref, small_out,
    far, mix, near, total, far_two, mix_two, near_two, part, other, final, small, heard, *sem,
):
    place, wire = Place(), Wire(*sem)
    y, z, h = place.y, place.z, place.h
    turns = [
        (place.fsdp, (y + 1 - 2 * (y % 2)) * 8 + z * 2 + h),
        (place.fsdp, ((y + 2) % 4) * 8 + z * 2 + h),
        (place.fsdp, y * 8 + (z + 1 - 2 * (z % 2)) * 2 + h),
        (place.fsdp, y * 8 + ((z + 2) % 4) * 2 + h),
        place.half,
    ]
    place.greet(place.around() + [turns[1], turns[3], place.half])
    ins = (one_ref, two_ref)
    parts = {0: pl.ds(0, CUT), 1: pl.ds(CUT, PIECE - CUT)}

    def chunk(t, da, db):
        origin = place.ring(t, da, db)
        return origin // 2

    def plus(*terms):
        result = terms[0].astype(F32)
        for term in terms[1:]:
            result = result + term.astype(F32)
        return result.astype(BF)

    small[...] = small_ref[...]
    passing = wire.push(small, heard.at[0], turns[0])
    order = (2, 1, 3, 0)
    way = {2: 1, 1: 1, 3: -1, 0: -1}
    first, second, loose = {}, {}, {}
    for db in order:
        for t in (0, 1):
            first[t, db] = wire.push(
                ins[t].at[chunk(t, 2, db)], far.at[t, db], place.near(t, 0, way[db])
            )
    for db in order:
        for t in (0, 1):
            loose[t, db] = wire.push(
                ins[t].at[chunk(t, -way[db], db)], near.at[t, db, 1], place.near(t, 0, -way[db])
            )
    for db in order:
        for t in (0, 1):
            first[t, db].wait_recv()
            mix[t, db] = plus(ins[t][chunk(t, way[db], db)], far[t, db])
            second[t, db] = wire.push(mix.at[t, db], near.at[t, db, 0], place.near(t, 0, way[db]))

    def hear(step):
        wire.sent[step_numbers[-1]].wait_send()
        wire.sent[step_numbers[-1]].wait_recv()
        small[...] += heard[step]
        waited.add(step_numbers[-1])
        if step < 4:
            step_numbers.append(len(wire.sent))
            wire.push(small, heard.at[step + 1], turns[step + 1])

    step_numbers, waited = [0], set()

    def settle(t, db):
        second[t, db].wait_recv()
        loose[t, db].wait_recv()
        total[t, db] = plus(ins[t][chunk(t, 0, db)], near[t, db, 0], near[t, db, 1])

    third, fourth = {}, {}
    for t in (0, 1):
        settle(t, 2)
        third[t] = [
            wire.push(
                total.at[t, 2, parts[b]], far_two.at[t, parts[b]], place.near(t, 1, sign)
            )
            for b, sign in ((0, 1), (1, -1))
        ]
    hear(0)
    for t in (0, 1):
        fourth[t] = []
        for b, sign, db in ((0, 1, 1), (1, -1, 3)):
            settle(t, db)
            fourth[t].append(
                wire.push(
                    total.at[t, db, parts[1 - b]],
                    near_two.at[t, b, parts[1 - b]],
                    place.near(t, 1, sign),
                )
            )
    hear(1)
    for t in (0, 1):
        for b, sign, db in ((0, 1, 1), (1, -1, 3)):
            third[t][b].wait_recv()
            mix_two[t, parts[b]] = plus(total[t, db, parts[b]], far_two[t, parts[b]])
            fourth[t].append(
                wire.push(
                    mix_two.at[t, parts[b]], near_two.at[t, b, parts[b]], place.near(t, 1, sign)
                )
            )
    hear(2)
    swapped = []
    for t in (0, 1):
        settle(t, 0)
        for copy in fourth[t]:
            copy.wait_recv()
        part[t] = plus(total[t, 0], near_two[t, 0], near_two[t, 1])
        swapped.append(wire.push(part.at[t], other.at[t], place.half))
    hear(3)

    def spot(t, origin, b):
        return out_ref.at[1 - t, origin // 2, parts[b]]

    def own(t, b):
        return final.at[1 - t, parts[b]]

    def ready(t, b):
        if b == 0:
            swapped[1 - t].wait_recv()
            final[1 - t] = plus(part[1 - t], other[1 - t])
            wire.keep(final.at[1 - t], out_ref.at[1 - t, place.ctx // 2])

    spread(place, wire, own, spot, ready)
    hear(4)
    small_out[...] = small[...]
    for number, copy in enumerate(wire.sent):
        if number not in waited:
            copy.wait_send()
    for copy in wire.local:
        copy.wait()


def sum_over_ctx(one, two, small):
    shape = (16, PIECE, D)
    return pl.pallas_call(
        sum_kernel,
        out_shape=(
            jax.ShapeDtypeStruct((2,) + shape, BF),
            jax.ShapeDtypeStruct(small.shape, F32),
        ),
        in_specs=[VM, VM, VM],
        out_specs=(ANY, VM),
        scratch_shapes=[
            room(2, 4, PIECE, D),
            room(2, 4, PIECE, D),
            room(2, 4, 2, PIECE, D),
            room(2, 4, PIECE, D),
            room(2, PIECE, D),
            room(2, PIECE, D),
            room(2, 2, PIECE, D),
            room(2, PIECE, D),
            room(2, PIECE, D),
            room(2, PIECE, D),
            pltpu.VMEM(small.shape, F32),
            pltpu.VMEM((5,) + small.shape, F32),
        ]
        + sems(128, 4),
        compiler_params=pltpu.CompilerParams(
            collective_id=6, has_side_effects=True, vmem_limit_bytes=48 * 2**20
        ),
        name="sum_over_ctx",
    )(one.reshape(shape), two.reshape(shape), small)


def weight_kernel(left_ref, joined_ref, low_ref, pre_ref, rows_ref, sums_ref, turned):
    turned[...] = jnp.transpose(left_ref[...])
    ones = jnp.ones((8, left_ref.shape[0]), BF)

    def panel(out, rows, right, at):
        rows_ref[out, :] = contract(turned[rows, :], right, ((1,), (0,))).astype(BF)
        if at is not None:
            sums_ref[:, at : at + D] = contract(ones, right, ((1,), (0,)))

    low = low_ref[...]
    panel(slice(1536, 2304), slice(0, 768), low, None)
    panel(slice(576, 768), slice(960, 1152), low, 0)
    for i in range(3):
        panel(
            slice(i * 192, (i + 1) * 192), slice(768, 960), joined_ref[:, i * D : (i + 1) * D], (1 + i) * D
        )
    for i in range(4):
        panel(
            slice(768 + i * 192, 960 + i * 192),
            slice(1152, 1344),
            pre_ref[:, i * D : (i + 1) * D],
            (4 + i) * D,
        )


def weight_grads(left, joined, low, pre):
    return pl.pallas_call(
        weight_kernel,
        out_shape=(
            jax.ShapeDtypeStruct((2304, D), BF),
            jax.ShapeDtypeStruct((8, 8 * D), F32),
        ),
        in_specs=[VM] * 4,
        out_specs=(VM, VM),
        scratch_shapes=[room(left.shape[1], left.shape[0])],
        compiler_params=pltpu.CompilerParams(vmem_limit_bytes=40 * 2**20),
        cost_estimate=pl.CostEstimate(
            flops=2 * 512 * 1769472, bytes_accessed=12 * 2**20, transcendentals=0
        ),
        name="weight_grads",
    )(left, joined, low, pre)


def pair_rows(values):
    lane = lax.broadcasted_iota(jnp.int32, values.shape, 1)
    zero = jnp.zeros_like(values)
    return jnp.concatenate(
        [jnp.where(lane < HEAD_DIM, values, zero), jnp.where(lane >= HEAD_DIM, values, zero)], 0
    )


def contract(left, right, dims):
    return lax.dot_general(left, right, (dims, ((), ())), preferred_element_type=F32)


def allowed_at(tile, block):
    key = tile * TILE + lax.broadcasted_iota(jnp.int32, (TILE, 2 * BLOCK), 0)
    query = block * BLOCK + lax.broadcasted_iota(jnp.int32, (TILE, 2 * BLOCK), 1) % BLOCK
    return key <= query


def forward_kernel(ctx_ref, q_ref, k_ref, v_ref, mixed_ref, turned_ref, log_ref, top, mass, acc):
    ctx = ctx_ref[0]
    for b in (0, 1):
        block = ctx if b == 0 else BLOCKS - 1 - ctx
        rows = slice(b * BLOCK, (b + 1) * BLOCK)
        queries = [
            pair_rows(q_ref[rows, p * 128 : (p + 1) * 128] * jnp.asarray(0.125, BF))
            for p in range(PAIRS)
        ]

        def step(tile, masked):
            start = pl.multiple_of(tile * TILE, TILE)
            for p in range(PAIRS):
                cols = slice(p * 128, (p + 1) * 128)
                scores = contract(k_ref[pl.ds(start, TILE), cols], queries[p], ((1,), (1,)))
                if masked:
                    scores = jnp.where(allowed_at(tile, block), scores, masked_score)
                    new_top = jnp.max(scores, 0, keepdims=True)
                else:
                    old_top = top[p : p + 1, :]
                    new_top = jnp.maximum(old_top, jnp.max(scores, 0, keepdims=True))
                weights = jnp.exp(scores - new_top)
                fresh_mass = jnp.sum(weights, 0, keepdims=True)
                fresh = contract(
                    v_ref[pl.ds(start, TILE), cols], weights.astype(BF), ((0,), (0,))
                )
                if not masked:
                    fade = jnp.exp(old_top - new_top)
                    fresh_mass = fresh_mass + mass[p : p + 1, :] * fade
                    fresh = fresh + acc[p] * fade
                top[p : p + 1, :] = new_top
                mass[p : p + 1, :] = fresh_mass
                acc[p] = fresh

        step(block // 4, True)

        @pl.loop(0, block // 4)
        def _(tile):
            step(tile, False)

        for p in range(PAIRS):
            cols = slice(p * 128, (p + 1) * 128)
            done = acc[p] / mass[p : p + 1, :]
            turned = jnp.concatenate([done[:HEAD_DIM, :BLOCK], done[HEAD_DIM:, BLOCK:]], 0)
            turned_ref[cols, rows] = turned
            mixed_ref[rows, cols] = jnp.transpose(turned).astype(BF)
            row = b * PAIRS + p
            log_ref[row : row + 1, :] = top[p : p + 1, :] + jnp.log(mass[p : p + 1, :])


def attend_forward(ctx, queries, keys, values):
    return pl.pallas_call(
        forward_kernel,
        out_shape=(
            jax.ShapeDtypeStruct((2 * BLOCK, HALF), BF),
            jax.ShapeDtypeStruct((HALF, 2 * BLOCK), F32),
            jax.ShapeDtypeStruct((8, 2 * BLOCK), F32),
        ),
        in_specs=[SM, VM, VM, VM],
        out_specs=(VM, VM, VM),
        scratch_shapes=[
            pltpu.VMEM((8, 2 * BLOCK), F32),
            pltpu.VMEM((8, 2 * BLOCK), F32),
            pltpu.VMEM((PAIRS, 128, 2 * BLOCK), F32),
        ],
        compiler_params=pltpu.CompilerParams(vmem_limit_bytes=40 * 2**20),
        cost_estimate=pl.CostEstimate(
            flops=4 * 33 * 128 * 128 * 6 * 128, bytes_accessed=8 * 2**20, transcendentals=33 * 128 * 128 * 6
        ),
        name="attend_forward",
    )(ctx, queries, keys, values)


def backward_kernel(
    ctx_ref, q_ref, k_ref, v_ref, g_ref, turned_ref, log_ref, gq_ref, gk_ref, gv_ref, gk_acc, gv_acc, gq_acc
):
    ctx = ctx_ref[0]
    gk_acc[...] = jnp.zeros_like(gk_acc)
    gv_acc[...] = jnp.zeros_like(gv_acc)
    for b in (0, 1):
        block = ctx if b == 0 else BLOCKS - 1 - ctx
        rows = slice(b * BLOCK, (b + 1) * BLOCK)
        queries, grads, deltas = [], [], []
        for p in range(PAIRS):
            cols = slice(p * 128, (p + 1) * 128)
            queries.append(pair_rows(q_ref[rows, cols] * jnp.asarray(0.125, BF)))
            grad = g_ref[rows, cols]
            grads.append(pair_rows(grad))
            both = jnp.transpose(grad.astype(F32)) * turned_ref[cols, rows]
            deltas.append(
                jnp.concatenate(
                    [
                        jnp.sum(both[:HEAD_DIM], 0, keepdims=True),
                        jnp.sum(both[HEAD_DIM:], 0, keepdims=True),
                    ],
                    1,
                )
            )
        gq_acc[...] = jnp.zeros_like(gq_acc)

        def step(tile, masked):
            start = pl.multiple_of(tile * TILE, TILE)
            here = pl.ds(start, TILE)
            for p in range(PAIRS):
                cols = slice(p * 128, (p + 1) * 128)
                row = b * PAIRS + p
                keys = k_ref[here, cols]
                scores = contract(keys, queries[p], ((1,), (1,)))
                chances = jnp.exp(scores - log_ref[row : row + 1, :])
                if masked:
                    chances = jnp.where(allowed_at(tile, block), chances, 0.0)
                grad_chance = contract(v_ref[here, cols], grads[p], ((1,), (1,)))
                grad_score = (chances * (grad_chance - deltas[p])).astype(BF)
                gv_acc[here, cols] += contract(chances.astype(BF), grads[p], ((1,), (0,)))
                gk_acc[here, cols] += contract(grad_score, queries[p], ((1,), (0,)))
                gq_acc[p] += contract(keys, grad_score, ((0,), (0,)))

        step(block // 4, True)

        @pl.loop(0, block // 4)
        def _(tile):
            step(tile, False)

        for p in range(PAIRS):
            cols = slice(p * 128, (p + 1) * 128)
            done = gq_acc[p] * 0.125
            turned = jnp.concatenate([done[:HEAD_DIM, :BLOCK], done[HEAD_DIM:, BLOCK:]], 0)
            gq_ref[rows, cols] = jnp.transpose(turned)
    gk_ref[...] = gk_acc[...].astype(BF)
    gv_ref[...] = gv_acc[...].astype(BF)


def attend_backward(ctx, queries, keys, values, grad_mixed, turned, log_total):
    whole = jax.ShapeDtypeStruct((BLOCKS * BLOCK, HALF), BF)
    return pl.pallas_call(
        backward_kernel,
        out_shape=(jax.ShapeDtypeStruct((2 * BLOCK, HALF), F32), whole, whole),
        in_specs=[SM] + [VM] * 6,
        out_specs=(VM, VM, VM),
        scratch_shapes=[
            pltpu.VMEM((BLOCKS * BLOCK, HALF), F32),
            pltpu.VMEM((BLOCKS * BLOCK, HALF), F32),
            pltpu.VMEM((PAIRS, 128, 2 * BLOCK), F32),
        ],
        compiler_params=pltpu.CompilerParams(vmem_limit_bytes=48 * 2**20),
        cost_estimate=pl.CostEstimate(
            flops=10 * 33 * 128 * 128 * 6 * 128, bytes_accessed=16 * 2**20, transcendentals=33 * 128 * 128 * 6
        ),
        name="attend_backward",
    )(ctx, queries, keys, values, grad_mixed, turned, log_total)


def norm_parts(values):
    centre = jnp.mean(values, -1, keepdims=True)
    shifted = values - centre
    spread = jnp.mean(shifted * shifted, -1, keepdims=True)
    scale = lax.rsqrt(spread + epsilon)
    return shifted * scale, scale


def norm_input_grad(grad_norm, gain, unit, scale):
    e = grad_norm * gain
    return scale * (
        e - jnp.mean(e, -1, keepdims=True) - unit * jnp.mean(e * unit, -1, keepdims=True)
    )


def turn_tables(first_row, row_count):
    half_rot = ROTARY // 2
    positions = first_row + jnp.arange(row_count, dtype=jnp.int32)
    exponent = jnp.arange(half_rot, dtype=F32) * (2.0 / ROTARY)
    frequency = jnp.power(10000.0, -exponent)
    angle = positions.astype(F32)[:, None] * frequency[None, :]
    cosine, sine = jnp.cos(angle), jnp.sin(angle)
    rest = jnp.zeros((row_count, HEAD_DIM - ROTARY), F32)
    none = jnp.zeros_like(sine)
    keep = jnp.tile(jnp.concatenate([cosine, cosine, rest + 1.0], 1), (1, HEADS))
    low = jnp.tile(jnp.concatenate([-sine, none, rest], 1), (1, HEADS))
    high = jnp.tile(jnp.concatenate([none, sine, rest], 1), (1, HEADS))
    return keep, low, high


def rotate(values, tables):
    keep, low, high = tables
    shift = ROTARY // 2
    return values * keep + jnp.roll(values, -shift, 1) * low + jnp.roll(values, shift, 1) * high


def rotate_back(values, tables):
    keep, low, high = tables
    shift = ROTARY // 2
    return (
        values * keep + jnp.roll(values * low, shift, 1) + jnp.roll(values * high, -shift, 1)
    )


def dot(left, right):
    return jnp.dot(left, right, preferred_element_type=F32)


def phi_parts(values):
    cumulative = 0.5 * (1.0 + lax.erf(values * (2.0**-0.5)))
    density = jnp.exp(-0.5 * values * values) * (0.5 / jnp.pi) ** 0.5
    return cumulative, density


def shards(
    tokens,
    cotangent,
    ln1_gain,
    ln1_bias,
    ln2_gain,
    ln2_bias,
    qkv_weight,
    qkv_bias,
    out_weight,
    out_bias,
    up_weight,
    up_bias,
    down_weight,
    down_bias,
):
    row_count = tokens.shape[1]
    fsdp = lax.axis_index("fsdp")
    ctx = lax.axis_index("ctx")
    upper = ctx % 2 == 1
    ctx_word = ctx.astype(jnp.int32).reshape(1)
    tables = turn_tables(ctx * row_count, row_count)

    def mine(values):
        return jnp.where(upper, values[:, HALF:], values[:, :HALF])

    def theirs(values):
        return jnp.where(upper, values[:, :HALF], values[:, HALF:])

    def join(own, other):
        return jnp.where(
            upper, jnp.concatenate([other, own], 1), jnp.concatenate([own, other], 1)
        )

    vectors = (ln1_gain, ln1_bias, ln2_gain, ln2_bias, out_bias, down_bias, qkv_bias, up_bias)
    packed = jnp.concatenate([vector.reshape(-1) for vector in vectors])
    packed = jnp.pad(packed, (0, 16 * HALF - packed.shape[0])).reshape(16, HALF)
    first_weight, table = gather_first(qkv_weight, packed)
    table = table.reshape(4, 16 * HALF).astype(F32)
    full_vectors, start = [], 0
    for vector in vectors:
        width = vector.shape[1]
        piece = table[:, start : start + LAYERS * width].reshape(4, LAYERS, width)
        full_vectors.append(jnp.transpose(piece, (1, 0, 2)).reshape(LAYERS, 4 * width))
        start += LAYERS * width
    gain_one, bias_one, gain_two, bias_two, b_out, b_down, b_qkv, b_up = full_vectors

    qkv_full = [first_weight, None]
    gathered = [None] * LAYERS
    stream = tokens[0].astype(F32)
    saved = []
    for layer_index in range(LAYERS):
        w_qkv = qkv_full[layer_index]
        unit, scale = norm_parts(stream)
        norm_one = (unit * gain_one[layer_index] + bias_one[layer_index]).astype(BF)
        norm_two = (unit * gain_two[layer_index] + bias_two[layer_index]).astype(BF)
        joined = dot(norm_one, w_qkv) + b_qkv[layer_index]
        queries = rotate(joined[:, :D], tables).astype(BF)
        key_rows = rotate(joined[:, D : 2 * D], tables).astype(BF)
        value_rows = joined[:, 2 * D :].astype(BF)
        jobs = [(layer_index, out_weight), (layer_index, up_weight), (layer_index, down_weight)]
        if layer_index + 1 < LAYERS:
            jobs.append((layer_index + 1, qkv_weight))
        other_queries, keys, values, w_out, w_up, w_down, *more = gather_pair(
            "gather_pair_%d" % layer_index,
            1 + layer_index,
            (theirs(queries), theirs(key_rows), theirs(value_rows)),
            (mine(key_rows), mine(value_rows)),
            jobs,
        )
        if more:
            qkv_full[layer_index + 1] = more[0]
        gathered[layer_index] = (w_qkv, w_out, w_up, w_down)
        queries = jnp.concatenate([mine(queries), other_queries], 0)
        keys = keys.reshape(BLOCKS * BLOCK, HALF)
        values = values.reshape(BLOCKS * BLOCK, HALF)
        mixed_two, turned, log_total = attend_forward(ctx_word, queries, keys, values)
        mixed_low = join(mixed_two[:BLOCK], mirrored(mixed_two[BLOCK:]))
        hidden_pre = dot(norm_two, w_up) + b_up[layer_index]
        hidden_low = (hidden_pre * phi_parts(hidden_pre)[0]).astype(BF)
        mlp_branch = dot(hidden_low, w_down)
        blank = jnp.zeros((row_count, 64), BF)
        stacked = jnp.stack(
            [
                jnp.concatenate(
                    [
                        hidden_low[:, d * D : (d + 1) * D],
                        norm_one[:, d * 192 : (d + 1) * 192],
                        mixed_low[:, d * 192 : (d + 1) * 192],
                        norm_two[:, d * 192 : (d + 1) * 192],
                        blank,
                    ],
                    1,
                )
                for d in range(4)
            ],
            0,
        )
        saved.append((unit, scale, queries, keys, values, turned, log_total, hidden_pre, stacked))
        stream = (
            stream + dot(mixed_low, w_out) + b_out[layer_index] + mlp_branch + b_down[layer_index]
        )

    gradient = cotangent[0].astype(F32)
    waiting, low_rows, pre_rows, left_rows = (), [None] * 2, [None] * 2, [None] * 2
    joined_rows, norm_rows = [None] * 2, [None] * 2
    for layer_index in range(LAYERS - 1, -1, -1):
        w_qkv, w_out, w_up, w_down = gathered[layer_index]
        unit, scale, queries, keys, values, turned, log_total, hidden_pre, stacked = saved[
            layer_index
        ]
        grad_low = gradient.astype(BF)
        grad_mixed = contract(grad_low, w_out, ((1,), (1,))).astype(BF)
        grad_mixed = jnp.concatenate([mine(grad_mixed), mirrored(theirs(grad_mixed))], 0)
        cumulative, density = phi_parts(hidden_pre)
        grad_hidden = contract(grad_low, w_down, ((1,), (1,)))
        grad_pre = (grad_hidden * (cumulative + hidden_pre * density)).astype(BF)
        grad_norm_two = contract(grad_pre, w_up, ((1,), (1,)))
        grad_query, grad_keys, grad_values = attend_backward(
            ctx_word, queries, keys, values, grad_mixed, turned, log_total
        )
        whole = (BLOCKS, BLOCK, HALF)
        own_pair, back_pair, back_query, left, low, pre, *more = scatter_pair(
            "scatter_pair_%d" % layer_index,
            3 + layer_index,
            grad_keys.reshape(whole),
            grad_values.reshape(whole),
            grad_query[BLOCK:].astype(BF),
            stacked,
            (grad_low, grad_pre) + waiting,
        )
        left_rows[layer_index], low_rows[layer_index], pre_rows[layer_index] = left, low, pre
        if more:
            joined_rows[layer_index + 1], norm_rows[layer_index + 1] = more
        grad_query = join(grad_query[:BLOCK], back_query.astype(F32))
        grad_key = join(own_pair[0], back_pair[0].astype(F32))
        grad_value = join(own_pair[1], back_pair[1].astype(F32))
        grad_joined = jnp.concatenate(
            [rotate_back(grad_query, tables), rotate_back(grad_key, tables), grad_value], 1
        ).astype(BF)
        grad_norm_one = contract(grad_joined, w_qkv, ((1,), (1,)))
        norm_sums = jnp.stack(
            [
                jnp.sum(grad_norm_one * unit, 0),
                jnp.sum(grad_norm_one, 0),
                jnp.sum(grad_norm_two * unit, 0),
                jnp.sum(grad_norm_two, 0),
            ],
            0,
        )
        waiting = (grad_joined, jnp.pad(norm_sums, ((0, 12), (0, 0))).astype(BF))
        gradient = (
            gradient
            + norm_input_grad(grad_norm_one, gain_one[layer_index], unit, scale)
            + norm_input_grad(grad_norm_two, gain_two[layer_index], unit, scale)
        )
    joined_rows[0], norm_rows[0] = gather_late(*waiting)

    def own_part(vector, width):
        return lax.dynamic_slice_in_dim(vector, fsdp * width, width, vector.ndim - 1)

    packs, lines = [], []
    for layer_index in range(LAYERS):
        rows, sums = weight_grads(
            left_rows[layer_index],
            joined_rows[layer_index],
            low_rows[layer_index],
            pre_rows[layer_index],
        )
        packs.append(rows)
        sums = sums[0]
        norms = own_part(jnp.sum(norm_rows[layer_index].reshape(4, 16, D)[:, :4].astype(F32), 0), 192)
        lines += [
            jnp.pad(own_part(sums[:D], 192), (0, D - 192)),
            jnp.pad(own_part(sums[D : 4 * D], 576), (0, D - 576)),
            own_part(sums[4 * D :], D),
            norms.reshape(D),
        ]
    summed, small = sum_over_ctx(packs[0], packs[1], jnp.stack(lines, 0))
    grads = []
    for layer_index in range(LAYERS):
        rows = summed[layer_index].reshape(2304, D)
        line = small[4 * layer_index : 4 * layer_index + 4]
        norms = line[3].reshape(4, 192)
        grads.append(
            (
                norms[0],
                norms[1],
                norms[2],
                norms[3],
                jnp.concatenate([rows[i * 192 : (i + 1) * 192] for i in range(3)], 1),
                line[1, :576],
                rows[576:768],
                line[0, :192],
                jnp.concatenate([rows[768 + i * 192 : 960 + i * 192] for i in range(4)], 1),
                line[2],
                rows[1536:],
                line[0, :192],
            )
        )
    stacked = [
        jnp.stack([grads[layer_index][member] for layer_index in range(LAYERS)], 0).astype(F32)
        for member in range(12)
    ]
    return (stream.astype(BF)[None], gradient[None], *stacked)


def solution(mesh):
    matrix, vector = P(None, "fsdp", None), P(None, "fsdp")
    rows = P("fsdp", "ctx", None)
    params = (
        vector,
        vector,
        vector,
        vector,
        matrix,
        vector,
        matrix,
        vector,
        matrix,
        vector,
        matrix,
        vector,
    )
    return jax.shard_map(
        shards,
        mesh=mesh,
        in_specs=(rows, rows) + params,
        out_specs=(rows, rows) + params,
        check_vma=False,
    )
```

time: 2200 us -> 719 us (0.33)
  waiting for transfers between devices: 1550 us -> 8.16 us
  Pallas kernels: 0 us -> 535 us
  matrix products: 260 us -> 32 us
  blocking collectives: 222 us -> 0 us
  other arithmetic: 67.2 us -> 35 us
    all_gather x12 -> x0, waiting for transfers between devices: 572 us -> none  [the longest x2 225 us: attend_forward(): lax.all_gather(key_rows, 'ctx', axis=0, tiled=True)]
    pallas_call x0 -> x13, Pallas kernels: none -> 535 us  [the longest x2 220 us: gather_pair(): pl.pallas_call(functools.partial(gather_kernel, layers), out_shape=(jax.S...]
    unnamed x25 -> x0, waiting for transfers between devices: 452 us -> none
    reduce_scatter x8 -> x0, waiting for transfers between devices: 339 us -> none  [the longest x2 106 us: reduce_grads(): lax.psum_scatter(part_down_w.astype(jnp.bfloat16), 'fsdp', scatter_dimens...]
    dot_general x38 -> x16, matrix products: 260 us -> 32 us  [the longest x8 18.5 us: dot(): return jnp.dot(left, right, preferred_element_type=F32)]
    psum x1 -> x0, waiting for transfers between devices: 192 us -> none  [reduce_grads(): lax.psum(own_qkv_w.astype(jnp.bfloat16), 'ctx').astype(jnp.float32)]
    psum x1 -> x0, blocking collectives: 186 us -> none  [reduce_grads(): lax.psum(own_gain_one.astype(jnp.bfloat16), 'ctx').astype(jnp.float32)]
    reduce_sum x12 -> x5, other arithmetic: 31.6 us -> 2.13 us  [the longest x2 1.64 us: shards(): jnp.sum(norm_rows[layer_index].reshape(4, 16, D)[:, :4].astype(F32), 0)]
  transfers between devices with their start and end apart: 23 -> 4, of which waited for: 19 -> 1; matrix products, arithmetic and copies ran while one was open for 12% -> 4% of each run, Pallas kernels for 0% -> 2%
where the time goes in v1:
time: 719 us; the launch traced here: 710 us
  Pallas kernels  535 us (74%)
  local copies, waits for them, and re-layouts  87.5 us (12%)
  other arithmetic  35 us (5%)
  matrix products  32 us (4%)
  starting transfers between devices  10.3 us (1%)
  waiting for transfers between devices  8.16 us (1%)
    pallas_call x2, Pallas kernels, gather_pair(): pl.pallas_call(functools.partial(gather_kernel, layers), out_shape=(jax.S...  220 us
    pallas_call x2, Pallas kernels, scatter_pair(): pl.pallas_call(functools.partial(scatter_kernel, len(sources)), out_shape...  105 us
    pallas_call x1, Pallas kernels, sum_over_ctx(): pl.pallas_call(sum_kernel, out_shape=(jax.ShapeDtypeStruct((2,) + shape,...  94.2 us
    pallas_call x2, Pallas kernels, attend_backward(): pl.pallas_call(backward_kernel, out_shape=(jax.ShapeDtypeStruct((2 * BLOC...  32.8 us
    unnamed x246, local copies, waits for them, and re-layouts  32.6 us
    pallas_call x1, Pallas kernels, gather_first(): pl.pallas_call(first_kernel, out_shape=(full_shape(weight), full_shape(ve...  31.5 us
    pallas_call x2, Pallas kernels, attend_forward(): pl.pallas_call(forward_kernel, out_shape=(jax.ShapeDtypeStruct((2 * BLOCK...  24.9 us
    pallas_call x1, Pallas kernels, gather_late(): pl.pallas_call(late_kernel, out_shape=(rows_shape(one), rows_shape(two)),...  21.1 us
  transfers between devices with their start and end apart: 4, of which 1 were waited for; matrix products, arithmetic and copies ran while one was open for 4% of the time, Pallas kernels for 2%

profile of v1, /device:TPU:0, one launch (start us, length us, event | category | flops | bytes accessed | tf_op | source)
XLA Modules:
  0.0 710.3 jit_solution(16473431825254484327)
XLA Ops:
  9.1 31.5 %gather_first.1 = (bf16[768,2304]{1,0:T(8,128)(2,1)}, bf16[64,384]{1,0:T(8,128)(2,1)}) custom-call(bf16[2,192,2304]{2,1,0:T(8,128)(2,1)} %refs_3_.1, bf16[16,384]{1,0:T(8,128)(2,1)} %reshape.280.vector_ref), custom_call_target="tpu_custom_call" | custom-call | tf_op jit(solution)/shard_map/gather_first/pallas_call | solution.py:295
  46.7 3.5 fusion.119
  50.8 1.2 fusion.103
  53.8 1.2 copy.31
  55.0 1.7 fusion.55
  58.1 1.6 broadcast_select_fusion.10
  59.7 123.4 %gather_pair_0.1 = (bf16[128,384]{1,0:T(8,128)(2,1)}, bf16[32,128,384]{2,1,0:T(8,128)(2,1)}, bf16[32,128,384]{2,1,0:T(8,128)(2,1)}, bf16[768,768]{1,0:T(8,128)(2...) custom-call(bf16[128,384]{1,0:T(8,128)(2,1)} %get-tuple-element.258.q_ref, ...), custom_call_target="tpu_custom_call" | custom-call | tf_op jit(solution)/shard_map/gather_pair_0/pallas_call | solution.py:362
  184.1 1.9 copy-done.1
  185.9 1.9 copy-done.2
  187.8 12.4 %attend_forward.2 = (bf16[256,384]{1,0:T(8,128)(2,1)S(1)}, f32[384,256]{1,0:T(8,128)S(1)}, f32[8,256]{1,0:T(8,128)S(1)}) custom-call(s32[1]{0:T(128)} %bitcast.1.ctx_ref, bf16[256,384]{1,0:T(8,128)(2,1)S(1)} %pad_maximum_fusion.4.q_ref, bf16[4096,384]{1,0:T(8,128)(2,1)S(1)} %bitcast.188, bf16[4096,384]{1,0:T(8,128)(2,1)S(1)} %bitcast.190), custom_call_target="tpu_custom_call" | custom-call | flops 1660944384 | bytes 8388608 | tf_op jit(solution)/shard_map/attend_forward/pallas_call | solution.py:821
  203.3 5.1 multiply_convert_fusion.1
  209.3 1.6 fusion.122
  213.7 1.6 fusion.120
  219.8 96.2 %gather_pair_1.1 = (bf16[128,384]{1,0:T(8,128)(2,1)}, bf16[32,128,384]{2,1,0:T(8,128)(2,1)}, bf16[32,128,384]{2,1,0:T(8,128)(2,1)}, bf16[768,768]{1,0:T(8,128)(2...) custom-call(bf16[128,384]{1,0:T(8,128)(2,1)} %get-tuple-element.252.q_ref, ...), custom_call_target="tpu_custom_call" | custom-call | tf_op jit(solution)/shard_map/gather_pair_1/pallas_call | solution.py:362
  316.0 3.6 multiply_convert_fusion
  320.5 1.6 fusion.123
  323.5 12.5 %attend_forward.3 = (bf16[256,384]{1,0:T(8,128)(2,1)S(1)}, f32[384,256]{1,0:T(8,128)S(1)}, f32[8,256]{1,0:T(8,128)S(1)}) custom-call(s32[1]{0:T(128)} %bitcast.1.ctx_ref, bf16[256,384]{1,0:T(8,128)(2,1)S(1)} %pad_maximum_fusion.5.q_ref, bf16[4096,384]{1,0:T(8,128)(2,1)S(1)} %bitcast.192, bf16[4096,384]{1,0:T(8,128)(2,1)S(1)} %bitcast.194), custom_call_target="tpu_custom_call" | custom-call | flops 1660944384 | bytes 8388608 | tf_op jit(solution)/shard_map/attend_forward/pallas_call | solution.py:821
  336.7 1.3 collective-permute-start.1
  337.9 1.7 fusion.1.refs_1_
  339.7 2.5 fusion.124
  343.5 6.9 collective-permute-start.2
  350.5 1.7 concatenate.204
  352.2 1.7 concatenate.203
  355.7 1.6 pad_maximum_fusion.1.stack_ref
  359.1 16.5 %attend_backward.2 = (f32[256,384]{1,0:T(8,128)S(1)}, bf16[4096,384]{1,0:T(8,128)(2,1)S(1)}, bf16[4096,384]{1,0:T(8,128)(2,1)}) custom-call(s32[1]{0:T(128)} %bitcast.1.ctx_ref, bf16[256,384]{1,0:T(8,128)(2,1)S(1)} %pad_maximum_fusion.5.q_ref, bf16[4096,384]{1,0:T(8,128)(2,1)} %bitcast.191, bf16[4096,384]{1,0:T(8,128)(2,1)} %bitcast.193, ...), custom_call_target="tpu_custom_call" | custom-call | flops 4152360960 | bytes 16777216 | tf_op jit(solution)/shard_map/attend_backward/pallas_call | solution.py:904
  375.6 1.7 copy-done.5
  380.5 1.9 concatenate.188
  382.4 1.9 concatenate.187
  384.2 1.8 concatenate.186
  386.1 1.8 concatenate.185
  387.9 1.5 pad_maximum_fusion.stack_ref
  389.5 1.9 copy-done.6
  391.3 53.6 %scatter_pair_1.1 = (f32[2,128,384]{2,1,0:T(8,128)S(1)}, bf16[2,128,384]{2,1,0:T(8,128)(2,1)S(1)}, bf16[128,384]{1,0:T(8,128)(2,1)S(1)}, bf16[512,1408]{1,0:T(8,...) custom-call(bf16[32,128,384]{2,1,0:T(8,128)(2,1)S(1)} %bitcast.195, ...), custom_call_target="tpu_custom_call" | custom-call | tf_op jit(solution)/shard_map/scatter_pair_1/pallas_call | solution.py:488
  444.9 1.1 copy-done.16
  446.2 1.1 copy-done.31
  450.8 1.5 multiply_reduce_fusion.1
  454.2 1.7 fusion.2.refs_1_
  456.0 2.4 fusion.125
  458.4 1.1 collective-permute-start.3
  460.7 8.2 %collective-permute-done.3 = bf16[128,384]{1,0:T(8,128)(2,1)S(1)} collective-permute-done((bf16[128,384]{1,0:T(8,128)(2,1)S(1)}, bf16[128,384]{1,0:T(8,128)(2,1)S(1)}, u32[]{:S(2)}, u32[]{:S(2)}) %collective-permute-start.3) | collective-permute-done | bytes 98336 | tf_op jit(solution)/shard_map/ppermute | solution.py:31
  468.9 16.3 %attend_backward.3 = (f32[256,384]{1,0:T(8,128)S(1)}, bf16[4096,384]{1,0:T(8,128)(2,1)S(1)}, bf16[4096,384]{1,0:T(8,128)(2,1)}) custom-call(s32[1]{0:T(128)} %bitcast.1.ctx_ref, bf16[256,384]{1,0:T(8,128)(2,1)S(1)} %pad_maximum_fusion.4.q_ref, bf16[4096,384]{1,0:T(8,128)(2,1)} %bitcast.187, bf16[4096,384]{1,0:T(8,128)(2,1)} %bitcast.189, ...), custom_call_target="tpu_custom_call" | custom-call | flops 4152360960 | bytes 16777216 | tf_op jit(solution)/shard_map/attend_backward/pallas_call | solution.py:904
  485.2 1.7 copy-done.11
  486.9 51.0 %scatter_pair_0.1 = (f32[2,128,384]{2,1,0:T(8,128)S(1)}, bf16[2,128,384]{2,1,0:T(8,128)(2,1)S(1)}, bf16[128,384]{1,0:T(8,128)(2,1)S(1)}, bf16[512,1408]{1,0:T(8,...) custom-call(bf16[32,128,384]{2,1,0:T(8,128)(2,1)} %bitcast.196, ...), custom_call_target="tpu_custom_call" | custom-call | tf_op jit(solution)/shard_map/scatter_pair_0/pallas_call | solution.py:488
  537.9 1.4 copy-done.12
  539.3 1.1 copy-done.18
  540.7 1.4 copy-done.9
  545.2 2.6 fusion.44
  548.5 21.1 %gather_late.1 = (bf16[512,2304]{1,0:T(8,128)(2,1)}, bf16[64,768]{1,0:T(8,128)(2,1)}) custom-call(bf16[128,2304]{1,0:T(8,128)(2,1)} %pad_maximum_fusion.3.one_ref, bf16[16,768]{1,0:T(8,128)(2,1)} %fusion.90.two_ref), custom_call_target="tpu_custom_call" | custom-call | tf_op jit(solution)/shard_map/gather_late/pallas_call | solution.py:535
  569.6 1.9 copy-done.10
  571.5 1.7 copy-done.14
  573.1 1.4 copy-done.19
  574.5 1.1 copy-done.23
  575.6 3.0 weight_grads.2
  579.3 3.0 weight_grads.3
  582.3 1.8 copy-done
  590.9 1.3 constant_dynamic-slice_fusion.4
  592.2 1.3 constant_dynamic-slice_fusion.1
  595.0 1.4 stack.169.small_ref
  597.1 94.2 %sum_over_ctx.1 = (bf16[2,16,144,768]{3,2,1,0:T(8,128)(2,1)}, f32[8,768]{1,0:T(8,128)S(1)}) custom-call(bf16[16,144,768]{2,1,0:T(8,128)(2,1)S(1)} %bitcast.185, bf16[16,144,768]{2,1,0:T(8,128)(2,1)} %bitcast.186, f32[8,768]{1,0:T(8,128)S(1)} %copy-done.24), custom_call_target="tpu_custom_call" | custom-call | tf_op jit(solution)/shard_map/sum_over_ctx/pallas_call | solution.py:679
  691.4 3.5 fusion.97
  698.6 2.0 maximum_convert_fusion.2
  701.2 1.1 maximum_convert_fusion.3
  702.6 2.5 maximum_convert_fusion
  705.7 2.5 maximum_convert_fusion.1
  (435 shorter events, 68.1 us)
Async XLA Ops:
  0.6 42.4 %copy-start.36 = (bf16[1,128,768]{2,1,0:T(8,128)(2,1)S(1)}, bf16[1,128,768]{2,1,0:T(8,128)(2,1)}, u32[]{:S(2)}) copy-start(bf16[1,128,768]{2,1,0:T(8,128)(2,1)} %param.14) | copy-start | bytes 589828
  41.5 5.3 copy-start.66
  43.1 7.1 %copy-start.81 = (f32[768]{0:T(1024)}, f32[768]{0:T(1024)S(1)}, u32[]{:S(2)}) copy-start(f32[768]{0:T(1024)S(1)} %mul.330) | copy-start | bytes 9220
  43.2 7.0 copy-start.97
  43.4 6.8 copy-start.102
  45.0 5.2 copy-start.83
  52.5 165.4 %copy-start.28 = (f32[128,768]{1,0:T(8,128)}, f32[128,768]{1,0:T(8,128)S(1)}, u32[]{:S(2)}) copy-start(f32[128,768]{1,0:T(8,128)S(1)} %copy.29) | copy-start | bytes 1179652
  52.9 165.0 %copy-start.30 = (f32[128,768]{1,0:T(8,128)}, f32[128,768]{1,0:T(8,128)S(1)}, u32[]{:S(2)}) copy-start(f32[128,768]{1,0:T(8,128)S(1)} %copy.30) | copy-start | bytes 1179652
  54.9 163.0 %copy-start.32 = (f32[128,768]{1,0:T(8,128)}, f32[128,768]{1,0:T(8,128)S(1)}, u32[]{:S(2)}) copy-start(f32[128,768]{1,0:T(8,128)S(1)} %copy.31) | copy-start | bytes 1179652
  187.8 14.1 %slice-start.8 = ((f32[4,6144]{1,0:T(4,128)}), f32[4,1536]{1,0:T(4,128)S(1)}, s32[]{:S(2)}) async-start(f32[4,6144]{1,0:T(4,128)} %copy-done.66), calls=%async_computation.8 | async-start | bytes 49152 | tf_op jit(solution)/shard_map/slice | solution.py:1018
  187.8 14.3 %copy-start.95 = (f32[4,192]{1,0:T(4,128)S(1)}, f32[4,192]{1,0:T(4,128)}, u32[]{:S(2)}) copy-start(f32[4,192]{1,0:T(4,128)} %get-tuple-element.141) | copy-start | bytes 9220
  187.8 14.4 %copy-start.90 = (f32[4,384]{1,0:T(4,128)S(1)}, f32[4,384]{1,0:T(4,128)}, u32[]{:S(2)}) copy-start(f32[4,384]{1,0:T(4,128)} %get-tuple-element.262) | copy-start | bytes 18436
  187.8 14.6 %copy-start.50 = (bf16[128,768]{1,0:T(8,128)(2,1)S(1)}, bf16[128,768]{1,0:T(8,128)(2,1)}, u32[]{:S(2)}) copy-start(bf16[128,768]{1,0:T(8,128)(2,1)} %get-tuple-element.216) | copy-start | bytes 589828
  200.9 11.7 %collective-permute-start = (bf16[128,384]{1,0:T(8,128)(2,1)}, bf16[128,384]{1,0:T(8,128)(2,1)}, u32[]{:S(2)}, u32[]{:S(2)}) collective-permute-start(bf16[128,384]{1,0:T(8,128)(2,1)} %get-tuple-element.255), channel_id=1, source_target_pairs={{0,31},{1,30},{2,29},{3,28},{4,27},{5,26},{6,25},{7,24},{8,23},{9,... | collective-permute-start | bytes 294920 | tf_op jit(solution)/shard_map/ppermute | solution.py:31
  202.2 13.4 %copy-start.85 = (f32[768]{0:T(1024)}, f32[768]{0:T(1024)S(1)}, u32[]{:S(2)}) copy-start(f32[768]{0:T(1024)S(1)} %mul.353) | copy-start | bytes 9220
  202.4 6.9 slice-start.4
  203.3 6.0 slice-start.5
  209.3 4.4 copy-start.41
  211.3 4.3 copy-start.87
  215.8 100.2 %copy-start.51 = (bf16[128,768]{1,0:T(8,128)(2,1)}, bf16[128,768]{1,0:T(8,128)(2,1)S(1)}, u32[]{:S(2)}) copy-start(bf16[128,768]{1,0:T(8,128)(2,1)S(1)} %get-tuple-element.202) | copy-start | bytes 589828
  316.0 4.5 copy-start.38
  320.5 3.0 copy-start.4
  323.5 14.5 %copy-start.15 = (bf16[1,128,768]{2,1,0:T(8,128)(2,1)S(1)}, bf16[1,128,768]{2,1,0:T(8,128)(2,1)}, u32[]{:S(2)}) copy-start(bf16[1,128,768]{2,1,0:T(8,128)(2,1)} %param.15) | copy-start | bytes 589828
  336.0 3.7 copy-start.26
  336.0 3.7 slice-start.2
  336.7 41.4 %collective-permute-start.1 = (bf16[128,384]{1,0:T(8,128)(2,1)}, bf16[128,384]{1,0:T(8,128)(2,1)}, u32[]{:S(2)}, u32[]{:S(2)}) collective-permute-start(bf16[128,384]{1,0:T(8,128)(2,1)} %get-tuple-element.249), channel_id=1, source_target_pairs={{0,31},{1,30},{2,29},{3,28},{4,27},{5,26},{6,25},{7,24},{8,23},{9,... | collective-permute-start | bytes 294920 | tf_op jit(solution)/shard_map/ppermute | solution.py:31
  342.2 8.3 %copy-start.63 = (bf16[128,768]{1,0:T(8,128)(2,1)S(1)}, bf16[128,768]{1,0:T(8,128)(2,1)}, u32[]{:S(2)}) copy-start(bf16[128,768]{1,0:T(8,128)(2,1)} %get-tuple-element.190) | copy-start | bytes 589828
  342.2 8.3 %copy-start.73 = (bf16[128,192]{1,0:T(8,128)(2,1)S(1)}, bf16[128,192]{1,0:T(8,128)(2,1)}, u32[]{:S(2)}) copy-start(bf16[128,192]{1,0:T(8,128)(2,1)} %get-tuple-element.220) | copy-start | bytes 147460
  342.2 8.3 %copy-start.74 = (bf16[128,192]{1,0:T(8,128)(2,1)S(1)}, bf16[128,192]{1,0:T(8,128)(2,1)}, u32[]{:S(2)}) copy-start(bf16[128,192]{1,0:T(8,128)(2,1)} %get-tuple-element.302) | copy-start | bytes 147460
  342.2 10.0 %copy-start.62 = (bf16[128,768]{1,0:T(8,128)(2,1)S(1)}, bf16[128,768]{1,0:T(8,128)(2,1)}, u32[]{:S(2)}) copy-start(bf16[128,768]{1,0:T(8,128)(2,1)} %get-tuple-element.191) | copy-start | bytes 589828
  342.2 10.0 %copy-start.71 = (bf16[128,192]{1,0:T(8,128)(2,1)S(1)}, bf16[128,192]{1,0:T(8,128)(2,1)}, u32[]{:S(2)}) copy-start(bf16[128,192]{1,0:T(8,128)(2,1)} %get-tuple-element.221) | copy-start | bytes 147460
  342.2 10.0 %copy-start.72 = (bf16[128,192]{1,0:T(8,128)(2,1)S(1)}, bf16[128,192]{1,0:T(8,128)(2,1)}, u32[]{:S(2)}) copy-start(bf16[128,192]{1,0:T(8,128)(2,1)} %get-tuple-element.301) | copy-start | bytes 147460
  342.2 11.7 %copy-start.61 = (bf16[128,768]{1,0:T(8,128)(2,1)S(1)}, bf16[128,768]{1,0:T(8,128)(2,1)}, u32[]{:S(2)}) copy-start(bf16[128,768]{1,0:T(8,128)(2,1)} %get-tuple-element.192) | copy-start | bytes 589828
  342.2 11.7 %copy-start.69 = (bf16[128,192]{1,0:T(8,128)(2,1)S(1)}, bf16[128,192]{1,0:T(8,128)(2,1)}, u32[]{:S(2)}) copy-start(bf16[128,192]{1,0:T(8,128)(2,1)} %get-tuple-element.222) | copy-start | bytes 147460
  342.2 11.7 %copy-start.70 = (bf16[128,192]{1,0:T(8,128)(2,1)S(1)}, bf16[128,192]{1,0:T(8,128)(2,1)}, u32[]{:S(2)}) copy-start(bf16[128,192]{1,0:T(8,128)(2,1)} %get-tuple-element.300) | copy-start | bytes 147460
  342.2 11.7 %copy-start.78 = (bf16[128,192]{1,0:T(8,128)(2,1)S(1)}, bf16[128,192]{1,0:T(8,128)(2,1)}, u32[]{:S(2)}) copy-start(bf16[128,192]{1,0:T(8,128)(2,1)} %get-tuple-element.226) | copy-start | bytes 147460
  342.8 12.0 %copy-start.60 = (bf16[128,768]{1,0:T(8,128)(2,1)S(1)}, bf16[128,768]{1,0:T(8,128)(2,1)}, u32[]{:S(2)}) copy-start(bf16[128,768]{1,0:T(8,128)(2,1)} %get-tuple-element.189) | copy-start | bytes 589828
  342.8 12.0 %copy-start.67 = (bf16[128,192]{1,0:T(8,128)(2,1)S(1)}, bf16[128,192]{1,0:T(8,128)(2,1)}, u32[]{:S(2)}) copy-start(bf16[128,192]{1,0:T(8,128)(2,1)} %get-tuple-element.219) | copy-start | bytes 147460
  342.8 12.0 %copy-start.68 = (bf16[128,192]{1,0:T(8,128)(2,1)S(1)}, bf16[128,192]{1,0:T(8,128)(2,1)}, u32[]{:S(2)}) copy-start(bf16[128,192]{1,0:T(8,128)(2,1)} %get-tuple-element.303) | copy-start | bytes 147460
  342.8 12.0 %copy-start.77 = (bf16[128,192]{1,0:T(8,128)(2,1)S(1)}, bf16[128,192]{1,0:T(8,128)(2,1)}, u32[]{:S(2)}) copy-start(bf16[128,192]{1,0:T(8,128)(2,1)} %get-tuple-element.223) | copy-start | bytes 147460
  343.5 14.7 %collective-permute-start.2 = (bf16[128,384]{1,0:T(8,128)(2,1)}, bf16[128,384]{1,0:T(8,128)(2,1)}, u32[]{:S(2)}, u32[]{:S(2)}) collective-permute-start(bf16[128,384]{1,0:T(8,128)(2,1)} %get-tuple-element.248), channel_id=1, source_target_pairs={{0,31},{1,30},{2,29},{3,28},{4,27},{5,26},{6,25},{7,24},{8,23},{9,... | collective-permute-start | bytes 294920 | tf_op jit(solution)/shard_map/ppermute | solution.py:31
  355.7 3.4 copy-start.27
  378.0 8.1 %copy-start.75 = (bf16[128,192]{1,0:T(8,128)(2,1)S(1)}, bf16[128,192]{1,0:T(8,128)(2,1)}, u32[]{:S(2)}) copy-start(bf16[128,192]{1,0:T(8,128)(2,1)} %get-tuple-element.235) | copy-start | bytes 147460
  379.7 6.4 copy-start.76
  391.3 54.8 %copy-start.53 = (f32[128,384]{1,0:T(8,128)S(1)}, f32[128,384]{1,0:T(8,128)}, u32[]{:S(2)}) copy-start(f32[128,384]{1,0:T(8,128)} %slice.687) | copy-start | bytes 589828
  449.0 5.1 slice-start.6
  450.8 3.3 slice-start.7
  452.4 3.5 slice-start
  455.9 3.7 copy-start.40
  455.9 3.7 copy-start.49
  455.9 3.7 copy-start.54
  456.0 3.7 copy-start.91
  456.0 3.7 copy-start.92
  458.4 10.4 %collective-permute-start.3 = (bf16[128,384]{1,0:T(8,128)(2,1)S(1)}, bf16[128,384]{1,0:T(8,128)(2,1)S(1)}, u32[]{:S(2)}, u32[]{:S(2)}) collective-permute-start(bf16[128,384]{1,0:T(8,128)(2,1)S(1)} %get-tuple-element.232), channel_id=1, source_target_pairs={{0,31},{1,30},{2,29},{3,28},{4,27},{5,26},{6,25},{7,24},{8,23},{9,... | collective-permute-start | bytes 294920 | tf_op jit(solution)/shard_map/ppermute | solution.py:31
  540.4 3.0 copy-start.25
  575.6 3.6 copy-start.8
  575.6 3.6 copy-start.13
  575.6 3.6 copy-start.17
  575.6 3.6 copy-start.21
  696.1 13.1 %copy-start.96 = (f32[2,192]{1,0:T(2,128)}, f32[2,192]{1,0:T(2,128)S(1)}, u32[]{:S(2)}) copy-start(f32[2,192]{1,0:T(2,128)S(1)} %pad_maximum_fusion.14) | copy-start | bytes 4612
  705.7 2.5 copy-start.58
  705.7 2.5 copy-start.65
  705.7 2.5 copy-start.99
  705.7 2.5 copy-start.104
  (60 other events, 97.9 us)

commit v2 on v1

--- a/solution.py
+++ b/solution.py
@@ -68,7 +68,7 @@
 class Wire:
     def __init__(self, send_sem, recv_sem, local_sem=None):
         self.send_sem, self.recv_sem, self.local_sem = send_sem, recv_sem, local_sem
-        self.sent, self.local = [], []
+        self.sent, self.local, self.bounced = [], [], []
 
     def push(self, source, target, partner):
         number = len(self.sent)
@@ -84,10 +84,22 @@
         self.sent.append(copy)
         return copy
 
-    def keep(self, source, target):
-        copy = pltpu.make_async_copy(source, target, self.local_sem.at[len(self.local)])
+    def keep(self, source, target, bounce=None):
+        if bounce is None:
+            copy = pltpu.make_async_copy(source, target, self.local_sem.at[len(self.local)])
+        else:
+            copy = pltpu.make_async_copy(source, bounce, self.local_sem.at[len(self.local)])
+            self.bounced.append((len(self.local), bounce, target))
         copy.start()
         self.local.append(copy)
+
+    def flush(self):
+        for number, bounce, target in self.bounced:
+            self.local[number].wait()
+            copy = pltpu.make_async_copy(bounce, target, self.local_sem.at[number])
+            copy.start()
+            self.local[number] = copy
+        self.bounced = []
 
     def drain(self):
         for copy in self.sent:
@@ -96,13 +108,11 @@
             copy.wait()
 
 
-def share_param(place, wire, source, target):
+def share_param(place, wire, source, target, bounce):
     rows = source.shape[0]
     cut = rows // 2
     mine, far = place.fsdp * rows, ((place.fsdp + 2) % 4) * rows
-    parts = (
-        [(0, cut, 1), (cut, cut, 3)] if rows % 32 == 0 else [(0, rows, 1)]
-    )
+    parts = [(0, cut, 1), (cut, cut, 3)]
     across = [
         wire.push(
             source.at[pl.ds(start, count)],
@@ -112,7 +122,7 @@
         for start, count, step in parts
     ]
     beside = wire.push(source, target.at[pl.ds(mine, rows)], place.beside)
-    wire.keep(source, target.at[pl.ds(mine, rows)])
+    wire.keep(source, target.at[pl.ds(mine, rows)], bounce)
     last = [beside]
 
     def onward(copy, start, count):
@@ -159,31 +169,38 @@
     return steps, last
 
 
-def share_slices(place, wire, source, target, stage):
-    rows = source.shape[1]
+def share_columns(place, wire, source, target, stage):
+    rows = source.shape[0]
     cut = rows // 2
     fsdp, core = place.fsdp, place.core
     parts = [(0, cut, 1), (cut, cut, 3)]
+
+    def panel(start, count, shard):
+        return source.at[pl.ds(start, count), pl.ds(pl.multiple_of(shard * D, D), D)]
+
     passing, last = [], []
     for start, count, step in parts:
-        partner = place.along_x(step)
         passing.append(
             wire.push(
-                source.at[3 - fsdp, pl.ds(start, count)], stage.at[pl.ds(start, count)], partner
+                panel(start, count, 3 - fsdp),
+                stage.at[pl.ds(start, count)],
+                place.along_x(step),
             )
         )
     for start, count, step in parts:
         last.append(
             wire.push(
-                source.at[(fsdp + 2) % 4, pl.ds(start, count)],
+                panel(start, count, (fsdp + 2) % 4),
                 target.at[pl.ds(2 * rows + start, count)],
                 place.along_x(step),
             )
         )
     last.append(
-        wire.push(source.at[fsdp + 1 - 2 * core], target.at[pl.ds(rows, rows)], place.beside)
+        wire.push(
+            panel(0, rows, fsdp + 1 - 2 * core), target.at[pl.ds(rows, rows)], place.beside
+        )
     )
-    wire.keep(source.at[fsdp], target.at[pl.ds(0, rows)])
+    wire.keep(panel(0, rows, fsdp), target.at[pl.ds(0, rows)])
 
     def onward(copy, start, count):
         copy.wait_recv()
@@ -279,12 +296,18 @@
     return jax.ShapeDtypeStruct((4 * shard.shape[-2], shard.shape[-1]), BF)
 
 
-def first_kernel(weight_ref, vector_ref, weight_out, vector_out, *sem):
+def first_kernel(weight_ref, vector_ref, weight_out, vector_out, bounce, *sem):
     place, wire = Place(), Wire(*sem)
     place.greet([place.beside, place.along_x(1), place.along_x(3)])
-    steps, last = share_param(place, wire, vector_ref, vector_out)
-    more, ends = share_param(place, wire, weight_ref.at[0], weight_out)
-    for step in more + steps:
+    far = vector_out.at[(place.fsdp + 2) % 4]
+    across = wire.push(vector_ref, vector_out.at[place.fsdp], place.along_x(1))
+    last = [wire.push(vector_ref, vector_out.at[place.fsdp], place.beside)]
+    wire.keep(vector_ref, vector_out.at[place.fsdp])
+    steps, ends = share_param(place, wire, weight_ref.at[0], weight_out, bounce)
+    wire.flush()
+    across.wait_recv()
+    last.append(wire.push(far, far, place.beside))
+    for step in steps:
         step()
     for copy in last + ends:
         copy.wait_recv()
@@ -294,11 +317,13 @@
 def gather_first(weight, vectors):
     return pl.pallas_call(
         first_kernel,
-        out_shape=(full_shape(weight), full_shape(vectors)),
-        in_specs=[ANY] * 2,
-        out_specs=(ANY,) * 2,
-        scratch_shapes=sems(16, 4),
-        compiler_params=pltpu.CompilerParams(collective_id=0, has_side_effects=True),
+        out_shape=(full_shape(weight), jax.ShapeDtypeStruct((4,) + vectors.shape, F32)),
+        in_specs=[ANY, VM],
+        out_specs=(ANY, ANY),
+        scratch_shapes=[room(*weight.shape[1:])] + sems(16, 4),
+        compiler_params=pltpu.CompilerParams(
+            collective_id=0, has_side_effects=True, vmem_limit_bytes=16 * 2**20
+        ),
         name="gather_first",
     )(weight, vectors)
 
@@ -308,6 +333,7 @@
     weights, refs = refs[:count], refs[count:]
     q_out, k_out, v_out = refs[:3]
     weights_out, refs = refs[3 : 3 + count], refs[3 + count :]
+    bounces, refs = refs[:count], refs[count:]
     place, wire = Place(), Wire(*refs)
     place.greet(
         place.around() + [place.mirror, place.beside, place.along_x(1), place.along_x(3)]
@@ -325,8 +351,8 @@
     def ready(t, b):
         if b == 1:
             if t == 0:
-                for layer, weight, target in zip(jobs, weights, weights_out):
-                    work.append(share_param(place, wire, weight.at[layer], target))
+                for layer, weight, target, bounce in zip(jobs, weights, weights_out, bounces):
+                    work.append(share_param(place, wire, weight.at[layer], target, bounce))
             swapped[t].wait_recv()
 
     def spot(t, origin, b):
@@ -346,7 +372,9 @@
         own,
         spot,
         ready,
-        [lambda: None] * 4 + [functools.partial(onward, 0), functools.partial(onward, 1)],
+        [wire.flush]
+        + [lambda: None] * 3
+        + [functools.partial(onward, 0), functools.partial(onward, 1)],
     )
     swapped[2].wait_recv()
     for _, last in work:
@@ -363,17 +391,19 @@
         functools.partial(gather_kernel, layers),
         out_shape=(jax.ShapeDtypeStruct((BLOCK, HALF), BF), whole, whole)
         + tuple(full_shape(weight) for weight in weights),
-        in_specs=[ANY] * (5 + len(jobs)),
+        in_specs=[VM] * 5 + [ANY] * len(jobs),
         out_specs=(ANY,) * (3 + len(jobs)),
-        scratch_shapes=sems(96, 8),
-        compiler_params=pltpu.CompilerParams(collective_id=number, has_side_effects=True),
+        scratch_shapes=[room(*weight.shape[1:]) for weight in weights] + sems(96, 8),
+        compiler_params=pltpu.CompilerParams(
+            collective_id=number, has_side_effects=True, vmem_limit_bytes=24 * 2**20
+        ),
         name=name,
     )(*away, *own, *weights)
 
 
-def scatter_kernel(count, gk_ref, gv_ref, gq_ref, stack_ref, *refs):
+def scatter_kernel(count, gk_ref, gv_ref, gq_ref, hidden_ref, *refs):
     sources, refs = refs[:count], refs[count:]
-    own_out, back_out, back_q, stack_out = refs[:4]
+    own_out, back_out, back_q, hidden_out = refs[:4]
     targets, refs = refs[4 : 4 + count], refs[4 + count :]
     far, near, mix, total, last_far, last_near, last_mix, leave, stage = refs[:9]
     place, wire = Place(), Wire(*refs[9:])
@@ -397,7 +427,7 @@
                 for b, sign in ((0, 1), (1, -1))
             ]
     swapped = [wire.push(gq_ref, back_q, place.mirror)]
-    work = [share_slices(place, wire, stack_ref, stack_out, stage)]
+    work = [share_columns(place, wire, hidden_ref, hidden_out, stage)]
     for source, target in zip(sources, targets):
         work.append(share_rows(place, wire, source, target))
     for da in order:
@@ -484,17 +514,17 @@
     return jax.ShapeDtypeStruct((4 * source.shape[0], source.shape[1]), BF)
 
 
-def scatter_pair(name, number, grad_keys, grad_values, away, stacked, sources):
+def scatter_pair(name, number, grad_keys, grad_values, away, hidden, sources):
     return pl.pallas_call(
         functools.partial(scatter_kernel, len(sources)),
         out_shape=(
             jax.ShapeDtypeStruct((2, BLOCK, HALF), F32),
             jax.ShapeDtypeStruct((2, BLOCK, HALF), BF),
             jax.ShapeDtypeStruct((BLOCK, HALF), BF),
-            rows_shape(stacked[0]),
+            jax.ShapeDtypeStruct((4 * BLOCK, D), BF),
         )
         + tuple(rows_shape(source) for source in sources),
-        in_specs=[VM, VM] + [ANY] * (2 + len(sources)),
+        in_specs=[VM] * (4 + len(sources)),
         out_specs=(VM,) + (ANY,) * (3 + len(sources)),
         scratch_shapes=[
             room(2, 4, 2, BLOCK, HALF),
@@ -505,14 +535,14 @@
             room(2, 2, 2, BLOCK, HALF),
             room(2, 2, BLOCK, HALF),
             room(2, BLOCK, HALF),
-            room(*stacked.shape[1:]),
+            room(BLOCK, D),
         ]
-        + sems(112, 8),
+        + sems(128, 12),
         compiler_params=pltpu.CompilerParams(
-            collective_id=number, has_side_effects=True, vmem_limit_bytes=40 * 2**20
+            collective_id=number, has_side_effects=True, vmem_limit_bytes=44 * 2**20
         ),
         name=name,
-    )(grad_keys, grad_values, away, stacked, *sources)
+    )(grad_keys, grad_values, away, hidden, *sources)
 
 
 def late_kernel(one_ref, two_ref, one_out, two_out, *sem):
@@ -535,7 +565,7 @@
     return pl.pallas_call(
         late_kernel,
         out_shape=(rows_shape(one), rows_shape(two)),
-        in_specs=[ANY] * 2,
+        in_specs=[VM] * 2,
         out_specs=(ANY,) * 2,
         scratch_shapes=sems(16, 4),
         compiler_params=pltpu.CompilerParams(collective_id=5, has_side_effects=True),
@@ -548,7 +578,7 @@
 
 
 def sum_kernel(
-    one_ref, two_ref, small_ref, out_ref, small_out,
+    one_ref, two_ref, small_one, small_two, out_ref, small_out,
     far, mix, near, total, far_two, mix_two, near_two, part, other, final, small, heard, *sem,
 ):
     place, wire = Place(), Wire(*sem)
@@ -574,7 +604,8 @@
             result = result + term.astype(F32)
         return result.astype(BF)
 
-    small[...] = small_ref[...]
+    small[0] = small_one[...]
+    small[1] = small_two[...]
     passing = wire.push(small, heard.at[0], turns[0])
     order = (2, 1, 3, 0)
     way = {2: 1, 1: 1, 3: -1, 0: -1}
@@ -674,15 +705,16 @@
         copy.wait()
 
 
-def sum_over_ctx(one, two, small):
+def sum_over_ctx(one, two, small_one, small_two):
     shape = (16, PIECE, D)
+    small_shape = (2,) + small_one.shape
     return pl.pallas_call(
         sum_kernel,
         out_shape=(
             jax.ShapeDtypeStruct((2,) + shape, BF),
-            jax.ShapeDtypeStruct(small.shape, F32),
+            jax.ShapeDtypeStruct(small_shape, F32),
         ),
-        in_specs=[VM, VM, VM],
+        in_specs=[VM] * 4,
         out_specs=(ANY, VM),
         scratch_shapes=[
             room(2, 4, PIECE, D),
@@ -695,58 +727,65 @@
             room(2, PIECE, D),
             room(2, PIECE, D),
             room(2, PIECE, D),
-            pltpu.VMEM(small.shape, F32),
-            pltpu.VMEM((5,) + small.shape, F32),
+            pltpu.VMEM(small_shape, F32),
+            pltpu.VMEM((5,) + small_shape, F32),
         ]
         + sems(128, 4),
         compiler_params=pltpu.CompilerParams(
             collective_id=6, has_side_effects=True, vmem_limit_bytes=48 * 2**20
         ),
         name="sum_over_ctx",
-    )(one.reshape(shape), two.reshape(shape), small)
-
-
-def weight_kernel(left_ref, joined_ref, low_ref, pre_ref, rows_ref, sums_ref, turned):
-    turned[...] = jnp.transpose(left_ref[...])
-    ones = jnp.ones((8, left_ref.shape[0]), BF)
-
-    def panel(out, rows, right, at):
-        rows_ref[out, :] = contract(turned[rows, :], right, ((1,), (0,))).astype(BF)
-        if at is not None:
-            sums_ref[:, at : at + D] = contract(ones, right, ((1,), (0,)))
+    )(one.reshape(shape), two.reshape(shape), small_one, small_two)
+
+
+def weight_kernel(
+    fsdp_ref, one_ref, mixed_ref, two_ref, hidden_ref, joined_ref, low_ref, pre_ref, norm_ref,
+    rows_ref, sums_ref, turned, turned_hidden,
+):
+    start = pl.multiple_of(fsdp_ref[0] * 192, 64)
+    lefts = []
+    for i, ref in enumerate((one_ref, mixed_ref, two_ref)):
+        turned[i] = jnp.transpose(ref[...])
+        lefts.append(turned[i, pl.ds(start, 192), :])
+    turned_hidden[...] = jnp.transpose(hidden_ref[...])
+    ones = jnp.ones((8, low_ref.shape[0]), BF)
+
+    def panel(first, left, right, line):
+        rows = left.shape[0]
+        rows_ref[first : first + rows, :] = contract(left, right, ((1,), (0,))).astype(BF)
+        if line is not None:
+            sums_ref[line : line + 1, :] = contract(ones, right, ((1,), (0,)))[:1]
 
     low = low_ref[...]
-    panel(slice(1536, 2304), slice(0, 768), low, None)
-    panel(slice(576, 768), slice(960, 1152), low, 0)
+    panel(1536, turned_hidden[...], low, None)
+    panel(576, lefts[1], low, 0)
     for i in range(3):
-        panel(
-            slice(i * 192, (i + 1) * 192), slice(768, 960), joined_ref[:, i * D : (i + 1) * D], (1 + i) * D
-        )
+        panel(i * 192, lefts[0], joined_ref[:, i * D : (i + 1) * D], 1 + i)
     for i in range(4):
-        panel(
-            slice(768 + i * 192, 960 + i * 192),
-            slice(1152, 1344),
-            pre_ref[:, i * D : (i + 1) * D],
-            (4 + i) * D,
-        )
-
-
-def weight_grads(left, joined, low, pre):
+        panel(768 + i * 192, lefts[2], pre_ref[:, i * D : (i + 1) * D], 4 + i)
+    norms = norm_ref[0:16, :].astype(F32)
+    for i in range(1, 4):
+        norms = norms + norm_ref[i * 16 : (i + 1) * 16, :].astype(F32)
+    sums_ref[8:16, :] = norms[:8]
+
+
+def weight_grads(fsdp, one, mixed, two, hidden, joined, low, pre, norms):
+    tokens = one.shape[0]
     return pl.pallas_call(
         weight_kernel,
         out_shape=(
             jax.ShapeDtypeStruct((2304, D), BF),
-            jax.ShapeDtypeStruct((8, 8 * D), F32),
+            jax.ShapeDtypeStruct((16, D), F32),
         ),
-        in_specs=[VM] * 4,
+        in_specs=[SM] + [VM] * 8,
         out_specs=(VM, VM),
-        scratch_shapes=[room(left.shape[1], left.shape[0])],
+        scratch_shapes=[room(3, D, tokens), room(D, tokens)],
         compiler_params=pltpu.CompilerParams(vmem_limit_bytes=40 * 2**20),
         cost_estimate=pl.CostEstimate(
             flops=2 * 512 * 1769472, bytes_accessed=12 * 2**20, transcendentals=0
         ),
         name="weight_grads",
-    )(left, joined, low, pre)
+    )(fsdp, one, mixed, two, hidden, joined, low, pre, norms)
 
 
 def pair_rows(values):
@@ -1008,16 +1047,15 @@
         )
 
     vectors = (ln1_gain, ln1_bias, ln2_gain, ln2_bias, out_bias, down_bias, qkv_bias, up_bias)
-    packed = jnp.concatenate([vector.reshape(-1) for vector in vectors])
-    packed = jnp.pad(packed, (0, 16 * HALF - packed.shape[0])).reshape(16, HALF)
+    packed = jnp.concatenate(vectors, 1).astype(F32)
+    packed = jnp.pad(packed, ((0, 8 - LAYERS), (0, 2560 - packed.shape[1])))
     first_weight, table = gather_first(qkv_weight, packed)
-    table = table.reshape(4, 16 * HALF).astype(F32)
     full_vectors, start = [], 0
     for vector in vectors:
         width = vector.shape[1]
-        piece = table[:, start : start + LAYERS * width].reshape(4, LAYERS, width)
+        piece = table[:, :LAYERS, start : start + width]
         full_vectors.append(jnp.transpose(piece, (1, 0, 2)).reshape(LAYERS, 4 * width))
-        start += LAYERS * width
+        start += width
     gain_one, bias_one, gain_two, bias_two, b_out, b_down, b_qkv, b_up = full_vectors
 
     qkv_full = [first_weight, None]
@@ -1054,34 +1092,19 @@
         hidden_pre = dot(norm_two, w_up) + b_up[layer_index]
         hidden_low = (hidden_pre * phi_parts(hidden_pre)[0]).astype(BF)
         mlp_branch = dot(hidden_low, w_down)
-        blank = jnp.zeros((row_count, 64), BF)
-        stacked = jnp.stack(
-            [
-                jnp.concatenate(
-                    [
-                        hidden_low[:, d * D : (d + 1) * D],
-                        norm_one[:, d * 192 : (d + 1) * 192],
-                        mixed_low[:, d * 192 : (d + 1) * 192],
-                        norm_two[:, d * 192 : (d + 1) * 192],
-                        blank,
-                    ],
-                    1,
-                )
-                for d in range(4)
-            ],
-            0,
-        )
-        saved.append((unit, scale, queries, keys, values, turned, log_total, hidden_pre, stacked))
+        lefts = (norm_one, mixed_low, norm_two)
+        saved.append(
+            (unit, scale, queries, keys, values, turned, log_total, hidden_pre, hidden_low, lefts)
+        )
         stream = (
             stream + dot(mixed_low, w_out) + b_out[layer_index] + mlp_branch + b_down[layer_index]
         )
 
     gradient = cotangent[0].astype(F32)
-    waiting, low_rows, pre_rows, left_rows = (), [None] * 2, [None] * 2, [None] * 2
-    joined_rows, norm_rows = [None] * 2, [None] * 2
+    waiting, early_rows, late_rows = (), [None] * 2, [None] * 2
     for layer_index in range(LAYERS - 1, -1, -1):
         w_qkv, w_out, w_up, w_down = gathered[layer_index]
-        unit, scale, queries, keys, values, turned, log_total, hidden_pre, stacked = saved[
+        unit, scale, queries, keys, values, turned, log_total, hidden_pre, hidden_low, lefts = saved[
             layer_index
         ]
         grad_low = gradient.astype(BF)
@@ -1095,18 +1118,18 @@
             ctx_word, queries, keys, values, grad_mixed, turned, log_total
         )
         whole = (BLOCKS, BLOCK, HALF)
-        own_pair, back_pair, back_query, left, low, pre, *more = scatter_pair(
+        own_pair, back_pair, back_query, *gathered_rows = scatter_pair(
             "scatter_pair_%d" % layer_index,
             3 + layer_index,
             grad_keys.reshape(whole),
             grad_values.reshape(whole),
             grad_query[BLOCK:].astype(BF),
-            stacked,
-            (grad_low, grad_pre) + waiting,
-        )
-        left_rows[layer_index], low_rows[layer_index], pre_rows[layer_index] = left, low, pre
-        if more:
-            joined_rows[layer_index + 1], norm_rows[layer_index + 1] = more
+            hidden_low,
+            lefts + (grad_low, grad_pre) + waiting,
+        )
+        early_rows[layer_index] = gathered_rows[:6]
+        if waiting:
+            late_rows[layer_index + 1] = gathered_rows[6:]
         grad_query = join(grad_query[:BLOCK], back_query.astype(F32))
         grad_key = join(own_pair[0], back_pair[0].astype(F32))
         grad_value = join(own_pair[1], back_pair[1].astype(F32))
@@ -1129,55 +1152,46 @@
             + norm_input_grad(grad_norm_one, gain_one[layer_index], unit, scale)
             + norm_input_grad(grad_norm_two, gain_two[layer_index], unit, scale)
         )
-    joined_rows[0], norm_rows[0] = gather_late(*waiting)
-
-    def own_part(vector, width):
-        return lax.dynamic_slice_in_dim(vector, fsdp * width, width, vector.ndim - 1)
-
+    late_rows[0] = gather_late(*waiting)
+    fsdp_word = fsdp.astype(jnp.int32).reshape(1)
     packs, lines = [], []
     for layer_index in range(LAYERS):
-        rows, sums = weight_grads(
-            left_rows[layer_index],
-            joined_rows[layer_index],
-            low_rows[layer_index],
-            pre_rows[layer_index],
-        )
+        hidden, one, mixed, two, low, pre = early_rows[layer_index]
+        joined, norms = late_rows[layer_index]
+        rows, sums = weight_grads(fsdp_word, one, mixed, two, hidden, joined, low, pre, norms)
         packs.append(rows)
-        sums = sums[0]
-        norms = own_part(jnp.sum(norm_rows[layer_index].reshape(4, 16, D)[:, :4].astype(F32), 0), 192)
-        lines += [
-            jnp.pad(own_part(sums[:D], 192), (0, D - 192)),
-            jnp.pad(own_part(sums[D : 4 * D], 576), (0, D - 576)),
-            own_part(sums[4 * D :], D),
-            norms.reshape(D),
-        ]
-    summed, small = sum_over_ctx(packs[0], packs[1], jnp.stack(lines, 0))
-    grads = []
-    for layer_index in range(LAYERS):
-        rows = summed[layer_index].reshape(2304, D)
-        line = small[4 * layer_index : 4 * layer_index + 4]
-        norms = line[3].reshape(4, 192)
-        grads.append(
-            (
-                norms[0],
-                norms[1],
-                norms[2],
-                norms[3],
-                jnp.concatenate([rows[i * 192 : (i + 1) * 192] for i in range(3)], 1),
-                line[1, :576],
-                rows[576:768],
-                line[0, :192],
-                jnp.concatenate([rows[768 + i * 192 : 960 + i * 192] for i in range(4)], 1),
-                line[2],
-                rows[1536:],
-                line[0, :192],
-            )
-        )
-    stacked = [
-        jnp.stack([grads[layer_index][member] for layer_index in range(LAYERS)], 0).astype(F32)
-        for member in range(12)
-    ]
-    return (stream.astype(BF)[None], gradient[None], *stacked)
+        lines.append(sums)
+    summed, small = sum_over_ctx(*packs, *lines)
+
+    def own_part(vectors, width):
+        return lax.dynamic_slice_in_dim(vectors, fsdp * width, width, vectors.ndim - 1)
+
+    bias_sum = own_part(small[:, 0], 192)
+    joined_sum = own_part(small[:, 1:4].reshape(LAYERS, 3 * D), 576)
+    up_sum = own_part(small[:, 4:8].reshape(LAYERS, 4 * D), D)
+    norm_sums = own_part(small[:, 8:12], 192)
+    rows = summed.reshape(LAYERS, 2304, D)
+
+    def panels(first, count):
+        pieces = [rows[:, first + i * 192 : first + (i + 1) * 192] for i in range(count)]
+        return jnp.concatenate(pieces, 2).astype(F32)
+
+    return (
+        stream.astype(BF)[None],
+        gradient[None],
+        norm_sums[:, 0],
+        norm_sums[:, 1],
+        norm_sums[:, 2],
+        norm_sums[:, 3],
+        panels(0, 3),
+        joined_sum,
+        panels(576, 1),
+        bias_sum,
+        panels(768, 4),
+        up_sum,
+        rows[:, 1536:].astype(F32),
+        bias_sum,
+    )
 
 
 def solution(mesh):

time: 719 us -> 566 us (0.79)
  Pallas kernels: 535 us -> 408 us
  local copies, waits for them, and re-layouts: 87.5 us -> 72.6 us
  other arithmetic: 35 us -> 24.9 us
    pallas_call x2, Pallas kernels: 220 us -> 109 us  [gather_pair(): pl.pallas_call(functools.partial(gather_kernel, layers), out_shape=(jax.S...]
    unnamed x246 -> x206, local copies, waits for them, and re-layouts: 32.6 us -> 46.7 us
    pallas_call x1, Pallas kernels: 31.5 us -> 17.8 us  [gather_first(): pl.pallas_call(first_kernel, out_shape=(full_shape(weight), jax.ShapeDtyp...]
    slice x23 -> x2, local copies, waits for them, and re-layouts: 12.1 us -> 0.1 us  [the longest x1 0.1 us: shards(): norm_sums[:, 3]]
    concatenate x9 -> x1, local copies, waits for them, and re-layouts: 12.8 us -> 0.9 us  [shards(): packed = jnp.concatenate(vectors, 1).astype(F32)]
    pallas_call x1, Pallas kernels: 21.1 us -> 11.4 us  [gather_late(): pl.pallas_call(late_kernel, out_shape=(rows_shape(one), rows_shape(two)),...]
    reshape x17 -> x0, local copies, waits for them, and re-layouts: 7.33 us -> none  [the longest x8 6.09 us: shards(): packed = jnp.concatenate([vector.reshape(-1) for vector in vectors])]
  transfers between devices with their start and end apart: 4 -> 4, of which waited for: 1 -> 2; matrix products, arithmetic and copies ran while one was open for 4% -> 5% of each run, Pallas kernels for 2% -> 3%
where the time goes in v2:
time: 566 us; the launch traced here: 558 us
  Pallas kernels  408 us (72%)
  local copies, waits for them, and re-layouts  72.6 us (13%)
  matrix products  26.8 us (5%)
  other arithmetic  24.9 us (4%)
  starting transfers between devices  14.5 us (3%)
  waiting for transfers between devices  8.75 us (2%)
    pallas_call x2, Pallas kernels, gather_pair(): pl.pallas_call(functools.partial(gather_kernel, layers), out_shape=(jax.S...  109 us
    pallas_call x2, Pallas kernels, scatter_pair(): pl.pallas_call(functools.partial(scatter_kernel, len(sources)), out_shape...  109 us
    pallas_call x1, Pallas kernels, sum_over_ctx(): pl.pallas_call(sum_kernel, out_shape=(jax.ShapeDtypeStruct((2,) + shape,...  96.7 us
    unnamed x206, local copies, waits for them, and re-layouts  46.7 us
    pallas_call x2, Pallas kernels, attend_backward(): pl.pallas_call(backward_kernel, out_shape=(jax.ShapeDtypeStruct((2 * BLOC...  33 us
    pallas_call x2, Pallas kernels, attend_forward(): pl.pallas_call(forward_kernel, out_shape=(jax.ShapeDtypeStruct((2 * BLOCK...  25 us
    pallas_call x1, Pallas kernels, gather_first(): pl.pallas_call(first_kernel, out_shape=(full_shape(weight), jax.ShapeDtyp...  17.8 us
    dot_general x8, matrix products, dot(): return jnp.dot(left, right, preferred_element_type=F32)  15.4 us
  transfers between devices with their start and end apart: 4, of which 2 were waited for; matrix products, arithmetic and copies ran while one was open for 5% of the time, Pallas kernels for 3%

profile of v2, /device:TPU:0, one launch (start us, length us, event | category | flops | bytes accessed | tf_op | source)
XLA Modules:
  0.0 557.8 jit_solution(1669514643843856782)
XLA Ops:
  1.6 1.5 copy-done.4
  3.1 17.8 %gather_first.1 = (bf16[768,2304]{1,0:T(8,128)(2,1)S(1)}, f32[4,8,2560]{2,1,0:T(8,128)S(1)}) custom-call(bf16[2,192,2304]{2,1,0:T(8,128)(2,1)S(1)} %copy-done.4, f32[8,2560]{1,0:T(8,128)S(1)} %pad_convert_fusion.vector_ref), custom_call_target="tpu_custom_call" | custom-call | tf_op jit(solution)/shard_map/gather_first/pallas_call | solution.py:318
  20.9 1.8 copy-done.10
  26.3 3.5 fusion.105
  31.0 1.4 fusion.101
  34.1 2.3 fusion.55
  37.8 1.5 copy-done.5
  39.3 60.4 %gather_pair_0.1 = (bf16[128,384]{1,0:T(8,128)(2,1)S(1)}, bf16[32,128,384]{2,1,0:T(8,128)(2,1)S(1)}, bf16[32,128,384]{2,1,0:T(8,128)(2,1)S(1)}, bf16[768,768]{1,...) custom-call(bf16[128,384]{1,0:T(8,128)(2,1)S(1)} %get-tuple-element., ...), custom_call_target="tpu_custom_call" | custom-call | tf_op jit(solution)/shard_map/gather_pair_0/pallas_call | solution.py:390
  99.8 2.2 copy-done
  102.0 2.2 copy-done.6
  104.1 1.8 copy-done.12
  105.9 12.5 %attend_forward.2 = (bf16[256,384]{1,0:T(8,128)(2,1)S(1)}, f32[384,256]{1,0:T(8,128)S(1)}, f32[8,256]{1,0:T(8,128)S(1)}) custom-call(s32[1]{0:T(128)} %bitcast.1.ctx_ref, bf16[256,384]{1,0:T(8,128)(2,1)S(1)} %pad_maximum_fusion.2.q_ref, bf16[4096,384]{1,0:T(8,128)(2,1)S(1)} %bitcast.192, bf16[4096,384]{1,0:T(8,128)(2,1)S(1)} %bitcast.194), custom_call_target="tpu_custom_call" | custom-call | flops 1660944384 | bytes 8388608 | tf_op jit(solution)/shard_map/attend_forward/pallas_call | solution.py:860
  118.5 1.7 copy-done.17
  121.0 2.4 collective-permute-start
  125.0 1.4 add.286
  126.3 1.4 mul.349
  127.7 4.8 multiply_convert_fusion.1
  132.5 1.6 fusion.108
  134.7 1.3 add.282
  136.0 1.3 add.271
  137.4 1.4 add.300
  138.7 1.3 mul.358
  140.1 1.4 add.289
  141.4 1.3 add.308
  142.8 1.3 add.297
  145.3 1.9 fusion.106
  152.2 48.4 %gather_pair_1.1 = (bf16[128,384]{1,0:T(8,128)(2,1)S(1)}, bf16[32,128,384]{2,1,0:T(8,128)(2,1)S(1)}, bf16[32,128,384]{2,1,0:T(8,128)(2,1)S(1)}, bf16[768,768]{1,...) custom-call(bf16[128,384]{1,0:T(8,128)(2,1)S(1)} %get-tuple-element.228.q_ref, ...), custom_call_target="tpu_custom_call" | custom-call | tf_op jit(solution)/shard_map/gather_pair_1/pallas_call | solution.py:390
  200.6 1.8 copy-done.18
  202.4 3.0 copy-done.19
  205.5 12.5 %attend_forward.3 = (bf16[256,384]{1,0:T(8,128)(2,1)S(1)}, f32[384,256]{1,0:T(8,128)S(1)}, f32[8,256]{1,0:T(8,128)S(1)}) custom-call(s32[1]{0:T(128)} %bitcast.1.ctx_ref, bf16[256,384]{1,0:T(8,128)(2,1)S(1)} %pad_maximum_fusion.3.q_ref, bf16[4096,384]{1,0:T(8,128)(2,1)S(1)} %bitcast.197, bf16[4096,384]{1,0:T(8,128)(2,1)S(1)} %bitcast.198), custom_call_target="tpu_custom_call" | custom-call | flops 1660944384 | bytes 8388608 | tf_op jit(solution)/shard_map/attend_forward/pallas_call | solution.py:860
  218.0 2.8 collective-permute-start.1
  220.8 1.1 multiply_convert_fusion
  222.9 1.7 fusion.1.refs_4_
  225.1 5.5 collective-permute-start.2
  230.6 1.7 fusion.110
  232.3 3.2 collective-permute-done.2
  235.6 16.6 %attend_backward.2 = (f32[256,384]{1,0:T(8,128)S(1)}, bf16[4096,384]{1,0:T(8,128)(2,1)S(1)}, bf16[4096,384]{1,0:T(8,128)(2,1)}) custom-call(s32[1]{0:T(128)} %bitcast.1.ctx_ref, bf16[256,384]{1,0:T(8,128)(2,1)S(1)} %pad_maximum_fusion.3.q_ref, bf16[4096,384]{1,0:T(8,128)(2,1)} %bitcast.196, bf16[4096,384]{1,0:T(8,128)(2,1)} %bitcast.199, ...), custom_call_target="tpu_custom_call" | custom-call | flops 4152360960 | bytes 16777216 | tf_op jit(solution)/shard_map/attend_backward/pallas_call | solution.py:943
  252.1 1.8 copy-done.21
  254.0 53.4 %scatter_pair_1.1 = (f32[2,128,384]{2,1,0:T(8,128)S(1)}, bf16[2,128,384]{2,1,0:T(8,128)(2,1)S(1)}, bf16[128,384]{1,0:T(8,128)(2,1)S(1)}, bf16[512,768]{1,0:T(8,1...) custom-call(bf16[32,128,384]{2,1,0:T(8,128)(2,1)} %bitcast.200, ...), custom_call_target="tpu_custom_call" | custom-call | tf_op jit(solution)/shard_map/scatter_pair_1/pallas_call | solution.py:518
  311.1 1.2 copy-done.67
  315.3 1.5 multiply_reduce_fusion.1
  318.7 1.7 fusion.2.refs_4_
  320.5 1.7 fusion.111
  322.2 3.8 collective-permute-start.3
  327.1 5.5 collective-permute-done.3
  332.7 16.4 %attend_backward.3 = (f32[256,384]{1,0:T(8,128)S(1)}, bf16[4096,384]{1,0:T(8,128)(2,1)S(1)}, bf16[4096,384]{1,0:T(8,128)(2,1)}) custom-call(s32[1]{0:T(128)} %bitcast.1.ctx_ref, bf16[256,384]{1,0:T(8,128)(2,1)S(1)} %copy-done.36, bf16[4096,384]{1,0:T(8,128)(2,1)} %bitcast.193, bf16[4096,384]{1,0:T(8,128)(2,1)} %bitcast.195, ...), custom_call_target="tpu_custom_call" | custom-call | flops 4152360960 | bytes 16777216 | tf_op jit(solution)/shard_map/attend_backward/pallas_call | solution.py:943
  349.1 1.7 copy-done.25
  350.9 55.3 %scatter_pair_0.1 = (f32[2,128,384]{2,1,0:T(8,128)S(1)}, bf16[2,128,384]{2,1,0:T(8,128)(2,1)S(1)}, bf16[128,384]{1,0:T(8,128)(2,1)S(1)}, bf16[512,768]{1,0:T(8,1...) custom-call(bf16[32,128,384]{2,1,0:T(8,128)(2,1)} %bitcast.201, ...), custom_call_target="tpu_custom_call" | custom-call | tf_op jit(solution)/shard_map/scatter_pair_0/pallas_call | solution.py:518
  410.9 2.1 fusion.44
  413.8 11.4 %gather_late.1 = (bf16[512,2304]{1,0:T(8,128)(2,1)}, bf16[64,768]{1,0:T(8,128)(2,1)}) custom-call(bf16[128,2304]{1,0:T(8,128)(2,1)} %pad_maximum_fusion.1.one_ref, bf16[16,768]{1,0:T(8,128)(2,1)} %fusion.90.two_ref), custom_call_target="tpu_custom_call" | custom-call | tf_op jit(solution)/shard_map/gather_late/pallas_call | solution.py:565
  425.2 1.9 copy-done.24
  427.1 1.7 copy-done.26
  428.8 1.1 copy-done.50
  429.9 1.1 copy-done.52
  431.0 1.1 copy-done.54
  432.2 1.1 copy-done.56
  434.2 3.1 weight_grads.2
  437.4 3.1 weight_grads.3
  440.5 1.8 copy-done.15
  442.3 96.7 %sum_over_ctx.1 = (bf16[2,16,144,768]{3,2,1,0:T(8,128)(2,1)}, f32[2,16,768]{2,1,0:T(8,128)S(1)}) custom-call(bf16[16,144,768]{2,1,0:T(8,128)(2,1)S(1)} %bitcast.190, bf16[16,144,768]{2,1,0:T(8,128)(2,1)} %bitcast.191, f32[16,768]{1,0:T(8,128)S(1)} %get-tuple-element.120.small_one, f32[16,768]{1,0:T(8,128)S(1)} %get-tuple-element.121.small_two), custom_call_target="tpu_custom_call" | custom-call | tf_op jit(solution)/shard_map/sum_over_ctx/pallas_call | solution.py:711
  539.1 3.8 fusion.97
  542.9 4.2 slice_convert_fusion
  551.0 2.0 maximum_convert_fusion.1
  553.0 2.8 maximum_convert_fusion
  (312 shorter events, 40.6 us)
Async XLA Ops:
  3.1 21.2 %copy-start.70 = (bf16[1,128,768]{2,1,0:T(8,128)(2,1)S(1)}, bf16[1,128,768]{2,1,0:T(8,128)(2,1)}, u32[]{:S(2)}) copy-start(bf16[1,128,768]{2,1,0:T(8,128)(2,1)} %param.14) | copy-start | bytes 589828
  20.9 1.8 copy-start.10
  22.7 7.2 %copy-start.58 = (f32[4,8,2560]{2,1,0:T(8,128)}, f32[4,8,2560]{2,1,0:T(8,128)S(1)}, u32[]{:S(2)}) copy-start(f32[4,8,2560]{2,1,0:T(8,128)S(1)} %get-tuple-element.69) | copy-start | bytes 983044
  24.4 5.5 copy-start.90
  24.6 5.3 copy-start.92
  26.3 101.4 %copy-start.32 = (bf16[128,768]{1,0:T(8,128)(2,1)}, bf16[128,768]{1,0:T(8,128)(2,1)S(1)}, u32[]{:S(2)}) copy-start(bf16[128,768]{1,0:T(8,128)(2,1)S(1)} %get-tuple-element.216.refs_2_) | copy-start | bytes 589828
  34.1 3.4 copy-start.1
  34.1 3.4 copy-start.2
  99.8 2.2 copy-start
  102.0 2.2 copy-start.6
  105.9 12.6 %copy-start.8 = (bf16[768,768]{1,0:T(8,128)(2,1)}, bf16[768,768]{1,0:T(8,128)(2,1)S(1)}, u32[]{:S(2)}) copy-start(bf16[768,768]{1,0:T(8,128)(2,1)S(1)} %get-tuple-element.75) | copy-start | bytes 3538948
  105.9 12.6 %copy-start.16 = (bf16[32,128,384]{2,1,0:T(8,128)(2,1)}, bf16[32,128,384]{2,1,0:T(8,128)(2,1)S(1)}, u32[]{:S(2)}) copy-start(bf16[32,128,384]{2,1,0:T(8,128)(2,1)S(1)} %get-tuple-element.72) | copy-start | bytes 9437188
  105.9 12.6 %copy-start.35 = (bf16[256,384]{1,0:T(8,128)(2,1)}, bf16[256,384]{1,0:T(8,128)(2,1)S(1)}, u32[]{:S(2)}) copy-start(bf16[256,384]{1,0:T(8,128)(2,1)S(1)} %pad_maximum_fusion.2.q_ref) | copy-start | bytes 589828
  120.2 7.5 %copy-start.59 = (f32[384,256]{1,0:T(8,128)}, f32[384,256]{1,0:T(8,128)S(1)}, u32[]{:S(2)}) copy-start(f32[384,256]{1,0:T(8,128)S(1)} %get-tuple-element.94.turned_ref) | copy-start | bytes 1179652
  121.0 23.2 %collective-permute-start = (bf16[128,384]{1,0:T(8,128)(2,1)}, bf16[128,384]{1,0:T(8,128)(2,1)}, u32[]{:S(2)}, u32[]{:S(2)}) collective-permute-start(bf16[128,384]{1,0:T(8,128)(2,1)} %get-tuple-element.231), channel_id=1, source_target_pairs={{0,31},{1,30},{2,29},{3,28},{4,27},{5,26},{6,25},{7,24},{8,23},{9,... | collective-permute-start | bytes 294920 | tf_op jit(solution)/shard_map/ppermute | solution.py:31
  127.7 4.8 copy-start.7
  132.5 12.8 %copy-start.71 = (bf16[1,128,768]{2,1,0:T(8,128)(2,1)S(1)}, bf16[1,128,768]{2,1,0:T(8,128)(2,1)}, u32[]{:S(2)}) copy-start(bf16[1,128,768]{2,1,0:T(8,128)(2,1)} %param.14) | copy-start | bytes 589828
  144.1 3.3 copy-start.81
  144.1 3.3 copy-start.82
  144.1 3.3 copy-start.87
  144.1 3.3 copy-start.88
  145.3 3.1 copy-start.30
  145.3 3.1 copy-start.13
  145.3 3.1 copy-start.79
  202.4 15.5 %copy-start.20 = (bf16[32,128,384]{2,1,0:T(8,128)(2,1)}, bf16[32,128,384]{2,1,0:T(8,128)(2,1)S(1)}, u32[]{:S(2)}) copy-start(bf16[32,128,384]{2,1,0:T(8,128)(2,1)S(1)} %get-tuple-element.81) | copy-start | bytes 9437188
  202.4 3.0 copy-start.19
  205.5 15.3 %copy-start.34 = (bf16[128,768]{1,0:T(8,128)(2,1)S(1)}, bf16[128,768]{1,0:T(8,128)(2,1)}, u32[]{:S(2)}) copy-start(bf16[128,768]{1,0:T(8,128)(2,1)} %get-tuple-element.196.refs_2_) | copy-start | bytes 589828
  205.5 15.3 %copy-start.80 = (f32[1,4,768]{2,0,1:T(1,128)S(1)}, f32[1,4,768]{2,0,1:T(1,128)}, u32[]{:S(2)}) copy-start(f32[1,4,768]{2,0,1:T(1,128)} %get-tuple-element.243) | copy-start | bytes 36868
  218.0 36.0 %collective-permute-start.1 = (bf16[128,384]{1,0:T(8,128)(2,1)S(1)}, bf16[128,384]{1,0:T(8,128)(2,1)S(1)}, u32[]{:S(2)}, u32[]{:S(2)}) collective-permute-start(bf16[128,384]{1,0:T(8,128)(2,1)S(1)} %get-tuple-element.225), channel_id=1, source_target_pairs={{0,31},{1,30},{2,29},{3,28},{4,27},{5,26},{6,25},{7,24},{8,23},{9,... | collective-permute-start | bytes 294920 | tf_op jit(solution)/shard_map/ppermute | solution.py:31
  225.1 10.4 %collective-permute-start.2 = (bf16[128,384]{1,0:T(8,128)(2,1)S(1)}, bf16[128,384]{1,0:T(8,128)(2,1)S(1)}, u32[]{:S(2)}, u32[]{:S(2)}) collective-permute-start(bf16[128,384]{1,0:T(8,128)(2,1)S(1)} %get-tuple-element.224), channel_id=1, source_target_pairs={{0,31},{1,30},{2,29},{3,28},{4,27},{5,26},{6,25},{7,24},{8,23},{9,... | collective-permute-start | bytes 294920 | tf_op jit(solution)/shard_map/ppermute | solution.py:31
  311.0 2.1 copy-start.37
  313.3 2.0 copy-start.14
  313.3 2.1 copy-start.69
  313.7 4.9 slice-start.2
  315.3 3.3 slice-start.3
  316.9 1.9 copy-start.77
  318.1 2.3 slice-start
  320.5 5.6 %copy-start.85 = (f32[768]{0:T(1024)S(1)}, f32[768]{0:T(1024)}, u32[]{:S(2)}) copy-start(f32[768]{0:T(1024)} %add.308) | copy-start | bytes 9220
  320.5 5.6 %copy-start.86 = (f32[768]{0:T(1024)S(1)}, f32[768]{0:T(1024)}, u32[]{:S(2)}) copy-start(f32[768]{0:T(1024)} %add.297) | copy-start | bytes 9220
  322.2 88.0 %copy-start.74 = (f32[128,768]{1,0:T(8,128)}, f32[128,768]{1,0:T(8,128)S(1)}, u32[]{:S(2)}) copy-start(f32[128,768]{1,0:T(8,128)S(1)} %fusion.111) | copy-start | bytes 1179652
  322.2 10.5 %copy-start.36 = (bf16[256,384]{1,0:T(8,128)(2,1)S(1)}, bf16[256,384]{1,0:T(8,128)(2,1)}, u32[]{:S(2)}) copy-start(bf16[256,384]{1,0:T(8,128)(2,1)} %copy-done.35) | copy-start | bytes 589828
  322.2 10.5 %copy-start.60 = (f32[384,256]{1,0:T(8,128)S(1)}, f32[384,256]{1,0:T(8,128)}, u32[]{:S(2)}) copy-start(f32[384,256]{1,0:T(8,128)} %copy-done.59) | copy-start | bytes 1179652
  322.2 10.4 %collective-permute-start.3 = (bf16[128,384]{1,0:T(8,128)(2,1)S(1)}, bf16[128,384]{1,0:T(8,128)(2,1)S(1)}, u32[]{:S(2)}, u32[]{:S(2)}) collective-permute-start(bf16[128,384]{1,0:T(8,128)(2,1)S(1)} %get-tuple-element.220), channel_id=1, source_target_pairs={{0,31},{1,30},{2,29},{3,28},{4,27},{5,26},{6,25},{7,24},{8,23},{9,... | collective-permute-start | bytes 294920 | tf_op jit(solution)/shard_map/ppermute | solution.py:31
  332.7 18.2 %copy-start.31 = (bf16[128,768]{1,0:T(8,128)(2,1)S(1)}, bf16[128,768]{1,0:T(8,128)(2,1)}, u32[]{:S(2)}) copy-start(bf16[128,768]{1,0:T(8,128)(2,1)} %copy-done.30) | copy-start | bytes 589828
  332.7 18.2 %copy-start.33 = (bf16[128,768]{1,0:T(8,128)(2,1)S(1)}, bf16[128,768]{1,0:T(8,128)(2,1)}, u32[]{:S(2)}) copy-start(bf16[128,768]{1,0:T(8,128)(2,1)} %copy-done.32) | copy-start | bytes 589828
  406.2 1.9 copy-start.55
  408.7 2.2 copy-start.11
  408.7 2.2 copy-start.72
  408.7 2.2 copy-start.91
  408.8 2.2 copy-start.93
  410.9 14.3 %copy-start.48 = (bf16[512,768]{1,0:T(8,128)(2,1)S(1)}, bf16[512,768]{1,0:T(8,128)(2,1)}, u32[]{:S(2)}) copy-start(bf16[512,768]{1,0:T(8,128)(2,1)} %copy-done.47) | copy-start | bytes 2359300
  425.2 1.9 copy-start.24
  434.2 3.2 copy-start.23
  434.2 3.2 copy-start.38
  434.2 3.2 copy-start.40
  434.2 3.2 copy-start.42
  434.2 3.2 copy-start.44
  434.2 3.2 copy-start.46
  440.5 1.8 copy-start.15
  549.7 7.1 %copy-start.89 = (f32[2,1,192]{2,0,1:T(2,128)}, f32[2,1,192]{2,0,1:T(2,128)S(1)}, u32[]{:S(2)}) copy-start(f32[2,1,192]{2,0,1:T(2,128)S(1)} %copy.67) | copy-start | bytes 4612
  553.0 2.8 copy-start.73
  553.0 2.8 copy-start.75
  553.0 2.8 copy-start.76
  553.0 2.8 copy-start.78
  (38 other events, 49.6 us)

commit v3 on v2

--- a/solution.py
+++ b/solution.py
@@ -343,17 +343,17 @@
     swapped = [
         wire.push(source, out.at[ctx], place.mirror) for source, out in zip((k_ref, v_ref), outs)
     ]
-    swapped.append(wire.push(q_ref, q_out, place.mirror))
     for t in (0, 1):
         wire.keep(ins[t], outs[t].at[ctx])
     work = []
 
     def ready(t, b):
         if b == 1:
-            if t == 0:
+            swapped[t].wait_recv()
+            if t == 1:
+                swapped.append(wire.push(q_ref, q_out, place.mirror))
                 for layer, weight, target, bounce in zip(jobs, weights, weights_out, bounces):
                     work.append(share_param(place, wire, weight.at[layer], target, bounce))
-            swapped[t].wait_recv()
 
     def spot(t, origin, b):
         return outs[t].at[origin if b == 0 else BLOCKS - 1 - origin]
@@ -416,92 +416,87 @@
         origin = place.ring(t, da, db)
         return origin if b == 0 else BLOCKS - 1 - origin
 
-    order = (2, 1, 3, 0)
-    first, second = {}, {}
-    for da in order:
-        for t in (0, 1):
-            first[t, da] = [
-                wire.push(
-                    ins[t].at[block_at(t, da, 2, b)], far.at[t, da, b], place.near(t, 1, sign)
-                )
-                for b, sign in ((0, 1), (1, -1))
-            ]
+    order = [(da, t) for da in (2, 1, 3, 0) for t in (0, 1)]
+    way = {0: 1, 1: -1}
+    first, second, loose = {}, {}, {}
+    for b in (1, 0):
+        for da, t in order:
+            first[t, da, b] = wire.push(
+                ins[t].at[block_at(t, da, 2, b)], far.at[t, da, b], place.near(t, 1, way[b])
+            )
     swapped = [wire.push(gq_ref, back_q, place.mirror)]
+    for b in (1, 0):
+        for da, t in order:
+            loose[t, da, b] = wire.push(
+                ins[t].at[block_at(t, da, -way[b], b)],
+                near.at[t, da, 1, b],
+                place.near(t, 1, -way[b]),
+            )
     work = [share_columns(place, wire, hidden_ref, hidden_out, stage)]
     for source, target in zip(sources, targets):
         work.append(share_rows(place, wire, source, target))
-    for da in order:
+    for b in (1, 0):
+        for da, t in order:
+            first[t, da, b].wait_recv()
+            mix[t, da, b] = (
+                ins[t][block_at(t, da, way[b], b)].astype(F32) + far[t, da, b].astype(F32)
+            ).astype(BF)
+            second[t, da, b] = wire.push(
+                mix.at[t, da, b], near.at[t, da, 0, b], place.near(t, 1, way[b])
+            )
+
+    def settle(t, da, b):
+        loose[t, da, b].wait_recv()
+        second[t, da, b].wait_recv()
+        total[t, da, b] = (
+            ins[t][block_at(t, da, 0, b)].astype(F32)
+            + near[t, da, 0, b].astype(F32)
+            + near[t, da, 1, b].astype(F32)
+        ).astype(BF)
+
+    third, fourth = {}, {}
+    for b in (1, 0):
         for t in (0, 1):
-            copies = []
-            for b, sign, db in ((0, 1, 1), (1, -1, 3)):
-                copies.append(
-                    wire.push(
-                        ins[t].at[block_at(t, da, db, 1 - b)],
-                        near.at[t, da, b, 1 - b],
-                        place.near(t, 1, sign),
-                    )
+            settle(t, 2, b)
+            third[t, b] = wire.push(
+                total.at[t, 2, b], last_far.at[t, b], place.near(t, 0, way[b])
+            )
+        for t in (0, 1):
+            settle(t, 1, b)
+            settle(t, 3, b)
+            fourth[t, b] = [
+                wire.push(
+                    total.at[t, -way[b] % 4, b], last_near.at[t, 1, b], place.near(t, 0, -way[b])
                 )
-                first[t, da][b].wait_recv()
-                mix[t, da, b] = (
-                    ins[t][block_at(t, da, db, b)].astype(F32) + far[t, da, b].astype(F32)
-                ).astype(BF)
-                copies.append(
-                    wire.push(mix.at[t, da, b], near.at[t, da, b, b], place.near(t, 1, sign))
-                )
-            second[t, da] = copies
-
-    def settle(t, da):
-        for copy in second[t, da]:
+            ]
+        for t in (0, 1):
+            third[t, b].wait_recv()
+            last_mix[t, b] = (
+                total[t, way[b] % 4, b].astype(F32) + last_far[t, b].astype(F32)
+            ).astype(BF)
+            fourth[t, b].append(
+                wire.push(last_mix.at[t, b], last_near.at[t, 0, b], place.near(t, 0, way[b]))
+            )
+        for t in (0, 1):
+            settle(t, 0, b)
+
+    def final(t, b):
+        for copy in fourth[t, b]:
             copy.wait_recv()
-        for b in (0, 1):
-            total[t, da, b] = (
-                ins[t][block_at(t, da, 0, b)].astype(F32)
-                + near[t, da, 0, b].astype(F32)
-                + near[t, da, 1, b].astype(F32)
-            ).astype(BF)
-
-    third, fourth = {}, {}
+        return (
+            total[t, 0, b].astype(F32)
+            + last_near[t, 0, b].astype(F32)
+            + last_near[t, 1, b].astype(F32)
+        )
+
     for t in (0, 1):
-        settle(t, 2)
-        third[t] = [
-            wire.push(total.at[t, 2, b], last_far.at[t, b], place.near(t, 0, sign))
-            for b, sign in ((0, 1), (1, -1))
-        ]
-    for t in (0, 1):
-        fourth[t] = []
-        for b, sign, da in ((0, 1, 1), (1, -1, 3)):
-            settle(t, da)
-            fourth[t].append(
-                wire.push(
-                    total.at[t, da, 1 - b], last_near.at[t, b, 1 - b], place.near(t, 0, sign)
-                )
-            )
-    for t in (0, 1):
-        for b, sign, da in ((0, 1, 1), (1, -1, 3)):
-            third[t][b].wait_recv()
-            last_mix[t, b] = (total[t, da, b].astype(F32) + last_far[t, b].astype(F32)).astype(BF)
-            fourth[t].append(
-                wire.push(last_mix.at[t, b], last_near.at[t, b, b], place.near(t, 0, sign))
-            )
-    for t in (0, 1):
-        settle(t, 0)
+        leave[t] = final(t, 1).astype(BF)
+        swapped.append(wire.push(leave.at[t], back_out.at[t], place.mirror))
     for steps, _ in work:
         for step in steps:
             step()
     for t in (0, 1):
-        for copy in fourth[t]:
-            copy.wait_recv()
-        for b in (1, 0):
-            done = (
-                total[t, 0, b].astype(F32)
-                + last_near[t, 0, b].astype(F32)
-                + last_near[t, 1, b].astype(F32)
-            )
-            if b == 1:
-                leave[t] = done.astype(BF)
-                swapped.append(wire.push(leave.at[t], back_out.at[t], place.mirror))
-            else:
-                own_out[t] = done
+        own_out[t] = final(t, 0)
     for _, last in work:
         for copy in last:
             copy.wait_recv()
@@ -806,13 +801,16 @@
     return key <= query
 
 
-def forward_kernel(ctx_ref, q_ref, k_ref, v_ref, mixed_ref, turned_ref, log_ref, top, mass, acc):
+def forward_kernel(
+    ctx_ref, q_own, q_away, k_ref, v_ref, mixed_own, mixed_away, turned_ref, log_ref, top, mass, acc
+):
     ctx = ctx_ref[0]
     for b in (0, 1):
         block = ctx if b == 0 else BLOCKS - 1 - ctx
         rows = slice(b * BLOCK, (b + 1) * BLOCK)
+        q_ref, mixed_ref = (q_own, mixed_own) if b == 0 else (q_away, mixed_away)
         queries = [
-            pair_rows(q_ref[rows, p * 128 : (p + 1) * 128] * jnp.asarray(0.125, BF))
+            pair_rows(q_ref[:, p * 128 : (p + 1) * 128] * jnp.asarray(0.125, BF))
             for p in range(PAIRS)
         ]
 
@@ -851,21 +849,22 @@
             done = acc[p] / mass[p : p + 1, :]
             turned = jnp.concatenate([done[:HEAD_DIM, :BLOCK], done[HEAD_DIM:, BLOCK:]], 0)
             turned_ref[cols, rows] = turned
-            mixed_ref[rows, cols] = jnp.transpose(turned).astype(BF)
+            mixed_ref[:, cols] = jnp.transpose(turned).astype(BF)
             row = b * PAIRS + p
             log_ref[row : row + 1, :] = top[p : p + 1, :] + jnp.log(mass[p : p + 1, :])
 
 
-def attend_forward(ctx, queries, keys, values):
+def attend_forward(ctx, own, away, keys, values):
     return pl.pallas_call(
         forward_kernel,
         out_shape=(
-            jax.ShapeDtypeStruct((2 * BLOCK, HALF), BF),
+            jax.ShapeDtypeStruct((BLOCK, HALF), BF),
+            jax.ShapeDtypeStruct((BLOCK, HALF), BF),
             jax.ShapeDtypeStruct((HALF, 2 * BLOCK), F32),
             jax.ShapeDtypeStruct((8, 2 * BLOCK), F32),
         ),
-        in_specs=[SM, VM, VM, VM],
-        out_specs=(VM, VM, VM),
+        in_specs=[SM, VM, VM, VM, VM],
+        out_specs=(VM, VM, VM, VM),
         scratch_shapes=[
             pltpu.VMEM((8, 2 * BLOCK), F32),
             pltpu.VMEM((8, 2 * BLOCK), F32),
@@ -876,11 +875,12 @@
             flops=4 * 33 * 128 * 128 * 6 * 128, bytes_accessed=8 * 2**20, transcendentals=33 * 128 * 128 * 6
         ),
         name="attend_forward",
-    )(ctx, queries, keys, values)
+    )(ctx, own, away, keys, values)
 
 
 def backward_kernel(
-    ctx_ref, q_ref, k_ref, v_ref, g_ref, turned_ref, log_ref, gq_ref, gk_ref, gv_ref, gk_acc, gv_acc, gq_acc
+    ctx_ref, q_own, q_away, k_ref, v_ref, g_own, g_away, turned_ref, log_ref,
+    gq_own, gq_away, gk_ref, gv_ref, gk_acc, gv_acc, gq_acc,
 ):
     ctx = ctx_ref[0]
     gk_acc[...] = jnp.zeros_like(gk_acc)
@@ -889,10 +889,11 @@
         block = ctx if b == 0 else BLOCKS - 1 - ctx
         rows = slice(b * BLOCK, (b + 1) * BLOCK)
         queries, grads, deltas = [], [], []
+        q_ref, g_ref, gq_ref = (q_own, g_own, gq_own) if b == 0 else (q_away, g_away, gq_away)
         for p in range(PAIRS):
             cols = slice(p * 128, (p + 1) * 128)
-            queries.append(pair_rows(q_ref[rows, cols] * jnp.asarray(0.125, BF)))
-            grad = g_ref[rows, cols]
+            queries.append(pair_rows(q_ref[:, cols] * jnp.asarray(0.125, BF)))
+            grad = g_ref[:, cols]
             grads.append(pair_rows(grad))
             both = jnp.transpose(grad.astype(F32)) * turned_ref[cols, rows]
             deltas.append(
@@ -933,18 +934,23 @@
             cols = slice(p * 128, (p + 1) * 128)
             done = gq_acc[p] * 0.125
             turned = jnp.concatenate([done[:HEAD_DIM, :BLOCK], done[HEAD_DIM:, BLOCK:]], 0)
-            gq_ref[rows, cols] = jnp.transpose(turned)
+            gq_ref[:, cols] = jnp.transpose(turned).astype(gq_ref.dtype)
     gk_ref[...] = gk_acc[...].astype(BF)
     gv_ref[...] = gv_acc[...].astype(BF)
 
 
-def attend_backward(ctx, queries, keys, values, grad_mixed, turned, log_total):
+def attend_backward(ctx, own, away, keys, values, grad_own, grad_away, turned, log_total):
     whole = jax.ShapeDtypeStruct((BLOCKS * BLOCK, HALF), BF)
     return pl.pallas_call(
         backward_kernel,
-        out_shape=(jax.ShapeDtypeStruct((2 * BLOCK, HALF), F32), whole, whole),
-        in_specs=[SM] + [VM] * 6,
-        out_specs=(VM, VM, VM),
+        out_shape=(
+            jax.ShapeDtypeStruct((BLOCK, HALF), F32),
+            jax.ShapeDtypeStruct((BLOCK, HALF), BF),
+            whole,
+            whole,
+        ),
+        in_specs=[SM] + [VM] * 8,
+        out_specs=(VM,) * 4,
         scratch_shapes=[
             pltpu.VMEM((BLOCKS * BLOCK, HALF), F32),
             pltpu.VMEM((BLOCKS * BLOCK, HALF), F32),
@@ -955,7 +961,12 @@
             flops=10 * 33 * 128 * 128 * 6 * 128, bytes_accessed=16 * 2**20, transcendentals=33 * 128 * 128 * 6
         ),
         name="attend_backward",
-    )(ctx, queries, keys, values, grad_mixed, turned, log_total)
+    )(ctx, own, away, keys, values, grad_own, grad_away, turned, log_total)
+
+
+GAIN_ONE, BIAS_ONE, GAIN_TWO, BIAS_TWO, BIAS_OUT, BIAS_DOWN, BIAS_QKV, BIAS_UP = (
+    0, 1, 2, 3, 4, 5, 6, 9,
+)
 
 
 def norm_parts(values):
@@ -982,34 +993,230 @@
     cosine, sine = jnp.cos(angle), jnp.sin(angle)
     rest = jnp.zeros((row_count, HEAD_DIM - ROTARY), F32)
     none = jnp.zeros_like(sine)
-    keep = jnp.tile(jnp.concatenate([cosine, cosine, rest + 1.0], 1), (1, HEADS))
-    low = jnp.tile(jnp.concatenate([-sine, none, rest], 1), (1, HEADS))
-    high = jnp.tile(jnp.concatenate([none, sine, rest], 1), (1, HEADS))
-    return keep, low, high
-
-
-def rotate(values, tables):
-    keep, low, high = tables
-    shift = ROTARY // 2
-    return values * keep + jnp.roll(values, -shift, 1) * low + jnp.roll(values, shift, 1) * high
-
-
-def rotate_back(values, tables):
-    keep, low, high = tables
+    keep = jnp.concatenate([cosine, cosine, rest + 1.0] * 2, 1)
+    low = jnp.concatenate([-sine, none, rest] * 2, 1)
+    high = jnp.concatenate([none, sine, rest] * 2, 1)
+    return jnp.stack([keep, low, high], 0)
+
+
+def rotate(values, table_ref):
     shift = ROTARY // 2
     return (
-        values * keep + jnp.roll(values * low, shift, 1) + jnp.roll(values * high, -shift, 1)
-    )
-
-
-def dot(left, right):
-    return jnp.dot(left, right, preferred_element_type=F32)
+        values * table_ref[0]
+        + pltpu.roll(values, 128 - shift, 1) * table_ref[1]
+        + pltpu.roll(values, shift, 1) * table_ref[2]
+    )
+
+
+def rotate_back(values, table_ref):
+    shift = ROTARY // 2
+    return (
+        values * table_ref[0]
+        + pltpu.roll(values * table_ref[1], shift, 1)
+        + pltpu.roll(values * table_ref[2], 128 - shift, 1)
+    )
 
 
 def phi_parts(values):
     cumulative = 0.5 * (1.0 + lax.erf(values * (2.0**-0.5)))
     density = jnp.exp(-0.5 * values * values) * (0.5 / jnp.pi) ** 0.5
     return cumulative, density
+
+
+def line(vec_ref, row):
+    return vec_ref[row : row + 1, :]
+
+
+def put_halves(upper_ref, low, high, mine_ref, theirs_ref):
+    upper = upper_ref[0] == 1
+
+    @pl.when(upper)
+    def _():
+        mine_ref[...] = high
+        theirs_ref[...] = low
+
+    @pl.when(jnp.logical_not(upper))
+    def _():
+        mine_ref[...] = low
+        theirs_ref[...] = high
+
+
+def put_joined(upper_ref, mine, theirs, out_ref, first):
+    upper = upper_ref[0] == 1
+    low, high = slice(first, first + HALF), slice(first + HALF, first + D)
+
+    @pl.when(upper)
+    def _():
+        out_ref[:, low] = theirs
+        out_ref[:, high] = mine
+
+    @pl.when(jnp.logical_not(upper))
+    def _():
+        out_ref[:, low] = mine
+        out_ref[:, high] = theirs
+
+
+def enter(upper_ref, stream, vec_ref, weight_ref, table_ref, one_ref, two_ref, *parts):
+    unit, _ = norm_parts(stream)
+    one = (unit * line(vec_ref, GAIN_ONE) + line(vec_ref, BIAS_ONE)).astype(BF)
+    one_ref[...] = one
+    two_ref[...] = (unit * line(vec_ref, GAIN_TWO) + line(vec_ref, BIAS_TWO)).astype(BF)
+    for i in range(3):
+        joined = contract(one, weight_ref[:, i * D : (i + 1) * D], ((1,), (0,)))
+        joined = joined + line(vec_ref, BIAS_QKV + i)
+        groups = [joined[:, g * 128 : (g + 1) * 128] for g in range(6)]
+        if i < 2:
+            groups = [rotate(group, table_ref) for group in groups]
+        groups = [group.astype(BF) for group in groups]
+        put_halves(
+            upper_ref,
+            jnp.concatenate(groups[:3], 1),
+            jnp.concatenate(groups[3:], 1),
+            parts[2 * i],
+            parts[2 * i + 1],
+        )
+
+
+def enter_kernel(upper_ref, tokens_ref, vec_ref, weight_ref, table_ref, *outs):
+    enter(upper_ref, tokens_ref[...].astype(F32), vec_ref, weight_ref, table_ref, *outs)
+
+
+def leave(upper_ref, stream_ref, own_ref, away_ref, weight_ref, mlp_ref, vec_ref, mixed_ref):
+    put_joined(upper_ref, own_ref[...], away_ref[...], mixed_ref, 0)
+    return (
+        stream_ref[...].astype(F32)
+        + contract(mixed_ref[...], weight_ref[...], ((1,), (0,)))
+        + line(vec_ref, BIAS_OUT)
+        + mlp_ref[...]
+        + line(vec_ref, BIAS_DOWN)
+    )
+
+
+def pass_kernel(
+    upper_ref, stream_ref, own_ref, away_ref, out_ref, mlp_ref, vec_ref,
+    next_vec_ref, weight_ref, table_ref, mixed_ref, next_ref, *outs,
+):
+    stream = leave(upper_ref, stream_ref, own_ref, away_ref, out_ref, mlp_ref, vec_ref, mixed_ref)
+    next_ref[...] = stream
+    enter(upper_ref, stream, next_vec_ref, weight_ref, table_ref, *outs)
+
+
+def last_kernel(
+    upper_ref, stream_ref, own_ref, away_ref, out_ref, mlp_ref, vec_ref, mixed_ref, next_ref
+):
+    next_ref[...] = leave(
+        upper_ref, stream_ref, own_ref, away_ref, out_ref, mlp_ref, vec_ref, mixed_ref
+    ).astype(BF)
+
+
+def mlp_kernel(two_ref, up_ref, down_ref, vec_ref, pre_ref, hidden_ref, mlp_ref):
+    two = two_ref[...]
+    for i in range(FF // D):
+        cols = slice(i * D, (i + 1) * D)
+        pre = contract(two, up_ref[:, cols], ((1,), (0,))) + line(vec_ref, BIAS_UP + i)
+        pre_ref[:, cols] = pre
+        hidden = (pre * phi_parts(pre)[0]).astype(BF)
+        hidden_ref[:, cols] = hidden
+        fresh = contract(hidden, down_ref[cols, :], ((1,), (0,)))
+        mlp_ref[...] = fresh if i == 0 else mlp_ref[...] + fresh
+
+
+def back(upper_ref, gradient, weight_ref, low_ref, mine_ref, theirs_ref):
+    low = gradient.astype(BF)
+    low_ref[...] = low
+    mixed = contract(low, weight_ref[...], ((1,), (1,))).astype(BF)
+    put_halves(upper_ref, mixed[:, :HALF], mixed[:, HALF:], mine_ref, theirs_ref)
+
+
+def back_kernel(upper_ref, cotangent_ref, weight_ref, *outs):
+    back(upper_ref, cotangent_ref[...].astype(F32), weight_ref, *outs)
+
+
+def mlp_back_kernel(low_ref, pre_ref, up_ref, down_ref, grad_pre_ref, norm_ref):
+    low = low_ref[...]
+    for i in range(FF // D):
+        cols = slice(i * D, (i + 1) * D)
+        pre = pre_ref[:, cols]
+        cumulative, density = phi_parts(pre)
+        hidden = contract(low, down_ref[cols, :], ((1,), (1,)))
+        grad_pre = (hidden * (cumulative + pre * density)).astype(BF)
+        grad_pre_ref[:, cols] = grad_pre
+        fresh = contract(grad_pre, up_ref[:, cols], ((1,), (1,)))
+        norm_ref[...] = fresh if i == 0 else norm_ref[...] + fresh
+
+
+def join_kernel(
+    more, upper_ref, own_ref, back_ref, own_q, back_q, table_ref, weight_ref, stream_ref, vec_ref,
+    two_ref, gradient_ref, *refs,
+):
+    next_weight, refs = (refs[:1], refs[1:]) if more else ((), refs)
+    joined_ref, sums_ref, next_ref, *outs = refs
+
+    def turned(values):
+        groups = [rotate_back(values[:, g * 128 : (g + 1) * 128], table_ref) for g in range(3)]
+        return jnp.concatenate(groups, 1).astype(BF)
+
+    put_joined(upper_ref, turned(own_q[...]), turned(back_q[...].astype(F32)), joined_ref, 0)
+    put_joined(upper_ref, turned(own_ref[0]), turned(back_ref[0].astype(F32)), joined_ref, D)
+    put_joined(upper_ref, own_ref[1].astype(BF), back_ref[1], joined_ref, 2 * D)
+    one = contract(joined_ref[...], weight_ref[...], ((1,), (1,)))
+    two = two_ref[...]
+    unit, scale = norm_parts(stream_ref[...].astype(F32))
+    sums = [jnp.sum(values, 0, keepdims=True) for values in (one * unit, one, two * unit, two)]
+    sums_ref[...] = jnp.concatenate(sums + [jnp.zeros((12, D), F32)], 0).astype(BF)
+    gradient = (
+        gradient_ref[...].astype(F32)
+        + norm_input_grad(one, line(vec_ref, GAIN_ONE), unit, scale)
+        + norm_input_grad(two, line(vec_ref, GAIN_TWO), unit, scale)
+    )
+    next_ref[...] = gradient
+    if more:
+        back(upper_ref, gradient, next_weight[0], *outs)
+
+
+def unpack_kernel(rows_ref, qkv_ref, out_ref, up_ref, down_ref):
+    for i in range(3):
+        qkv_ref[0, :, i * D : (i + 1) * D] = rows_ref[0, i * 192 : (i + 1) * 192, :].astype(F32)
+    out_ref[0] = rows_ref[0, 576:768, :].astype(F32)
+    for i in range(4):
+        up_ref[0, :, i * D : (i + 1) * D] = rows_ref[
+            0, 768 + i * 192 : 960 + i * 192, :
+        ].astype(F32)
+    down_ref[0] = rows_ref[0, 1536:, :].astype(F32)
+
+
+def unpack(rows):
+    shapes = [(192, 3 * D), (192, D), (192, FF), (D, D)]
+    return pl.pallas_call(
+        unpack_kernel,
+        grid=(LAYERS,),
+        out_shape=tuple(jax.ShapeDtypeStruct((LAYERS,) + shape, F32) for shape in shapes),
+        in_specs=[pl.BlockSpec((1, 2304, D), lambda i: (i, 0, 0))],
+        out_specs=tuple(pl.BlockSpec((1,) + shape, lambda i: (i, 0, 0)) for shape in shapes),
+        compiler_params=pltpu.CompilerParams(vmem_limit_bytes=40 * 2**20),
+        name="unpack",
+    )(rows)
+
+
+def dense(name, kernel, specs, outs, args, flops):
+    shapes = tuple(
+        jax.ShapeDtypeStruct((BLOCK, size) if isinstance(size, int) else size, kind)
+        for size, kind in outs
+    )
+    return pl.pallas_call(
+        kernel,
+        out_shape=shapes,
+        in_specs=specs,
+        out_specs=(VM,) * len(shapes),
+        compiler_params=pltpu.CompilerParams(vmem_limit_bytes=32 * 2**20),
+        cost_estimate=pl.CostEstimate(
+            flops=2 * BLOCK * flops, bytes_accessed=2 * flops, transcendentals=0
+        ),
+        name=name,
+    )(*args)
+
+
+ENTER_OUTS = ((D, BF),) * 2 + ((HALF, BF),) * 6
 
 
 def shards(
@@ -1031,91 +1238,113 @@
     row_count = tokens.shape[1]
     fsdp = lax.axis_index("fsdp")
     ctx = lax.axis_index("ctx")
-    upper = ctx % 2 == 1
     ctx_word = ctx.astype(jnp.int32).reshape(1)
+    upper = (ctx % 2).astype(jnp.int32).reshape(1)
     tables = turn_tables(ctx * row_count, row_count)
-
-    def mine(values):
-        return jnp.where(upper, values[:, HALF:], values[:, :HALF])
-
-    def theirs(values):
-        return jnp.where(upper, values[:, :HALF], values[:, HALF:])
-
-    def join(own, other):
-        return jnp.where(
-            upper, jnp.concatenate([other, own], 1), jnp.concatenate([own, other], 1)
-        )
 
     vectors = (ln1_gain, ln1_bias, ln2_gain, ln2_bias, out_bias, down_bias, qkv_bias, up_bias)
     packed = jnp.concatenate(vectors, 1).astype(F32)
     packed = jnp.pad(packed, ((0, 8 - LAYERS), (0, 2560 - packed.shape[1])))
     first_weight, table = gather_first(qkv_weight, packed)
-    full_vectors, start = [], 0
-    for vector in vectors:
-        width = vector.shape[1]
-        piece = table[:, :LAYERS, start : start + width]
-        full_vectors.append(jnp.transpose(piece, (1, 0, 2)).reshape(LAYERS, 4 * width))
-        start += width
-    gain_one, bias_one, gain_two, bias_two, b_out, b_down, b_qkv, b_up = full_vectors
+    table = table[:, :LAYERS]
+    six = table[:, :, :1152].reshape(4, LAYERS, 6, 192)
+    vecs = jnp.concatenate(
+        [
+            jnp.transpose(six, (1, 2, 0, 3)).reshape(LAYERS, 6, D),
+            jnp.transpose(table[:, :, 1152:1728], (1, 0, 2)).reshape(LAYERS, 3, D),
+            jnp.transpose(table[:, :, 1728:2496], (1, 0, 2)).reshape(LAYERS, 4, D),
+        ],
+        1,
+    )
+    vecs = [vecs[layer_index] for layer_index in range(LAYERS)]
 
     qkv_full = [first_weight, None]
     gathered = [None] * LAYERS
-    stream = tokens[0].astype(F32)
+    stream = tokens[0]
+    entered = dense(
+        "enter",
+        enter_kernel,
+        [SM] + [VM] * 4,
+        ENTER_OUTS,
+        (upper, stream, vecs[0], first_weight, tables),
+        D * 3 * D,
+    )
     saved = []
     for layer_index in range(LAYERS):
-        w_qkv = qkv_full[layer_index]
-        unit, scale = norm_parts(stream)
-        norm_one = (unit * gain_one[layer_index] + bias_one[layer_index]).astype(BF)
-        norm_two = (unit * gain_two[layer_index] + bias_two[layer_index]).astype(BF)
-        joined = dot(norm_one, w_qkv) + b_qkv[layer_index]
-        queries = rotate(joined[:, :D], tables).astype(BF)
-        key_rows = rotate(joined[:, D : 2 * D], tables).astype(BF)
-        value_rows = joined[:, 2 * D :].astype(BF)
+        norm_one, norm_two, q_own, q_away, k_own, k_away, v_own, v_away = entered
         jobs = [(layer_index, out_weight), (layer_index, up_weight), (layer_index, down_weight)]
         if layer_index + 1 < LAYERS:
             jobs.append((layer_index + 1, qkv_weight))
-        other_queries, keys, values, w_out, w_up, w_down, *more = gather_pair(
+        q_other, keys, values, w_out, w_up, w_down, *more = gather_pair(
             "gather_pair_%d" % layer_index,
             1 + layer_index,
-            (theirs(queries), theirs(key_rows), theirs(value_rows)),
-            (mine(key_rows), mine(value_rows)),
+            (q_away, k_away, v_away),
+            (k_own, v_own),
             jobs,
         )
         if more:
             qkv_full[layer_index + 1] = more[0]
-        gathered[layer_index] = (w_qkv, w_out, w_up, w_down)
-        queries = jnp.concatenate([mine(queries), other_queries], 0)
+        gathered[layer_index] = (qkv_full[layer_index], w_out, w_up, w_down)
         keys = keys.reshape(BLOCKS * BLOCK, HALF)
         values = values.reshape(BLOCKS * BLOCK, HALF)
-        mixed_two, turned, log_total = attend_forward(ctx_word, queries, keys, values)
-        mixed_low = join(mixed_two[:BLOCK], mirrored(mixed_two[BLOCK:]))
-        hidden_pre = dot(norm_two, w_up) + b_up[layer_index]
-        hidden_low = (hidden_pre * phi_parts(hidden_pre)[0]).astype(BF)
-        mlp_branch = dot(hidden_low, w_down)
+        mixed_own, mixed_away, turned, log_total = attend_forward(
+            ctx_word, q_own, q_other, keys, values
+        )
+        mixed_back = mirrored(mixed_away)
+        hidden_pre, hidden_low, mlp_branch = dense(
+            "mlp",
+            mlp_kernel,
+            [VM] * 4,
+            ((FF, F32), (FF, BF), (D, F32)),
+            (norm_two, w_up, w_down, vecs[layer_index]),
+            2 * D * FF,
+        )
+        before = stream
+        common = (upper, stream, mixed_own, mixed_back, w_out, mlp_branch, vecs[layer_index])
+        if more:
+            mixed_low, stream, *entered = dense(
+                "pass_on",
+                pass_kernel,
+                [SM] + [VM] * 9,
+                ((D, BF), (D, F32)) + ENTER_OUTS,
+                common + (vecs[layer_index + 1], more[0], tables),
+                D * 4 * D,
+            )
+        else:
+            mixed_low, output = dense(
+                "last", last_kernel, [SM] + [VM] * 6, ((D, BF), (D, BF)), common, D * D
+            )
         lefts = (norm_one, mixed_low, norm_two)
         saved.append(
-            (unit, scale, queries, keys, values, turned, log_total, hidden_pre, hidden_low, lefts)
-        )
-        stream = (
-            stream + dot(mixed_low, w_out) + b_out[layer_index] + mlp_branch + b_down[layer_index]
-        )
-
-    gradient = cotangent[0].astype(F32)
+            (before, q_own, q_other, keys, values, turned, log_total, hidden_pre, hidden_low, lefts)
+        )
+
+    gradient = cotangent[0]
     waiting, early_rows, late_rows = (), [None] * 2, [None] * 2
+    grad_low, grad_own, grad_away = dense(
+        "back",
+        back_kernel,
+        [SM, VM, VM],
+        ((D, BF), (HALF, BF), (HALF, BF)),
+        (upper, gradient, gathered[LAYERS - 1][1]),
+        D * D,
+    )
     for layer_index in range(LAYERS - 1, -1, -1):
         w_qkv, w_out, w_up, w_down = gathered[layer_index]
-        unit, scale, queries, keys, values, turned, log_total, hidden_pre, hidden_low, lefts = saved[
-            layer_index
-        ]
-        grad_low = gradient.astype(BF)
-        grad_mixed = contract(grad_low, w_out, ((1,), (1,))).astype(BF)
-        grad_mixed = jnp.concatenate([mine(grad_mixed), mirrored(theirs(grad_mixed))], 0)
-        cumulative, density = phi_parts(hidden_pre)
-        grad_hidden = contract(grad_low, w_down, ((1,), (1,)))
-        grad_pre = (grad_hidden * (cumulative + hidden_pre * density)).astype(BF)
-        grad_norm_two = contract(grad_pre, w_up, ((1,), (1,)))
-        grad_query, grad_keys, grad_values = attend_backward(
-            ctx_word, queries, keys, values, grad_mixed, turned, log_total
+        before, q_own, q_other, keys, values, turned, log_total, hidden_pre, hidden_low, lefts = (
+            saved[layer_index]
+        )
+        grad_back = mirrored(grad_away)
+        grad_pre, grad_norm_two = dense(
+            "mlp_back",
+            mlp_back_kernel,
+            [VM] * 4,
+            ((FF, BF), (D, F32)),
+            (grad_low, hidden_pre, w_up, w_down),
+            2 * D * FF,
+        )
+        gq_own, gq_away, grad_keys, grad_values = attend_backward(
+            ctx_word, q_own, q_other, keys, values, grad_own, grad_back, turned, log_total
         )
         whole = (BLOCKS, BLOCK, HALF)
         own_pair, back_pair, back_query, *gathered_rows = scatter_pair(
@@ -1123,35 +1352,39 @@
             3 + layer_index,
             grad_keys.reshape(whole),
             grad_values.reshape(whole),
-            grad_query[BLOCK:].astype(BF),
+            gq_away,
             hidden_low,
             lefts + (grad_low, grad_pre) + waiting,
         )
         early_rows[layer_index] = gathered_rows[:6]
         if waiting:
             late_rows[layer_index + 1] = gathered_rows[6:]
-        grad_query = join(grad_query[:BLOCK], back_query.astype(F32))
-        grad_key = join(own_pair[0], back_pair[0].astype(F32))
-        grad_value = join(own_pair[1], back_pair[1].astype(F32))
-        grad_joined = jnp.concatenate(
-            [rotate_back(grad_query, tables), rotate_back(grad_key, tables), grad_value], 1
-        ).astype(BF)
-        grad_norm_one = contract(grad_joined, w_qkv, ((1,), (1,)))
-        norm_sums = jnp.stack(
-            [
-                jnp.sum(grad_norm_one * unit, 0),
-                jnp.sum(grad_norm_one, 0),
-                jnp.sum(grad_norm_two * unit, 0),
-                jnp.sum(grad_norm_two, 0),
-            ],
-            0,
-        )
-        waiting = (grad_joined, jnp.pad(norm_sums, ((0, 12), (0, 0))).astype(BF))
-        gradient = (
-            gradient
-            + norm_input_grad(grad_norm_one, gain_one[layer_index], unit, scale)
-            + norm_input_grad(grad_norm_two, gain_two[layer_index], unit, scale)
-        )
+        going_on = layer_index > 0
+        grad_joined, norm_sums, gradient, *outs = dense(
+            "join_%d" % layer_index,
+            functools.partial(join_kernel, going_on),
+            [SM] + [VM] * (11 if going_on else 10),
+            ((3 * D, BF), ((16, D), BF), (D, F32))
+            + (((D, BF), (HALF, BF), (HALF, BF)) if going_on else ()),
+            (
+                upper,
+                own_pair,
+                back_pair,
+                gq_own,
+                back_query,
+                tables,
+                w_qkv,
+                before,
+                vecs[layer_index],
+                grad_norm_two,
+                gradient,
+            )
+            + ((gathered[layer_index - 1][1],) if going_on else ()),
+            D * 3 * D,
+        )
+        waiting = (grad_joined, norm_sums)
+        if going_on:
+            grad_low, grad_own, grad_away = outs
     late_rows[0] = gather_late(*waiting)
     fsdp_word = fsdp.astype(jnp.int32).reshape(1)
     packs, lines = [], []
@@ -1170,26 +1403,21 @@
     joined_sum = own_part(small[:, 1:4].reshape(LAYERS, 3 * D), 576)
     up_sum = own_part(small[:, 4:8].reshape(LAYERS, 4 * D), D)
     norm_sums = own_part(small[:, 8:12], 192)
-    rows = summed.reshape(LAYERS, 2304, D)
-
-    def panels(first, count):
-        pieces = [rows[:, first + i * 192 : first + (i + 1) * 192] for i in range(count)]
-        return jnp.concatenate(pieces, 2).astype(F32)
-
+    qkv_grad, out_grad, up_grad, down_grad = unpack(summed.reshape(LAYERS, 2304, D))
     return (
-        stream.astype(BF)[None],
+        output[None],
         gradient[None],
         norm_sums[:, 0],
         norm_sums[:, 1],
         norm_sums[:, 2],
         norm_sums[:, 3],
-        panels(0, 3),
+        qkv_grad,
         joined_sum,
-        panels(576, 1),
+        out_grad,
         bias_sum,
-        panels(768, 4),
+        up_grad,
         up_sum,
-        rows[:, 1536:].astype(F32),
+        down_grad,
         bias_sum,
     )
 

time: 566 us -> 561 us (level)
  Pallas kernels: 408 us -> 441 us
  matrix products: 26.8 us -> 0 us
  other arithmetic: 24.9 us -> 2.94 us
  local copies, waits for them, and re-layouts: 72.6 us -> 83.2 us
  waiting for transfers between devices: 8.75 us -> 0.01 us
  starting transfers between devices: 14.5 us -> 21 us
    pallas_call x4 -> x15, Pallas kernels: 58 us -> 86.9 us  [the longest x2 32.9 us: attend_backward(): pl.pallas_call(backward_kernel, out_shape=(jax.ShapeDtypeStruct((BLOCK, H...]
    dot_general x16 -> x0, matrix products: 26.8 us -> none  [the longest x8 15.4 us: dot(): return jnp.dot(left, right, preferred_element_type=F32)]
    unnamed x206 -> x256, local copies, waits for them, and re-layouts: 46.7 us -> 61.7 us
    convert_element_type x12 -> x0, other arithmetic: 13.9 us -> none  [the longest x2 4.79 us: panels(): return jnp.concatenate(pieces, 2).astype(F32)]
    add x11 -> x1, local copies, waits for them, and re-layouts: 9.69 us -> 0.63 us  [turn_tables(): keep = jnp.concatenate([cosine, cosine, rest + 1.0] * 2, 1)]
    ppermute x4, waiting for transfers between devices: 8.75 us -> 0.01 us  [mirrored(): return lax.ppermute(values, ('fsdp', 'ctx'), pairs)]
    slice x27 -> x1, local copies, waits for them, and re-layouts: 7.64 us -> 0.83 us  [shards(): six = table[:, :, :1152].reshape(4, LAYERS, 6, 192)]
    ppermute x4, starting transfers between devices: 14.5 us -> 21 us  [mirrored(): return lax.ppermute(values, ('fsdp', 'ctx'), pairs)]
  transfers between devices with their start and end apart: 4 -> 4, of which waited for: 2 -> 0; matrix products, arithmetic and copies ran while one was open for 5% -> 0% of each run, Pallas kernels for 3% -> 7%
where the time goes in v3:
time: 561 us; the launch traced here: 551 us
  Pallas kernels  441 us (79%)
  local copies, waits for them, and re-layouts  83.2 us (15%)
  starting transfers between devices  21 us (4%)
    pallas_call x2, Pallas kernels, gather_pair(): pl.pallas_call(functools.partial(gather_kernel, layers), out_shape=(jax.S...  114 us
    pallas_call x2, Pallas kernels, scatter_pair(): pl.pallas_call(functools.partial(scatter_kernel, len(sources)), out_shape...  104 us
    pallas_call x1, Pallas kernels, sum_over_ctx(): pl.pallas_call(sum_kernel, out_shape=(jax.ShapeDtypeStruct((2,) + shape,...  98.8 us
    unnamed x256, local copies, waits for them, and re-layouts  61.7 us
    pallas_call x2, Pallas kernels, attend_backward(): pl.pallas_call(backward_kernel, out_shape=(jax.ShapeDtypeStruct((BLOCK, H...  32.9 us
    pallas_call x2, Pallas kernels, attend_forward(): pl.pallas_call(forward_kernel, out_shape=(jax.ShapeDtypeStruct((BLOCK, HA...  25.6 us
    pallas_call x10, Pallas kernels, dense(): pl.pallas_call(kernel, out_shape=shapes, in_specs=specs, out_specs=(VM,)...  23 us
    ppermute x4, starting transfers between devices, mirrored(): return lax.ppermute(values, ('fsdp', 'ctx'), pairs)  21 us
  transfers between devices with their start and end apart: 4, of which 0 were waited for; matrix products, arithmetic and copies ran while one was open for 0% of the time, Pallas kernels for 7%

profile of v3, /device:TPU:0, one launch (start us, length us, event | category | flops | bytes accessed | tf_op | source)
XLA Modules:
  0.0 551.0 jit_solution(7971553896799476938)
XLA Ops:
  1.6 1.5 copy-done.13
  3.1 17.8 %gather_first.1 = (bf16[768,2304]{1,0:T(8,128)(2,1)S(1)}, f32[4,8,2560]{2,1,0:T(8,128)S(1)}) custom-call(bf16[2,192,2304]{2,1,0:T(8,128)(2,1)S(1)} %copy-done.13, f32[8,2560]{1,0:T(8,128)S(1)} %pad_convert_fusion.vector_ref), custom_call_target="tpu_custom_call" | custom-call | tf_op jit(solution)/shard_map/gather_first/pallas_call | solution.py:318
  20.9 1.1 copy.37
  25.7 1.8 concatenate.18
  27.5 1.8 concatenate.19
  29.3 1.4 slice_bitcast_fusion.2
  30.7 1.5 reshape.99
  32.2 1.5 copy.40
  33.7 1.5 reshape.116
  35.2 1.3 copy.36
  36.6 1.4 reshape.101
  40.1 1.9 concatenate.17
  42.0 1.1 pad_maximum_fusion.table_ref
  43.1 1.2 copy-done.36
  45.1 1.6 enter.1
  46.8 1.8 copy-done.10
  48.6 1.1 copy-done.34
  49.6 63.3 %gather_pair_0.1 = (bf16[128,384]{1,0:T(8,128)(2,1)S(1)}, bf16[32,128,384]{2,1,0:T(8,128)(2,1)S(1)}, bf16[32,128,384]{2,1,0:T(8,128)(2,1)S(1)}, bf16[768,768]{1,...) custom-call(bf16[128,384]{1,0:T(8,128)(2,1)S(1)} %get-tuple-element., ...), custom_call_target="tpu_custom_call" | custom-call | tf_op jit(solution)/shard_map/gather_pair_0/pallas_call | solution.py:390
  113.0 2.2 copy-done
  115.1 2.2 copy-done.2
  117.3 1.0 copy-done.18
  118.3 13.1 %attend_forward.2 = (bf16[128,384]{1,0:T(8,128)(2,1)S(1)}, bf16[128,384]{1,0:T(8,128)(2,1)}, f32[384,256]{1,0:T(8,128)S(1)}, f32[8,256]{1,0:T(8,128)S(1)}) custom-call(s32[1]{0:T(128)} %bitcast.2.ctx_ref, bf16[128,384]{1,0:T(8,128)(2,1)S(1)} %get-tuple-element.121.q_own, bf16[128,384]{1,0:T(8,128)(2,1)S(1)} %get-tuple-element.127.q_away, ...), custom_call_target="tpu_custom_call" | custom-call | flops 1660944384 | bytes 8388608 | tf_op jit(solution)/shard_map/attend_forward/pallas_call | solution.py:858
  131.4 1.7 copy-done.22
  133.1 1.6 copy-done.23
  136.2 4.9 collective-permute-start
  141.1 2.3 copy-done.1
  143.4 2.3 copy-done.3
  147.5 1.9 mlp.2
  149.5 4.1 pass_on.1
  153.7 50.5 %gather_pair_1.1 = (bf16[128,384]{1,0:T(8,128)(2,1)S(1)}, bf16[32,128,384]{2,1,0:T(8,128)(2,1)S(1)}, bf16[32,128,384]{2,1,0:T(8,128)(2,1)S(1)}, bf16[768,768]{1,...) custom-call(bf16[128,384]{1,0:T(8,128)(2,1)S(1)} %get-tuple-element.140.q_ref, ...), custom_call_target="tpu_custom_call" | custom-call | tf_op jit(solution)/shard_map/gather_pair_1/pallas_call | solution.py:390
  204.9 1.7 collective-permute-start.2
  206.6 12.5 %attend_forward.3 = (bf16[128,384]{1,0:T(8,128)(2,1)S(1)}, bf16[128,384]{1,0:T(8,128)(2,1)S(1)}, f32[384,256]{1,0:T(8,128)S(1)}, f32[8,256]{1,0:T(8,128)S(1)}) custom-call(s32[1]{0:T(128)} %bitcast.2.ctx_ref, bf16[128,384]{1,0:T(8,128)(2,1)S(1)} %get-tuple-element.139.q_own, bf16[128,384]{1,0:T(8,128)(2,1)S(1)} %get-tuple-element.145.q_away, ...), custom_call_target="tpu_custom_call" | custom-call | flops 1660944384 | bytes 8388608 | tf_op jit(solution)/shard_map/attend_forward/pallas_call | solution.py:858
  219.1 6.2 %collective-permute-start.1 = (bf16[128,384]{1,0:T(8,128)(2,1)S(1)}, bf16[128,384]{1,0:T(8,128)(2,1)S(1)}, u32[]{:S(2)}, u32[]{:S(2)}) collective-permute-start(bf16[128,384]{1,0:T(8,128)(2,1)S(1)} %get-tuple-element.149), channel_id=1, source_target_pairs={{0,31},{1,30},{2,29},{3,28},{4,27},{5,26},{6,25},{7,24},{8,23},{9,... | collective-permute-start | bytes 294920 | tf_op jit(solution)/shard_map/ppermute | solution.py:31
  225.3 1.9 mlp.3
  227.2 2.9 mlp_back.2
  231.9 16.5 %attend_backward.2 = (f32[128,384]{1,0:T(8,128)S(1)}, bf16[128,384]{1,0:T(8,128)(2,1)S(1)}, bf16[4096,384]{1,0:T(8,128)(2,1)S(1)}, bf16[4096,384]{1,0:T(8,128)(2,1)}) custom-call(s32[1]{0:T(128)} %bitcast.2.ctx_ref, bf16[128,384]{1,0:T(8,128)(2,1)S(1)} %copy-done.114, bf16[128,384]{1,0:T(8,128)(2,1)S(1)} %get-tuple-element.145.q_away, ...), custom_call_target="tpu_custom_call" | custom-call | flops 4152360960 | bytes 16777216 | tf_op jit(solution)/shard_map/attend_backward/pallas_call | solution.py:944
  248.3 1.6 copy-done.26
  251.6 1.0 last.1
  252.7 1.7 copy-done.72
  254.4 1.1 copy-done.74
  258.3 51.4 %scatter_pair_1.1 = (f32[2,128,384]{2,1,0:T(8,128)S(1)}, bf16[2,128,384]{2,1,0:T(8,128)(2,1)S(1)}, bf16[128,384]{1,0:T(8,128)(2,1)S(1)}, bf16[512,768]{1,0:T(8,1...) custom-call(bf16[32,128,384]{2,1,0:T(8,128)(2,1)} %bitcast.66, ...), custom_call_target="tpu_custom_call" | custom-call | tf_op jit(solution)/shard_map/scatter_pair_1/pallas_call | solution.py:513
  310.7 4.2 copy-done.7
  314.8 1.3 copy-done.20
  316.1 1.0 copy-done.95
  317.1 3.1 join_1.1
  320.3 8.2 %collective-permute-start.3 = (bf16[128,384]{1,0:T(8,128)(2,1)S(1)}, bf16[128,384]{1,0:T(8,128)(2,1)S(1)}, u32[]{:S(2)}, u32[]{:S(2)}) collective-permute-start(bf16[128,384]{1,0:T(8,128)(2,1)S(1)} %get-tuple-element.175), channel_id=1, source_target_pairs={{0,31},{1,30},{2,29},{3,28},{4,27},{5,26},{6,25},{7,24},{8,23},{9,... | collective-permute-start | bytes 294920 | tf_op jit(solution)/shard_map/ppermute | solution.py:31
  328.6 2.9 mlp_back.3
  332.4 16.4 %attend_backward.3 = (f32[128,384]{1,0:T(8,128)S(1)}, bf16[128,384]{1,0:T(8,128)(2,1)S(1)}, bf16[4096,384]{1,0:T(8,128)(2,1)S(1)}, bf16[4096,384]{1,0:T(8,128)(2,1)}) custom-call(s32[1]{0:T(128)} %bitcast.2.ctx_ref, bf16[128,384]{1,0:T(8,128)(2,1)S(1)} %copy-done.108, bf16[128,384]{1,0:T(8,128)(2,1)S(1)} %copy-done.110, bf16[4096,384]{1,0:T(8,128)(2,1)} %bitcast.59, ...), custom_call_target="tpu_custom_call" | custom-call | flops 4152360960 | bytes 16777216 | tf_op jit(solution)/shard_map/attend_backward/pallas_call | solution.py:944
  348.8 1.7 copy-done.30
  350.5 52.7 %scatter_pair_0.1 = (f32[2,128,384]{2,1,0:T(8,128)S(1)}, bf16[2,128,384]{2,1,0:T(8,128)(2,1)S(1)}, bf16[128,384]{1,0:T(8,128)(2,1)S(1)}, bf16[512,768]{1,0:T(8,1...) custom-call(bf16[32,128,384]{2,1,0:T(8,128)(2,1)} %bitcast.67, ...), custom_call_target="tpu_custom_call" | custom-call | tf_op jit(solution)/shard_map/scatter_pair_0/pallas_call | solution.py:513
  404.2 3.1 join_0.1
  408.8 13.9 %gather_late.1 = (bf16[512,2304]{1,0:T(8,128)(2,1)}, bf16[64,768]{1,0:T(8,128)(2,1)}) custom-call(bf16[128,2304]{1,0:T(8,128)(2,1)} %copy-done.87, bf16[16,768]{1,0:T(8,128)(2,1)} %copy-done.115), custom_call_target="tpu_custom_call" | custom-call | tf_op jit(solution)/shard_map/gather_late/pallas_call | solution.py:560
  422.8 1.9 copy-done.28
  424.7 1.7 copy-done.32
  426.3 1.1 copy-done.58
  427.5 1.1 copy-done.60
  428.6 3.1 weight_grads.3
  431.7 1.8 copy-done.21
  433.6 1.1 copy-done.62
  434.7 1.1 copy-done.64
  435.8 3.1 weight_grads.2
  438.9 98.8 %sum_over_ctx.1 = (bf16[2,16,144,768]{3,2,1,0:T(8,128)(2,1)}, f32[2,16,768]{2,1,0:T(8,128)S(1)}) custom-call(bf16[16,144,768]{2,1,0:T(8,128)(2,1)S(1)} %bitcast.57, bf16[16,144,768]{2,1,0:T(8,128)(2,1)} %bitcast.56, f32[16,768]{1,0:T(8,128)S(1)} %get-tuple-element.216.small_one, f32[16,768]{1,0:T(8,128)S(1)} %get-tuple-element.217.small_two), custom_call_target="tpu_custom_call" | custom-call | tf_op jit(solution)/shard_map/sum_over_ctx/pallas_call | solution.py:706
  537.8 3.0 copy-done.12
  540.8 5.4 unpack.1
  (253 shorter events, 26.0 us)
Async XLA Ops:
  20.9 25.8 %copy-start.4 = (bf16[768,2304]{1,0:T(8,128)(2,1)}, bf16[768,2304]{1,0:T(8,128)(2,1)S(1)}, u32[]{:S(2)}) copy-start(bf16[768,2304]{1,0:T(8,128)(2,1)S(1)} %get-tuple-element.120.weight_ref) | copy-start | bytes 10616836
  42.0 4.8 copy-start.8
  42.0 4.8 copy-start.14
  46.7 66.2 %copy-start.77 = (bf16[128,768]{1,0:T(8,128)(2,1)}, bf16[128,768]{1,0:T(8,128)(2,1)S(1)}, u32[]{:S(2)}) copy-start(bf16[128,768]{1,0:T(8,128)(2,1)S(1)} %get-tuple-element.133.two_ref.refs_2_) | copy-start | bytes 589828
  46.7 66.2 %copy-start.98 = (bf16[128,768]{1,0:T(8,128)(2,1)}, bf16[128,768]{1,0:T(8,128)(2,1)S(1)}, u32[]{:S(2)}) copy-start(bf16[128,768]{1,0:T(8,128)(2,1)S(1)} %get-tuple-element.182.refs_0_) | copy-start | bytes 589828
  46.7 71.6 %copy-start.107 = (bf16[128,384]{1,0:T(8,128)(2,1)}, bf16[128,384]{1,0:T(8,128)(2,1)S(1)}, u32[]{:S(2)}) copy-start(bf16[128,384]{1,0:T(8,128)(2,1)S(1)} %get-tuple-element.121.q_own) | copy-start | bytes 294916
  118.3 13.1 %copy-start.109 = (bf16[128,384]{1,0:T(8,128)(2,1)}, bf16[128,384]{1,0:T(8,128)(2,1)S(1)}, u32[]{:S(2)}) copy-start(bf16[128,384]{1,0:T(8,128)(2,1)S(1)} %get-tuple-element.127.q_away) | copy-start | bytes 294916
  118.3 31.1 %copy-start.6 = (bf16[768,2304]{1,0:T(8,128)(2,1)}, bf16[768,2304]{1,0:T(8,128)(2,1)S(1)}, u32[]{:S(2)}) copy-start(bf16[768,2304]{1,0:T(8,128)(2,1)S(1)} %get-tuple-element.137.weight_ref) | copy-start | bytes 10616836
  136.2 13.3 %collective-permute-start = (bf16[128,384]{1,0:T(8,128)(2,1)}, bf16[128,384]{1,0:T(8,128)(2,1)}, u32[]{:S(2)}, u32[]{:S(2)}) collective-permute-start(bf16[128,384]{1,0:T(8,128)(2,1)} %get-tuple-element.131), channel_id=1, source_target_pairs={{0,31},{1,30},{2,29},{3,28},{4,27},{5,26},{6,25},{7,24},{8,23},{9,... | collective-permute-start | bytes 294920 | tf_op jit(solution)/shard_map/ppermute | solution.py:31
  153.6 51.2 %copy-start.41 = (f32[128,768]{1,0:T(8,128)}, f32[128,768]{1,0:T(8,128)S(1)}, u32[]{:S(2)}) copy-start(f32[128,768]{1,0:T(8,128)S(1)} %get-tuple-element.138.stream_ref) | copy-start | bytes 1179652
  153.6 51.2 %copy-start.80 = (bf16[128,768]{1,0:T(8,128)(2,1)}, bf16[128,768]{1,0:T(8,128)(2,1)S(1)}, u32[]{:S(2)}) copy-start(bf16[128,768]{1,0:T(8,128)(2,1)S(1)} %get-tuple-element.151.two_ref.refs_2_) | copy-start | bytes 589828
  153.6 51.2 %copy-start.100 = (bf16[128,768]{1,0:T(8,128)(2,1)}, bf16[128,768]{1,0:T(8,128)(2,1)S(1)}, u32[]{:S(2)}) copy-start(bf16[128,768]{1,0:T(8,128)(2,1)S(1)} %get-tuple-element.183.refs_1_) | copy-start | bytes 589828
  153.6 51.2 %copy-start.102 = (bf16[128,768]{1,0:T(8,128)(2,1)}, bf16[128,768]{1,0:T(8,128)(2,1)S(1)}, u32[]{:S(2)}) copy-start(bf16[128,768]{1,0:T(8,128)(2,1)S(1)} %get-tuple-element.164.refs_0_) | copy-start | bytes 589828
  153.6 52.9 %copy-start.113 = (bf16[128,384]{1,0:T(8,128)(2,1)}, bf16[128,384]{1,0:T(8,128)(2,1)S(1)}, u32[]{:S(2)}) copy-start(bf16[128,384]{1,0:T(8,128)(2,1)S(1)} %get-tuple-element.139.q_own) | copy-start | bytes 294916
  153.7 50.6 %copy-start.49 = (bf16[1,128,768]{2,1,0:T(8,128)(2,1)S(1)}, bf16[1,128,768]{2,1,0:T(8,128)(2,1)}, u32[]{:S(2)}) copy-start(bf16[1,128,768]{2,1,0:T(8,128)(2,1)} %param.15) | copy-start | bytes 589828
  204.2 14.9 %copy-start.24 = (bf16[32,128,384]{2,1,0:T(8,128)(2,1)}, bf16[32,128,384]{2,1,0:T(8,128)(2,1)S(1)}, u32[]{:S(2)}) copy-start(bf16[32,128,384]{2,1,0:T(8,128)(2,1)S(1)} %get-tuple-element.146) | copy-start | bytes 9437188
  204.2 14.9 %copy-start.25 = (bf16[32,128,384]{2,1,0:T(8,128)(2,1)}, bf16[32,128,384]{2,1,0:T(8,128)(2,1)S(1)}, u32[]{:S(2)}) copy-start(bf16[32,128,384]{2,1,0:T(8,128)(2,1)S(1)} %get-tuple-element.147) | copy-start | bytes 9437188
  204.9 22.4 %copy-start.83 = (bf16[128,768]{1,0:T(8,128)(2,1)}, bf16[128,768]{1,0:T(8,128)(2,1)S(1)}, u32[]{:S(2)}) copy-start(bf16[128,768]{1,0:T(8,128)(2,1)S(1)} %get-tuple-element.166.low_ref.refs_3_) | copy-start | bytes 589828
  204.9 27.0 %collective-permute-start.2 = (bf16[128,384]{1,0:T(8,128)(2,1)S(1)}, bf16[128,384]{1,0:T(8,128)(2,1)S(1)}, u32[]{:S(2)}, u32[]{:S(2)}) collective-permute-start(bf16[128,384]{1,0:T(8,128)(2,1)S(1)} %get-tuple-element.157), channel_id=1, source_target_pairs={{0,31},{1,30},{2,29},{3,28},{4,27},{5,26},{6,25},{7,24},{8,23},{9,... | collective-permute-start | bytes 294920 | tf_op jit(solution)/shard_map/ppermute | solution.py:31
  206.6 18.7 %copy-start.81 = (bf16[128,768]{1,0:T(8,128)(2,1)S(1)}, bf16[128,768]{1,0:T(8,128)(2,1)}, u32[]{:S(2)}) copy-start(bf16[128,768]{1,0:T(8,128)(2,1)} %copy-done.80) | copy-start | bytes 589828
  219.1 30.9 %collective-permute-start.1 = (bf16[128,384]{1,0:T(8,128)(2,1)S(1)}, bf16[128,384]{1,0:T(8,128)(2,1)S(1)}, u32[]{:S(2)}, u32[]{:S(2)}) collective-permute-start(bf16[128,384]{1,0:T(8,128)(2,1)S(1)} %get-tuple-element.149), channel_id=1, source_target_pairs={{0,31},{1,30},{2,29},{3,28},{4,27},{5,26},{6,25},{7,24},{8,23},{9,... | collective-permute-start | bytes 294920 | tf_op jit(solution)/shard_map/ppermute | solution.py:31
  231.9 18.8 %copy-start.42 = (f32[128,768]{1,0:T(8,128)S(1)}, f32[128,768]{1,0:T(8,128)}, u32[]{:S(2)}) copy-start(f32[128,768]{1,0:T(8,128)} %copy-done.41) | copy-start | bytes 1179652
  231.9 18.8 %copy-start.48 = (f32[13,768]{1,0:T(8,128)S(1)}, f32[13,768]{1,0:T(8,128)}, u32[]{:S(2)}) copy-start(f32[13,768]{1,0:T(8,128)} %get-tuple-element.226.next_vec_ref.vec_ref) | copy-start | bytes 119812
  251.6 76.9 %slice-start = ((s8[4718592]{0:T(1024)(128)(4,1)}), s8[4194304]{0:T(1024)(128)(4,1)S(1)}, s32[]{:S(2)}) async-start(s8[4718592]{0:T(1024)(128)(4,1)} %bitcast.51), calls=%async_computation | async-start | bytes 8388608
  251.6 76.9 %slice-start.2 = ((s8[4718592]{0:T(1024)(128)(4,1)}), s8[4194304]{0:T(1024)(128)(4,1)S(1)}, s32[]{:S(2)}) async-start(s8[4718592]{0:T(1024)(128)(4,1)} %bitcast.53), calls=%async_computation.2 | async-start | bytes 8388608
  258.3 52.3 %copy-start.17 = (f32[3,128,128]{2,1,0:T(8,128)S(1)}, f32[3,128,128]{2,1,0:T(8,128)}, u32[]{:S(2)}) copy-start(f32[3,128,128]{2,1,0:T(8,128)} %copy-done.15) | copy-start | bytes 589828
  258.3 52.4 %copy-start.50 = (bf16[1,128,768]{2,1,0:T(8,128)(2,1)S(1)}, bf16[1,128,768]{2,1,0:T(8,128)(2,1)}, u32[]{:S(2)}) copy-start(bf16[1,128,768]{2,1,0:T(8,128)(2,1)} %param.15) | copy-start | bytes 589828
  258.3 52.4 %copy-start.97 = (f32[128,384]{1,0:T(8,128)S(1)}, f32[128,384]{1,0:T(8,128)}, u32[]{:S(2)}) copy-start(f32[128,384]{1,0:T(8,128)} %copy-done.96) | copy-start | bytes 589828
  258.3 70.3 %slice-start.1 = ((s8[4718592]{0:T(1024)(128)(4,1)}), s8[524288]{0:T(1024)(128)(4,1)S(1)}, s32[]{:S(2)}) async-start(s8[4718592]{0:T(1024)(128)(4,1)} %bitcast.51), calls=%async_computation.1 | async-start | bytes 1048576
  258.3 70.3 %slice-start.3 = ((s8[4718592]{0:T(1024)(128)(4,1)}), s8[524288]{0:T(1024)(128)(4,1)S(1)}, s32[]{:S(2)}) async-start(s8[4718592]{0:T(1024)(128)(4,1)} %bitcast.53), calls=%async_computation.3 | async-start | bytes 1048576
  310.6 9.6 %copy-start.27 = (bf16[512,3072]{1,0:T(8,128)(2,1)}, bf16[512,3072]{1,0:T(8,128)(2,1)S(1)}, u32[]{:S(2)}) copy-start(bf16[512,3072]{1,0:T(8,128)(2,1)S(1)} %get-tuple-element.213.pre_ref) | copy-start | bytes 9437188
  310.6 9.6 %copy-start.51 = (bf16[512,768]{1,0:T(8,128)(2,1)}, bf16[512,768]{1,0:T(8,128)(2,1)S(1)}, u32[]{:S(2)}) copy-start(bf16[512,768]{1,0:T(8,128)(2,1)S(1)} %get-tuple-element.210.hidden_ref) | copy-start | bytes 2359300
  310.6 9.6 %copy-start.53 = (bf16[512,768]{1,0:T(8,128)(2,1)}, bf16[512,768]{1,0:T(8,128)(2,1)S(1)}, u32[]{:S(2)}) copy-start(bf16[512,768]{1,0:T(8,128)(2,1)S(1)} %get-tuple-element.207.one_ref) | copy-start | bytes 2359300
  310.6 9.6 %copy-start.55 = (bf16[512,768]{1,0:T(8,128)(2,1)}, bf16[512,768]{1,0:T(8,128)(2,1)S(1)}, u32[]{:S(2)}) copy-start(bf16[512,768]{1,0:T(8,128)(2,1)S(1)} %get-tuple-element.208.mixed_ref) | copy-start | bytes 2359300
  310.6 9.6 %copy-start.57 = (bf16[512,768]{1,0:T(8,128)(2,1)}, bf16[512,768]{1,0:T(8,128)(2,1)S(1)}, u32[]{:S(2)}) copy-start(bf16[512,768]{1,0:T(8,128)(2,1)S(1)} %get-tuple-element.209.two_ref) | copy-start | bytes 2359300
  317.1 11.4 %copy-start.40 = (f32[128,3072]{1,0:T(8,128)S(1)}, f32[128,3072]{1,0:T(8,128)}, u32[]{:S(2)}) copy-start(f32[128,3072]{1,0:T(8,128)} %copy-done.39) | copy-start | bytes 4718596
  320.3 11.3 %copy-start.85 = (bf16[128,768]{1,0:T(8,128)(2,1)}, bf16[128,768]{1,0:T(8,128)(2,1)S(1)}, u32[]{:S(2)}) copy-start(bf16[128,768]{1,0:T(8,128)(2,1)S(1)} %get-tuple-element.184.low_ref.refs_3_) | copy-start | bytes 589828
  320.3 11.3 %copy-start.88 = (bf16[128,2304]{1,0:T(8,128)(2,1)}, bf16[128,2304]{1,0:T(8,128)(2,1)S(1)}, u32[]{:S(2)}) copy-start(bf16[128,2304]{1,0:T(8,128)(2,1)S(1)} %get-tuple-element.187.refs_5_) | copy-start | bytes 1769476
  320.3 11.2 %copy-start.90 = (f32[128,768]{1,0:T(8,128)}, f32[128,768]{1,0:T(8,128)S(1)}, u32[]{:S(2)}) copy-start(f32[128,768]{1,0:T(8,128)S(1)} %get-tuple-element.194.gradient_ref) | copy-start | bytes 1179652
  320.3 12.0 %collective-permute-start.3 = (bf16[128,384]{1,0:T(8,128)(2,1)S(1)}, bf16[128,384]{1,0:T(8,128)(2,1)S(1)}, u32[]{:S(2)}, u32[]{:S(2)}) collective-permute-start(bf16[128,384]{1,0:T(8,128)(2,1)S(1)} %get-tuple-element.175), channel_id=1, source_target_pairs={{0,31},{1,30},{2,29},{3,28},{4,27},{5,26},{6,25},{7,24},{8,23},{9,... | collective-permute-start | bytes 294920 | tf_op jit(solution)/shard_map/ppermute | solution.py:31
  332.3 18.1 %copy-start.76 = (bf16[128,3072]{1,0:T(8,128)(2,1)S(1)}, bf16[128,3072]{1,0:T(8,128)(2,1)}, u32[]{:S(2)}) copy-start(bf16[128,3072]{1,0:T(8,128)(2,1)} %copy-done.75) | copy-start | bytes 2359300
  332.3 18.1 %copy-start.79 = (bf16[128,768]{1,0:T(8,128)(2,1)S(1)}, bf16[128,768]{1,0:T(8,128)(2,1)}, u32[]{:S(2)}) copy-start(bf16[128,768]{1,0:T(8,128)(2,1)} %copy-done.77) | copy-start | bytes 589828
  332.3 18.1 %copy-start.86 = (bf16[128,768]{1,0:T(8,128)(2,1)S(1)}, bf16[128,768]{1,0:T(8,128)(2,1)}, u32[]{:S(2)}) copy-start(bf16[128,768]{1,0:T(8,128)(2,1)} %copy-done.85) | copy-start | bytes 589828
  332.3 18.1 %copy-start.89 = (bf16[128,2304]{1,0:T(8,128)(2,1)S(1)}, bf16[128,2304]{1,0:T(8,128)(2,1)}, u32[]{:S(2)}) copy-start(bf16[128,2304]{1,0:T(8,128)(2,1)} %copy-done.88) | copy-start | bytes 1769476
  332.4 18.1 %copy-start.99 = (bf16[128,768]{1,0:T(8,128)(2,1)S(1)}, bf16[128,768]{1,0:T(8,128)(2,1)}, u32[]{:S(2)}) copy-start(bf16[128,768]{1,0:T(8,128)(2,1)} %copy-done.98) | copy-start | bytes 589828
  332.4 18.1 %copy-start.101 = (bf16[128,768]{1,0:T(8,128)(2,1)S(1)}, bf16[128,768]{1,0:T(8,128)(2,1)}, u32[]{:S(2)}) copy-start(bf16[128,768]{1,0:T(8,128)(2,1)} %copy-done.100) | copy-start | bytes 589828
  350.5 53.7 %copy-start.5 = (bf16[768,2304]{1,0:T(8,128)(2,1)S(1)}, bf16[768,2304]{1,0:T(8,128)(2,1)}, u32[]{:S(2)}) copy-start(bf16[768,2304]{1,0:T(8,128)(2,1)} %copy-done.4) | copy-start | bytes 10616836
  350.5 53.7 %copy-start.38 = (bf16[1,128,768]{2,1,0:T(8,128)(2,1)S(1)}, bf16[1,128,768]{2,1,0:T(8,128)(2,1)}, u32[]{:S(2)}) copy-start(bf16[1,128,768]{2,1,0:T(8,128)(2,1)} %param.14) | copy-start | bytes 589828
  350.5 53.7 %copy-start.46 = (f32[13,768]{1,0:T(8,128)S(1)}, f32[13,768]{1,0:T(8,128)}, u32[]{:S(2)}) copy-start(f32[13,768]{1,0:T(8,128)} %get-tuple-element.227.vec_ref) | copy-start | bytes 119812
  350.5 53.7 %copy-start.91 = (f32[128,768]{1,0:T(8,128)S(1)}, f32[128,768]{1,0:T(8,128)}, u32[]{:S(2)}) copy-start(f32[128,768]{1,0:T(8,128)} %copy-done.90) | copy-start | bytes 1179652
  350.5 53.7 %copy-start.93 = (f32[128,768]{1,0:T(8,128)S(1)}, f32[128,768]{1,0:T(8,128)}, u32[]{:S(2)}) copy-start(f32[128,768]{1,0:T(8,128)} %copy-done.92) | copy-start | bytes 1179652
  404.1 4.7 copy-start.61
  404.1 4.7 copy-start.63
  404.1 4.7 copy-start.65
  404.1 4.7 copy-start.67
  404.1 18.6 %copy-start.52 = (bf16[512,768]{1,0:T(8,128)(2,1)S(1)}, bf16[512,768]{1,0:T(8,128)(2,1)}, u32[]{:S(2)}) copy-start(bf16[512,768]{1,0:T(8,128)(2,1)} %copy-done.51) | copy-start | bytes 2359300
  404.1 18.6 %copy-start.54 = (bf16[512,768]{1,0:T(8,128)(2,1)S(1)}, bf16[512,768]{1,0:T(8,128)(2,1)}, u32[]{:S(2)}) copy-start(bf16[512,768]{1,0:T(8,128)(2,1)} %copy-done.53) | copy-start | bytes 2359300
  404.1 18.6 %copy-start.56 = (bf16[512,768]{1,0:T(8,128)(2,1)S(1)}, bf16[512,768]{1,0:T(8,128)(2,1)}, u32[]{:S(2)}) copy-start(bf16[512,768]{1,0:T(8,128)(2,1)} %copy-done.55) | copy-start | bytes 2359300
  428.6 4.9 copy-start.29
  428.6 4.9 copy-start.33
  428.6 4.9 copy-start.66
  428.6 4.9 copy-start.68
  428.6 4.9 copy-start.70
  428.6 4.9 copy-start.104
  (63 other events, 124.5 us)

commit v4 on v3

--- a/solution.py
+++ b/solution.py
@@ -267,7 +267,6 @@
             for t in (0, 1):
                 landed(t, da, db)
                 push(t, da, db, keep, 1, onward)
-            pause()
     while between:
         pause()
     for da in (0, 1, 3, 2):
@@ -322,7 +321,7 @@
         out_specs=(ANY, ANY),
         scratch_shapes=[room(*weight.shape[1:])] + sems(16, 4),
         compiler_params=pltpu.CompilerParams(
-            collective_id=0, has_side_effects=True, vmem_limit_bytes=16 * 2**20
+            collective_id=0, has_side_effects=True, vmem_limit_bytes=60 * 2**20
         ),
         name="gather_first",
     )(weight, vectors)
@@ -349,11 +348,12 @@
 
     def ready(t, b):
         if b == 1:
+            if t == 0:
+                for layer, weight, target, bounce in zip(jobs, weights, weights_out, bounces):
+                    work.append(share_param(place, wire, weight.at[layer], target, bounce))
             swapped[t].wait_recv()
             if t == 1:
                 swapped.append(wire.push(q_ref, q_out, place.mirror))
-                for layer, weight, target, bounce in zip(jobs, weights, weights_out, bounces):
-                    work.append(share_param(place, wire, weight.at[layer], target, bounce))
 
     def spot(t, origin, b):
         return outs[t].at[origin if b == 0 else BLOCKS - 1 - origin]
@@ -372,9 +372,7 @@
         own,
         spot,
         ready,
-        [wire.flush]
-        + [lambda: None] * 3
-        + [functools.partial(onward, 0), functools.partial(onward, 1)],
+        [wire.flush, functools.partial(onward, 0), functools.partial(onward, 1)],
     )
     swapped[2].wait_recv()
     for _, last in work:
@@ -395,7 +393,7 @@
         out_specs=(ANY,) * (3 + len(jobs)),
         scratch_shapes=[room(*weight.shape[1:]) for weight in weights] + sems(96, 8),
         compiler_params=pltpu.CompilerParams(
-            collective_id=number, has_side_effects=True, vmem_limit_bytes=24 * 2**20
+            collective_id=number, has_side_effects=True, vmem_limit_bytes=60 * 2**20
         ),
         name=name,
     )(*away, *own, *weights)
@@ -432,10 +430,12 @@
                 near.at[t, da, 1, b],
                 place.near(t, 1, -way[b]),
             )
-    work = [share_columns(place, wire, hidden_ref, hidden_out, stage)]
-    for source, target in zip(sources, targets):
-        work.append(share_rows(place, wire, source, target))
+    work = []
     for b in (1, 0):
+        if b == 0:
+            work.append(share_columns(place, wire, hidden_ref, hidden_out, stage))
+            for source, target in zip(sources, targets):
+                work.append(share_rows(place, wire, source, target))
         for da, t in order:
             first[t, da, b].wait_recv()
             mix[t, da, b] = (
@@ -534,7 +534,7 @@
         ]
         + sems(128, 12),
         compiler_params=pltpu.CompilerParams(
-            collective_id=number, has_side_effects=True, vmem_limit_bytes=44 * 2**20
+            collective_id=number, has_side_effects=True, vmem_limit_bytes=60 * 2**20
         ),
         name=name,
     )(grad_keys, grad_values, away, hidden, *sources)
@@ -727,7 +727,7 @@
         ]
         + sems(128, 4),
         compiler_params=pltpu.CompilerParams(
-            collective_id=6, has_side_effects=True, vmem_limit_bytes=48 * 2**20
+            collective_id=6, has_side_effects=True, vmem_limit_bytes=60 * 2**20
         ),
         name="sum_over_ctx",
     )(one.reshape(shape), two.reshape(shape), small_one, small_two)
@@ -775,7 +775,7 @@
         in_specs=[SM] + [VM] * 8,
         out_specs=(VM, VM),
         scratch_shapes=[room(3, D, tokens), room(D, tokens)],
-        compiler_params=pltpu.CompilerParams(vmem_limit_bytes=40 * 2**20),
+        compiler_params=pltpu.CompilerParams(vmem_limit_bytes=60 * 2**20),
         cost_estimate=pl.CostEstimate(
             flops=2 * 512 * 1769472, bytes_accessed=12 * 2**20, transcendentals=0
         ),
@@ -870,7 +870,7 @@
             pltpu.VMEM((8, 2 * BLOCK), F32),
             pltpu.VMEM((PAIRS, 128, 2 * BLOCK), F32),
         ],
-        compiler_params=pltpu.CompilerParams(vmem_limit_bytes=40 * 2**20),
+        compiler_params=pltpu.CompilerParams(vmem_limit_bytes=60 * 2**20),
         cost_estimate=pl.CostEstimate(
             flops=4 * 33 * 128 * 128 * 6 * 128, bytes_accessed=8 * 2**20, transcendentals=33 * 128 * 128 * 6
         ),
@@ -956,7 +956,7 @@
             pltpu.VMEM((BLOCKS * BLOCK, HALF), F32),
             pltpu.VMEM((PAIRS, 128, 2 * BLOCK), F32),
         ],
-        compiler_params=pltpu.CompilerParams(vmem_limit_bytes=48 * 2**20),
+        compiler_params=pltpu.CompilerParams(vmem_limit_bytes=60 * 2**20),
         cost_estimate=pl.CostEstimate(
             flops=10 * 33 * 128 * 128 * 6 * 128, bytes_accessed=16 * 2**20, transcendentals=33 * 128 * 128 * 6
         ),
@@ -985,18 +985,17 @@
 
 
 def turn_tables(first_row, row_count):
+    shape = (row_count, 128)
+    feature = lax.broadcasted_iota(jnp.int32, shape, 1) % HEAD_DIM
+    position = first_row + lax.broadcasted_iota(jnp.int32, shape, 0)
     half_rot = ROTARY // 2
-    positions = first_row + jnp.arange(row_count, dtype=jnp.int32)
-    exponent = jnp.arange(half_rot, dtype=F32) * (2.0 / ROTARY)
-    frequency = jnp.power(10000.0, -exponent)
-    angle = positions.astype(F32)[:, None] * frequency[None, :]
+    exponent = (feature % half_rot).astype(F32) * (2.0 / ROTARY)
+    angle = position.astype(F32) * jnp.power(10000.0, -exponent)
     cosine, sine = jnp.cos(angle), jnp.sin(angle)
-    rest = jnp.zeros((row_count, HEAD_DIM - ROTARY), F32)
-    none = jnp.zeros_like(sine)
-    keep = jnp.concatenate([cosine, cosine, rest + 1.0] * 2, 1)
-    low = jnp.concatenate([-sine, none, rest] * 2, 1)
-    high = jnp.concatenate([none, sine, rest] * 2, 1)
-    return jnp.stack([keep, low, high], 0)
+    keep = jnp.where(feature < ROTARY, cosine, 1.0)
+    low = jnp.where(feature < half_rot, -sine, 0.0)
+    high = jnp.where((feature >= half_rot) & (feature < ROTARY), sine, 0.0)
+    return keep, low, high
 
 
 def rotate(values, table_ref):
@@ -1077,7 +1076,8 @@
         )
 
 
-def enter_kernel(upper_ref, tokens_ref, vec_ref, weight_ref, table_ref, *outs):
+def enter_kernel(upper_ref, tokens_ref, vec_ref, weight_ref, keep, low, high, *outs):
+    table_ref = (keep[...], low[...], high[...])
     enter(upper_ref, tokens_ref[...].astype(F32), vec_ref, weight_ref, table_ref, *outs)
 
 
@@ -1094,8 +1094,9 @@
 
 def pass_kernel(
     upper_ref, stream_ref, own_ref, away_ref, out_ref, mlp_ref, vec_ref,
-    next_vec_ref, weight_ref, table_ref, mixed_ref, next_ref, *outs,
+    next_vec_ref, weight_ref, keep, low, high, mixed_ref, next_ref, *outs,
 ):
+    table_ref = (keep[...], low[...], high[...])
     stream = leave(upper_ref, stream_ref, own_ref, away_ref, out_ref, mlp_ref, vec_ref, mixed_ref)
     next_ref[...] = stream
     enter(upper_ref, stream, next_vec_ref, weight_ref, table_ref, *outs)
@@ -1146,9 +1147,10 @@
 
 
 def join_kernel(
-    more, upper_ref, own_ref, back_ref, own_q, back_q, table_ref, weight_ref, stream_ref, vec_ref,
-    two_ref, gradient_ref, *refs,
+    more, upper_ref, own_ref, back_ref, own_q, back_q, keep, low, high, weight_ref, stream_ref,
+    vec_ref, two_ref, gradient_ref, *refs,
 ):
+    table_ref = (keep[...], low[...], high[...])
     next_weight, refs = (refs[:1], refs[1:]) if more else ((), refs)
     joined_ref, sums_ref, next_ref, *outs = refs
 
@@ -1193,7 +1195,7 @@
         out_shape=tuple(jax.ShapeDtypeStruct((LAYERS,) + shape, F32) for shape in shapes),
         in_specs=[pl.BlockSpec((1, 2304, D), lambda i: (i, 0, 0))],
         out_specs=tuple(pl.BlockSpec((1,) + shape, lambda i: (i, 0, 0)) for shape in shapes),
-        compiler_params=pltpu.CompilerParams(vmem_limit_bytes=40 * 2**20),
+        compiler_params=pltpu.CompilerParams(vmem_limit_bytes=60 * 2**20),
         name="unpack",
     )(rows)
 
@@ -1208,12 +1210,36 @@
         out_shape=shapes,
         in_specs=specs,
         out_specs=(VM,) * len(shapes),
-        compiler_params=pltpu.CompilerParams(vmem_limit_bytes=32 * 2**20),
+        compiler_params=pltpu.CompilerParams(vmem_limit_bytes=60 * 2**20),
         cost_estimate=pl.CostEstimate(
             flops=2 * BLOCK * flops, bytes_accessed=2 * flops, transcendentals=0
         ),
         name=name,
     )(*args)
+
+
+def vector_kernel(table_ref, *out_refs):
+    for layer_index, out_ref in enumerate(out_refs):
+        at = slice(layer_index, layer_index + 1)
+        for row in range(6):
+            pieces = [table_ref[f, at, row * 192 : (row + 1) * 192] for f in range(4)]
+            out_ref[row : row + 1, :] = jnp.concatenate(pieces, 1)
+        joined = jnp.concatenate([table_ref[f, at, 1152:1728] for f in range(4)], 1)
+        for i in range(3):
+            out_ref[BIAS_QKV + i : BIAS_QKV + i + 1, :] = joined[:, i * D : (i + 1) * D]
+        for f in range(4):
+            out_ref[BIAS_UP + f : BIAS_UP + f + 1, :] = table_ref[f, at, 1728:2496]
+        out_ref[13:, :] = jnp.zeros((3, D), F32)
+
+
+def order_vectors(table):
+    return pl.pallas_call(
+        vector_kernel,
+        out_shape=(jax.ShapeDtypeStruct((16, D), F32),) * LAYERS,
+        in_specs=[VM],
+        out_specs=(VM,) * LAYERS,
+        name="order_vectors",
+    )(table)
 
 
 ENTER_OUTS = ((D, BF),) * 2 + ((HALF, BF),) * 6
@@ -1246,27 +1272,16 @@
     packed = jnp.concatenate(vectors, 1).astype(F32)
     packed = jnp.pad(packed, ((0, 8 - LAYERS), (0, 2560 - packed.shape[1])))
     first_weight, table = gather_first(qkv_weight, packed)
-    table = table[:, :LAYERS]
-    six = table[:, :, :1152].reshape(4, LAYERS, 6, 192)
-    vecs = jnp.concatenate(
-        [
-            jnp.transpose(six, (1, 2, 0, 3)).reshape(LAYERS, 6, D),
-            jnp.transpose(table[:, :, 1152:1728], (1, 0, 2)).reshape(LAYERS, 3, D),
-            jnp.transpose(table[:, :, 1728:2496], (1, 0, 2)).reshape(LAYERS, 4, D),
-        ],
-        1,
-    )
-    vecs = [vecs[layer_index] for layer_index in range(LAYERS)]
-
+    vecs = order_vectors(table)
     qkv_full = [first_weight, None]
     gathered = [None] * LAYERS
     stream = tokens[0]
     entered = dense(
         "enter",
         enter_kernel,
-        [SM] + [VM] * 4,
+        [SM] + [VM] * 6,
         ENTER_OUTS,
-        (upper, stream, vecs[0], first_weight, tables),
+        (upper, stream, vecs[0], first_weight, *tables),
         D * 3 * D,
     )
     saved = []
@@ -1305,9 +1320,9 @@
             mixed_low, stream, *entered = dense(
                 "pass_on",
                 pass_kernel,
-                [SM] + [VM] * 9,
+                [SM] + [VM] * 11,
                 ((D, BF), (D, F32)) + ENTER_OUTS,
-                common + (vecs[layer_index + 1], more[0], tables),
+                common + (vecs[layer_index + 1], more[0], *tables),
                 D * 4 * D,
             )
         else:
@@ -1363,7 +1378,7 @@
         grad_joined, norm_sums, gradient, *outs = dense(
             "join_%d" % layer_index,
             functools.partial(join_kernel, going_on),
-            [SM] + [VM] * (11 if going_on else 10),
+            [SM] + [VM] * (13 if going_on else 12),
             ((3 * D, BF), ((16, D), BF), (D, F32))
             + (((D, BF), (HALF, BF), (HALF, BF)) if going_on else ()),
             (
@@ -1372,7 +1387,7 @@
                 back_pair,
                 gq_own,
                 back_query,
-                tables,
+                *tables,
                 w_qkv,
                 before,
                 vecs[layer_index],

time: 561 us -> 540 us (0.963)
  local copies, waits for them, and re-layouts: 83.2 us -> 10.3 us
  Pallas kernels: 441 us -> 502 us
    unnamed x256 -> x20, local copies, waits for them, and re-layouts: 61.7 us -> 7.11 us
    pallas_call x10, Pallas kernels: 23 us -> 58.9 us  [dense(): pl.pallas_call(kernel, out_shape=shapes, in_specs=specs, out_specs=(VM,)...]
    pallas_call x2, Pallas kernels: 6.19 us -> 17.2 us  [weight_grads(): pl.pallas_call(weight_kernel, out_shape=(jax.ShapeDtypeStruct((2304, D),...]
    pallas_call x2, Pallas kernels: 104 us -> 113 us  [scatter_pair(): pl.pallas_call(functools.partial(scatter_kernel, len(sources)), out_shape...]
    pallas_call x2, Pallas kernels: 114 us -> 107 us  [gather_pair(): pl.pallas_call(functools.partial(gather_kernel, layers), out_shape=(jax.S...]
    pallas_call x2, Pallas kernels: 25.6 us -> 32.3 us  [attend_forward(): pl.pallas_call(forward_kernel, out_shape=(jax.ShapeDtypeStruct((BLOCK, HA...]
    reshape x4 -> x0, local copies, waits for them, and re-layouts: 5.93 us -> none  [the longest x2 3 us: shards(): jnp.transpose(six, (1, 2, 0, 3)).reshape(LAYERS, 6, D)]
  transfers between devices with their start and end apart: 4 -> 4, of which waited for: 0 -> 1; matrix products, arithmetic and copies ran while one was open for 0% -> 0% of each run, Pallas kernels for 7% -> 12%
where the time goes in v4:
time: 540 us; the launch traced here: 532 us
  Pallas kernels  502 us (93%)
  starting transfers between devices  15.5 us (3%)
  local copies, waits for them, and re-layouts  10.3 us (2%)
    pallas_call x2, Pallas kernels, scatter_pair(): pl.pallas_call(functools.partial(scatter_kernel, len(sources)), out_shape...  113 us
    pallas_call x2, Pallas kernels, gather_pair(): pl.pallas_call(functools.partial(gather_kernel, layers), out_shape=(jax.S...  107 us
    pallas_call x1, Pallas kernels, sum_over_ctx(): pl.pallas_call(sum_kernel, out_shape=(jax.ShapeDtypeStruct((2,) + shape,...  99.4 us
    pallas_call x10, Pallas kernels, dense(): pl.pallas_call(kernel, out_shape=shapes, in_specs=specs, out_specs=(VM,)...  58.9 us
    pallas_call x2, Pallas kernels, attend_backward(): pl.pallas_call(backward_kernel, out_shape=(jax.ShapeDtypeStruct((BLOCK, H...  34.4 us
    pallas_call x2, Pallas kernels, attend_forward(): pl.pallas_call(forward_kernel, out_shape=(jax.ShapeDtypeStruct((BLOCK, HA...  32.3 us
    pallas_call x1, Pallas kernels, gather_first(): pl.pallas_call(first_kernel, out_shape=(full_shape(weight), jax.ShapeDtyp...  19.1 us
    pallas_call x2, Pallas kernels, weight_grads(): pl.pallas_call(weight_kernel, out_shape=(jax.ShapeDtypeStruct((2304, D),...  17.2 us
  transfers between devices with their start and end apart: 4, of which 1 were waited for; matrix products, arithmetic and copies ran while one was open for 0% of the time, Pallas kernels for 12%

profile of v4, /device:TPU:0, one launch (start us, length us, event | category | flops | bytes accessed | tf_op | source)
XLA Modules:
  0.0 531.5 jit_solution(13610881240862105580)
XLA Ops:
  0.7 0.9 concatenate.3
  1.6 0.6 pad_convert_fusion.vector_ref
  2.2 19.1 %gather_first.1 = (bf16[768,2304]{1,0:T(8,128)(2,1)}, f32[4,8,2560]{2,1,0:T(8,128)}) custom-call(bf16[2,192,2304]{2,1,0:T(8,128)(2,1)} %refs_3_.1, f32[8,2560]{1,0:T(8,128)} %pad_convert_fusion.vector_ref), custom_call_target="tpu_custom_call" | custom-call | tf_op jit(solution)/shard_map/gather_first/pallas_call | solution.py:317
  21.4 1.7 order_vectors.1
  23.1 1.0 fusion.8
  24.1 4.7 enter.1
  28.8 60.3 %gather_pair_0.1 = (bf16[128,384]{1,0:T(8,128)(2,1)}, bf16[32,128,384]{2,1,0:T(8,128)(2,1)}, bf16[32,128,384]{2,1,0:T(8,128)(2,1)}, bf16[768,768]{1,0:T(8,128)(2...) custom-call(bf16[128,384]{1,0:T(8,128)(2,1)} %get-tuple-element.125.q_ref, ...), custom_call_target="tpu_custom_call" | custom-call | tf_op jit(solution)/shard_map/gather_pair_0/pallas_call | solution.py:388
  89.2 16.1 %attend_forward.2 = (bf16[128,384]{1,0:T(8,128)(2,1)}, bf16[128,384]{1,0:T(8,128)(2,1)}, f32[384,256]{1,0:T(8,128)}, f32[8,256]{1,0:T(8,128)}) custom-call(s32[1]{0:T(128)} %bitcast.2.ctx_ref, bf16[128,384]{1,0:T(8,128)(2,1)} %get-tuple-element.124.q_own, bf16[128,384]{1,0:T(8,128)(2,1)} %get-tuple-element.130.q_away, bf16[4096,384]{1,0:T(8,128)(2,1)} %bitcast.42, ...), custom_call_target="tpu_custom_call" | custom-call | flops 1660944384 | bytes 8388608 | tf_op jit(solution)/shard_map/attend_forward/pallas_call | solution.py:858
  105.3 3.0 collective-permute-start
  108.3 7.0 %mlp.2 = (f32[128,3072]{1,0:T(8,128)}, bf16[128,3072]{1,0:T(8,128)(2,1)}, f32[128,768]{1,0:T(8,128)}) custom-call(bf16[128,768]{1,0:T(8,128)(2,1)} %get-tuple-element.136.two_ref.refs_2_, bf16[768,3072]{1,0:T(8,128)(2,1)} %get-tuple-element.137.up_ref, bf16[3072,768]{1,0:T(8,128)(2,1)} %get-tuple-element.138.down_ref, f32[16,768]{1,0:T(8,128)} %get-tuple-element.122.vec_ref), custom_call_target="tpu_custom_call" | custom-call | flops 1207959552 | bytes 9437184 | tf_op jit(solution)/shard_map/mlp/pallas_call | solution.py:1208
  115.3 1.1 collective-permute-done.away_ref
  116.4 0.0 copy-start.1
  116.5 0.6 copy-done.1
  117.1 6.3 %pass_on.1 = (bf16[128,768]{1,0:T(8,128)(2,1)}, f32[128,768]{1,0:T(8,128)}, bf16[128,768]{1,0:T(8,128)(2,1)}, bf16[128,768]{1,0:T(8,128)(2,1)}, bf16[128,384]{1,...) custom-call(s32[1]{0:T(128)} %bitcast.upper_ref, ...), custom_call_target="tpu_custom_call" | custom-call | flops 603979776 | bytes 4718592 | tf_op jit(solution)/shard_map/pass_on/pallas_call | solution.py:1208
  123.3 46.5 %gather_pair_1.1 = (bf16[128,384]{1,0:T(8,128)(2,1)}, bf16[32,128,384]{2,1,0:T(8,128)(2,1)}, bf16[32,128,384]{2,1,0:T(8,128)(2,1)}, bf16[768,768]{1,0:T(8,128)(2...) custom-call(bf16[128,384]{1,0:T(8,128)(2,1)} %get-tuple-element.144.q_ref, ...), custom_call_target="tpu_custom_call" | custom-call | tf_op jit(solution)/shard_map/gather_pair_1/pallas_call | solution.py:388
  169.8 2.7 back.1
  172.5 3.7 collective-permute-start.2
  176.2 16.1 %attend_forward.3 = (bf16[128,384]{1,0:T(8,128)(2,1)}, bf16[128,384]{1,0:T(8,128)(2,1)}, f32[384,256]{1,0:T(8,128)}, f32[8,256]{1,0:T(8,128)}) custom-call(s32[1]{0:T(128)} %bitcast.2.ctx_ref, bf16[128,384]{1,0:T(8,128)(2,1)} %get-tuple-element.143.q_own, bf16[128,384]{1,0:T(8,128)(2,1)} %get-tuple-element.149.q_away, bf16[4096,384]{1,0:T(8,128)(2,1)} %bitcast.46, ...), custom_call_target="tpu_custom_call" | custom-call | flops 1660944384 | bytes 8388608 | tf_op jit(solution)/shard_map/attend_forward/pallas_call | solution.py:858
  192.3 4.1 collective-permute-start.1
  196.4 7.0 %mlp.3 = (f32[128,3072]{1,0:T(8,128)}, bf16[128,3072]{1,0:T(8,128)(2,1)}, f32[128,768]{1,0:T(8,128)}) custom-call(bf16[128,768]{1,0:T(8,128)(2,1)} %get-tuple-element.155.two_ref.refs_2_, bf16[768,3072]{1,0:T(8,128)(2,1)} %get-tuple-element.156.up_ref, bf16[3072,768]{1,0:T(8,128)(2,1)} %get-tuple-element.157.down_ref, ...), custom_call_target="tpu_custom_call" | custom-call | flops 1207959552 | bytes 9437184 | tf_op jit(solution)/shard_map/mlp/pallas_call | solution.py:1208
  203.4 7.9 %mlp_back.2 = (bf16[128,3072]{1,0:T(8,128)(2,1)}, f32[128,768]{1,0:T(8,128)}) custom-call(bf16[128,768]{1,0:T(8,128)(2,1)} %get-tuple-element.170.low_ref.refs_3_, f32[128,3072]{1,0:T(8,128)} %get-tuple-element.171.pre_ref, bf16[768,3072]{1,0:T(8,128)(2,1)} %get-tuple-element.156.up_ref, bf16[3072,768]{1,0:T(8,128)(2,1)} %get-tuple-element.157.down_ref), custom_call_target="tpu_custom_call" | custom-call | flops 1207959552 | bytes 9437184 | tf_op jit(solution)/shard_map/mlp_back/pallas_call | solution.py:1208
  211.2 0.0 collective-permute-done.2.g_away
  211.2 0.0 copy-start.3
  211.2 0.6 copy-done.3
  211.9 17.3 %attend_backward.2 = (f32[128,384]{1,0:T(8,128)}, bf16[128,384]{1,0:T(8,128)(2,1)}, bf16[4096,384]{1,0:T(8,128)(2,1)}, bf16[4096,384]{1,0:T(8,128)(2,1)}) custom-call(s32[1]{0:T(128)} %bitcast.2.ctx_ref, bf16[128,384]{1,0:T(8,128)(2,1)} %get-tuple-element.143.q_own, bf16[128,384]{1,0:T(8,128)(2,1)} %get-tuple-element.149.q_away, bf16[4096,384]{1,0:T(8,128)(2,1)} %bitcast.47, ...), custom_call_target="tpu_custom_call" | custom-call | flops 4152360960 | bytes 16777216 | tf_op jit(solution)/shard_map/attend_backward/pallas_call | solution.py:944
  229.2 0.0 collective-permute-done.1.away_ref
  229.2 0.0 copy-start
  229.2 0.6 copy-done
  229.8 2.6 last.1
  232.4 54.6 %scatter_pair_1.1 = (f32[2,128,384]{2,1,0:T(8,128)}, bf16[2,128,384]{2,1,0:T(8,128)(2,1)}, bf16[128,384]{1,0:T(8,128)(2,1)}, bf16[512,768]{1,0:T(8,128)(2,1)}, b...) custom-call(bf16[32,128,384]{2,1,0:T(8,128)(2,1)} %bitcast.50, ...), custom_call_target="tpu_custom_call" | custom-call | tf_op jit(solution)/shard_map/scatter_pair_1/pallas_call | solution.py:513
  287.0 7.2 %join_1.1 = (bf16[128,2304]{1,0:T(8,128)(2,1)}, bf16[16,768]{1,0:T(8,128)(2,1)}, f32[128,768]{1,0:T(8,128)}, bf16[128,768]{1,0:T(8,128)(2,1)}, bf16[128,384]{1,0:T(8,128)(2,1)}, /*index=5*/bf16[128,384]{1,0:T(8,128)(2,1)}) custom-call(s32[1]{0:T(128)} %bitcast.upper_ref, f32[2,128,384]{2,1,0:T(8,128)} %get-tuple-element.173.own_ref, ...), custom_call_target="tpu_custom_call" | custom-call | flops 452984832 | bytes 3538944 | tf_op jit(solution)/shard_map/join_1/pallas_call | solution.py:1208
  294.2 4.8 collective-permute-start.3
  298.9 7.9 %mlp_back.3 = (bf16[128,3072]{1,0:T(8,128)(2,1)}, f32[128,768]{1,0:T(8,128)}) custom-call(bf16[128,768]{1,0:T(8,128)(2,1)} %get-tuple-element.188.low_ref.refs_3_, f32[128,3072]{1,0:T(8,128)} %get-tuple-element.189.pre_ref, bf16[768,3072]{1,0:T(8,128)(2,1)} %get-tuple-element.137.up_ref, bf16[3072,768]{1,0:T(8,128)(2,1)} %get-tuple-element.138.down_ref), custom_call_target="tpu_custom_call" | custom-call | flops 1207959552 | bytes 9437184 | tf_op jit(solution)/shard_map/mlp_back/pallas_call | solution.py:1208
  306.8 0.0 collective-permute-done.3.g_away
  306.8 0.0 copy-start.4
  306.8 0.6 copy-done.4
  307.5 17.1 %attend_backward.3 = (f32[128,384]{1,0:T(8,128)}, bf16[128,384]{1,0:T(8,128)(2,1)}, bf16[4096,384]{1,0:T(8,128)(2,1)}, bf16[4096,384]{1,0:T(8,128)(2,1)}) custom-call(s32[1]{0:T(128)} %bitcast.2.ctx_ref, bf16[128,384]{1,0:T(8,128)(2,1)} %get-tuple-element.124.q_own, bf16[128,384]{1,0:T(8,128)(2,1)} %get-tuple-element.130.q_away, bf16[4096,384]{1,0:T(8,128)(2,1)} %bitcast.43, ...), custom_call_target="tpu_custom_call" | custom-call | flops 4152360960 | bytes 16777216 | tf_op jit(solution)/shard_map/attend_backward/pallas_call | solution.py:944
  324.6 58.2 %scatter_pair_0.1 = (f32[2,128,384]{2,1,0:T(8,128)}, bf16[2,128,384]{2,1,0:T(8,128)(2,1)}, bf16[128,384]{1,0:T(8,128)(2,1)}, bf16[512,768]{1,0:T(8,128)(2,1)}, b...) custom-call(bf16[32,128,384]{2,1,0:T(8,128)(2,1)} %bitcast.52, ...), custom_call_target="tpu_custom_call" | custom-call | tf_op jit(solution)/shard_map/scatter_pair_0/pallas_call | solution.py:513
  382.8 5.8 %join_0.1 = (bf16[128,2304]{1,0:T(8,128)(2,1)}, bf16[16,768]{1,0:T(8,128)(2,1)}, f32[128,768]{1,0:T(8,128)}) custom-call(s32[1]{0:T(128)} %bitcast.upper_ref, f32[2,128,384]{2,1,0:T(8,128)} %get-tuple-element.193.own_ref, bf16[2,128,384]{2,1,0:T(8,128)(2,1)} %get-tuple-element.194.back_ref, f32[128,384]{1,0:T(8,128)} %get-tuple-element.195.own_q, ...), custom_call_target="tpu_custom_call" | custom-call | flops 452984832 | bytes 3538944 | tf_op jit(solution)/shard_map/join_0/pallas_call | solution.py:1208
  388.5 11.6 %gather_late.1 = (bf16[512,2304]{1,0:T(8,128)(2,1)}, bf16[64,768]{1,0:T(8,128)(2,1)}) custom-call(bf16[128,2304]{1,0:T(8,128)(2,1)} %get-tuple-element.204.one_ref, bf16[16,768]{1,0:T(8,128)(2,1)} %get-tuple-element.205.two_ref), custom_call_target="tpu_custom_call" | custom-call | tf_op jit(solution)/shard_map/gather_late/pallas_call | solution.py:560
  400.2 8.6 %weight_grads.3 = (bf16[2304,768]{1,0:T(8,128)(2,1)}, f32[16,768]{1,0:T(8,128)}) custom-call(s32[1]{0:T(128)} %bitcast.14.fsdp_ref, bf16[512,768]{1,0:T(8,128)(2,1)} %get-tuple-element.211.one_ref, bf16[512,768]{1,0:T(8,128)(2,1)} %get-tuple-element.212.mixed_ref, bf16[512,768]{1,0:T(8,128)(2,1)} %get-tuple-element.213.two_ref, ...), custom_call_target="tpu_custom_call" | custom-call | flops 1811939328 | bytes 12582912 | tf_op jit(solution)/shard_map/weight_grads/pallas_call | solution.py:769
  408.8 8.6 %weight_grads.2 = (bf16[2304,768]{1,0:T(8,128)(2,1)}, f32[16,768]{1,0:T(8,128)}) custom-call(s32[1]{0:T(128)} %bitcast.14.fsdp_ref, bf16[512,768]{1,0:T(8,128)(2,1)} %get-tuple-element.200.one_ref, bf16[512,768]{1,0:T(8,128)(2,1)} %get-tuple-element.201.mixed_ref, bf16[512,768]{1,0:T(8,128)(2,1)} %get-tuple-element.202.two_ref, ...), custom_call_target="tpu_custom_call" | custom-call | flops 1811939328 | bytes 12582912 | tf_op jit(solution)/shard_map/weight_grads/pallas_call | solution.py:769
  417.4 99.4 %sum_over_ctx.1 = (bf16[2,16,144,768]{3,2,1,0:T(8,128)(2,1)}, f32[2,16,768]{2,1,0:T(8,128)}) custom-call(bf16[16,144,768]{2,1,0:T(8,128)(2,1)} %bitcast.41, bf16[16,144,768]{2,1,0:T(8,128)(2,1)} %bitcast.40, f32[16,768]{1,0:T(8,128)} %get-tuple-element.220.small_one, f32[16,768]{1,0:T(8,128)} %get-tuple-element.221.small_two), custom_call_target="tpu_custom_call" | custom-call | tf_op jit(solution)/shard_map/sum_over_ctx/pallas_call | solution.py:706
  516.8 0.8 slice_bitcast_fusion
  517.7 0.8 slice_bitcast_fusion.1
  518.5 0.8 slice.30
  519.3 7.4 %unpack.1 = (f32[2,192,2304]{2,1,0:T(8,128)}, f32[2,192,768]{2,1,0:T(8,128)}, f32[2,192,3072]{2,1,0:T(8,128)}, f32[2,768,768]{2,1,0:T(8,128)}) custom-call(bf16[2,2304,768]{2,1,0:T(8,128)(2,1)} %bitcast.39), custom_call_target="tpu_custom_call" | custom-call | tf_op jit(solution)/shard_map/unpack/pallas_call | solution.py:1192
  526.7 0.1 constant_dynamic-slice_fusion.6
  526.8 0.6 copy.41
  527.4 0.6 copy.42
  528.0 0.6 copy.43
  528.5 0.6 copy.44
  529.1 0.1 constant_dynamic-slice_fusion.4
  529.2 0.0 copy-start.2
  529.2 0.6 constant_dynamic-slice_fusion.3
  529.8 0.7 constant_dynamic-slice_fusion.5
  530.5 0.6 copy.46
  531.1 0.0 copy-done.2
  (6 shorter events, 0.0 us)
Async XLA Ops:
  105.3 11.1 %collective-permute-start = (bf16[128,384]{1,0:T(8,128)(2,1)}, bf16[128,384]{1,0:T(8,128)(2,1)S(1)}, u32[]{:S(2)}, u32[]{:S(2)}) collective-permute-start(bf16[128,384]{1,0:T(8,128)(2,1)} %get-tuple-element.134), channel_id=1, source_target_pairs={{0,31},{1,30},{2,29},{3,28},{4,27},{5,26},{6,25},{7,24},{8,23},{9,... | collective-permute-start | bytes 294920 | tf_op jit(solution)/shard_map/ppermute | solution.py:31
  116.4 0.6 copy-start.1
  172.5 38.7 %collective-permute-start.2 = (bf16[128,384]{1,0:T(8,128)(2,1)}, bf16[128,384]{1,0:T(8,128)(2,1)S(1)}, u32[]{:S(2)}, u32[]{:S(2)}) collective-permute-start(bf16[128,384]{1,0:T(8,128)(2,1)} %get-tuple-element.161), channel_id=1, source_target_pairs={{0,31},{1,30},{2,29},{3,28},{4,27},{5,26},{6,25},{7,24},{8,23},{9,... | collective-permute-start | bytes 294920 | tf_op jit(solution)/shard_map/ppermute | solution.py:31
  192.3 36.9 %collective-permute-start.1 = (bf16[128,384]{1,0:T(8,128)(2,1)}, bf16[128,384]{1,0:T(8,128)(2,1)S(1)}, u32[]{:S(2)}, u32[]{:S(2)}) collective-permute-start(bf16[128,384]{1,0:T(8,128)(2,1)} %get-tuple-element.153), channel_id=1, source_target_pairs={{0,31},{1,30},{2,29},{3,28},{4,27},{5,26},{6,25},{7,24},{8,23},{9,... | collective-permute-start | bytes 294920 | tf_op jit(solution)/shard_map/ppermute | solution.py:31
  211.2 0.6 copy-start.3
  229.2 0.6 copy-start
  294.2 12.6 %collective-permute-start.3 = (bf16[128,384]{1,0:T(8,128)(2,1)}, bf16[128,384]{1,0:T(8,128)(2,1)S(1)}, u32[]{:S(2)}, u32[]{:S(2)}) collective-permute-start(bf16[128,384]{1,0:T(8,128)(2,1)} %get-tuple-element.179), channel_id=1, source_target_pairs={{0,31},{1,30},{2,29},{3,28},{4,27},{5,26},{6,25},{7,24},{8,23},{9,... | collective-permute-start | bytes 294920 | tf_op jit(solution)/shard_map/ppermute | solution.py:31
  306.8 0.6 copy-start.4
  529.2 1.8 copy-start.2

commit v5 on v4

--- a/solution.py
+++ b/solution.py
@@ -568,12 +568,13 @@
     )(one, two)
 
 
-PIECE = 144
-CUT = 80
+PIECE = 96
+CUT = 48
+PACK = 32 * PIECE
 
 
 def sum_kernel(
-    one_ref, two_ref, small_one, small_two, out_ref, small_out,
+    rows_ref, small_ref, out_ref, small_out,
     far, mix, near, total, far_two, mix_two, near_two, part, other, final, small, heard, *sem,
 ):
     place, wire = Place(), Wire(*sem)
@@ -586,7 +587,7 @@
         place.half,
     ]
     place.greet(place.around() + [turns[1], turns[3], place.half])
-    ins = (one_ref, two_ref)
+    ins = (rows_ref.at[0], rows_ref.at[1])
     parts = {0: pl.ds(0, CUT), 1: pl.ds(CUT, PIECE - CUT)}
 
     def chunk(t, da, db):
@@ -599,8 +600,7 @@
             result = result + term.astype(F32)
         return result.astype(BF)
 
-    small[0] = small_one[...]
-    small[1] = small_two[...]
+    small[...] = small_ref[...]
     passing = wire.push(small, heard.at[0], turns[0])
     order = (2, 1, 3, 0)
     way = {2: 1, 1: 1, 3: -1, 0: -1}
@@ -700,16 +700,16 @@
         copy.wait()
 
 
-def sum_over_ctx(one, two, small_one, small_two):
-    shape = (16, PIECE, D)
-    small_shape = (2,) + small_one.shape
+def sum_over_ctx(rows, small):
+    shape = (2, 16, PIECE, D)
+    small_shape = small.shape
     return pl.pallas_call(
         sum_kernel,
         out_shape=(
-            jax.ShapeDtypeStruct((2,) + shape, BF),
+            jax.ShapeDtypeStruct(shape, BF),
             jax.ShapeDtypeStruct(small_shape, F32),
         ),
-        in_specs=[VM] * 4,
+        in_specs=[VM] * 2,
         out_specs=(ANY, VM),
         scratch_shapes=[
             room(2, 4, PIECE, D),
@@ -730,57 +730,138 @@
             collective_id=6, has_side_effects=True, vmem_limit_bytes=60 * 2**20
         ),
         name="sum_over_ctx",
-    )(one.reshape(shape), two.reshape(shape), small_one, small_two)
-
-
-def weight_kernel(
-    fsdp_ref, one_ref, mixed_ref, two_ref, hidden_ref, joined_ref, low_ref, pre_ref, norm_ref,
-    rows_ref, sums_ref, turned, turned_hidden,
-):
-    start = pl.multiple_of(fsdp_ref[0] * 192, 64)
-    lefts = []
-    for i, ref in enumerate((one_ref, mixed_ref, two_ref)):
-        turned[i] = jnp.transpose(ref[...])
-        lefts.append(turned[i, pl.ds(start, 192), :])
-    turned_hidden[...] = jnp.transpose(hidden_ref[...])
-    ones = jnp.ones((8, low_ref.shape[0]), BF)
-
-    def panel(first, left, right, line):
-        rows = left.shape[0]
-        rows_ref[first : first + rows, :] = contract(left, right, ((1,), (0,))).astype(BF)
-        if line is not None:
-            sums_ref[line : line + 1, :] = contract(ones, right, ((1,), (0,)))[:1]
-
-    low = low_ref[...]
-    panel(1536, turned_hidden[...], low, None)
-    panel(576, lefts[1], low, 0)
+    )(rows.reshape(shape), small)
+
+
+def fetch(sources, buffers, sem):
+    copies = []
+    for number, (source, buffer) in enumerate(zip(sources, buffers)):
+        copy = pltpu.make_async_copy(source, buffer, sem.at[number])
+        copy.start()
+        copies.append(copy)
+
+    def take(number):
+        copies[number].wait()
+        return buffers[number]
+
+    return take
+
+
+def own_columns(fsdp_ref, values, turned):
+    turned[...] = jnp.transpose(values)
+    return turned[pl.ds(pl.multiple_of(fsdp_ref[0] * 192, 64), 192), :]
+
+
+def column_sums(right):
+    return contract(jnp.ones((8, right.shape[0]), BF), right, ((1,), (0,)))[:1]
+
+
+def panel(rows_ref, first, left, right):
+    rows_ref[first : first + left.shape[0], :] = contract(left, right, ((1,), (0,))).astype(BF)
+
+
+def early_panels(fsdp_ref, take, rows_ref, turned, put):
+    low = take(0)[...]
+    left = own_columns(fsdp_ref, take(1)[...], turned)
+    panel(rows_ref, 0, left, low)
+    put(0, column_sums(low))
+    turned[...] = jnp.transpose(take(2)[...])
+    panel(rows_ref, 960, turned[...], low)
+    left = own_columns(fsdp_ref, take(3)[...], turned)
+    pre = take(4)
+    for i in range(4):
+        right = pre[:, i * D : (i + 1) * D]
+        panel(rows_ref, 192 + i * 192, left, right)
+        put(1 + i, column_sums(right))
+
+
+def late_panels(fsdp_ref, one, joined, rows_ref, first, turned, put):
+    left = own_columns(fsdp_ref, one, turned)
     for i in range(3):
-        panel(i * 192, lefts[0], joined_ref[:, i * D : (i + 1) * D], 1 + i)
-    for i in range(4):
-        panel(768 + i * 192, lefts[2], pre_ref[:, i * D : (i + 1) * D], 4 + i)
-    norms = norm_ref[0:16, :].astype(F32)
-    for i in range(1, 4):
-        norms = norms + norm_ref[i * 16 : (i + 1) * 16, :].astype(F32)
-    sums_ref[8:16, :] = norms[:8]
-
-
-def weight_grads(fsdp, one, mixed, two, hidden, joined, low, pre, norms):
-    tokens = one.shape[0]
+        right = joined[:, i * D : (i + 1) * D]
+        panel(rows_ref, first + i * 192, left, right)
+        put(i, column_sums(right))
+
+
+def early_kernel(fsdp_ref, *refs):
+    sources, (rows_ref, sums_ref), buffers = refs[:5], refs[5:7], refs[7:12]
+    turned, sem = refs[12:]
+    take = fetch(sources, buffers, sem)
+    sums_ref[...] = jnp.zeros_like(sums_ref)
+
+    def put(i, row):
+        sums_ref[i : i + 1, :] = row
+
+    early_panels(fsdp_ref, take, rows_ref, turned, put)
+
+
+def rooms(arrays):
+    return [pltpu.VMEM(array.shape, array.dtype) for array in arrays]
+
+
+def early_grads(fsdp, low, mixed, hidden, two, pre):
+    arrays = (low, mixed, hidden, two, pre)
     return pl.pallas_call(
-        weight_kernel,
-        out_shape=(
-            jax.ShapeDtypeStruct((2304, D), BF),
-            jax.ShapeDtypeStruct((16, D), F32),
-        ),
-        in_specs=[SM] + [VM] * 8,
+        early_kernel,
+        out_shape=(jax.ShapeDtypeStruct((1728, D), BF), jax.ShapeDtypeStruct((8, D), F32)),
+        in_specs=[SM] + [ANY] * 5,
         out_specs=(VM, VM),
-        scratch_shapes=[room(3, D, tokens), room(D, tokens)],
+        scratch_shapes=rooms(arrays) + [room(D, low.shape[0]), pltpu.SemaphoreType.DMA((5,))],
         compiler_params=pltpu.CompilerParams(vmem_limit_bytes=60 * 2**20),
         cost_estimate=pl.CostEstimate(
-            flops=2 * 512 * 1769472, bytes_accessed=12 * 2**20, transcendentals=0
+            flops=2 * 512 * 1327104, bytes_accessed=9 * 2**20, transcendentals=0
         ),
-        name="weight_grads",
-    )(fsdp, one, mixed, two, hidden, joined, low, pre, norms)
+        name="early_grads",
+    )(fsdp, *arrays)
+
+
+def last_grads_kernel(fsdp_ref, norm_one, norm_two, sums_in, *refs):
+    sources, (rows_ref, sums_ref), buffers = refs[:9], refs[9:11], refs[11:20]
+    turned, sem = refs[20:]
+    take = fetch(sources, buffers, sem)
+    sums_ref[...] = jnp.zeros_like(sums_ref)
+
+    def put_early(i, row):
+        at = 0 if i == 0 else 3 + i
+        sums_ref[0, at : at + 1, :] = row
+
+    early_panels(fsdp_ref, take, rows_ref, turned, put_early)
+    for layer_index in range(LAYERS):
+
+        def put_late(i, row):
+            sums_ref[layer_index, 1 + i : 2 + i, :] = row
+
+        one, joined = take(5 + 2 * layer_index)[...], take(6 + 2 * layer_index)
+        late_panels(
+            fsdp_ref, one, joined, rows_ref, 1728 + 576 * layer_index, turned, put_late
+        )
+        norm_ref = (norm_one, norm_two)[layer_index]
+        norms = norm_ref[0:16, :].astype(F32)
+        for i in range(1, 4):
+            norms = norms + norm_ref[i * 16 : (i + 1) * 16, :].astype(F32)
+        sums_ref[layer_index, 8:16, :] = norms[:8]
+    rows_ref[2880:, :] = jnp.zeros((PACK - 2880, D), BF)
+    sums_ref[1, 0:1, :] = sums_in[0:1, :]
+    sums_ref[1, 4:8, :] = sums_in[1:5, :]
+
+
+def last_grads(fsdp, norm_one, norm_two, sums, arrays):
+    return pl.pallas_call(
+        last_grads_kernel,
+        out_shape=(
+            jax.ShapeDtypeStruct((PACK, D), BF),
+            jax.ShapeDtypeStruct((LAYERS, 16, D), F32),
+        ),
+        in_specs=[SM, VM, VM, VM] + [ANY] * 9,
+        out_specs=(VM, VM),
+        scratch_shapes=rooms(arrays)
+        + [room(D, arrays[0].shape[0]), pltpu.SemaphoreType.DMA((9,))],
+        compiler_params=pltpu.CompilerParams(vmem_limit_bytes=60 * 2**20),
+        cost_estimate=pl.CostEstimate(
+            flops=2 * 512 * 2211840, bytes_accessed=16 * 2**20, transcendentals=0
+        ),
+        name="last_grads",
+    )(fsdp, norm_one, norm_two, sums, *arrays)
 
 
 def pair_rows(values):
@@ -1110,15 +1191,27 @@
     ).astype(BF)
 
 
-def mlp_kernel(two_ref, up_ref, down_ref, vec_ref, pre_ref, hidden_ref, mlp_ref):
+def fetch_panels(up_ref, down_ref, up_buffer, down_buffer, sem):
+    sources, buffers = [], []
+    for i in range(FF // D):
+        cols = slice(i * D, (i + 1) * D)
+        sources += [up_ref.at[:, cols], down_ref.at[cols, :]]
+        buffers += [up_buffer.at[i], down_buffer.at[cols, :]]
+    return fetch(sources, buffers, sem)
+
+
+def mlp_kernel(
+    two_ref, vec_ref, up_ref, down_ref, pre_ref, hidden_ref, mlp_ref, up_buffer, down_buffer, sem
+):
+    take = fetch_panels(up_ref, down_ref, up_buffer, down_buffer, sem)
     two = two_ref[...]
     for i in range(FF // D):
         cols = slice(i * D, (i + 1) * D)
-        pre = contract(two, up_ref[:, cols], ((1,), (0,))) + line(vec_ref, BIAS_UP + i)
+        pre = contract(two, take(2 * i)[...], ((1,), (0,))) + line(vec_ref, BIAS_UP + i)
         pre_ref[:, cols] = pre
         hidden = (pre * phi_parts(pre)[0]).astype(BF)
         hidden_ref[:, cols] = hidden
-        fresh = contract(hidden, down_ref[cols, :], ((1,), (0,)))
+        fresh = contract(hidden, take(2 * i + 1)[...], ((1,), (0,)))
         mlp_ref[...] = fresh if i == 0 else mlp_ref[...] + fresh
 
 
@@ -1133,17 +1226,23 @@
     back(upper_ref, cotangent_ref[...].astype(F32), weight_ref, *outs)
 
 
-def mlp_back_kernel(low_ref, pre_ref, up_ref, down_ref, grad_pre_ref, norm_ref):
+def mlp_back_kernel(
+    low_ref, pre_ref, up_ref, down_ref, grad_pre_ref, norm_ref, up_buffer, down_buffer, sem
+):
+    take = fetch_panels(up_ref, down_ref, up_buffer, down_buffer, sem)
     low = low_ref[...]
     for i in range(FF // D):
         cols = slice(i * D, (i + 1) * D)
         pre = pre_ref[:, cols]
         cumulative, density = phi_parts(pre)
-        hidden = contract(low, down_ref[cols, :], ((1,), (1,)))
+        hidden = contract(low, take(2 * i + 1)[...], ((1,), (1,)))
         grad_pre = (hidden * (cumulative + pre * density)).astype(BF)
         grad_pre_ref[:, cols] = grad_pre
-        fresh = contract(grad_pre, up_ref[:, cols], ((1,), (1,)))
+        fresh = contract(grad_pre, take(2 * i)[...], ((1,), (1,)))
         norm_ref[...] = fresh if i == 0 else norm_ref[...] + fresh
+
+
+PANEL_ROOMS = (room(FF // D, D, D), room(FF, D), pltpu.SemaphoreType.DMA((2 * FF // D,)))
 
 
 def join_kernel(
@@ -1176,31 +1275,47 @@
         back(upper_ref, gradient, next_weight[0], *outs)
 
 
-def unpack_kernel(rows_ref, qkv_ref, out_ref, up_ref, down_ref):
-    for i in range(3):
-        qkv_ref[0, :, i * D : (i + 1) * D] = rows_ref[0, i * 192 : (i + 1) * 192, :].astype(F32)
-    out_ref[0] = rows_ref[0, 576:768, :].astype(F32)
-    for i in range(4):
-        up_ref[0, :, i * D : (i + 1) * D] = rows_ref[
-            0, 768 + i * 192 : 960 + i * 192, :
-        ].astype(F32)
-    down_ref[0] = rows_ref[0, 1536:, :].astype(F32)
-
-
-def unpack(rows):
+def unpack_kernel(early_ref, rows_ref, qkv_ref, out_ref, up_ref, down_ref):
+    layer_index = pl.program_id(0)
+
+    def put(source, late):
+        for i in range(3):
+            qkv_ref[0, :, i * D : (i + 1) * D] = rows_ref[
+                late + i * 192 : late + (i + 1) * 192, :
+            ].astype(F32)
+        out_ref[0] = source[:192, :].astype(F32)
+        for i in range(4):
+            up_ref[0, :, i * D : (i + 1) * D] = source[
+                192 + i * 192 : 384 + i * 192, :
+            ].astype(F32)
+        down_ref[0] = source[960:1728, :].astype(F32)
+
+    @pl.when(layer_index == 0)
+    def _():
+        put(rows_ref, 1728)
+
+    @pl.when(layer_index == 1)
+    def _():
+        put(early_ref, 2304)
+
+
+def unpack(early, rows):
     shapes = [(192, 3 * D), (192, D), (192, FF), (D, D)]
     return pl.pallas_call(
         unpack_kernel,
         grid=(LAYERS,),
         out_shape=tuple(jax.ShapeDtypeStruct((LAYERS,) + shape, F32) for shape in shapes),
-        in_specs=[pl.BlockSpec((1, 2304, D), lambda i: (i, 0, 0))],
+        in_specs=[
+            pl.BlockSpec((1728, D), lambda i: (0, 0)),
+            pl.BlockSpec((PACK, D), lambda i: (0, 0)),
+        ],
         out_specs=tuple(pl.BlockSpec((1,) + shape, lambda i: (i, 0, 0)) for shape in shapes),
         compiler_params=pltpu.CompilerParams(vmem_limit_bytes=60 * 2**20),
         name="unpack",
-    )(rows)
-
-
-def dense(name, kernel, specs, outs, args, flops):
+    )(early, rows)
+
+
+def dense(name, kernel, specs, outs, args, flops, scratch=()):
     shapes = tuple(
         jax.ShapeDtypeStruct((BLOCK, size) if isinstance(size, int) else size, kind)
         for size, kind in outs
@@ -1210,6 +1325,7 @@
         out_shape=shapes,
         in_specs=specs,
         out_specs=(VM,) * len(shapes),
+        scratch_shapes=list(scratch),
         compiler_params=pltpu.CompilerParams(vmem_limit_bytes=60 * 2**20),
         cost_estimate=pl.CostEstimate(
             flops=2 * BLOCK * flops, bytes_accessed=2 * flops, transcendentals=0
@@ -1266,6 +1382,7 @@
     ctx = lax.axis_index("ctx")
     ctx_word = ctx.astype(jnp.int32).reshape(1)
     upper = (ctx % 2).astype(jnp.int32).reshape(1)
+    fsdp_word = fsdp.astype(jnp.int32).reshape(1)
     tables = turn_tables(ctx * row_count, row_count)
 
     vectors = (ln1_gain, ln1_bias, ln2_gain, ln2_bias, out_bias, down_bias, qkv_bias, up_bias)
@@ -1273,7 +1390,10 @@
     packed = jnp.pad(packed, ((0, 8 - LAYERS), (0, 2560 - packed.shape[1])))
     first_weight, table = gather_first(qkv_weight, packed)
     vecs = order_vectors(table)
-    qkv_full = [first_weight, None]
+    qkv_full = [first_weight] + [
+        lax.all_gather(qkv_weight[layer_index], "fsdp", axis=0, tiled=True)
+        for layer_index in range(1, LAYERS)
+    ]
     gathered = [None] * LAYERS
     stream = tokens[0]
     entered = dense(
@@ -1288,17 +1408,13 @@
     for layer_index in range(LAYERS):
         norm_one, norm_two, q_own, q_away, k_own, k_away, v_own, v_away = entered
         jobs = [(layer_index, out_weight), (layer_index, up_weight), (layer_index, down_weight)]
-        if layer_index + 1 < LAYERS:
-            jobs.append((layer_index + 1, qkv_weight))
-        q_other, keys, values, w_out, w_up, w_down, *more = gather_pair(
+        q_other, keys, values, w_out, w_up, w_down = gather_pair(
             "gather_pair_%d" % layer_index,
             1 + layer_index,
             (q_away, k_away, v_away),
             (k_own, v_own),
             jobs,
         )
-        if more:
-            qkv_full[layer_index + 1] = more[0]
         gathered[layer_index] = (qkv_full[layer_index], w_out, w_up, w_down)
         keys = keys.reshape(BLOCKS * BLOCK, HALF)
         values = values.reshape(BLOCKS * BLOCK, HALF)
@@ -1309,20 +1425,21 @@
         hidden_pre, hidden_low, mlp_branch = dense(
             "mlp",
             mlp_kernel,
-            [VM] * 4,
+            [VM, VM, ANY, ANY],
             ((FF, F32), (FF, BF), (D, F32)),
-            (norm_two, w_up, w_down, vecs[layer_index]),
+            (norm_two, vecs[layer_index], w_up, w_down),
             2 * D * FF,
+            PANEL_ROOMS,
         )
         before = stream
         common = (upper, stream, mixed_own, mixed_back, w_out, mlp_branch, vecs[layer_index])
-        if more:
+        if layer_index + 1 < LAYERS:
             mixed_low, stream, *entered = dense(
                 "pass_on",
                 pass_kernel,
                 [SM] + [VM] * 11,
                 ((D, BF), (D, F32)) + ENTER_OUTS,
-                common + (vecs[layer_index + 1], more[0], *tables),
+                common + (vecs[layer_index + 1], qkv_full[layer_index + 1], *tables),
                 D * 4 * D,
             )
         else:
@@ -1353,10 +1470,11 @@
         grad_pre, grad_norm_two = dense(
             "mlp_back",
             mlp_back_kernel,
-            [VM] * 4,
+            [VM, VM, ANY, ANY],
             ((FF, BF), (D, F32)),
             (grad_low, hidden_pre, w_up, w_down),
             2 * D * FF,
+            PANEL_ROOMS,
         )
         gq_own, gq_away, grad_keys, grad_values = attend_backward(
             ctx_word, q_own, q_other, keys, values, grad_own, grad_back, turned, log_total
@@ -1372,6 +1490,10 @@
             lefts + (grad_low, grad_pre) + waiting,
         )
         early_rows[layer_index] = gathered_rows[:6]
+        if layer_index > 0:
+            hidden, _, mixed, two, low, pre = early_rows[layer_index]
+            early_pack, early_sums = early_grads(fsdp_word, low, mixed, hidden, two, pre)
+            early_total = lax.psum(early_pack, "ctx")
         if waiting:
             late_rows[layer_index + 1] = gathered_rows[6:]
         going_on = layer_index > 0
@@ -1401,15 +1523,16 @@
         if going_on:
             grad_low, grad_own, grad_away = outs
     late_rows[0] = gather_late(*waiting)
-    fsdp_word = fsdp.astype(jnp.int32).reshape(1)
-    packs, lines = [], []
-    for layer_index in range(LAYERS):
-        hidden, one, mixed, two, low, pre = early_rows[layer_index]
-        joined, norms = late_rows[layer_index]
-        rows, sums = weight_grads(fsdp_word, one, mixed, two, hidden, joined, low, pre, norms)
-        packs.append(rows)
-        lines.append(sums)
-    summed, small = sum_over_ctx(*packs, *lines)
+    hidden, one, mixed, two, low, pre = early_rows[0]
+    (joined, norms), (joined_one, norms_one) = late_rows
+    pack, sums = last_grads(
+        fsdp_word,
+        norms,
+        norms_one,
+        early_sums,
+        (low, mixed, hidden, two, pre, one, joined, early_rows[1][1], joined_one),
+    )
+    summed, small = sum_over_ctx(pack, sums)
 
     def own_part(vectors, width):
         return lax.dynamic_slice_in_dim(vectors, fsdp * width, width, vectors.ndim - 1)
@@ -1418,7 +1541,7 @@
     joined_sum = own_part(small[:, 1:4].reshape(LAYERS, 3 * D), 576)
     up_sum = own_part(small[:, 4:8].reshape(LAYERS, 4 * D), D)
     norm_sums = own_part(small[:, 8:12], 192)
-    qkv_grad, out_grad, up_grad, down_grad = unpack(summed.reshape(LAYERS, 2304, D))
+    qkv_grad, out_grad, up_grad, down_grad = unpack(early_total, summed.reshape(PACK, D))
     return (
         output[None],
         gradient[None],

time: 540 us -> 700 us (1.30)
  waiting for transfers between devices: 1.14 us -> 143 us
  between operations: 1.22 us -> 14.7 us
    psum x0 -> x1, waiting for transfers between devices: none -> 139 us  [shards(): early_total = lax.psum(early_pack, 'ctx')]
    pallas_call x3, Pallas kernels: 117 us -> 102 us  [the longest x1 85.2 us: sum_over_ctx(): pl.pallas_call(sum_kernel, out_shape=(jax.ShapeDtypeStruct(shape, BF), ja...]
    pallas_call x2, Pallas kernels: 113 us -> 123 us  [scatter_pair(): pl.pallas_call(functools.partial(scatter_kernel, len(sources)), out_shape...]
  transfers between devices with their start and end apart: 4 -> 6, of which waited for: 1 -> 2; matrix products, arithmetic and copies ran while one was open for 0% -> 1% of each run, Pallas kernels for 12% -> 54%
where the time goes in v5:
time: 700 us; the launch traced here: 691 us
  Pallas kernels  503 us (72%)
  waiting for transfers between devices  143 us (20%)
  starting transfers between devices  16.3 us (2%)
  between operations  14.7 us (2%)
  local copies, waits for them, and re-layouts  12.4 us (2%)
    psum x1, waiting for transfers between devices, shards(): early_total = lax.psum(early_pack, 'ctx')  139 us
    pallas_call x2, Pallas kernels, scatter_pair(): pl.pallas_call(functools.partial(scatter_kernel, len(sources)), out_shape...  123 us
    pallas_call x2, Pallas kernels, gather_pair(): pl.pallas_call(functools.partial(gather_kernel, layers), out_shape=(jax.S...  108 us
    pallas_call x1, Pallas kernels, sum_over_ctx(): pl.pallas_call(sum_kernel, out_shape=(jax.ShapeDtypeStruct(shape, BF), ja...  85.2 us
    pallas_call x10, Pallas kernels, dense(): pl.pallas_call(kernel, out_shape=shapes, in_specs=specs, out_specs=(VM,)...  59.1 us
    pallas_call x2, Pallas kernels, attend_backward(): pl.pallas_call(backward_kernel, out_shape=(jax.ShapeDtypeStruct((BLOCK, H...  34.2 us
    pallas_call x2, Pallas kernels, attend_forward(): pl.pallas_call(forward_kernel, out_shape=(jax.ShapeDtypeStruct((BLOCK, HA...  32.3 us
    pallas_call x1, Pallas kernels, gather_first(): pl.pallas_call(first_kernel, out_shape=(full_shape(weight), jax.ShapeDtyp...  19.2 us
  transfers between devices with their start and end apart: 6, of which 2 were waited for; matrix products, arithmetic and copies ran while one was open for 1% of the time, Pallas kernels for 54%

profile of v5, /device:TPU:0, one launch (start us, length us, event | category | flops | bytes accessed | tf_op | source)
XLA Modules:
  0.0 691.0 jit_solution(12063238366968834468)
XLA Ops:
  7.2 0.0 all-gather.3.cloned.1.call-start
  7.2 2.1 slice.27
  9.4 0.0 all-gather.3.cloned.1.call-update
  9.4 0.0 all-reduce.3.cloned.1.call-start
  9.4 0.9 concatenate.3
  10.4 0.6 pad_convert_fusion.vector_ref
  11.0 19.2 %gather_first.1 = (bf16[768,2304]{1,0:T(8,128)(2,1)}, f32[4,8,2560]{2,1,0:T(8,128)}) custom-call(bf16[2,192,2304]{2,1,0:T(8,128)(2,1)} %weight_ref.1, f32[8,2560]{1,0:T(8,128)} %pad_convert_fusion.vector_ref), custom_call_target="tpu_custom_call" | custom-call | tf_op jit(solution)/shard_map/gather_first/pallas_call | solution.py:317
  30.2 1.7 order_vectors.1
  32.0 1.0 fusion.8
  33.0 4.7 enter.1
  37.7 61.3 %gather_pair_0.1 = (bf16[128,384]{1,0:T(8,128)(2,1)}, bf16[32,128,384]{2,1,0:T(8,128)(2,1)}, bf16[32,128,384]{2,1,0:T(8,128)(2,1)}, bf16[768,768]{1,0:T(8,128)(2...) custom-call(bf16[128,384]{1,0:T(8,128)(2,1)} %get-tuple-element.124.q_ref, ...), custom_call_target="tpu_custom_call" | custom-call | tf_op jit(solution)/shard_map/gather_pair_0/pallas_call | solution.py:388
  99.0 16.1 %attend_forward.2 = (bf16[128,384]{1,0:T(8,128)(2,1)}, bf16[128,384]{1,0:T(8,128)(2,1)}, f32[384,256]{1,0:T(8,128)}, f32[8,256]{1,0:T(8,128)}) custom-call(s32[1]{0:T(128)} %bitcast.2.ctx_ref, bf16[128,384]{1,0:T(8,128)(2,1)} %get-tuple-element.123.q_own, bf16[128,384]{1,0:T(8,128)(2,1)} %get-tuple-element.129.q_away, bf16[4096,384]{1,0:T(8,128)(2,1)} %bitcast.43, ...), custom_call_target="tpu_custom_call" | custom-call | flops 1660944384 | bytes 8388608 | tf_op jit(solution)/shard_map/attend_forward/pallas_call | solution.py:939
  115.1 0.4 collective-permute-start
  115.5 6.3 mlp.2
  121.8 3.9 collective-permute-done.away_ref
  125.7 0.0 copy-start.1
  125.7 0.0 all-gather.3.cloned.1.call-done
  125.7 0.6 copy-done.1
  126.3 6.1 pass_on.1
  132.4 46.4 %gather_pair_1.1 = (bf16[128,384]{1,0:T(8,128)(2,1)}, bf16[32,128,384]{2,1,0:T(8,128)(2,1)}, bf16[32,128,384]{2,1,0:T(8,128)(2,1)}, bf16[768,768]{1,0:T(8,128)(2...) custom-call(bf16[128,384]{1,0:T(8,128)(2,1)} %get-tuple-element.142.q_ref, ...), custom_call_target="tpu_custom_call" | custom-call | tf_op jit(solution)/shard_map/gather_pair_1/pallas_call | solution.py:388
  178.8 2.7 back.1
  181.5 4.0 collective-permute-start.2
  185.5 16.2 %attend_forward.3 = (bf16[128,384]{1,0:T(8,128)(2,1)}, bf16[128,384]{1,0:T(8,128)(2,1)}, f32[384,256]{1,0:T(8,128)}, f32[8,256]{1,0:T(8,128)}) custom-call(s32[1]{0:T(128)} %bitcast.2.ctx_ref, bf16[128,384]{1,0:T(8,128)(2,1)} %get-tuple-element.141.q_own, bf16[128,384]{1,0:T(8,128)(2,1)} %get-tuple-element.147.q_away, bf16[4096,384]{1,0:T(8,128)(2,1)} %bitcast.47, ...), custom_call_target="tpu_custom_call" | custom-call | flops 1660944384 | bytes 8388608 | tf_op jit(solution)/shard_map/attend_forward/pallas_call | solution.py:939
  201.7 3.7 collective-permute-start.1
  205.4 6.3 mlp.3
  211.7 8.6 %mlp_back.2 = (bf16[128,3072]{1,0:T(8,128)(2,1)}, f32[128,768]{1,0:T(8,128)}) custom-call(bf16[128,768]{1,0:T(8,128)(2,1)} %get-tuple-element.168.low_ref.refs_3_, f32[128,3072]{1,0:T(8,128)} %get-tuple-element.169.pre_ref, bf16[768,3072]{1,0:T(8,128)(2,1)} %get-tuple-element.154.up_ref, bf16[3072,768]{1,0:T(8,128)(2,1)} %get-tuple-element.155.down_ref), custom_call_target="tpu_custom_call" | custom-call | flops 1207959552 | bytes 9437184 | tf_op jit(solution)/shard_map/mlp_back/pallas_call | solution.py:1323
  220.4 0.0 collective-permute-done.2.g_away
  220.4 0.0 copy-start.3
  220.4 0.6 copy-done.3
  221.0 17.1 %attend_backward.2 = (f32[128,384]{1,0:T(8,128)}, bf16[128,384]{1,0:T(8,128)(2,1)}, bf16[4096,384]{1,0:T(8,128)(2,1)}, bf16[4096,384]{1,0:T(8,128)(2,1)}) custom-call(s32[1]{0:T(128)} %bitcast.2.ctx_ref, bf16[128,384]{1,0:T(8,128)(2,1)} %get-tuple-element.141.q_own, bf16[128,384]{1,0:T(8,128)(2,1)} %get-tuple-element.147.q_away, bf16[4096,384]{1,0:T(8,128)(2,1)} %bitcast.48, ...), custom_call_target="tpu_custom_call" | custom-call | flops 4152360960 | bytes 16777216 | tf_op jit(solution)/shard_map/attend_backward/pallas_call | solution.py:1025
  238.1 0.0 collective-permute-done.1.away_ref
  238.1 0.6 copy-done
  238.8 2.8 last.1
  241.5 54.4 %scatter_pair_1.1 = (f32[2,128,384]{2,1,0:T(8,128)}, bf16[2,128,384]{2,1,0:T(8,128)(2,1)}, bf16[128,384]{1,0:T(8,128)(2,1)}, bf16[512,768]{1,0:T(8,128)(2,1)}, b...) custom-call(bf16[32,128,384]{2,1,0:T(8,128)(2,1)} %bitcast.51, ...), custom_call_target="tpu_custom_call" | custom-call | tf_op jit(solution)/shard_map/scatter_pair_1/pallas_call | solution.py:513
  295.9 6.2 early_grads.1
  302.1 0.0 all-reduce.3.cloned.1.call-update
  302.2 7.2 %join_1.1 = (bf16[128,2304]{1,0:T(8,128)(2,1)}, bf16[16,768]{1,0:T(8,128)(2,1)}, f32[128,768]{1,0:T(8,128)}, bf16[128,768]{1,0:T(8,128)(2,1)}, bf16[128,384]{1,0:T(8,128)(2,1)}, /*index=5*/bf16[128,384]{1,0:T(8,128)(2,1)}) custom-call(s32[1]{0:T(128)} %bitcast.upper_ref, f32[2,128,384]{2,1,0:T(8,128)} %get-tuple-element.171.own_ref, ...), custom_call_target="tpu_custom_call" | custom-call | flops 452984832 | bytes 3538944 | tf_op jit(solution)/shard_map/join_1/pallas_call | solution.py:1323
  309.4 8.1 %collective-permute-start.3 = (bf16[128,384]{1,0:T(8,128)(2,1)}, bf16[128,384]{1,0:T(8,128)(2,1)S(1)}, u32[]{:S(2)}, u32[]{:S(2)}) collective-permute-start(bf16[128,384]{1,0:T(8,128)(2,1)} %get-tuple-element.177), channel_id=1, source_target_pairs={{0,31},{1,30},{2,29},{3,28},{4,27},{5,26},{6,25},{7,24},{8,23},{9,... | collective-permute-start | bytes 294920 | tf_op jit(solution)/shard_map/ppermute | solution.py:31
  317.5 8.6 %mlp_back.3 = (bf16[128,3072]{1,0:T(8,128)(2,1)}, f32[128,768]{1,0:T(8,128)}) custom-call(bf16[128,768]{1,0:T(8,128)(2,1)} %get-tuple-element.186.low_ref.refs_3_, f32[128,3072]{1,0:T(8,128)} %get-tuple-element.187.pre_ref, bf16[768,3072]{1,0:T(8,128)(2,1)} %get-tuple-element.136.up_ref, bf16[3072,768]{1,0:T(8,128)(2,1)} %get-tuple-element.137.down_ref), custom_call_target="tpu_custom_call" | custom-call | flops 1207959552 | bytes 9437184 | tf_op jit(solution)/shard_map/mlp_back/pallas_call | solution.py:1323
  326.1 0.0 collective-permute-done.3.g_away
  326.1 0.0 copy-start.4
  326.1 0.6 copy-done.4
  326.7 17.1 %attend_backward.3 = (f32[128,384]{1,0:T(8,128)}, bf16[128,384]{1,0:T(8,128)(2,1)}, bf16[4096,384]{1,0:T(8,128)(2,1)}, bf16[4096,384]{1,0:T(8,128)(2,1)}) custom-call(s32[1]{0:T(128)} %bitcast.2.ctx_ref, bf16[128,384]{1,0:T(8,128)(2,1)} %get-tuple-element.123.q_own, bf16[128,384]{1,0:T(8,128)(2,1)} %get-tuple-element.129.q_away, bf16[4096,384]{1,0:T(8,128)(2,1)} %bitcast.44, ...), custom_call_target="tpu_custom_call" | custom-call | flops 4152360960 | bytes 16777216 | tf_op jit(solution)/shard_map/attend_backward/pallas_call | solution.py:1025
  343.8 68.8 %scatter_pair_0.1 = (f32[2,128,384]{2,1,0:T(8,128)}, bf16[2,128,384]{2,1,0:T(8,128)(2,1)}, bf16[128,384]{1,0:T(8,128)(2,1)}, bf16[512,768]{1,0:T(8,128)(2,1)}, b...) custom-call(bf16[32,128,384]{2,1,0:T(8,128)(2,1)} %bitcast.53, ...), custom_call_target="tpu_custom_call" | custom-call | tf_op jit(solution)/shard_map/scatter_pair_0/pallas_call | solution.py:513
  412.7 5.8 join_0.1
  418.4 15.0 %gather_late.1 = (bf16[512,2304]{1,0:T(8,128)(2,1)}, bf16[64,768]{1,0:T(8,128)(2,1)}) custom-call(bf16[128,2304]{1,0:T(8,128)(2,1)} %get-tuple-element.198.one_ref, bf16[16,768]{1,0:T(8,128)(2,1)} %get-tuple-element.199.two_ref), custom_call_target="tpu_custom_call" | custom-call | tf_op jit(solution)/shard_map/gather_late/pallas_call | solution.py:560
  433.4 10.4 %last_grads.1 = (bf16[3072,768]{1,0:T(8,128)(2,1)}, f32[2,16,768]{2,1,0:T(8,128)}) custom-call(s32[1]{0:T(128)} %bitcast.15.fsdp_ref, bf16[64,768]{1,0:T(8,128)(2,1)} %get-tuple-element.200.norm_one, bf16[64,768]{1,0:T(8,128)(2,1)} %get-tuple-element.201.norm_two, f32[8,768]{1,0:T(8,128)} %get-tuple-element.207.sums_in, ...), custom_call_target="tpu_custom_call" | custom-call | flops 2264924160 | bytes 16777216 | tf_op jit(solution)/shard_map/last_grads/pallas_call | solution.py:849
  443.8 85.2 %sum_over_ctx.1 = (bf16[2,16,96,768]{3,2,1,0:T(8,128)(2,1)}, f32[2,16,768]{2,1,0:T(8,128)}) custom-call(bf16[2,16,96,768]{3,2,1,0:T(8,128)(2,1)} %bitcast.42, f32[2,16,768]{2,1,0:T(8,128)} %get-tuple-element.218.small_ref), custom_call_target="tpu_custom_call" | custom-call | tf_op jit(solution)/shard_map/sum_over_ctx/pallas_call | solution.py:706
  529.0 0.8 slice.34
  529.8 0.8 slice_bitcast_fusion
  530.7 0.1 constant_dynamic-slice_fusion.6
  530.8 0.6 copy.41
  531.4 0.6 copy.42
  531.9 0.6 copy.43
  532.5 0.6 copy.44
  533.1 0.8 slice_bitcast_fusion.1
  533.9 0.1 constant_dynamic-slice_fusion.4
  534.0 0.0 copy-start.2
  534.0 0.7 constant_dynamic-slice_fusion.5
  534.7 0.6 constant_dynamic-slice_fusion.3
  535.3 139.2 %all-reduce.3.cloned.1.call-done.early_ref = bf16[1728,768]{1,0:T(8,128)(2,1)} async-done(((bf16[1728,768]{1,0:T(8,128)(2,1)}), bf16[1728,768]{1,0:T(8,128)(2,1)}) %all-reduce.3.cloned.1.call-update) | async-done | bytes 2654224 | tf_op jit(solution)/shard_map/psum | solution.py:1496
  674.5 8.7 %unpack.1 = (f32[2,192,2304]{2,1,0:T(8,128)}, f32[2,192,768]{2,1,0:T(8,128)}, f32[2,192,3072]{2,1,0:T(8,128)}, f32[2,768,768]{2,1,0:T(8,128)}) custom-call(bf16[1728,768]{1,0:T(8,128)(2,1)} %all-reduce.3.cloned.1.call-done.early_ref, bf16[3072,768]{1,0:T(8,128)(2,1)} %bitcast.41), custom_call_target="tpu_custom_call" | custom-call | tf_op jit(solution)/shard_map/unpack/pallas_call | solution.py:1304
  683.2 0.0 copy-done.2
  683.2 0.6 copy.47
  (7 shorter events, 0.0 us)
Async XLA Ops:
  7.2 118.5 %all-gather.3.cloned.1.call-start = ((), (), s32[]{:S(2)}) async-start(), calls=%async_computation.1 | async-start | bytes 4423680 | tf_op jit(solution)/shard_map/all_gather | solution.py:1394
  9.4 665.1 %all-reduce.3.cloned.1.call-start = ((), (), s32[]{:S(2)}) async-start(), calls=%async_computation | async-start | bytes 5308416 | tf_op jit(solution)/shard_map/psum | solution.py:1496
  115.1 10.6 %collective-permute-start = (bf16[128,384]{1,0:T(8,128)(2,1)}, bf16[128,384]{1,0:T(8,128)(2,1)S(1)}, u32[]{:S(2)}, u32[]{:S(2)}) collective-permute-start(bf16[128,384]{1,0:T(8,128)(2,1)} %get-tuple-element.133), channel_id=1, source_target_pairs={{0,31},{1,30},{2,29},{3,28},{4,27},{5,26},{6,25},{7,24},{8,23},{9,... | collective-permute-start | bytes 294920 | tf_op jit(solution)/shard_map/ppermute | solution.py:31
  125.7 0.6 copy-start.1
  181.5 38.9 %collective-permute-start.2 = (bf16[128,384]{1,0:T(8,128)(2,1)}, bf16[128,384]{1,0:T(8,128)(2,1)S(1)}, u32[]{:S(2)}, u32[]{:S(2)}) collective-permute-start(bf16[128,384]{1,0:T(8,128)(2,1)} %get-tuple-element.159), channel_id=1, source_target_pairs={{0,31},{1,30},{2,29},{3,28},{4,27},{5,26},{6,25},{7,24},{8,23},{9,... | collective-permute-start | bytes 294920 | tf_op jit(solution)/shard_map/ppermute | solution.py:31
  201.7 36.4 %collective-permute-start.1 = (bf16[128,384]{1,0:T(8,128)(2,1)}, bf16[128,384]{1,0:T(8,128)(2,1)S(1)}, u32[]{:S(2)}, u32[]{:S(2)}) collective-permute-start(bf16[128,384]{1,0:T(8,128)(2,1)} %get-tuple-element.151), channel_id=1, source_target_pairs={{0,31},{1,30},{2,29},{3,28},{4,27},{5,26},{6,25},{7,24},{8,23},{9,... | collective-permute-start | bytes 294920 | tf_op jit(solution)/shard_map/ppermute | solution.py:31
  220.4 0.6 copy-start.3
  238.1 0.6 copy-start
  309.4 16.7 %collective-permute-start.3 = (bf16[128,384]{1,0:T(8,128)(2,1)}, bf16[128,384]{1,0:T(8,128)(2,1)S(1)}, u32[]{:S(2)}, u32[]{:S(2)}) collective-permute-start(bf16[128,384]{1,0:T(8,128)(2,1)} %get-tuple-element.177), channel_id=1, source_target_pairs={{0,31},{1,30},{2,29},{3,28},{4,27},{5,26},{6,25},{7,24},{8,23},{9,... | collective-permute-start | bytes 294920 | tf_op jit(solution)/shard_map/ppermute | solution.py:31
  326.1 0.6 copy-start.4
  534.0 149.2 %copy-start.2 = (f32[2,1,192]{2,0,1:T(2,128)}, f32[2,1,192]{2,0,1:T(2,128)S(1)}, u32[]{:S(2)}) copy-start(f32[2,1,192]{2,0,1:T(2,128)S(1)} %copy.40) | copy-start | bytes 4612
Sparse Core Ops, SparseCore 0:
  10.3 52.0 all-gather.2
  302.3 372.1 all-reduce.2

commit v6 on v4

--- a/solution.py
+++ b/solution.py
@@ -399,12 +399,23 @@
     )(*away, *own, *weights)
 
 
-def scatter_kernel(count, gk_ref, gv_ref, gq_ref, hidden_ref, *refs):
+def scatter_kernel(count, gk_ref, gv_ref, gq_ref, hidden_ref, pre_ref, up_ref, down_ref, *refs):
     sources, refs = refs[:count], refs[count:]
-    own_out, back_out, back_q, hidden_out = refs[:4]
-    targets, refs = refs[4 : 4 + count], refs[4 + count :]
+    own_out, norm_out, back_out, back_q, hidden_out, grad_pre_out = refs[:6]
+    targets, refs = refs[6 : 6 + count], refs[6 + count :]
     far, near, mix, total, last_far, last_near, last_mix, leave, stage = refs[:9]
-    place, wire = Place(), Wire(*refs[9:])
+    up_buffer, down_buffer, grad_pre, load_sem = refs[9:13]
+    place, wire = Place(), Wire(*refs[13:])
+    loads = []
+    for i in range(FF // D):
+        cols = slice(i * D, (i + 1) * D)
+        for source, buffer in (
+            (down_ref.at[cols, :], down_buffer.at[cols, :]),
+            (up_ref.at[:, cols], up_buffer.at[i]),
+        ):
+            load = pltpu.make_async_copy(source, buffer, load_sem.at[len(loads)])
+            load.start()
+            loads.append(load)
     place.greet(
         place.around() + [place.mirror, place.beside, place.along_x(1), place.along_x(3)]
     )
@@ -430,12 +441,13 @@
                 near.at[t, da, 1, b],
                 place.near(t, 1, -way[b]),
             )
-    work = []
+    work = [share_columns(place, wire, hidden_ref, hidden_out, stage)]
+    for source, target in zip(sources, targets):
+        work.append(share_rows(place, wire, source, target))
     for b in (1, 0):
         if b == 0:
-            work.append(share_columns(place, wire, hidden_ref, hidden_out, stage))
-            for source, target in zip(sources, targets):
-                work.append(share_rows(place, wire, source, target))
+            mlp_back(sources[3][...], pre_ref, loads, up_buffer, down_buffer, grad_pre, norm_out)
+            work.append(share_rows(place, wire, grad_pre, grad_pre_out))
         for da, t in order:
             first[t, da, b].wait_recv()
             mix[t, da, b] = (
@@ -509,18 +521,34 @@
     return jax.ShapeDtypeStruct((4 * source.shape[0], source.shape[1]), BF)
 
 
-def scatter_pair(name, number, grad_keys, grad_values, away, hidden, sources):
+def mlp_back(low, pre_ref, loads, up_buffer, down_buffer, grad_pre_ref, norm_ref):
+    for i in range(FF // D):
+        cols = slice(i * D, (i + 1) * D)
+        pre = pre_ref[:, cols]
+        cumulative, density = phi_parts(pre)
+        loads[2 * i].wait()
+        hidden = contract(low, down_buffer[cols, :], ((1,), (1,)))
+        grad_pre = (hidden * (cumulative + pre * density)).astype(BF)
+        grad_pre_ref[:, cols] = grad_pre
+        loads[2 * i + 1].wait()
+        fresh = contract(grad_pre, up_buffer[i], ((1,), (1,)))
+        norm_ref[...] = fresh if i == 0 else norm_ref[...] + fresh
+
+
+def scatter_pair(name, number, grad_keys, grad_values, away, hidden, pre, up, down, sources):
     return pl.pallas_call(
         functools.partial(scatter_kernel, len(sources)),
         out_shape=(
             jax.ShapeDtypeStruct((2, BLOCK, HALF), F32),
+            jax.ShapeDtypeStruct((BLOCK, D), F32),
             jax.ShapeDtypeStruct((2, BLOCK, HALF), BF),
             jax.ShapeDtypeStruct((BLOCK, HALF), BF),
             jax.ShapeDtypeStruct((4 * BLOCK, D), BF),
+            jax.ShapeDtypeStruct((4 * BLOCK, FF), BF),
         )
         + tuple(rows_shape(source) for source in sources),
-        in_specs=[VM] * (4 + len(sources)),
-        out_specs=(VM,) + (ANY,) * (3 + len(sources)),
+        in_specs=[VM] * 5 + [ANY] * 2 + [VM] * len(sources),
+        out_specs=(VM, VM) + (ANY,) * (4 + len(sources)),
         scratch_shapes=[
             room(2, 4, 2, BLOCK, HALF),
             room(2, 4, 2, 2, BLOCK, HALF),
@@ -531,13 +559,17 @@
             room(2, 2, BLOCK, HALF),
             room(2, BLOCK, HALF),
             room(BLOCK, D),
+            room(FF // D, D, D),
+            room(FF, D),
+            room(BLOCK, FF),
+            pltpu.SemaphoreType.DMA((2 * FF // D,)),
         ]
         + sems(128, 12),
         compiler_params=pltpu.CompilerParams(
             collective_id=number, has_side_effects=True, vmem_limit_bytes=60 * 2**20
         ),
         name=name,
-    )(grad_keys, grad_values, away, hidden, *sources)
+    )(grad_keys, grad_values, away, hidden, pre, up, down, *sources)
 
 
 def late_kernel(one_ref, two_ref, one_out, two_out, *sem):
@@ -801,14 +833,66 @@
     return key <= query
 
 
+def low_block(ctx):
+    return jnp.minimum(ctx, BLOCKS - 1 - ctx)
+
+
+def by_height(ctx, own, away, two):
+    @pl.when(ctx < BLOCKS // 2)
+    def _():
+        two[0] = own[...]
+        two[1] = away[...]
+
+    @pl.when(ctx >= BLOCKS // 2)
+    def _():
+        two[0] = away[...]
+        two[1] = own[...]
+
+
+def from_height(ctx, two, own, away):
+    @pl.when(ctx < BLOCKS // 2)
+    def _():
+        own[...] = two[0].astype(own.dtype)
+        away[...] = two[1].astype(away.dtype)
+
+    @pl.when(ctx >= BLOCKS // 2)
+    def _():
+        own[...] = two[1].astype(own.dtype)
+        away[...] = two[0].astype(away.dtype)
+
+
+TILES = BLOCKS * BLOCK // TILE
+
+
+def load_tiles(pairs, sem):
+    loads = []
+    for tile in range(TILES):
+        rows = pl.ds(tile * TILE, TILE)
+        for source, buffer in pairs:
+            load = pltpu.make_async_copy(source.at[rows], buffer.at[rows], sem.at[len(loads)])
+            load.start()
+            loads.append(load)
+    return loads
+
+
+def wait_tiles(loads, b):
+    half = len(loads) // 2
+    for load in loads[b * half : (b + 1) * half]:
+        load.wait()
+
+
 def forward_kernel(
-    ctx_ref, q_own, q_away, k_ref, v_ref, mixed_own, mixed_away, turned_ref, log_ref, top, mass, acc
+    ctx_ref, q_own, q_away, k_in, v_in, mixed_own, mixed_away, turned_ref, log_ref,
+    top, mass, acc, k_ref, v_ref, q_two, mixed_two, sem,
 ):
     ctx = ctx_ref[0]
+    loads = load_tiles(((k_in, k_ref), (v_in, v_ref)), sem)
+    by_height(ctx, q_own, q_away, q_two)
     for b in (0, 1):
-        block = ctx if b == 0 else BLOCKS - 1 - ctx
+        block = low_block(ctx) if b == 0 else BLOCKS - 1 - low_block(ctx)
+        wait_tiles(loads, b)
         rows = slice(b * BLOCK, (b + 1) * BLOCK)
-        q_ref, mixed_ref = (q_own, mixed_own) if b == 0 else (q_away, mixed_away)
+        q_ref, mixed_ref = q_two.at[b], mixed_two.at[b]
         queries = [
             pair_rows(q_ref[:, p * 128 : (p + 1) * 128] * jnp.asarray(0.125, BF))
             for p in range(PAIRS)
@@ -852,6 +936,7 @@
             mixed_ref[:, cols] = jnp.transpose(turned).astype(BF)
             row = b * PAIRS + p
             log_ref[row : row + 1, :] = top[p : p + 1, :] + jnp.log(mass[p : p + 1, :])
+    from_height(ctx, mixed_two, mixed_own, mixed_away)
 
 
 def attend_forward(ctx, own, away, keys, values):
@@ -863,12 +948,17 @@
             jax.ShapeDtypeStruct((HALF, 2 * BLOCK), F32),
             jax.ShapeDtypeStruct((8, 2 * BLOCK), F32),
         ),
-        in_specs=[SM, VM, VM, VM, VM],
+        in_specs=[SM, VM, VM, ANY, ANY],
         out_specs=(VM, VM, VM, VM),
         scratch_shapes=[
             pltpu.VMEM((8, 2 * BLOCK), F32),
             pltpu.VMEM((8, 2 * BLOCK), F32),
             pltpu.VMEM((PAIRS, 128, 2 * BLOCK), F32),
+            room(BLOCKS * BLOCK, HALF),
+            room(BLOCKS * BLOCK, HALF),
+            room(2, BLOCK, HALF),
+            room(2, BLOCK, HALF),
+            pltpu.SemaphoreType.DMA((2 * TILES,)),
         ],
         compiler_params=pltpu.CompilerParams(vmem_limit_bytes=60 * 2**20),
         cost_estimate=pl.CostEstimate(
@@ -879,17 +969,22 @@
 
 
 def backward_kernel(
-    ctx_ref, q_own, q_away, k_ref, v_ref, g_own, g_away, turned_ref, log_ref,
-    gq_own, gq_away, gk_ref, gv_ref, gk_acc, gv_acc, gq_acc,
+    ctx_ref, q_own, q_away, k_in, v_in, g_own, g_away, turned_ref, log_ref,
+    gq_own, gq_away, gk_ref, gv_ref,
+    gk_acc, gv_acc, gq_acc, k_ref, v_ref, q_two, g_two, gq_two, sem,
 ):
     ctx = ctx_ref[0]
+    loads = load_tiles(((k_in, k_ref), (v_in, v_ref)), sem)
+    by_height(ctx, q_own, q_away, q_two)
+    by_height(ctx, g_own, g_away, g_two)
     gk_acc[...] = jnp.zeros_like(gk_acc)
     gv_acc[...] = jnp.zeros_like(gv_acc)
     for b in (0, 1):
-        block = ctx if b == 0 else BLOCKS - 1 - ctx
+        block = low_block(ctx) if b == 0 else BLOCKS - 1 - low_block(ctx)
+        wait_tiles(loads, b)
         rows = slice(b * BLOCK, (b + 1) * BLOCK)
         queries, grads, deltas = [], [], []
-        q_ref, g_ref, gq_ref = (q_own, g_own, gq_own) if b == 0 else (q_away, g_away, gq_away)
+        q_ref, g_ref, gq_ref = q_two.at[b], g_two.at[b], gq_two.at[b]
         for p in range(PAIRS):
             cols = slice(p * 128, (p + 1) * 128)
             queries.append(pair_rows(q_ref[:, cols] * jnp.asarray(0.125, BF)))
@@ -935,6 +1030,7 @@
             done = gq_acc[p] * 0.125
             turned = jnp.concatenate([done[:HEAD_DIM, :BLOCK], done[HEAD_DIM:, BLOCK:]], 0)
             gq_ref[:, cols] = jnp.transpose(turned).astype(gq_ref.dtype)
+    from_height(ctx, gq_two, gq_own, gq_away)
     gk_ref[...] = gk_acc[...].astype(BF)
     gv_ref[...] = gv_acc[...].astype(BF)
 
@@ -949,12 +1045,18 @@
             whole,
             whole,
         ),
-        in_specs=[SM] + [VM] * 8,
+        in_specs=[SM, VM, VM, ANY, ANY] + [VM] * 4,
         out_specs=(VM,) * 4,
         scratch_shapes=[
             pltpu.VMEM((BLOCKS * BLOCK, HALF), F32),
             pltpu.VMEM((BLOCKS * BLOCK, HALF), F32),
             pltpu.VMEM((PAIRS, 128, 2 * BLOCK), F32),
+            room(BLOCKS * BLOCK, HALF),
+            room(BLOCKS * BLOCK, HALF),
+            room(2, BLOCK, HALF),
+            room(2, BLOCK, HALF),
+            pltpu.VMEM((2, BLOCK, HALF), F32),
+            pltpu.SemaphoreType.DMA((2 * TILES,)),
         ],
         compiler_params=pltpu.CompilerParams(vmem_limit_bytes=60 * 2**20),
         cost_estimate=pl.CostEstimate(
@@ -1131,19 +1233,6 @@
 
 def back_kernel(upper_ref, cotangent_ref, weight_ref, *outs):
     back(upper_ref, cotangent_ref[...].astype(F32), weight_ref, *outs)
-
-
-def mlp_back_kernel(low_ref, pre_ref, up_ref, down_ref, grad_pre_ref, norm_ref):
-    low = low_ref[...]
-    for i in range(FF // D):
-        cols = slice(i * D, (i + 1) * D)
-        pre = pre_ref[:, cols]
-        cumulative, density = phi_parts(pre)
-        hidden = contract(low, down_ref[cols, :], ((1,), (1,)))
-        grad_pre = (hidden * (cumulative + pre * density)).astype(BF)
-        grad_pre_ref[:, cols] = grad_pre
-        fresh = contract(grad_pre, up_ref[:, cols], ((1,), (1,)))
-        norm_ref[...] = fresh if i == 0 else norm_ref[...] + fresh
 
 
 def join_kernel(
@@ -1350,30 +1439,25 @@
             saved[layer_index]
         )
         grad_back = mirrored(grad_away)
-        grad_pre, grad_norm_two = dense(
-            "mlp_back",
-            mlp_back_kernel,
-            [VM] * 4,
-            ((FF, BF), (D, F32)),
-            (grad_low, hidden_pre, w_up, w_down),
-            2 * D * FF,
-        )
         gq_own, gq_away, grad_keys, grad_values = attend_backward(
             ctx_word, q_own, q_other, keys, values, grad_own, grad_back, turned, log_total
         )
         whole = (BLOCKS, BLOCK, HALF)
-        own_pair, back_pair, back_query, *gathered_rows = scatter_pair(
+        own_pair, grad_norm_two, back_pair, back_query, hidden, pre, *gathered_rows = scatter_pair(
             "scatter_pair_%d" % layer_index,
             3 + layer_index,
             grad_keys.reshape(whole),
             grad_values.reshape(whole),
             gq_away,
             hidden_low,
-            lefts + (grad_low, grad_pre) + waiting,
-        )
-        early_rows[layer_index] = gathered_rows[:6]
+            hidden_pre,
+            w_up,
+            w_down,
+            lefts + (grad_low,) + waiting,
+        )
+        early_rows[layer_index] = (hidden, *gathered_rows[:4], pre)
         if waiting:
-            late_rows[layer_index + 1] = gathered_rows[6:]
+            late_rows[layer_index + 1] = gathered_rows[4:]
         going_on = layer_index > 0
         grad_joined, norm_sums, gradient, *outs = dense(
             "join_%d" % layer_index,

time: 540 us -> 530 us (0.981)
  Pallas kernels: 502 us -> 486 us
  waiting for transfers between devices: 1.14 us -> 7.13 us
    pallas_call x10 -> x8, Pallas kernels: 58.9 us -> 43.2 us  [dense(): pl.pallas_call(kernel, out_shape=shapes, in_specs=specs, out_specs=(VM,)...]
    ppermute x4, waiting for transfers between devices: 1.14 us -> 7.13 us  [mirrored(): return lax.ppermute(values, ('fsdp', 'ctx'), pairs)]
  transfers between devices with their start and end apart: 4 -> 4, of which waited for: 1 -> 2; matrix products, arithmetic and copies ran while one was open for 0% -> 0% of each run, Pallas kernels for 12% -> 4%
where the time goes in v6:
time: 530 us; the launch traced here: 522 us
  Pallas kernels  486 us (92%)
  starting transfers between devices  15.5 us (3%)
  local copies, waits for them, and re-layouts  10.2 us (2%)
  waiting for transfers between devices  7.13 us (1%)
    pallas_call x2, Pallas kernels, scatter_pair(): pl.pallas_call(functools.partial(scatter_kernel, len(sources)), out_shape...  111 us
    pallas_call x2, Pallas kernels, gather_pair(): pl.pallas_call(functools.partial(gather_kernel, layers), out_shape=(jax.S...  107 us
    pallas_call x1, Pallas kernels, sum_over_ctx(): pl.pallas_call(sum_kernel, out_shape=(jax.ShapeDtypeStruct((2,) + shape,...  100 us
    pallas_call x8, Pallas kernels, dense(): pl.pallas_call(kernel, out_shape=shapes, in_specs=specs, out_specs=(VM,)...  43.2 us
    pallas_call x2, Pallas kernels, attend_backward(): pl.pallas_call(backward_kernel, out_shape=(jax.ShapeDtypeStruct((BLOCK, H...  33.5 us
    pallas_call x2, Pallas kernels, attend_forward(): pl.pallas_call(forward_kernel, out_shape=(jax.ShapeDtypeStruct((BLOCK, HA...  32.5 us
    pallas_call x1, Pallas kernels, gather_first(): pl.pallas_call(first_kernel, out_shape=(full_shape(weight), jax.ShapeDtyp...  19.1 us
    pallas_call x2, Pallas kernels, weight_grads(): pl.pallas_call(weight_kernel, out_shape=(jax.ShapeDtypeStruct((2304, D),...  17.2 us
  transfers between devices with their start and end apart: 4, of which 2 were waited for; matrix products, arithmetic and copies ran while one was open for 0% of the time, Pallas kernels for 4%

profile of v6, /device:TPU:0, one launch (start us, length us, event | category | flops | bytes accessed | tf_op | source)
XLA Modules:
  0.0 521.8 jit_solution(5102854091785330828)
XLA Ops:
  0.7 0.9 concatenate.3
  1.6 0.6 pad_convert_fusion.vector_ref
  2.2 19.1 %gather_first.1 = (bf16[768,2304]{1,0:T(8,128)(2,1)}, f32[4,8,2560]{2,1,0:T(8,128)}) custom-call(bf16[2,192,2304]{2,1,0:T(8,128)(2,1)} %refs_3_.1, f32[8,2560]{1,0:T(8,128)} %pad_convert_fusion.vector_ref), custom_call_target="tpu_custom_call" | custom-call | tf_op jit(solution)/shard_map/gather_first/pallas_call | solution.py:317
  21.4 1.7 order_vectors.1
  23.1 1.0 fusion.8
  24.2 4.7 enter.1
  28.9 60.3 %gather_pair_0.1 = (bf16[128,384]{1,0:T(8,128)(2,1)}, bf16[32,128,384]{2,1,0:T(8,128)(2,1)}, bf16[32,128,384]{2,1,0:T(8,128)(2,1)}, bf16[768,768]{1,0:T(8,128)(2...) custom-call(bf16[128,384]{1,0:T(8,128)(2,1)} %get-tuple-element.123.q_ref, ...), custom_call_target="tpu_custom_call" | custom-call | tf_op jit(solution)/shard_map/gather_pair_0/pallas_call | solution.py:388
  89.2 16.2 %attend_forward.2 = (bf16[128,384]{1,0:T(8,128)(2,1)}, bf16[128,384]{1,0:T(8,128)(2,1)}, f32[384,256]{1,0:T(8,128)}, f32[8,256]{1,0:T(8,128)}) custom-call(s32[1]{0:T(128)} %bitcast.2.ctx_ref, bf16[128,384]{1,0:T(8,128)(2,1)} %get-tuple-element.122.q_own, bf16[128,384]{1,0:T(8,128)(2,1)} %get-tuple-element.128.q_away, bf16[4096,384]{1,0:T(8,128)(2,1)} %bitcast.46, ...), custom_call_target="tpu_custom_call" | custom-call | flops 1660944384 | bytes 8388608 | tf_op jit(solution)/shard_map/attend_forward/pallas_call | solution.py:943
  105.4 3.1 collective-permute-start
  108.6 7.0 %mlp.2 = (f32[128,3072]{1,0:T(8,128)}, bf16[128,3072]{1,0:T(8,128)(2,1)}, f32[128,768]{1,0:T(8,128)}) custom-call(bf16[128,768]{1,0:T(8,128)(2,1)} %get-tuple-element.134.two_ref.refs_2_, bf16[768,3072]{1,0:T(8,128)(2,1)} %get-tuple-element.135.up_ref, bf16[3072,768]{1,0:T(8,128)(2,1)} %get-tuple-element.136.down_ref, f32[16,768]{1,0:T(8,128)} %get-tuple-element.120.vec_ref), custom_call_target="tpu_custom_call" | custom-call | flops 1207959552 | bytes 9437184 | tf_op jit(solution)/shard_map/mlp/pallas_call | solution.py:1297
  115.5 1.1 collective-permute-done.away_ref
  116.7 0.0 copy-start.1
  116.7 0.6 copy-done.1
  117.3 6.3 %pass_on.1 = (bf16[128,768]{1,0:T(8,128)(2,1)}, f32[128,768]{1,0:T(8,128)}, bf16[128,768]{1,0:T(8,128)(2,1)}, bf16[128,768]{1,0:T(8,128)(2,1)}, bf16[128,384]{1,...) custom-call(s32[1]{0:T(128)} %bitcast.upper_ref, ...), custom_call_target="tpu_custom_call" | custom-call | flops 603979776 | bytes 4718592 | tf_op jit(solution)/shard_map/pass_on/pallas_call | solution.py:1297
  123.6 46.5 %gather_pair_1.1 = (bf16[128,384]{1,0:T(8,128)(2,1)}, bf16[32,128,384]{2,1,0:T(8,128)(2,1)}, bf16[32,128,384]{2,1,0:T(8,128)(2,1)}, bf16[768,768]{1,0:T(8,128)(2...) custom-call(bf16[128,384]{1,0:T(8,128)(2,1)} %get-tuple-element.142.q_ref, ...), custom_call_target="tpu_custom_call" | custom-call | tf_op jit(solution)/shard_map/gather_pair_1/pallas_call | solution.py:388
  170.0 16.3 %attend_forward.3 = (bf16[128,384]{1,0:T(8,128)(2,1)}, bf16[128,384]{1,0:T(8,128)(2,1)}, f32[384,256]{1,0:T(8,128)}, f32[8,256]{1,0:T(8,128)}) custom-call(s32[1]{0:T(128)} %bitcast.2.ctx_ref, bf16[128,384]{1,0:T(8,128)(2,1)} %get-tuple-element.141.q_own, bf16[128,384]{1,0:T(8,128)(2,1)} %get-tuple-element.147.q_away, bf16[4096,384]{1,0:T(8,128)(2,1)} %bitcast.50, ...), custom_call_target="tpu_custom_call" | custom-call | flops 1660944384 | bytes 8388608 | tf_op jit(solution)/shard_map/attend_forward/pallas_call | solution.py:943
  186.3 3.8 collective-permute-start.1
  190.1 2.7 back.1
  192.8 4.0 collective-permute-start.2
  196.9 7.0 %mlp.3 = (f32[128,3072]{1,0:T(8,128)}, bf16[128,3072]{1,0:T(8,128)(2,1)}, f32[128,768]{1,0:T(8,128)}) custom-call(bf16[128,768]{1,0:T(8,128)(2,1)} %get-tuple-element.153.two_ref.refs_2_, bf16[768,3072]{1,0:T(8,128)(2,1)} %get-tuple-element.154.up_ref, bf16[3072,768]{1,0:T(8,128)(2,1)} %get-tuple-element.155.down_ref, ...), custom_call_target="tpu_custom_call" | custom-call | flops 1207959552 | bytes 9437184 | tf_op jit(solution)/shard_map/mlp/pallas_call | solution.py:1297
  203.8 0.0 collective-permute-done.1.away_ref
  203.8 0.0 copy-start
  203.8 0.6 copy-done
  204.5 2.6 last.1
  207.1 0.0 collective-permute-done.2.g_away
  207.1 0.0 copy-start.4
  207.1 0.6 copy-done.4
  207.7 16.8 %attend_backward.2 = (f32[128,384]{1,0:T(8,128)}, bf16[128,384]{1,0:T(8,128)(2,1)}, bf16[4096,384]{1,0:T(8,128)(2,1)}, bf16[4096,384]{1,0:T(8,128)(2,1)}) custom-call(s32[1]{0:T(128)} %bitcast.2.ctx_ref, bf16[128,384]{1,0:T(8,128)(2,1)} %get-tuple-element.141.q_own, bf16[128,384]{1,0:T(8,128)(2,1)} %get-tuple-element.147.q_away, bf16[4096,384]{1,0:T(8,128)(2,1)} %bitcast.51, ...), custom_call_target="tpu_custom_call" | custom-call | flops 4152360960 | bytes 16777216 | tf_op jit(solution)/shard_map/attend_backward/pallas_call | solution.py:1040
  224.5 55.2 %scatter_pair_1.1 = (f32[2,128,384]{2,1,0:T(8,128)}, f32[128,768]{1,0:T(8,128)}, bf16[2,128,384]{2,1,0:T(8,128)(2,1)}, bf16[128,384]{1,0:T(8,128)(2,1)}, bf16[51...) custom-call(bf16[32,128,384]{2,1,0:T(8,128)(2,1)} %bitcast.44, ...), custom_call_target="tpu_custom_call" | custom-call | tf_op jit(solution)/shard_map/scatter_pair_1/pallas_call | solution.py:539
  279.7 7.2 %join_1.1 = (bf16[128,2304]{1,0:T(8,128)(2,1)}, bf16[16,768]{1,0:T(8,128)(2,1)}, f32[128,768]{1,0:T(8,128)}, bf16[128,768]{1,0:T(8,128)(2,1)}, bf16[128,384]{1,0:T(8,128)(2,1)}, /*index=5*/bf16[128,384]{1,0:T(8,128)(2,1)}) custom-call(s32[1]{0:T(128)} %bitcast.upper_ref, f32[2,128,384]{2,1,0:T(8,128)} %get-tuple-element.170.own_ref, ...), custom_call_target="tpu_custom_call" | custom-call | flops 452984832 | bytes 3538944 | tf_op jit(solution)/shard_map/join_1/pallas_call | solution.py:1297
  287.0 4.6 collective-permute-start.3
  291.5 6.0 %collective-permute-done.3.g_away = bf16[128,384]{1,0:T(8,128)(2,1)S(1)} collective-permute-done((bf16[128,384]{1,0:T(8,128)(2,1)}, bf16[128,384]{1,0:T(8,128)(2,1)S(1)}, u32[]{:S(2)}, u32[]{:S(2)}) %collective-permute-start.3) | collective-permute-done | bytes 98336 | tf_op jit(solution)/shard_map/ppermute | solution.py:31
  297.5 0.0 copy-start.3
  297.5 0.6 copy-done.3
  298.1 16.7 %attend_backward.3 = (f32[128,384]{1,0:T(8,128)}, bf16[128,384]{1,0:T(8,128)(2,1)}, bf16[4096,384]{1,0:T(8,128)(2,1)}, bf16[4096,384]{1,0:T(8,128)(2,1)}) custom-call(s32[1]{0:T(128)} %bitcast.2.ctx_ref, bf16[128,384]{1,0:T(8,128)(2,1)} %get-tuple-element.122.q_own, bf16[128,384]{1,0:T(8,128)(2,1)} %get-tuple-element.128.q_away, bf16[4096,384]{1,0:T(8,128)(2,1)} %bitcast.47, ...), custom_call_target="tpu_custom_call" | custom-call | flops 4152360960 | bytes 16777216 | tf_op jit(solution)/shard_map/attend_backward/pallas_call | solution.py:1040
  314.8 55.8 %scatter_pair_0.1 = (f32[2,128,384]{2,1,0:T(8,128)}, f32[128,768]{1,0:T(8,128)}, bf16[2,128,384]{2,1,0:T(8,128)(2,1)}, bf16[128,384]{1,0:T(8,128)(2,1)}, bf16[51...) custom-call(bf16[32,128,384]{2,1,0:T(8,128)(2,1)} %bitcast.42, ...), custom_call_target="tpu_custom_call" | custom-call | tf_op jit(solution)/shard_map/scatter_pair_0/pallas_call | solution.py:539
  370.6 5.8 %join_0.1 = (bf16[128,2304]{1,0:T(8,128)(2,1)}, bf16[16,768]{1,0:T(8,128)(2,1)}, f32[128,768]{1,0:T(8,128)}) custom-call(s32[1]{0:T(128)} %bitcast.upper_ref, f32[2,128,384]{2,1,0:T(8,128)} %get-tuple-element.189.own_ref, bf16[2,128,384]{2,1,0:T(8,128)(2,1)} %get-tuple-element.190.back_ref, f32[128,384]{1,0:T(8,128)} %get-tuple-element.191.own_q, ...), custom_call_target="tpu_custom_call" | custom-call | flops 452984832 | bytes 3538944 | tf_op jit(solution)/shard_map/join_0/pallas_call | solution.py:1297
  376.4 13.3 %gather_late.1 = (bf16[512,2304]{1,0:T(8,128)(2,1)}, bf16[64,768]{1,0:T(8,128)(2,1)}) custom-call(bf16[128,2304]{1,0:T(8,128)(2,1)} %get-tuple-element.200.one_ref, bf16[16,768]{1,0:T(8,128)(2,1)} %get-tuple-element.201.two_ref), custom_call_target="tpu_custom_call" | custom-call | tf_op jit(solution)/shard_map/gather_late/pallas_call | solution.py:592
  389.7 8.6 %weight_grads.2 = (bf16[2304,768]{1,0:T(8,128)(2,1)}, f32[16,768]{1,0:T(8,128)}) custom-call(s32[1]{0:T(128)} %bitcast.14.fsdp_ref, bf16[512,768]{1,0:T(8,128)(2,1)} %get-tuple-element.196.one_ref, bf16[512,768]{1,0:T(8,128)(2,1)} %get-tuple-element.197.mixed_ref, bf16[512,768]{1,0:T(8,128)(2,1)} %get-tuple-element.198.two_ref, ...), custom_call_target="tpu_custom_call" | custom-call | flops 1811939328 | bytes 12582912 | tf_op jit(solution)/shard_map/weight_grads/pallas_call | solution.py:801
  398.3 8.6 %weight_grads.3 = (bf16[2304,768]{1,0:T(8,128)(2,1)}, f32[16,768]{1,0:T(8,128)}) custom-call(s32[1]{0:T(128)} %bitcast.14.fsdp_ref, bf16[512,768]{1,0:T(8,128)(2,1)} %get-tuple-element.207.one_ref, bf16[512,768]{1,0:T(8,128)(2,1)} %get-tuple-element.208.mixed_ref, bf16[512,768]{1,0:T(8,128)(2,1)} %get-tuple-element.209.two_ref, ...), custom_call_target="tpu_custom_call" | custom-call | flops 1811939328 | bytes 12582912 | tf_op jit(solution)/shard_map/weight_grads/pallas_call | solution.py:801
  406.9 100.2 %sum_over_ctx.1 = (bf16[2,16,144,768]{3,2,1,0:T(8,128)(2,1)}, f32[2,16,768]{2,1,0:T(8,128)}) custom-call(bf16[16,144,768]{2,1,0:T(8,128)(2,1)} %bitcast.40, bf16[16,144,768]{2,1,0:T(8,128)(2,1)} %bitcast.41, f32[16,768]{1,0:T(8,128)} %get-tuple-element.216.small_one, f32[16,768]{1,0:T(8,128)} %get-tuple-element.217.small_two), custom_call_target="tpu_custom_call" | custom-call | tf_op jit(solution)/shard_map/sum_over_ctx/pallas_call | solution.py:738
  507.1 0.8 slice_bitcast_fusion
  508.0 0.8 slice_bitcast_fusion.1
  508.8 0.8 slice.30
  509.6 0.1 constant_dynamic-slice_fusion.6
  509.7 0.6 copy.44
  510.3 0.6 copy.43
  510.8 0.6 copy.42
  511.4 0.6 copy.41
  512.0 7.4 %unpack.1 = (f32[2,192,2304]{2,1,0:T(8,128)}, f32[2,192,768]{2,1,0:T(8,128)}, f32[2,192,3072]{2,1,0:T(8,128)}, f32[2,768,768]{2,1,0:T(8,128)}) custom-call(bf16[2,2304,768]{2,1,0:T(8,128)(2,1)} %bitcast.39), custom_call_target="tpu_custom_call" | custom-call | tf_op jit(solution)/shard_map/unpack/pallas_call | solution.py:1281
  519.4 0.1 constant_dynamic-slice_fusion.4
  519.5 0.0 copy-start.2
  519.5 0.7 constant_dynamic-slice_fusion.5
  520.2 0.6 constant_dynamic-slice_fusion.3
  520.8 0.6 copy.46
  521.4 0.0 copy-done.2
  (6 shorter events, 0.0 us)
Async XLA Ops:
  105.4 11.2 %collective-permute-start = (bf16[128,384]{1,0:T(8,128)(2,1)}, bf16[128,384]{1,0:T(8,128)(2,1)S(1)}, u32[]{:S(2)}, u32[]{:S(2)}) collective-permute-start(bf16[128,384]{1,0:T(8,128)(2,1)} %get-tuple-element.132), channel_id=1, source_target_pairs={{0,31},{1,30},{2,29},{3,28},{4,27},{5,26},{6,25},{7,24},{8,23},{9,... | collective-permute-start | bytes 294920 | tf_op jit(solution)/shard_map/ppermute | solution.py:31
  116.7 0.6 copy-start.1
  186.3 17.5 %collective-permute-start.1 = (bf16[128,384]{1,0:T(8,128)(2,1)}, bf16[128,384]{1,0:T(8,128)(2,1)S(1)}, u32[]{:S(2)}, u32[]{:S(2)}) collective-permute-start(bf16[128,384]{1,0:T(8,128)(2,1)} %get-tuple-element.151), channel_id=1, source_target_pairs={{0,31},{1,30},{2,29},{3,28},{4,27},{5,26},{6,25},{7,24},{8,23},{9,... | collective-permute-start | bytes 294920 | tf_op jit(solution)/shard_map/ppermute | solution.py:31
  192.8 14.3 %collective-permute-start.2 = (bf16[128,384]{1,0:T(8,128)(2,1)}, bf16[128,384]{1,0:T(8,128)(2,1)S(1)}, u32[]{:S(2)}, u32[]{:S(2)}) collective-permute-start(bf16[128,384]{1,0:T(8,128)(2,1)} %get-tuple-element.159), channel_id=1, source_target_pairs={{0,31},{1,30},{2,29},{3,28},{4,27},{5,26},{6,25},{7,24},{8,23},{9,... | collective-permute-start | bytes 294920 | tf_op jit(solution)/shard_map/ppermute | solution.py:31
  203.8 0.6 copy-start
  207.1 0.6 copy-start.4
  287.0 10.6 %collective-permute-start.3 = (bf16[128,384]{1,0:T(8,128)(2,1)}, bf16[128,384]{1,0:T(8,128)(2,1)S(1)}, u32[]{:S(2)}, u32[]{:S(2)}) collective-permute-start(bf16[128,384]{1,0:T(8,128)(2,1)} %get-tuple-element.176), channel_id=1, source_target_pairs={{0,31},{1,30},{2,29},{3,28},{4,27},{5,26},{6,25},{7,24},{8,23},{9,... | collective-permute-start | bytes 294920 | tf_op jit(solution)/shard_map/ppermute | solution.py:31
  297.5 0.6 copy-start.3
  519.5 1.9 copy-start.2

commit v7 on v6

--- a/solution.py
+++ b/solution.py
@@ -572,43 +572,24 @@
     )(grad_keys, grad_values, away, hidden, pre, up, down, *sources)
 
 
-def late_kernel(one_ref, two_ref, one_out, two_out, *sem):
-    place, wire = Place(), Wire(*sem)
-    place.greet([place.beside, place.along_x(1), place.along_x(3)])
-    work = [
-        share_rows(place, wire, one_ref, one_out),
-        share_rows(place, wire, two_ref, two_out),
-    ]
-    for steps, _ in work:
-        for step in steps:
-            step()
-    for _, last in work:
-        for copy in last:
-            copy.wait_recv()
-    wire.drain()
-
-
-def gather_late(one, two):
-    return pl.pallas_call(
-        late_kernel,
-        out_shape=(rows_shape(one), rows_shape(two)),
-        in_specs=[VM] * 2,
-        out_specs=(ANY,) * 2,
-        scratch_shapes=sems(16, 4),
-        compiler_params=pltpu.CompilerParams(collective_id=5, has_side_effects=True),
-        name="gather_late",
-    )(one, two)
-
-
 PIECE = 144
 CUT = 80
 
 
-def sum_kernel(
-    one_ref, two_ref, small_one, small_two, out_ref, small_out,
-    far, mix, near, total, far_two, mix_two, near_two, part, other, final, small, heard, *sem,
-):
-    place, wire = Place(), Wire(*sem)
+LOADS = 13
+
+
+def sum_kernel(joined_ref, norm_ref, norm_one, *refs):
+    sources, (out_ref, small_out), refs = refs[:LOADS], refs[LOADS : LOADS + 2], refs[LOADS + 2 :]
+    buffers, refs = refs[:LOADS], refs[LOADS:]
+    rows, joined_land, norm_land, turned, load_sem = refs[:5]
+    far, mix, near, total, far_two, mix_two, near_two, part, other, final, small, heard = refs[5:17]
+    place, wire = Place(), Wire(*refs[17:])
+    loads = []
+    for source, buffer in zip(sources, buffers):
+        load = pltpu.make_async_copy(source, buffer, load_sem.at[len(loads)])
+        load.start()
+        loads.append(load)
     y, z, h = place.y, place.z, place.h
     turns = [
         (place.fsdp, (y + 1 - 2 * (y % 2)) * 8 + z * 2 + h),
@@ -617,13 +598,15 @@
         (place.fsdp, y * 8 + ((z + 2) % 4) * 2 + h),
         place.half,
     ]
-    place.greet(place.around() + [turns[1], turns[3], place.half])
-    ins = (one_ref, two_ref)
+    place.greet(
+        place.around()
+        + [turns[1], turns[3], place.half, place.beside, place.along_x(1), place.along_x(3)]
+    )
     parts = {0: pl.ds(0, CUT), 1: pl.ds(CUT, PIECE - CUT)}
 
     def chunk(t, da, db):
-        origin = place.ring(t, da, db)
-        return origin // 2
+        start = pl.multiple_of(place.ring(t, da, db) // 2 * PIECE, 16)
+        return rows.at[t, pl.ds(start, PIECE)]
 
     def plus(*terms):
         result = terms[0].astype(F32)
@@ -631,26 +614,81 @@
             result = result + term.astype(F32)
         return result.astype(BF)
 
-    small[0] = small_one[...]
-    small[1] = small_two[...]
-    passing = wire.push(small, heard.at[0], turns[0])
     order = (2, 1, 3, 0)
     way = {2: 1, 1: 1, 3: -1, 0: -1}
     first, second, loose = {}, {}, {}
-    for db in order:
-        for t in (0, 1):
-            first[t, db] = wire.push(
-                ins[t].at[chunk(t, 2, db)], far.at[t, db], place.near(t, 0, way[db])
-            )
-    for db in order:
-        for t in (0, 1):
+
+    def take(number):
+        loads[number].wait()
+        return buffers[number]
+
+    def panel(t, start, left, right):
+        rows[t, start : start + left.shape[0], :] = contract(left, right, ((1,), (0,))).astype(BF)
+
+    def note(t, row, right):
+        ones = jnp.ones((8, right.shape[0]), BF)
+        small[1 - t, row : row + 1, :] = contract(ones, right, ((1,), (0,)))[:1]
+
+    def own_rows(values):
+        turned[...] = jnp.transpose(values)
+        return turned[pl.ds(pl.multiple_of(place.fsdp * 192, 64), 192), :]
+
+    def early_grads(t, at):
+        low = take(at)[...]
+        panel(t, 576, own_rows(take(at + 1)[...]), low)
+        note(t, 0, low)
+        turned[...] = jnp.transpose(take(at + 2)[...])
+        panel(t, 1536, turned[...], low)
+        left, pre = own_rows(take(at + 3)[...]), take(at + 4)
+        for i in range(4):
+            right = pre[:, i * D : (i + 1) * D]
+            panel(t, 768 + i * 192, left, right)
+            note(t, 4 + i, right)
+
+    def late_grads(t, one, joined, norms):
+        left = own_rows(one[...])
+        for i in range(3):
+            right = joined[:, i * D : (i + 1) * D]
+            panel(t, i * 192, left, right)
+            note(t, 1 + i, right)
+        sums = norms[0:16, :].astype(F32)
+        for i in range(1, 4):
+            sums = sums + norms[i * 16 : (i + 1) * 16, :].astype(F32)
+        small[1 - t, 8:16, :] = sums[:8]
+
+    def set_out(t):
+        for db in order:
+            first[t, db] = wire.push(chunk(t, 2, db), far.at[t, db], place.near(t, 0, way[db]))
+        for db in order:
             loose[t, db] = wire.push(
-                ins[t].at[chunk(t, -way[db], db)], near.at[t, db, 1], place.near(t, 0, -way[db])
-            )
+                chunk(t, -way[db], db), near.at[t, db, 1], place.near(t, 0, -way[db])
+            )
+
+    work = [
+        share_rows(place, wire, joined_ref, joined_land),
+        share_rows(place, wire, norm_ref, norm_land),
+    ]
+    early_grads(0, 0)
+    late_grads(0, take(5), take(6), norm_one)
+    set_out(0)
+    for steps, _ in work:
+        for step in steps:
+            step()
+    early_grads(1, 7)
+    for _, last in work:
+        for copy in last:
+            copy.wait_recv()
+    for copy in wire.local:
+        copy.wait()
+    settled = len(wire.local)
+    late_grads(1, take(12), joined_land, norm_land)
+    set_out(1)
+    step_numbers, waited = [len(wire.sent)], set()
+    wire.push(small, heard.at[0], turns[0])
     for db in order:
         for t in (0, 1):
             first[t, db].wait_recv()
-            mix[t, db] = plus(ins[t][chunk(t, way[db], db)], far[t, db])
+            mix[t, db] = plus(chunk(t, way[db], db)[...], far[t, db])
             second[t, db] = wire.push(mix.at[t, db], near.at[t, db, 0], place.near(t, 0, way[db]))
 
     def hear(step):
@@ -662,12 +700,10 @@
             step_numbers.append(len(wire.sent))
             wire.push(small, heard.at[step + 1], turns[step + 1])
 
-    step_numbers, waited = [0], set()
-
     def settle(t, db):
         second[t, db].wait_recv()
         loose[t, db].wait_recv()
-        total[t, db] = plus(ins[t][chunk(t, 0, db)], near[t, db, 0], near[t, db, 1])
+        total[t, db] = plus(chunk(t, 0, db)[...], near[t, db, 0], near[t, db, 1])
 
     third, fourth = {}, {}
     for t in (0, 1):
@@ -728,22 +764,29 @@
     for number, copy in enumerate(wire.sent):
         if number not in waited:
             copy.wait_send()
-    for copy in wire.local:
+    for copy in wire.local[settled:]:
         copy.wait()
 
 
-def sum_over_ctx(one, two, small_one, small_two):
+def sum_over_ctx(joined, norms, norms_one, arrays):
     shape = (16, PIECE, D)
-    small_shape = (2,) + small_one.shape
+    small_shape = (LAYERS, 16, D)
+    tokens = 4 * BLOCK
     return pl.pallas_call(
         sum_kernel,
         out_shape=(
             jax.ShapeDtypeStruct((2,) + shape, BF),
             jax.ShapeDtypeStruct(small_shape, F32),
         ),
-        in_specs=[VM] * 4,
+        in_specs=[VM] * 3 + [ANY] * LOADS,
         out_specs=(ANY, VM),
-        scratch_shapes=[
+        scratch_shapes=[room(*array.shape) for array in arrays]
+        + [
+            room(2, 16 * PIECE, D),
+            room(tokens, 3 * D),
+            room(64, D),
+            room(D, tokens),
+            pltpu.SemaphoreType.DMA((LOADS,)),
             room(2, 4, PIECE, D),
             room(2, 4, PIECE, D),
             room(2, 4, 2, PIECE, D),
@@ -762,57 +805,7 @@
             collective_id=6, has_side_effects=True, vmem_limit_bytes=60 * 2**20
         ),
         name="sum_over_ctx",
-    )(one.reshape(shape), two.reshape(shape), small_one, small_two)
-
-
-def weight_kernel(
-    fsdp_ref, one_ref, mixed_ref, two_ref, hidden_ref, joined_ref, low_ref, pre_ref, norm_ref,
-    rows_ref, sums_ref, turned, turned_hidden,
-):
-    start = pl.multiple_of(fsdp_ref[0] * 192, 64)
-    lefts = []
-    for i, ref in enumerate((one_ref, mixed_ref, two_ref)):
-        turned[i] = jnp.transpose(ref[...])
-        lefts.append(turned[i, pl.ds(start, 192), :])
-    turned_hidden[...] = jnp.transpose(hidden_ref[...])
-    ones = jnp.ones((8, low_ref.shape[0]), BF)
-
-    def panel(first, left, right, line):
-        rows = left.shape[0]
-        rows_ref[first : first + rows, :] = contract(left, right, ((1,), (0,))).astype(BF)
-        if line is not None:
-            sums_ref[line : line + 1, :] = contract(ones, right, ((1,), (0,)))[:1]
-
-    low = low_ref[...]
-    panel(1536, turned_hidden[...], low, None)
-    panel(576, lefts[1], low, 0)
-    for i in range(3):
-        panel(i * 192, lefts[0], joined_ref[:, i * D : (i + 1) * D], 1 + i)
-    for i in range(4):
-        panel(768 + i * 192, lefts[2], pre_ref[:, i * D : (i + 1) * D], 4 + i)
-    norms = norm_ref[0:16, :].astype(F32)
-    for i in range(1, 4):
-        norms = norms + norm_ref[i * 16 : (i + 1) * 16, :].astype(F32)
-    sums_ref[8:16, :] = norms[:8]
-
-
-def weight_grads(fsdp, one, mixed, two, hidden, joined, low, pre, norms):
-    tokens = one.shape[0]
-    return pl.pallas_call(
-        weight_kernel,
-        out_shape=(
-            jax.ShapeDtypeStruct((2304, D), BF),
-            jax.ShapeDtypeStruct((16, D), F32),
-        ),
-        in_specs=[SM] + [VM] * 8,
-        out_specs=(VM, VM),
-        scratch_shapes=[room(3, D, tokens), room(D, tokens)],
-        compiler_params=pltpu.CompilerParams(vmem_limit_bytes=60 * 2**20),
-        cost_estimate=pl.CostEstimate(
-            flops=2 * 512 * 1769472, bytes_accessed=12 * 2**20, transcendentals=0
-        ),
-        name="weight_grads",
-    )(fsdp, one, mixed, two, hidden, joined, low, pre, norms)
+    )(joined, norms, norms_one, *arrays)
 
 
 def pair_rows(values):
@@ -1282,7 +1275,7 @@
         unpack_kernel,
         grid=(LAYERS,),
         out_shape=tuple(jax.ShapeDtypeStruct((LAYERS,) + shape, F32) for shape in shapes),
-        in_specs=[pl.BlockSpec((1, 2304, D), lambda i: (i, 0, 0))],
+        in_specs=[pl.BlockSpec((1, 2304, D), lambda i: (LAYERS - 1 - i, 0, 0))],
         out_specs=tuple(pl.BlockSpec((1,) + shape, lambda i: (i, 0, 0)) for shape in shapes),
         compiler_params=pltpu.CompilerParams(vmem_limit_bytes=60 * 2**20),
         name="unpack",
@@ -1484,16 +1477,14 @@
         waiting = (grad_joined, norm_sums)
         if going_on:
             grad_low, grad_own, grad_away = outs
-    late_rows[0] = gather_late(*waiting)
-    fsdp_word = fsdp.astype(jnp.int32).reshape(1)
-    packs, lines = [], []
-    for layer_index in range(LAYERS):
+    arrays = []
+    for layer_index in (1, 0):
         hidden, one, mixed, two, low, pre = early_rows[layer_index]
-        joined, norms = late_rows[layer_index]
-        rows, sums = weight_grads(fsdp_word, one, mixed, two, hidden, joined, low, pre, norms)
-        packs.append(rows)
-        lines.append(sums)
-    summed, small = sum_over_ctx(*packs, *lines)
+        arrays += [low, mixed, hidden, two, pre, one]
+        if layer_index == 1:
+            joined_one, norms_one = late_rows[1]
+            arrays.append(joined_one)
+    summed, small = sum_over_ctx(*waiting, norms_one, arrays)
 
     def own_part(vectors, width):
         return lax.dynamic_slice_in_dim(vectors, fsdp * width, width, vectors.ndim - 1)

time: 530 us -> 504 us (0.951)
  Pallas kernels: 486 us -> 459 us
    pallas_call x3 -> x0, Pallas kernels: 30.5 us -> none  [the longest x2 17.2 us: weight_grads(): pl.pallas_call(weight_kernel, out_shape=(jax.ShapeDtypeStruct((2304, D),...]
where the time goes in v7:
time: 504 us; the launch traced here: 495 us
  Pallas kernels  459 us (91%)
  starting transfers between devices  15.5 us (3%)
  local copies, waits for them, and re-layouts  10.2 us (2%)
  waiting for transfers between devices  7.1 us (1%)
    pallas_call x2, Pallas kernels, scatter_pair(): pl.pallas_call(functools.partial(scatter_kernel, len(sources)), out_shape...  111 us
    pallas_call x2, Pallas kernels, gather_pair(): pl.pallas_call(functools.partial(gather_kernel, layers), out_shape=(jax.S...  107 us
    pallas_call x1, Pallas kernels, sum_over_ctx(): pl.pallas_call(sum_kernel, out_shape=(jax.ShapeDtypeStruct((2,) + shape,...  104 us
    pallas_call x8, Pallas kernels, dense(): pl.pallas_call(kernel, out_shape=shapes, in_specs=specs, out_specs=(VM,)...  43 us
    pallas_call x2, Pallas kernels, attend_backward(): pl.pallas_call(backward_kernel, out_shape=(jax.ShapeDtypeStruct((BLOCK, H...  33.5 us
    pallas_call x2, Pallas kernels, attend_forward(): pl.pallas_call(forward_kernel, out_shape=(jax.ShapeDtypeStruct((BLOCK, HA...  32.5 us
    pallas_call x1, Pallas kernels, gather_first(): pl.pallas_call(first_kernel, out_shape=(full_shape(weight), jax.ShapeDtyp...  19.1 us
    ppermute x4, starting transfers between devices, mirrored(): return lax.ppermute(values, ('fsdp', 'ctx'), pairs)  15.5 us
  transfers between devices with their start and end apart: 4, of which 2 were waited for; matrix products, arithmetic and copies ran while one was open for 0% of the time, Pallas kernels for 4%

profile of v7, /device:TPU:0, one launch (start us, length us, event | category | flops | bytes accessed | tf_op | source)
XLA Modules:
  0.0 495.0 jit_solution(17549781992357004950)
XLA Ops:
  0.7 0.9 concatenate.3
  1.6 0.6 pad_convert_fusion.vector_ref
  2.2 19.1 %gather_first.1 = (bf16[768,2304]{1,0:T(8,128)(2,1)}, f32[4,8,2560]{2,1,0:T(8,128)}) custom-call(bf16[2,192,2304]{2,1,0:T(8,128)(2,1)} %refs_3_.1, f32[8,2560]{1,0:T(8,128)} %pad_convert_fusion.vector_ref), custom_call_target="tpu_custom_call" | custom-call | tf_op jit(solution)/shard_map/gather_first/pallas_call | solution.py:317
  21.4 1.7 order_vectors.1
  23.1 1.0 fusion.8
  24.1 4.7 enter.1
  28.8 60.3 %gather_pair_0.1 = (bf16[128,384]{1,0:T(8,128)(2,1)}, bf16[32,128,384]{2,1,0:T(8,128)(2,1)}, bf16[32,128,384]{2,1,0:T(8,128)(2,1)}, bf16[768,768]{1,0:T(8,128)(2...) custom-call(bf16[128,384]{1,0:T(8,128)(2,1)} %get-tuple-element.117.q_ref, ...), custom_call_target="tpu_custom_call" | custom-call | tf_op jit(solution)/shard_map/gather_pair_0/pallas_call | solution.py:388
  89.2 16.3 %attend_forward.2 = (bf16[128,384]{1,0:T(8,128)(2,1)}, bf16[128,384]{1,0:T(8,128)(2,1)}, f32[384,256]{1,0:T(8,128)}, f32[8,256]{1,0:T(8,128)}) custom-call(s32[1]{0:T(128)} %bitcast.2.ctx_ref, bf16[128,384]{1,0:T(8,128)(2,1)} %get-tuple-element.116.q_own, bf16[128,384]{1,0:T(8,128)(2,1)} %get-tuple-element.122.q_away, bf16[4096,384]{1,0:T(8,128)(2,1)} %bitcast.41, ...), custom_call_target="tpu_custom_call" | custom-call | flops 1660944384 | bytes 8388608 | tf_op jit(solution)/shard_map/attend_forward/pallas_call | solution.py:936
  105.4 3.1 collective-permute-start
  108.5 7.0 %mlp.2 = (f32[128,3072]{1,0:T(8,128)}, bf16[128,3072]{1,0:T(8,128)(2,1)}, f32[128,768]{1,0:T(8,128)}) custom-call(bf16[128,768]{1,0:T(8,128)(2,1)} %get-tuple-element.128.two_ref.refs_2_, bf16[768,3072]{1,0:T(8,128)(2,1)} %get-tuple-element.129.up_ref, bf16[3072,768]{1,0:T(8,128)(2,1)} %get-tuple-element.130.down_ref, f32[16,768]{1,0:T(8,128)} %get-tuple-element.114.vec_ref), custom_call_target="tpu_custom_call" | custom-call | flops 1207959552 | bytes 9437184 | tf_op jit(solution)/shard_map/mlp/pallas_call | solution.py:1290
  115.5 1.1 collective-permute-done.away_ref
  116.6 0.0 copy-start.1
  116.6 0.6 copy-done.1
  117.3 6.3 %pass_on.1 = (bf16[128,768]{1,0:T(8,128)(2,1)}, f32[128,768]{1,0:T(8,128)}, bf16[128,768]{1,0:T(8,128)(2,1)}, bf16[128,768]{1,0:T(8,128)(2,1)}, bf16[128,384]{1,...) custom-call(s32[1]{0:T(128)} %bitcast.upper_ref, ...), custom_call_target="tpu_custom_call" | custom-call | flops 603979776 | bytes 4718592 | tf_op jit(solution)/shard_map/pass_on/pallas_call | solution.py:1290
  123.5 46.5 %gather_pair_1.1 = (bf16[128,384]{1,0:T(8,128)(2,1)}, bf16[32,128,384]{2,1,0:T(8,128)(2,1)}, bf16[32,128,384]{2,1,0:T(8,128)(2,1)}, bf16[768,768]{1,0:T(8,128)(2...) custom-call(bf16[128,384]{1,0:T(8,128)(2,1)} %get-tuple-element.136.q_ref, ...), custom_call_target="tpu_custom_call" | custom-call | tf_op jit(solution)/shard_map/gather_pair_1/pallas_call | solution.py:388
  170.0 16.3 %attend_forward.3 = (bf16[128,384]{1,0:T(8,128)(2,1)}, bf16[128,384]{1,0:T(8,128)(2,1)}, f32[384,256]{1,0:T(8,128)}, f32[8,256]{1,0:T(8,128)}) custom-call(s32[1]{0:T(128)} %bitcast.2.ctx_ref, bf16[128,384]{1,0:T(8,128)(2,1)} %get-tuple-element.135.q_own, bf16[128,384]{1,0:T(8,128)(2,1)} %get-tuple-element.141.q_away, bf16[4096,384]{1,0:T(8,128)(2,1)} %bitcast.45, ...), custom_call_target="tpu_custom_call" | custom-call | flops 1660944384 | bytes 8388608 | tf_op jit(solution)/shard_map/attend_forward/pallas_call | solution.py:936
  186.3 3.8 collective-permute-start.1
  190.1 2.7 back.1
  192.8 4.1 collective-permute-start.2
  196.8 7.0 %mlp.3 = (f32[128,3072]{1,0:T(8,128)}, bf16[128,3072]{1,0:T(8,128)(2,1)}, f32[128,768]{1,0:T(8,128)}) custom-call(bf16[128,768]{1,0:T(8,128)(2,1)} %get-tuple-element.147.two_ref.refs_2_, bf16[768,3072]{1,0:T(8,128)(2,1)} %get-tuple-element.148.up_ref, bf16[3072,768]{1,0:T(8,128)(2,1)} %get-tuple-element.149.down_ref, ...), custom_call_target="tpu_custom_call" | custom-call | flops 1207959552 | bytes 9437184 | tf_op jit(solution)/shard_map/mlp/pallas_call | solution.py:1290
  203.8 0.0 collective-permute-done.1.away_ref
  203.8 0.0 copy-start
  203.8 0.6 copy-done
  204.4 2.6 last.1
  207.0 0.0 collective-permute-done.2.g_away
  207.0 0.0 copy-start.4
  207.0 0.6 copy-done.4
  207.7 16.8 %attend_backward.2 = (f32[128,384]{1,0:T(8,128)}, bf16[128,384]{1,0:T(8,128)(2,1)}, bf16[4096,384]{1,0:T(8,128)(2,1)}, bf16[4096,384]{1,0:T(8,128)(2,1)}) custom-call(s32[1]{0:T(128)} %bitcast.2.ctx_ref, bf16[128,384]{1,0:T(8,128)(2,1)} %get-tuple-element.135.q_own, bf16[128,384]{1,0:T(8,128)(2,1)} %get-tuple-element.141.q_away, bf16[4096,384]{1,0:T(8,128)(2,1)} %bitcast.46, ...), custom_call_target="tpu_custom_call" | custom-call | flops 4152360960 | bytes 16777216 | tf_op jit(solution)/shard_map/attend_backward/pallas_call | solution.py:1033
  224.5 55.1 %scatter_pair_1.1 = (f32[2,128,384]{2,1,0:T(8,128)}, f32[128,768]{1,0:T(8,128)}, bf16[2,128,384]{2,1,0:T(8,128)(2,1)}, bf16[128,384]{1,0:T(8,128)(2,1)}, bf16[51...) custom-call(bf16[32,128,384]{2,1,0:T(8,128)(2,1)} %bitcast.39, ...), custom_call_target="tpu_custom_call" | custom-call | tf_op jit(solution)/shard_map/scatter_pair_1/pallas_call | solution.py:539
  279.6 7.2 %join_1.1 = (bf16[128,2304]{1,0:T(8,128)(2,1)}, bf16[16,768]{1,0:T(8,128)(2,1)}, f32[128,768]{1,0:T(8,128)}, bf16[128,768]{1,0:T(8,128)(2,1)}, bf16[128,384]{1,0:T(8,128)(2,1)}, /*index=5*/bf16[128,384]{1,0:T(8,128)(2,1)}) custom-call(s32[1]{0:T(128)} %bitcast.upper_ref, f32[2,128,384]{2,1,0:T(8,128)} %get-tuple-element.164.own_ref, ...), custom_call_target="tpu_custom_call" | custom-call | flops 452984832 | bytes 3538944 | tf_op jit(solution)/shard_map/join_1/pallas_call | solution.py:1290
  286.8 4.6 collective-permute-start.3
  291.4 6.0 %collective-permute-done.3.g_away = bf16[128,384]{1,0:T(8,128)(2,1)S(1)} collective-permute-done((bf16[128,384]{1,0:T(8,128)(2,1)}, bf16[128,384]{1,0:T(8,128)(2,1)S(1)}, u32[]{:S(2)}, u32[]{:S(2)}) %collective-permute-start.3) | collective-permute-done | bytes 98336 | tf_op jit(solution)/shard_map/ppermute | solution.py:31
  297.4 0.0 copy-start.3
  297.4 0.6 copy-done.3
  298.0 16.7 %attend_backward.3 = (f32[128,384]{1,0:T(8,128)}, bf16[128,384]{1,0:T(8,128)(2,1)}, bf16[4096,384]{1,0:T(8,128)(2,1)}, bf16[4096,384]{1,0:T(8,128)(2,1)}) custom-call(s32[1]{0:T(128)} %bitcast.2.ctx_ref, bf16[128,384]{1,0:T(8,128)(2,1)} %get-tuple-element.116.q_own, bf16[128,384]{1,0:T(8,128)(2,1)} %get-tuple-element.122.q_away, bf16[4096,384]{1,0:T(8,128)(2,1)} %bitcast.42, ...), custom_call_target="tpu_custom_call" | custom-call | flops 4152360960 | bytes 16777216 | tf_op jit(solution)/shard_map/attend_backward/pallas_call | solution.py:1033
  314.7 55.7 %scatter_pair_0.1 = (f32[2,128,384]{2,1,0:T(8,128)}, f32[128,768]{1,0:T(8,128)}, bf16[2,128,384]{2,1,0:T(8,128)(2,1)}, bf16[128,384]{1,0:T(8,128)(2,1)}, bf16[51...) custom-call(bf16[32,128,384]{2,1,0:T(8,128)(2,1)} %bitcast.37, ...), custom_call_target="tpu_custom_call" | custom-call | tf_op jit(solution)/shard_map/scatter_pair_0/pallas_call | solution.py:539
  370.4 5.5 %join_0.1 = (bf16[128,2304]{1,0:T(8,128)(2,1)}, bf16[16,768]{1,0:T(8,128)(2,1)}, f32[128,768]{1,0:T(8,128)}) custom-call(s32[1]{0:T(128)} %bitcast.upper_ref, f32[2,128,384]{2,1,0:T(8,128)} %get-tuple-element.183.own_ref, bf16[2,128,384]{2,1,0:T(8,128)(2,1)} %get-tuple-element.184.back_ref, f32[128,384]{1,0:T(8,128)} %get-tuple-element.185.own_q, ...), custom_call_target="tpu_custom_call" | custom-call | flops 452984832 | bytes 3538944 | tf_op jit(solution)/shard_map/join_0/pallas_call | solution.py:1290
  375.9 104.3 %sum_over_ctx.1 = (bf16[2,16,144,768]{3,2,1,0:T(8,128)(2,1)}, f32[2,16,768]{2,1,0:T(8,128)}) custom-call(bf16[128,2304]{1,0:T(8,128)(2,1)} %get-tuple-element.190.joined_ref, bf16[16,768]{1,0:T(8,128)(2,1)} %get-tuple-element.191.norm_ref, bf16[64,768]{1,0:T(8,128)(2,1)} %get-tuple-element.192.norm_one, bf16[512,768]{1,0:T(8,128)(2,1)} %get-tuple-element.193.refs_0_, ...), custom_call_target="tpu_custom_call" | custom-call | tf_op jit(solution)/shard_map/sum_over_ctx/pallas_call | solution.py:775
  480.3 0.8 slice_bitcast_fusion
  481.1 0.8 slice_bitcast_fusion.1
  481.9 0.8 slice.30
  482.7 0.1 constant_dynamic-slice_fusion.6
  482.8 0.6 copy.44
  483.4 0.6 copy.43
  484.0 0.6 copy.42
  484.6 0.6 copy.41
  485.1 7.4 %unpack.1 = (f32[2,192,2304]{2,1,0:T(8,128)}, f32[2,192,768]{2,1,0:T(8,128)}, f32[2,192,3072]{2,1,0:T(8,128)}, f32[2,768,768]{2,1,0:T(8,128)}) custom-call(bf16[2,2304,768]{2,1,0:T(8,128)(2,1)} %bitcast.36), custom_call_target="tpu_custom_call" | custom-call | tf_op jit(solution)/shard_map/unpack/pallas_call | solution.py:1274
  492.6 0.1 constant_dynamic-slice_fusion.4
  492.7 0.0 copy-start.2
  492.7 0.7 constant_dynamic-slice_fusion.5
  493.4 0.6 constant_dynamic-slice_fusion.3
  494.0 0.6 copy.46
  494.5 0.0 copy-done.2
  (6 shorter events, 0.0 us)
Async XLA Ops:
  105.4 11.2 %collective-permute-start = (bf16[128,384]{1,0:T(8,128)(2,1)}, bf16[128,384]{1,0:T(8,128)(2,1)S(1)}, u32[]{:S(2)}, u32[]{:S(2)}) collective-permute-start(bf16[128,384]{1,0:T(8,128)(2,1)} %get-tuple-element.126), channel_id=1, source_target_pairs={{0,31},{1,30},{2,29},{3,28},{4,27},{5,26},{6,25},{7,24},{8,23},{9,... | collective-permute-start | bytes 294920 | tf_op jit(solution)/shard_map/ppermute | solution.py:31
  116.6 0.6 copy-start.1
  186.3 17.5 %collective-permute-start.1 = (bf16[128,384]{1,0:T(8,128)(2,1)}, bf16[128,384]{1,0:T(8,128)(2,1)S(1)}, u32[]{:S(2)}, u32[]{:S(2)}) collective-permute-start(bf16[128,384]{1,0:T(8,128)(2,1)} %get-tuple-element.145), channel_id=1, source_target_pairs={{0,31},{1,30},{2,29},{3,28},{4,27},{5,26},{6,25},{7,24},{8,23},{9,... | collective-permute-start | bytes 294920 | tf_op jit(solution)/shard_map/ppermute | solution.py:31
  192.8 14.3 %collective-permute-start.2 = (bf16[128,384]{1,0:T(8,128)(2,1)}, bf16[128,384]{1,0:T(8,128)(2,1)S(1)}, u32[]{:S(2)}, u32[]{:S(2)}) collective-permute-start(bf16[128,384]{1,0:T(8,128)(2,1)} %get-tuple-element.153), channel_id=1, source_target_pairs={{0,31},{1,30},{2,29},{3,28},{4,27},{5,26},{6,25},{7,24},{8,23},{9,... | collective-permute-start | bytes 294920 | tf_op jit(solution)/shard_map/ppermute | solution.py:31
  203.8 0.6 copy-start
  207.0 0.6 copy-start.4
  286.8 10.6 %collective-permute-start.3 = (bf16[128,384]{1,0:T(8,128)(2,1)}, bf16[128,384]{1,0:T(8,128)(2,1)S(1)}, u32[]{:S(2)}, u32[]{:S(2)}) collective-permute-start(bf16[128,384]{1,0:T(8,128)(2,1)} %get-tuple-element.170), channel_id=1, source_target_pairs={{0,31},{1,30},{2,29},{3,28},{4,27},{5,26},{6,25},{7,24},{8,23},{9,... | collective-permute-start | bytes 294920 | tf_op jit(solution)/shard_map/ppermute | solution.py:31
  297.4 0.6 copy-start.3
  492.7 1.9 copy-start.2

commit v8 on v7

--- a/solution.py
+++ b/solution.py
@@ -399,10 +399,15 @@
     )(*away, *own, *weights)
 
 
-def scatter_kernel(count, gk_ref, gv_ref, gq_ref, hidden_ref, pre_ref, up_ref, down_ref, *refs):
+def scatter_kernel(
+    count, forward, gk_ref, gv_ref, gq_ref, hidden_ref, pre_ref, up_ref, down_ref, *refs
+):
     sources, refs = refs[:count], refs[count:]
     own_out, norm_out, back_out, back_q, hidden_out, grad_pre_out = refs[:6]
     targets, refs = refs[6 : 6 + count], refs[6 + count :]
+    if forward:
+        vec_ref, two_ref = hidden_ref, pre_ref
+        (mlp_out, hidden_ref, pre_ref), refs = (refs[0], *refs[-2:]), refs[1:-2]
     far, near, mix, total, last_far, last_near, last_mix, leave, stage = refs[:9]
     up_buffer, down_buffer, grad_pre, load_sem = refs[9:13]
     place, wire = Place(), Wire(*refs[13:])
@@ -416,6 +421,13 @@
             load = pltpu.make_async_copy(source, buffer, load_sem.at[len(loads)])
             load.start()
             loads.append(load)
+    loaded = set()
+
+    def ready(number):
+        if number not in loaded:
+            loads[number].wait()
+            loaded.add(number)
+
     place.greet(
         place.around() + [place.mirror, place.beside, place.along_x(1), place.along_x(3)]
     )
@@ -441,12 +453,25 @@
                 near.at[t, da, 1, b],
                 place.near(t, 1, -way[b]),
             )
-    work = [share_columns(place, wire, hidden_ref, hidden_out, stage)]
+    work = [] if forward else [share_columns(place, wire, hidden_ref, hidden_out, stage)]
     for source, target in zip(sources, targets):
         work.append(share_rows(place, wire, source, target))
     for b in (1, 0):
         if b == 0:
-            mlp_back(sources[3][...], pre_ref, loads, up_buffer, down_buffer, grad_pre, norm_out)
+            if forward:
+                two = two_ref[...]
+                for i in range(FF // D):
+                    cols = slice(i * D, (i + 1) * D)
+                    ready(2 * i + 1)
+                    pre = contract(two, up_buffer[i], ((1,), (0,))) + line(vec_ref, BIAS_UP + i)
+                    pre_ref[:, cols] = pre
+                    hidden = (pre * phi_parts(pre)[0]).astype(BF)
+                    hidden_ref[:, cols] = hidden
+                    ready(2 * i)
+                    fresh = contract(hidden, down_buffer[cols, :], ((1,), (0,)))
+                    mlp_out[...] = fresh if i == 0 else mlp_out[...] + fresh
+                work.append(share_columns(place, wire, hidden_ref, hidden_out, stage))
+            mlp_back(sources[3][...], pre_ref, ready, up_buffer, down_buffer, grad_pre, norm_out)
             work.append(share_rows(place, wire, grad_pre, grad_pre_out))
         for da, t in order:
             first[t, da, b].wait_recv()
@@ -521,23 +546,25 @@
     return jax.ShapeDtypeStruct((4 * source.shape[0], source.shape[1]), BF)
 
 
-def mlp_back(low, pre_ref, loads, up_buffer, down_buffer, grad_pre_ref, norm_ref):
+def mlp_back(low, pre_ref, ready, up_buffer, down_buffer, grad_pre_ref, norm_ref):
     for i in range(FF // D):
         cols = slice(i * D, (i + 1) * D)
         pre = pre_ref[:, cols]
         cumulative, density = phi_parts(pre)
-        loads[2 * i].wait()
+        ready(2 * i)
         hidden = contract(low, down_buffer[cols, :], ((1,), (1,)))
         grad_pre = (hidden * (cumulative + pre * density)).astype(BF)
         grad_pre_ref[:, cols] = grad_pre
-        loads[2 * i + 1].wait()
+        ready(2 * i + 1)
         fresh = contract(grad_pre, up_buffer[i], ((1,), (1,)))
         norm_ref[...] = fresh if i == 0 else norm_ref[...] + fresh
 
 
-def scatter_pair(name, number, grad_keys, grad_values, away, hidden, pre, up, down, sources):
+def scatter_pair(
+    name, number, forward, grad_keys, grad_values, away, hidden, pre, up, down, sources
+):
     return pl.pallas_call(
-        functools.partial(scatter_kernel, len(sources)),
+        functools.partial(scatter_kernel, len(sources), forward),
         out_shape=(
             jax.ShapeDtypeStruct((2, BLOCK, HALF), F32),
             jax.ShapeDtypeStruct((BLOCK, D), F32),
@@ -546,9 +573,10 @@
             jax.ShapeDtypeStruct((4 * BLOCK, D), BF),
             jax.ShapeDtypeStruct((4 * BLOCK, FF), BF),
         )
-        + tuple(rows_shape(source) for source in sources),
+        + tuple(rows_shape(source) for source in sources)
+        + ((jax.ShapeDtypeStruct((BLOCK, D), F32),) if forward else ()),
         in_specs=[VM] * 5 + [ANY] * 2 + [VM] * len(sources),
-        out_specs=(VM, VM) + (ANY,) * (4 + len(sources)),
+        out_specs=(VM, VM) + (ANY,) * (4 + len(sources)) + ((VM,) if forward else ()),
         scratch_shapes=[
             room(2, 4, 2, BLOCK, HALF),
             room(2, 4, 2, 2, BLOCK, HALF),
@@ -564,7 +592,8 @@
             room(BLOCK, FF),
             pltpu.SemaphoreType.DMA((2 * FF // D,)),
         ]
-        + sems(128, 12),
+        + sems(128, 12)
+        + ([room(BLOCK, FF), pltpu.VMEM((BLOCK, FF), F32)] if forward else []),
         compiler_params=pltpu.CompilerParams(
             collective_id=number, has_side_effects=True, vmem_limit_bytes=60 * 2**20
         ),
@@ -1197,11 +1226,17 @@
     enter(upper_ref, stream, next_vec_ref, weight_ref, table_ref, *outs)
 
 
-def last_kernel(
-    upper_ref, stream_ref, own_ref, away_ref, out_ref, mlp_ref, vec_ref, mixed_ref, next_ref
-):
-    next_ref[...] = leave(
-        upper_ref, stream_ref, own_ref, away_ref, out_ref, mlp_ref, vec_ref, mixed_ref
+def mixed_kernel(upper_ref, own_ref, away_ref, mixed_ref):
+    put_joined(upper_ref, own_ref[...], away_ref[...], mixed_ref, 0)
+
+
+def last_kernel(stream_ref, mixed_ref, weight_ref, mlp_ref, vec_ref, next_ref):
+    next_ref[...] = (
+        stream_ref[...].astype(F32)
+        + contract(mixed_ref[...], weight_ref[...], ((1,), (0,)))
+        + line(vec_ref, BIAS_OUT)
+        + mlp_ref[...]
+        + line(vec_ref, BIAS_DOWN)
     ).astype(BF)
 
 
@@ -1388,28 +1423,35 @@
             ctx_word, q_own, q_other, keys, values
         )
         mixed_back = mirrored(mixed_away)
-        hidden_pre, hidden_low, mlp_branch = dense(
-            "mlp",
-            mlp_kernel,
-            [VM] * 4,
-            ((FF, F32), (FF, BF), (D, F32)),
-            (norm_two, w_up, w_down, vecs[layer_index]),
-            2 * D * FF,
-        )
+        if layer_index + 1 < LAYERS:
+            hidden_pre, hidden_low, mlp_branch = dense(
+                "mlp",
+                mlp_kernel,
+                [VM] * 4,
+                ((FF, F32), (FF, BF), (D, F32)),
+                (norm_two, w_up, w_down, vecs[layer_index]),
+                2 * D * FF,
+            )
         before = stream
-        common = (upper, stream, mixed_own, mixed_back, w_out, mlp_branch, vecs[layer_index])
+        common = (upper, stream, mixed_own, mixed_back, w_out)
         if more:
             mixed_low, stream, *entered = dense(
                 "pass_on",
                 pass_kernel,
                 [SM] + [VM] * 11,
                 ((D, BF), (D, F32)) + ENTER_OUTS,
-                common + (vecs[layer_index + 1], more[0], *tables),
+                common + (mlp_branch, vecs[layer_index], vecs[layer_index + 1], more[0], *tables),
                 D * 4 * D,
             )
         else:
-            mixed_low, output = dense(
-                "last", last_kernel, [SM] + [VM] * 6, ((D, BF), (D, BF)), common, D * D
+            hidden_low, hidden_pre = vecs[layer_index], norm_two
+            (mixed_low,) = dense(
+                "mixed",
+                mixed_kernel,
+                [SM] + [VM] * 2,
+                ((D, BF),),
+                (upper, mixed_own, mixed_back),
+                0,
             )
         lefts = (norm_one, mixed_low, norm_two)
         saved.append(
@@ -1439,6 +1481,7 @@
         own_pair, grad_norm_two, back_pair, back_query, hidden, pre, *gathered_rows = scatter_pair(
             "scatter_pair_%d" % layer_index,
             3 + layer_index,
+            layer_index == LAYERS - 1,
             grad_keys.reshape(whole),
             grad_values.reshape(whole),
             gq_away,
@@ -1451,6 +1494,15 @@
         early_rows[layer_index] = (hidden, *gathered_rows[:4], pre)
         if waiting:
             late_rows[layer_index + 1] = gathered_rows[4:]
+        else:
+            (output,) = dense(
+                "last",
+                last_kernel,
+                [VM] * 5,
+                ((D, BF),),
+                (before, lefts[1], w_out, gathered_rows[4], vecs[layer_index]),
+                D * D,
+            )
         going_on = layer_index > 0
         grad_joined, norm_sums, gradient, *outs = dense(
             "join_%d" % layer_index,

time: 504 us -> 500 us (level)
    pallas_call x8, Pallas kernels: 43 us -> 37.6 us  [dense(): pl.pallas_call(kernel, out_shape=shapes, in_specs=specs, out_specs=(VM,)...]
  transfers between devices with their start and end apart: 4 -> 4, of which waited for: 2 -> 4; matrix products, arithmetic and copies ran while one was open for 0% -> 0% of each run, Pallas kernels for 4% -> 3%
where the time goes in v8:
time: 500 us; the launch traced here: 491 us
  Pallas kernels  454 us (91%)
  starting transfers between devices  17.2 us (3%)
  local copies, waits for them, and re-layouts  10.3 us (2%)
  waiting for transfers between devices  7.04 us (1%)
    pallas_call x2, Pallas kernels, scatter_pair(): pl.pallas_call(functools.partial(scatter_kernel, len(sources), forward),...  110 us
    pallas_call x2, Pallas kernels, gather_pair(): pl.pallas_call(functools.partial(gather_kernel, layers), out_shape=(jax.S...  107 us
    pallas_call x1, Pallas kernels, sum_over_ctx(): pl.pallas_call(sum_kernel, out_shape=(jax.ShapeDtypeStruct((2,) + shape,...  105 us
    pallas_call x8, Pallas kernels, dense(): pl.pallas_call(kernel, out_shape=shapes, in_specs=specs, out_specs=(VM,)...  37.6 us
    pallas_call x2, Pallas kernels, attend_backward(): pl.pallas_call(backward_kernel, out_shape=(jax.ShapeDtypeStruct((BLOCK, H...  33.5 us
    pallas_call x2, Pallas kernels, attend_forward(): pl.pallas_call(forward_kernel, out_shape=(jax.ShapeDtypeStruct((BLOCK, HA...  32.5 us
    pallas_call x1, Pallas kernels, gather_first(): pl.pallas_call(first_kernel, out_shape=(full_shape(weight), jax.ShapeDtyp...  19.1 us
    ppermute x4, starting transfers between devices, mirrored(): return lax.ppermute(values, ('fsdp', 'ctx'), pairs)  17.2 us
  transfers between devices with their start and end apart: 4, of which 4 were waited for; matrix products, arithmetic and copies ran while one was open for 0% of the time, Pallas kernels for 3%

profile of v8, /device:TPU:0, one launch (start us, length us, event | category | flops | bytes accessed | tf_op | source)
XLA Modules:
  0.0 491.5 jit_solution(11225313839303966733)
XLA Ops:
  0.7 0.9 concatenate.3
  1.6 0.6 pad_convert_fusion.vector_ref
  2.2 19.1 %gather_first.1 = (bf16[768,2304]{1,0:T(8,128)(2,1)}, f32[4,8,2560]{2,1,0:T(8,128)}) custom-call(bf16[2,192,2304]{2,1,0:T(8,128)(2,1)} %refs_3_.1, f32[8,2560]{1,0:T(8,128)} %pad_convert_fusion.vector_ref), custom_call_target="tpu_custom_call" | custom-call | tf_op jit(solution)/shard_map/gather_first/pallas_call | solution.py:317
  21.4 1.7 order_vectors.1
  23.1 1.0 fusion.8
  24.1 4.7 enter.1
  28.8 60.3 %gather_pair_0.1 = (bf16[128,384]{1,0:T(8,128)(2,1)}, bf16[32,128,384]{2,1,0:T(8,128)(2,1)}, bf16[32,128,384]{2,1,0:T(8,128)(2,1)}, bf16[768,768]{1,0:T(8,128)(2...) custom-call(bf16[128,384]{1,0:T(8,128)(2,1)} %get-tuple-element.113.q_ref, ...), custom_call_target="tpu_custom_call" | custom-call | tf_op jit(solution)/shard_map/gather_pair_0/pallas_call | solution.py:388
  89.2 16.2 %attend_forward.2 = (bf16[128,384]{1,0:T(8,128)(2,1)}, bf16[128,384]{1,0:T(8,128)(2,1)}, f32[384,256]{1,0:T(8,128)}, f32[8,256]{1,0:T(8,128)}) custom-call(s32[1]{0:T(128)} %bitcast.2.ctx_ref, bf16[128,384]{1,0:T(8,128)(2,1)} %get-tuple-element.112.q_own, bf16[128,384]{1,0:T(8,128)(2,1)} %get-tuple-element.118.q_away, bf16[4096,384]{1,0:T(8,128)(2,1)} %bitcast.41, ...), custom_call_target="tpu_custom_call" | custom-call | flops 1660944384 | bytes 8388608 | tf_op jit(solution)/shard_map/attend_forward/pallas_call | solution.py:965
  105.4 3.1 collective-permute-start
  108.6 7.0 %mlp.1 = (f32[128,3072]{1,0:T(8,128)}, bf16[128,3072]{1,0:T(8,128)(2,1)}, f32[128,768]{1,0:T(8,128)}) custom-call(bf16[128,768]{1,0:T(8,128)(2,1)} %get-tuple-element.124.two_ref.refs_2_, bf16[768,3072]{1,0:T(8,128)(2,1)} %get-tuple-element.125.up_ref, bf16[3072,768]{1,0:T(8,128)(2,1)} %get-tuple-element.126.down_ref, f32[16,768]{1,0:T(8,128)} %get-tuple-element.110.vec_ref), custom_call_target="tpu_custom_call" | custom-call | flops 1207959552 | bytes 9437184 | tf_op jit(solution)/shard_map/mlp/pallas_call | solution.py:1325
  115.5 1.1 collective-permute-done.away_ref
  116.7 0.0 copy-start.1
  116.7 0.6 copy-done.1
  117.3 6.2 %pass_on.1 = (bf16[128,768]{1,0:T(8,128)(2,1)}, f32[128,768]{1,0:T(8,128)}, bf16[128,768]{1,0:T(8,128)(2,1)}, bf16[128,768]{1,0:T(8,128)(2,1)}, bf16[128,384]{1,...) custom-call(s32[1]{0:T(128)} %bitcast.upper_ref, ...), custom_call_target="tpu_custom_call" | custom-call | flops 603979776 | bytes 4718592 | tf_op jit(solution)/shard_map/pass_on/pallas_call | solution.py:1325
  123.5 46.5 %gather_pair_1.1 = (bf16[128,384]{1,0:T(8,128)(2,1)}, bf16[32,128,384]{2,1,0:T(8,128)(2,1)}, bf16[32,128,384]{2,1,0:T(8,128)(2,1)}, bf16[768,768]{1,0:T(8,128)(2...) custom-call(bf16[128,384]{1,0:T(8,128)(2,1)} %get-tuple-element.132.q_ref, ...), custom_call_target="tpu_custom_call" | custom-call | tf_op jit(solution)/shard_map/gather_pair_1/pallas_call | solution.py:388
  169.9 16.3 %attend_forward.3 = (bf16[128,384]{1,0:T(8,128)(2,1)}, bf16[128,384]{1,0:T(8,128)(2,1)}, f32[384,256]{1,0:T(8,128)}, f32[8,256]{1,0:T(8,128)}) custom-call(s32[1]{0:T(128)} %bitcast.2.ctx_ref, bf16[128,384]{1,0:T(8,128)(2,1)} %get-tuple-element.131.q_own, bf16[128,384]{1,0:T(8,128)(2,1)} %get-tuple-element.137.q_away, bf16[4096,384]{1,0:T(8,128)(2,1)} %bitcast.45, ...), custom_call_target="tpu_custom_call" | custom-call | flops 1660944384 | bytes 8388608 | tf_op jit(solution)/shard_map/attend_forward/pallas_call | solution.py:965
  186.2 3.8 collective-permute-start.1
  190.0 2.7 back.1
  192.7 4.0 collective-permute-start.2
  196.8 0.1 collective-permute-done.1.away_ref
  196.9 0.0 copy-start
  196.9 0.6 copy-done
  197.5 1.6 mixed.1.refs_1_.mixed_ref
  199.1 4.1 collective-permute-done.2.g_away
  203.3 0.0 copy-start.4
  203.3 0.7 copy-done.4
  203.9 16.8 %attend_backward.2 = (f32[128,384]{1,0:T(8,128)}, bf16[128,384]{1,0:T(8,128)(2,1)}, bf16[4096,384]{1,0:T(8,128)(2,1)}, bf16[4096,384]{1,0:T(8,128)(2,1)}) custom-call(s32[1]{0:T(128)} %bitcast.2.ctx_ref, bf16[128,384]{1,0:T(8,128)(2,1)} %get-tuple-element.131.q_own, bf16[128,384]{1,0:T(8,128)(2,1)} %get-tuple-element.137.q_away, bf16[4096,384]{1,0:T(8,128)(2,1)} %bitcast.46, ...), custom_call_target="tpu_custom_call" | custom-call | flops 4152360960 | bytes 16777216 | tf_op jit(solution)/shard_map/attend_backward/pallas_call | solution.py:1062
  220.8 55.4 %scatter_pair_1.1 = (f32[2,128,384]{2,1,0:T(8,128)}, f32[128,768]{1,0:T(8,128)}, bf16[2,128,384]{2,1,0:T(8,128)(2,1)}, bf16[128,384]{1,0:T(8,128)(2,1)}, bf16[51...) custom-call(bf16[32,128,384]{2,1,0:T(8,128)(2,1)} %bitcast.39, ...), custom_call_target="tpu_custom_call" | custom-call | tf_op jit(solution)/shard_map/scatter_pair_1/pallas_call | solution.py:566
  276.2 7.2 %join_1.1 = (bf16[128,2304]{1,0:T(8,128)(2,1)}, bf16[16,768]{1,0:T(8,128)(2,1)}, f32[128,768]{1,0:T(8,128)}, bf16[128,768]{1,0:T(8,128)(2,1)}, bf16[128,384]{1,0:T(8,128)(2,1)}, /*index=5*/bf16[128,384]{1,0:T(8,128)(2,1)}) custom-call(s32[1]{0:T(128)} %bitcast.upper_ref, f32[2,128,384]{2,1,0:T(8,128)} %get-tuple-element.156.own_ref, ...), custom_call_target="tpu_custom_call" | custom-call | flops 452984832 | bytes 3538944 | tf_op jit(solution)/shard_map/join_1/pallas_call | solution.py:1325
  283.4 6.3 %collective-permute-start.3 = (bf16[128,384]{1,0:T(8,128)(2,1)}, bf16[128,384]{1,0:T(8,128)(2,1)S(1)}, u32[]{:S(2)}, u32[]{:S(2)}) collective-permute-start(bf16[128,384]{1,0:T(8,128)(2,1)} %get-tuple-element.162), channel_id=1, source_target_pairs={{0,31},{1,30},{2,29},{3,28},{4,27},{5,26},{6,25},{7,24},{8,23},{9,... | collective-permute-start | bytes 294920 | tf_op jit(solution)/shard_map/ppermute | solution.py:31
  289.7 2.6 last.1
  292.3 1.7 collective-permute-done.3.g_away
  294.0 0.0 copy-start.3
  294.0 0.6 copy-done.3
  294.6 16.7 %attend_backward.3 = (f32[128,384]{1,0:T(8,128)}, bf16[128,384]{1,0:T(8,128)(2,1)}, bf16[4096,384]{1,0:T(8,128)(2,1)}, bf16[4096,384]{1,0:T(8,128)(2,1)}) custom-call(s32[1]{0:T(128)} %bitcast.2.ctx_ref, bf16[128,384]{1,0:T(8,128)(2,1)} %get-tuple-element.112.q_own, bf16[128,384]{1,0:T(8,128)(2,1)} %get-tuple-element.118.q_away, bf16[4096,384]{1,0:T(8,128)(2,1)} %bitcast.42, ...), custom_call_target="tpu_custom_call" | custom-call | flops 4152360960 | bytes 16777216 | tf_op jit(solution)/shard_map/attend_backward/pallas_call | solution.py:1062
  311.3 55.0 %scatter_pair_0.1 = (f32[2,128,384]{2,1,0:T(8,128)}, f32[128,768]{1,0:T(8,128)}, bf16[2,128,384]{2,1,0:T(8,128)(2,1)}, bf16[128,384]{1,0:T(8,128)(2,1)}, bf16[51...) custom-call(bf16[32,128,384]{2,1,0:T(8,128)(2,1)} %bitcast.37, ...), custom_call_target="tpu_custom_call" | custom-call | tf_op jit(solution)/shard_map/scatter_pair_0/pallas_call | solution.py:566
  366.3 5.5 %join_0.1 = (bf16[128,2304]{1,0:T(8,128)(2,1)}, bf16[16,768]{1,0:T(8,128)(2,1)}, f32[128,768]{1,0:T(8,128)}) custom-call(s32[1]{0:T(128)} %bitcast.upper_ref, f32[2,128,384]{2,1,0:T(8,128)} %get-tuple-element.175.own_ref, bf16[2,128,384]{2,1,0:T(8,128)(2,1)} %get-tuple-element.176.back_ref, f32[128,384]{1,0:T(8,128)} %get-tuple-element.177.own_q, ...), custom_call_target="tpu_custom_call" | custom-call | flops 452984832 | bytes 3538944 | tf_op jit(solution)/shard_map/join_0/pallas_call | solution.py:1325
  371.8 105.0 %sum_over_ctx.1 = (bf16[2,16,144,768]{3,2,1,0:T(8,128)(2,1)}, f32[2,16,768]{2,1,0:T(8,128)}) custom-call(bf16[128,2304]{1,0:T(8,128)(2,1)} %get-tuple-element.182.joined_ref, bf16[16,768]{1,0:T(8,128)(2,1)} %get-tuple-element.183.norm_ref, bf16[64,768]{1,0:T(8,128)(2,1)} %get-tuple-element.184.norm_one, bf16[512,768]{1,0:T(8,128)(2,1)} %get-tuple-element.185.refs_0_, ...), custom_call_target="tpu_custom_call" | custom-call | tf_op jit(solution)/shard_map/sum_over_ctx/pallas_call | solution.py:804
  476.8 0.8 slice_bitcast_fusion
  477.6 0.8 slice_bitcast_fusion.1
  478.4 0.8 slice.30
  479.2 7.4 %unpack.1 = (f32[2,192,2304]{2,1,0:T(8,128)}, f32[2,192,768]{2,1,0:T(8,128)}, f32[2,192,3072]{2,1,0:T(8,128)}, f32[2,768,768]{2,1,0:T(8,128)}) custom-call(bf16[2,2304,768]{2,1,0:T(8,128)(2,1)} %bitcast.36), custom_call_target="tpu_custom_call" | custom-call | tf_op jit(solution)/shard_map/unpack/pallas_call | solution.py:1309
  486.7 0.1 constant_dynamic-slice_fusion.6
  486.8 0.6 copy.41
  487.3 0.6 copy.42
  487.9 0.6 copy.43
  488.5 0.6 copy.44
  489.1 0.1 constant_dynamic-slice_fusion.4
  489.2 0.0 copy-start.2
  489.2 0.6 constant_dynamic-slice_fusion.3
  489.8 0.7 constant_dynamic-slice_fusion.5
  490.4 0.6 copy.46
  491.0 0.0 copy-done.2
  (6 shorter events, 0.0 us)
Async XLA Ops:
  105.4 11.2 %collective-permute-start = (bf16[128,384]{1,0:T(8,128)(2,1)}, bf16[128,384]{1,0:T(8,128)(2,1)S(1)}, u32[]{:S(2)}, u32[]{:S(2)}) collective-permute-start(bf16[128,384]{1,0:T(8,128)(2,1)} %get-tuple-element.122), channel_id=1, source_target_pairs={{0,31},{1,30},{2,29},{3,28},{4,27},{5,26},{6,25},{7,24},{8,23},{9,... | collective-permute-start | bytes 294920 | tf_op jit(solution)/shard_map/ppermute | solution.py:31
  116.7 0.6 copy-start.1
  186.2 10.6 %collective-permute-start.1 = (bf16[128,384]{1,0:T(8,128)(2,1)}, bf16[128,384]{1,0:T(8,128)(2,1)S(1)}, u32[]{:S(2)}, u32[]{:S(2)}) collective-permute-start(bf16[128,384]{1,0:T(8,128)(2,1)} %get-tuple-element.141), channel_id=1, source_target_pairs={{0,31},{1,30},{2,29},{3,28},{4,27},{5,26},{6,25},{7,24},{8,23},{9,... | collective-permute-start | bytes 294920 | tf_op jit(solution)/shard_map/ppermute | solution.py:31
  192.7 10.6 %collective-permute-start.2 = (bf16[128,384]{1,0:T(8,128)(2,1)}, bf16[128,384]{1,0:T(8,128)(2,1)S(1)}, u32[]{:S(2)}, u32[]{:S(2)}) collective-permute-start(bf16[128,384]{1,0:T(8,128)(2,1)} %get-tuple-element.144), channel_id=1, source_target_pairs={{0,31},{1,30},{2,29},{3,28},{4,27},{5,26},{6,25},{7,24},{8,23},{9,... | collective-permute-start | bytes 294920 | tf_op jit(solution)/shard_map/ppermute | solution.py:31
  196.9 0.6 copy-start
  203.3 0.7 copy-start.4
  283.4 10.6 %collective-permute-start.3 = (bf16[128,384]{1,0:T(8,128)(2,1)}, bf16[128,384]{1,0:T(8,128)(2,1)S(1)}, u32[]{:S(2)}, u32[]{:S(2)}) collective-permute-start(bf16[128,384]{1,0:T(8,128)(2,1)} %get-tuple-element.162), channel_id=1, source_target_pairs={{0,31},{1,30},{2,29},{3,28},{4,27},{5,26},{6,25},{7,24},{8,23},{9,... | collective-permute-start | bytes 294920 | tf_op jit(solution)/shard_map/ppermute | solution.py:31
  294.0 0.6 copy-start.3
  489.2 1.8 copy-start.2
